TPU v7x, 32 devices: a whole 2x2x4 slice. The times are simulated.
32 devices in a mesh: band: 4 (over y, x), base: 8 (over z, core).
Axes of the slice: x: 2, y: 2, z: 4, core: 2. Of those that a mesh axis runs over, the one named last changes fastest.
Arguments:
- visibilities: bfloat16 [8, 16, 256, 256], P(None, 'base', 'band'), may hold values from -6 to 6
- model: bfloat16 [8, 16, 256, 256], P(None, 'base', 'band'), may hold values from -6 to 6
- start_gains: float32 [8, 128, 512], P(None, 'band', 'base'), may hold values from -1.5 to 2.5
- penalty: float32 [512], P('base'), may hold values from 0.5 to 5
- pairs: int32 [16, 2], P('base'), may hold values from 0 to 31, as said below
- flags: int32 [16, 256], P('base'), may hold values 0 or 1
- chan_band: int32 [256], P('band'), may hold values from 0 to 127, as said below
Outputs:
- gains: float32 [8, 128, 512], P(None, 'band', 'base')
- coefficients: float32 [8, 9, 512], P(None, None, 'base')
Inputs may be any that keep to these rules, and one draw needn't show every extreme that they name: `pairs`: each tile joins blocks a <= b, and no two tiles join the same pair of blocks. `chan_band`: the 64 channels of the k-th block of 64 channels map, never falling, onto the intervals k * 32 to k * 32 + 31, each interval holding one channel or more.
All inputs are finite; a program needn't handle non-finite values. No bound on the sum of `flags` on one device may be relied on, other than what follows from the above.
Results may differ from a plain program's by a relative error of at most 0.0003.
Values sent between devices are 32-bit elements; how exact they have to be, the bound alone decides.
No kernel may reach another device: no remote copies, remote signals or barrier semaphores. Data moves between devices by JAX's collectives and lax.ppermute only.
A program may use at most 128 MiB of HBM per device.

v0:
```python
import functools

import jax
import jax.numpy as jnp
from jax import lax
from jax.experimental import pallas as pl
from jax.experimental.pallas import tpu as pltpu
from jax.sharding import PartitionSpec as P

BLOCK = 16
NPOLY = 9
KPAD = 16
ITERS = 3
LANES = 128
F32 = jnp.float32
BF16 = jnp.bfloat16
HIGH = lax.Precision.HIGHEST

ridge = 0.5

GAIN_ROWS = 8 * BLOCK
TERM_ROWS = 12 * BLOCK


def nt(left, right, **kw):
    return lax.dot_general(
        left, right, (((1,), (1,)), ((), ())), preferred_element_type=F32, **kw
    )


def nn(left, right, **kw):
    return lax.dot_general(
        left, right, (((1,), (0,)), ((), ())), preferred_element_type=F32, **kw
    )


def pick(values, select, dot=nt):
    high = values.astype(BF16)
    low = (values - high.astype(F32)).astype(BF16)
    rows = values.shape[0]
    out = dot(jnp.concatenate([high, low], 0), select)
    return out[:rows] + out[rows:]


def iota(shape, axis):
    return lax.broadcasted_iota(jnp.int32, shape, axis)


def mul(a, b):
    re, im = [], []
    for r in range(2):
        for c in range(2):
            re.append(
                (a[2 * r] * b[c] + a[2 * r + 1] * b[2 + c])
                - (a[4 + 2 * r] * b[4 + c] + a[5 + 2 * r] * b[6 + c])
            )
            im.append(
                (a[2 * r] * b[4 + c] + a[2 * r + 1] * b[6 + c])
                + (a[4 + 2 * r] * b[c] + a[5 + 2 * r] * b[2 + c])
            )
    return re + im


def mul_herm(a, b):
    re, im = [], []
    for r in range(2):
        for c in range(2):
            re.append(
                (a[2 * r] * b[2 * c] + a[2 * r + 1] * b[2 * c + 1])
                + (a[4 + 2 * r] * b[4 + 2 * c] + a[5 + 2 * r] * b[5 + 2 * c])
            )
            im.append(
                (a[4 + 2 * r] * b[2 * c] + a[5 + 2 * r] * b[2 * c + 1])
                - (a[2 * r] * b[4 + 2 * c] + a[2 * r + 1] * b[5 + 2 * c])
            )
    return re + im


def herm_mul(a, b):
    re, im = [], []
    for r in range(2):
        for c in range(2):
            re.append(
                (a[r] * b[c] + a[2 + r] * b[2 + c]) + (a[4 + r] * b[4 + c] + a[6 + r] * b[6 + c])
            )
            im.append(
                (a[r] * b[4 + c] + a[2 + r] * b[6 + c]) - (a[4 + r] * b[c] + a[6 + r] * b[2 + c])
            )
    return re + im


def outer_rows(c):
    return [
        (c[0] * c[0] + c[1] * c[1]) + (c[4] * c[4] + c[5] * c[5]),
        (c[2] * c[2] + c[3] * c[3]) + (c[6] * c[6] + c[7] * c[7]),
        (c[0] * c[2] + c[1] * c[3]) + (c[4] * c[6] + c[5] * c[7]),
        (c[4] * c[2] + c[5] * c[3]) - (c[0] * c[6] + c[1] * c[7]),
    ]


def outer_columns(d):
    return [
        (d[0] * d[0] + d[2] * d[2]) + (d[4] * d[4] + d[6] * d[6]),
        (d[1] * d[1] + d[3] * d[3]) + (d[5] * d[5] + d[7] * d[7]),
        (d[0] * d[1] + d[2] * d[3]) + (d[4] * d[5] + d[6] * d[7]),
        (d[0] * d[5] + d[2] * d[7]) - (d[4] * d[1] + d[6] * d[3]),
    ]


def slot_key(index, pairs, scale, intervals):
    at = index // intervals
    tiles = len(pairs)
    block = jnp.zeros(index.shape, F32)
    for slot in range(2 * tiles):
        value = pairs[slot % tiles][slot // tiles]
        block = jnp.where(at == slot, value.astype(F32), block)
    if scale > 1:
        block = block * scale + (index % intervals).astype(F32)
    return block


def scalar_pairs(pair_ref):
    return [[pair_ref[t, side] for side in range(2)] for t in range(pair_ref.shape[0])]


def owner_key(index, me, blocks, intervals, none, scale=None):
    at = index // intervals
    key = me * blocks + at
    if scale != 1:
        key = key * intervals + index % intervals
    return jnp.where(at < blocks, key, none).astype(F32)


def cell_weights(pairs, flags):
    cells = flags.shape[1]
    cell = iota((1, cells), 1)
    diagonal = (cell // BLOCK == cell % BLOCK).astype(F32)
    rows = []
    for t, pair in enumerate(pairs):
        same = (pair[0] == pair[1]).astype(F32)
        rows.append(flags[t : t + 1, :] * (1.0 - same * diagonal))
    return rows


def greet_kernel(
    blocks, intervals, pair_hbm, start_hbm, penalty_hbm, flag_hbm, out_ref, top_ref, pair_ref, start_ref,
    penalty_ref, flag_ref, sems
):
    copies = [
        pltpu.make_async_copy(source, target, sems.at[n])
        for n, (source, target) in enumerate(
            [
                (start_hbm, start_ref),
                (pair_hbm, pair_ref),
                (flag_hbm, flag_ref),
                (penalty_hbm, penalty_ref),
            ]
        )
    ]
    for copy in copies:
        copy.start()
    for copy in copies[1:]:
        copy.wait()
    owned = blocks * BLOCK
    cells = flag_ref.shape[1]
    me = lax.axis_index("base")
    pairs = scalar_pairs(pair_ref)
    tiles = len(pairs)
    weights = cell_weights(pairs, flag_ref[...].astype(F32))
    lane = iota((cells, LANES), 1)
    cell = iota((cells, LANES), 0)
    at, inside = lane // BLOCK, lane % BLOCK
    member = jnp.where(at < tiles, cell // BLOCK, cell % BLOCK) == inside
    station_w = jnp.zeros((8, LANES), F32)
    for t in range(tiles):
        fold = (member & (at % tiles == t) & (at < 2 * tiles)).astype(BF16)
        station_w = station_w + nn(jnp.broadcast_to(weights[t], (8, cells)).astype(BF16), fold)
    lane = iota((8, LANES), 1)
    row = iota((8, LANES), 0)
    wide = intervals // BLOCK
    slot_at = jnp.where(lane // BLOCK < 2 * tiles, slot_key(lane * wide, pairs, 1, intervals), -2.0)
    owner_at = jnp.where(lane // BLOCK < blocks, (me * blocks + lane // BLOCK).astype(F32), -2.0)
    keys = jnp.where(row == 0, slot_key(lane, pairs, intervals, intervals), 0.0)
    keys = jnp.where(row == 1, owner_key(lane, me, blocks, intervals, -2), keys)
    keys = jnp.where(row == 3, owner_at, keys)
    keys = jnp.where(row == 4, station_w, keys)
    out_ref[GAIN_ROWS:, :] = jnp.where(row == 5, slot_at, keys)
    out_ref[GAIN_ROWS + 2 : GAIN_ROWS + 3, :owned] = penalty_ref[...]
    copies[0].wait()
    place = (iota((BLOCK, owned), 0) == iota((BLOCK, owned), 1) % BLOCK).astype(BF16)
    here = iota((LANES, owned), 0) // intervals == iota((LANES, owned), 1) // BLOCK
    for m in range(8):
        plane = start_ref[m]
        plane = jnp.where(here, jnp.concatenate([plane] * (LANES // intervals), 0), 0.0)
        high = plane.astype(BF16)
        low = (plane - high.astype(F32)).astype(BF16)
        plane = nt(place, high) + nt(place, low)
        out_ref[m * BLOCK : (m + 1) * BLOCK, :] = plane
        if (m + 1) * BLOCK <= top_ref.shape[0]:
            top_ref[m * BLOCK : (m + 1) * BLOCK, :] = plane


def prepare_kernel(
    blocks, intervals, bands, pair_ref, chan_ref, vis_ref, model_ref, flag_ref, vt_ref, mt_ref,
    key_ref, at_ref, basis_ref, chans_ref, expand_ref
):
    planes, width, cells = vis_ref.shape
    pairs = scalar_pairs(pair_ref)
    tiles = len(pairs)
    channels = width // tiles
    me = lax.axis_index("base")
    row = iota((2 * LANES, LANES), 0)
    lane = iota((2 * LANES, LANES), 1)
    for ref, scale in ((key_ref, intervals), (at_ref, 1)):
        ref[...] = jnp.where(
            row < LANES,
            slot_key(row, pairs, scale, intervals),
            owner_key(row - LANES, me, blocks, intervals, -1, scale),
        )
    band_at = lax.axis_index("band")
    local = chan_ref[...] - band_at * intervals
    chan = (band_at * channels + iota((1, channels), 1)).astype(F32)
    xpos = -1.0 + (2.0 * chan + 1.0) / (channels * bands)
    member = (iota((2 * LANES, channels), 0) % intervals == local).astype(F32)
    chans = jnp.sum(member, 1, keepdims=True)
    chans_ref[...] = nt(jnp.ones((8, channels), BF16), member.astype(BF16))
    centre = jnp.sum(member * xpos, 1, keepdims=True) / chans
    terms = [jnp.ones((2 * LANES, LANES), F32), jnp.broadcast_to(centre, (2 * LANES, LANES))]
    for order in range(2, NPOLY):
        terms.append(2.0 * terms[1] * terms[-1] - terms[-2])
    basis = jnp.zeros((2 * LANES, LANES), F32)
    for order in range(NPOLY):
        basis = jnp.where(lane % KPAD == order, terms[order], basis)
    basis_ref[...] = jnp.where(row // intervals == lane // KPAD, basis, 0.0)
    row = iota((LANES, 2 * width), 0)
    lane = iota((LANES, 2 * width), 1)
    wide = jnp.concatenate([local] * (2 * tiles), 1)
    expand = (row // intervals == lane // channels) & (row % intervals == wide)
    expand_ref[...] = expand.astype(BF16)
    ident = (iota((cells, cells), 0) == iota((cells, cells), 1)).astype(BF16)
    rows = cell_weights(pairs, flag_ref[...].astype(F32))
    weight = jnp.concatenate([jnp.broadcast_to(w, (channels, cells)) for w in rows], 0)
    for m in range(planes):
        vt_ref[m] = nt(ident, vis_ref[m]).reshape(BLOCK, BLOCK, width)
        masked = (model_ref[m].astype(F32) * weight).astype(BF16)
        mt_ref[m] = nt(ident, masked).reshape(BLOCK, BLOCK, width)


def tie_kernel(*refs):
    pass


def hand_on_kernel(whole_ref, *refs):
    out_ref = refs[-1]
    out_ref[...] = whole_ref[whole_ref.shape[0] - out_ref.shape[0] :, :]


def hand_on(whole, rows, others):
    vmem = pl.BlockSpec(memory_space=pltpu.VMEM)
    return pl.pallas_call(
        hand_on_kernel,
        out_shape=jax.ShapeDtypeStruct((rows, whole.shape[1]), whole.dtype),
        in_specs=[vmem] + [pl.BlockSpec(memory_space=pl.ANY)] * len(others),
        out_specs=vmem,
        compiler_params=pltpu.CompilerParams(vmem_limit_bytes=1024 * 1024),
    )(whole, *others)


def after(values, others):
    place = pl.BlockSpec(memory_space=pl.ANY)
    return pl.pallas_call(
        tie_kernel,
        out_shape=[jax.ShapeDtypeStruct(x.shape, x.dtype) for x in values],
        in_specs=[place] * (len(values) + len(others)),
        out_specs=[place] * len(values),
        input_output_aliases={n: n for n in range(len(values))},
        compiler_params=pltpu.CompilerParams(vmem_limit_bytes=1024 * 1024),
    )(*values, *others)


def normal_terms(gains, vt_ref, mt_ref, expand, first_s, second_s, a_s, b_s):
    wide = pick(gains, expand, nn)
    width = wide.shape[1] // 2
    first_s[...] = wide[:, :width].reshape(8, BLOCK, width)
    second_s[...] = wide[:, width:].reshape(8, BLOCK, width)
    half = BLOCK // 2

    def step(i, totals):
        partial = None
        new = []
        first = [first_s[m, pl.ds(i, 1), :] for m in range(8)]
        vis_all = [vt_ref[m, i].astype(F32) for m in range(8)]
        mdl_all = [mt_ref[m, i].astype(F32) for m in range(8)]
        for h in range(2):
            at = slice(h * half, (h + 1) * half)
            vis = [x[at] for x in vis_all]
            mdl = [x[at] for x in mdl_all]
            second = [second_s[m, at, :] for m in range(8)]
            along = mul_herm(mdl, second)
            terms = mul_herm(vis, along) + outer_rows(along)
            partial = terms if partial is None else [x + y for x, y in zip(partial, terms)]
            back = mul(first, mdl)
            terms = herm_mul(vis, back) + outer_columns(back)
            new += [x + y for x, y in zip(totals[12 * h : 12 * (h + 1)], terms)]
        for k in range(12):
            a_s[k, pl.ds(i, 1), :] = jnp.sum(partial[k], 0, keepdims=True)
        return tuple(new)

    zero = jnp.zeros((half, width), F32)
    totals = lax.fori_loop(0, BLOCK, step, (zero,) * 24)
    for h in range(2):
        for k in range(12):
            b_s[k, h * half : (h + 1) * half, :] = totals[12 * h + k]
    return jnp.concatenate(
        [a_s[...].reshape(TERM_ROWS, width), b_s[...].reshape(TERM_ROWS, width)], 1
    )


def key_match(rows, lanes):
    count = lanes.shape[1] // LANES
    return (jnp.concatenate([rows] * count, 1) == lanes).astype(BF16)


def beside(refs, form):
    refs = list(refs)
    pieces = []
    for parts in form:
        part = [refs.pop(0)[...] for _ in range(parts)]
        pieces.append(part[0] if parts == 1 else jnp.concatenate(part, 0))
    return jnp.concatenate(pieces, 1), refs


def first_kernel(form, *refs):
    every, refs = beside(refs, form)
    key_ref, expand_ref, vt_ref, mt_ref, gains_ref, out_ref, top_ref = refs[:7]
    scratch = refs[7:]
    select = key_match(key_ref[:LANES, :], every[GAIN_ROWS + 1 : GAIN_ROWS + 2])
    gains = pick(every[:GAIN_ROWS], select)
    gains_ref[...] = gains
    expand = expand_ref[...]
    terms = pick(normal_terms(gains, vt_ref, mt_ref, expand, *scratch), expand)
    out_ref[...] = terms
    top_ref[...] = terms[: top_ref.shape[0]]


def state_kernel(form, blocks, intervals, *refs):
    every, refs = beside(refs, form)
    key_ref, at_ref, gains_ref, chans_ref, z_ref, pen_ref, scale_ref, select_ref = refs
    rows = every[GAIN_ROWS:]
    z_ref[:, :LANES] = gains_ref[...]
    z_ref[:, LANES:] = every[:GAIN_ROWS, :LANES]
    select_ref[...] = key_match(key_ref[...], rows[0:1])
    lanes = rows.shape[1]
    diagonal = iota((BLOCK, lanes), 0) == iota((BLOCK, lanes), 1) % BLOCK
    at = at_ref[...]
    pen = pick(jnp.where(diagonal, rows[2:3], 0.0), key_match(at, rows[3:4]))
    unused = iota(pen.shape, 1) >= LANES + blocks * intervals
    pen_ref[...] = jnp.where(unused, 1.0, pen)
    weights = pick(jnp.where(diagonal, rows[4:5], 0.0), key_match(at, rows[5:6]))
    scale_ref[...] = 1.0 / jnp.maximum(weights * chans_ref[0:1, :], 1.0)


def solve(normal, scale, pen, consensus):
    part = [normal[BLOCK * k : BLOCK * (k + 1)] * scale for k in range(12)]
    rhs = [part[m] + pen * consensus[BLOCK * m : BLOCK * (m + 1)] for m in range(8)]
    h_first = part[8] + pen
    h_second = part[9] + pen
    h_real, h_imag = part[10], part[11]
    determ = h_first * h_second - h_real * h_real - h_imag * h_imag
    over = 1.0 / determ
    d_first, d_second = h_first * over, h_second * over
    d_real, d_imag = h_real * over, h_imag * over
    out = [None] * 8
    for r in range(2):
        x_re, y_re = rhs[2 * r], rhs[2 * r + 1]
        x_im, y_im = rhs[4 + 2 * r], rhs[5 + 2 * r]
        out[2 * r] = x_re * d_second - (y_re * d_real + y_im * d_imag)
        out[4 + 2 * r] = x_im * d_second - (y_im * d_real - y_re * d_imag)
        out[2 * r + 1] = y_re * d_first - (x_re * d_real - x_im * d_imag)
        out[5 + 2 * r] = y_im * d_first - (x_im * d_real + x_re * d_imag)
    return jnp.concatenate(out, 0)


def step_kernel(form, *refs):
    every, refs = beside(refs, form)
    select_ref, z_ref, pen_ref, scale_ref, expand_ref, vt_ref, mt_ref = refs[:7]
    gains_ref, out_ref, top_ref = refs[7:10]
    scratch = refs[10:]
    normal = pick(every, select_ref[...])
    gains = solve(normal, scale_ref[...], pen_ref[...], z_ref[...])
    gains_ref[...] = gains
    expand = expand_ref[...]
    terms = pick(normal_terms(gains[:, :LANES], vt_ref, mt_ref, expand, *scratch), expand)
    out_ref[...] = terms
    top_ref[...] = terms[: top_ref.shape[0]]


def first_total_kernel(gains_ref, basis_ref, out_ref):
    basis = basis_ref[...]
    total = nn(gains_ref[...], basis, precision=HIGH)
    part = basis[: basis.shape[0] // 8]
    gram = lax.dot_general(
        part, part, (((0,), (0,)), ((), ())), preferred_element_type=F32, precision=HIGH
    )
    out_ref[:GAIN_ROWS, :] = total
    out_ref[GAIN_ROWS:, :] = gram[:KPAD]


def total_kernel(gains_ref, dual_ref, basis_ref, out_ref):
    out_ref[...] = nn(gains_ref[...] + dual_ref[...], basis_ref[...], precision=HIGH)


def invert(gram):
    row, lane = iota(gram.shape, 0), iota(gram.shape, 1)
    inner = (row < NPOLY) & (lane < NPOLY)
    work = jnp.where(inner, gram + jnp.where(row == lane, ridge, 0.0), 0.0)
    for p in range(NPOLY):
        here = lane == p
        column = jnp.sum(jnp.where(here, work, 0.0), 1, keepdims=True)
        over = 1.0 / column[p : p + 1]
        pivot = jnp.where(here[:1], over, work[p : p + 1] * over)
        work = jnp.where(row == p, pivot, jnp.where(here, 0.0, work) - column * pivot)
    return work


def settle(total, inverse, basis_ref, gains, z_ref, dual_ref):
    coeff = nn(total, inverse, precision=HIGH)
    consensus = nt(coeff, basis_ref[...], precision=HIGH)
    z_ref[...] = 2.0 * consensus - gains
    dual_ref[...] = gains - consensus


def band_total(refs):
    totals = [ref[...] for ref in refs]
    while len(totals) > 1:
        totals = [totals[n] + totals[n + 1] for n in range(0, len(totals), 2)]
    return totals[0]


def first_consensus_kernel(
    one_ref, two_ref, gains_ref, basis_ref, z_ref, dual_ref, inverse_ref
):
    total = one_ref[...] + two_ref[...]
    small = invert(total[GAIN_ROWS:])
    row, lane = iota((LANES, LANES), 0), iota((LANES, LANES), 1)
    spread = ((row == lane % KPAD) & (row < KPAD)).astype(F32)
    wide = nn(jnp.concatenate([small] * (LANES // KPAD), 0), spread, precision=HIGH)
    inverse = jnp.where(row // KPAD == lane // KPAD, wide, 0.0)
    inverse_ref[...] = inverse
    settle(total[:GAIN_ROWS], inverse, basis_ref, gains_ref[...], z_ref, dual_ref)


def consensus_kernel(
    one_ref, two_ref, gains_ref, old_ref, basis_ref, inverse_ref, z_ref, dual_ref
):
    total = one_ref[...] + two_ref[...]
    gains = gains_ref[...] + old_ref[...]
    settle(total, inverse_ref[...], basis_ref, gains, z_ref, dual_ref)


def last_kernel(form, *refs):
    every, refs = beside(refs, form)
    select_ref, z_ref, pen_ref, scale_ref, dual_ref, basis_ref, gains_ref, out_ref = refs
    own = slice(LANES, 2 * LANES)
    normal = pick(every, select_ref[own, :])
    gains = solve(normal, scale_ref[:, own], pen_ref[:, own], z_ref[:, own])
    gains_ref[...] = gains
    total = nn(gains + dual_ref[:, own], basis_ref[own, :], precision=HIGH)
    half = GAIN_ROWS // 2
    low = iota((half, LANES), 1) < LANES // 2
    out_ref[...] = jnp.where(low, pltpu.roll(total[:half], LANES // 2, 1), total[half:])


def gains_kernel(blocks, intervals, gains_ref, out_ref):
    owned = blocks * BLOCK
    place = (iota((intervals, LANES), 0) == iota((intervals, LANES), 1) % intervals).astype(BF16)
    here = iota((owned, LANES), 0) // BLOCK == iota((owned, LANES), 1) // intervals
    for m in range(8):
        part = gains_ref[m * BLOCK : (m + 1) * BLOCK, :]
        out_ref[m] = turn(place, jnp.where(here, jnp.concatenate([part] * blocks, 0), 0.0))


def turn(place, values):
    high = values.astype(BF16)
    rest = values - high.astype(F32)
    mid = rest.astype(BF16)
    low = (rest - mid.astype(F32)).astype(BF16)
    return (nt(place, high) + nt(place, mid)) + nt(place, low)


def coefficient_kernel(bands, blocks, *refs):
    inverse_ref, out_ref = refs[bands:]
    coeff = nn(band_total(refs[:bands]), inverse_ref[...], precision=HIGH)
    owned = blocks * BLOCK
    place = (iota((KPAD, LANES), 0) == iota((KPAD, LANES), 1) % KPAD).astype(BF16)
    for m in range(8):
        first = (m // 4) * (LANES // 2 // KPAD)
        here = iota((owned, LANES), 0) // BLOCK == iota((owned, LANES), 1) // KPAD - first
        part = coeff[(m % 4) * BLOCK : (m % 4 + 1) * BLOCK]
        part = jnp.where(here, jnp.concatenate([part] * blocks, 0), 0.0)
        out_ref[:, m, :] = turn(place, part)[:NPOLY]


def call(kernel, operands, shapes, scratch=(), smem=0, held=False, flops=20_000_000, moved=None):
    vmem = pl.BlockSpec(memory_space=pltpu.VMEM)
    in_specs = [pl.BlockSpec(memory_space=pltpu.SMEM)] * smem + [vmem] * (len(operands) - smem)
    params = pltpu.CompilerParams(vmem_limit_bytes=12 * 1024 * 1024)
    if held:
        in_specs = [pl.BlockSpec(memory_space=pl.ANY)] * len(operands)
        params = pltpu.CompilerParams()
    if moved is None:
        moved = sum(x.size * x.dtype.itemsize for x in (*operands, *shapes))
    return pl.pallas_call(
        kernel,
        out_shape=shapes,
        in_specs=in_specs,
        out_specs=[vmem] * len(shapes),
        scratch_shapes=list(scratch),
        compiler_params=params,
        cost_estimate=pl.CostEstimate(flops=flops, bytes_accessed=moved, transcendentals=0),
    )(*operands)


def share_base(x, top, early=(), late=(), first=False):
    devices = lax.axis_size("base")
    chips = devices // 2

    def along(y, k):
        return lax.ppermute(y, "base", [(d, d ^ (2 * k)) for d in range(devices)])

    if chips == 4:
        two = along(x, 2)
        far = along(top, 3)
        one = along(x, 1)
        rest = along(hand_on(two, x.shape[0] - top.shape[0], early), 1)
        if first:
            (one,) = after([one], (far,))
        if late:
            (rest,) = after([rest], late)
        mine, form = [x, one, two, far, rest], [1, 1, 1, 2]
    else:
        mine = {0: x}
        step = chips // 2
        while step:
            for k in sorted(mine):
                mine[k + step] = along(mine[k], step)
            if early:
                (mine[step],) = after([mine[step]], early)
                early = ()
            step //= 2
        if late:
            (mine[chips - 1],) = after([mine[chips - 1]], late)
        mine, form = [mine[k] for k in sorted(mine)], [1] * chips
    other = [lax.ppermute(y, "base", [(d, d ^ 1) for d in range(devices)]) for y in mine]
    return mine + other, form + form


def share_band(x):
    devices = lax.axis_size("band")
    return [x] + [
        lax.ppermute(x, "band", [(d, d ^ k) for d in range(devices)]) for k in range(1, devices)
    ]


def sum_band(x):
    devices = lax.axis_size("band")
    step, came = 1, []
    while 2 * step < devices:
        came.append(lax.ppermute(x, "band", [(d, d ^ step) for d in range(devices)]))
        x = x + came[-1]
        step = 2 * step
    return (x, lax.ppermute(x, "band", [(d, d ^ step) for d in range(devices)])), came[:1]


def on_device(visibilities, model, start_gains, penalty, pairs, flags, chan_band):
    tiles, channels, cells = visibilities.shape[1:]
    intervals = start_gains.shape[1]
    owned = start_gains.shape[2]
    blocks = owned // BLOCK
    count = lax.axis_size("base")
    bands = lax.axis_size("band")
    width = tiles * channels

    def shape(*extent, dtype=F32):
        return jax.ShapeDtypeStruct(extent, dtype)

    wide = shape(GAIN_ROWS, 2 * LANES)
    narrow = shape(GAIN_ROWS, LANES)
    single = shape(BLOCK, 2 * LANES)
    messages = [shape(TERM_ROWS, LANES), shape(TERM_ROWS // 2, LANES)]
    square = shape(2 * LANES, LANES)
    planes = shape(8, BLOCK, BLOCK, width)

    greeting, top = call(
        functools.partial(greet_kernel, blocks, intervals),
        (pairs, start_gains, penalty.reshape(1, owned), flags),
        [shape(GAIN_ROWS + 8, LANES), shape(GAIN_ROWS // 2, LANES)],
        [
            pltpu.SMEM(pairs.shape, jnp.int32),
            pltpu.VMEM(start_gains.shape, F32),
            pltpu.VMEM((1, owned), F32),
            pltpu.VMEM(flags.shape, jnp.int32),
            pltpu.SemaphoreType.DMA((4,)),
        ],
        held=True,
    )
    vt, mt, keys, at, basis, chans, expand = call(
        functools.partial(prepare_kernel, blocks, intervals, bands),
        (
            pairs,
            chan_band.reshape(1, channels),
            visibilities.reshape(8, width, cells),
            model.reshape(8, width, cells),
            flags,
        ),
        [
            planes,
            planes,
            square,
            square,
            square,
            shape(8, 2 * LANES),
            shape(LANES, 2 * width, dtype=BF16),
        ],
        smem=1,
        moved=100_000,
    )
    greetings, form = share_base(greeting, top, early=(chans,), first=True)
    scratch = [pltpu.VMEM((8, BLOCK, width), F32)] * 2 + [pltpu.VMEM((12, BLOCK, width), F32)] * 2

    gains, *message = call(
        functools.partial(first_kernel, form),
        (*greetings, keys, expand, vt, mt),
        [narrow, *messages],
        scratch,
    )
    z, pen, scale, select = call(
        functools.partial(state_kernel, form, blocks, intervals),
        (*greetings, keys, at, gains, chans),
        [wide, single, single, shape(2 * LANES, count * LANES, dtype=BF16)],
    )
    pieces, form = share_base(*message, early=(scale,))
    gains, *message = call(
        functools.partial(step_kernel, form),
        (*pieces, select, z, pen, scale, expand, vt, mt),
        [wide, *messages],
        scratch,
    )
    (part,) = call(first_total_kernel, (gains, basis), [shape(GAIN_ROWS + KPAD, LANES)])
    parts, came = sum_band(part)
    z, dual, inverse = call(first_consensus_kernel, (*parts, gains, basis), [wide, wide, narrow])
    pieces, form = share_base(*message, early=came, late=(z,))
    gains, *message = call(
        functools.partial(step_kernel, form),
        (*pieces, select, z, pen, scale, expand, vt, mt),
        [wide, *messages],
        scratch,
    )
    (part,) = call(total_kernel, (gains, dual, basis), [narrow])
    parts, came = sum_band(part)
    z, dual = call(consensus_kernel, (*parts, gains, dual, basis, inverse), [wide, wide])
    pieces, form = share_base(*message, early=came, late=(z,))
    gains, part = call(
        functools.partial(last_kernel, form),
        (*pieces, select, z, pen, scale, dual, basis),
        [narrow, shape(GAIN_ROWS // 2, LANES)],
    )
    parts = share_band(part)
    (out,) = call(
        functools.partial(gains_kernel, blocks, intervals),
        (gains,),
        [shape(8, intervals, owned)],
    )
    (coefficients,) = call(
        functools.partial(coefficient_kernel, bands, blocks),
        (*parts, inverse),
        [shape(NPOLY, 8, owned)],
    )
    return (out, jnp.transpose(coefficients, (1, 0, 2)))


def solution(mesh):
    in_specs = (
        P(None, "base", "band", None),
        P(None, "base", "band", None),
        P(None, "band", "base"),
        P("base"),
        P("base", None),
        P("base", None),
        P("band"),
    )
    out_specs = (P(None, "band", "base"), P(None, None, "base"))
    return jax.shard_map(
        on_device, mesh=mesh, in_specs=in_specs, out_specs=out_specs, check_vma=False
    )
```

profile of v0, /device:TPU:0, one launch (start us, length us, event | category | flops | bytes accessed | tf_op | source)
XLA Modules:
  0.0 78.2 jit_solution(12803950983155126587)
XLA Ops:
  0.6 2.1 %shard_map.86 = (f32[136,128]{1,0:T(8,128)}, f32[64,128]{1,0:T(8,128)}) custom-call(s32[2,2]{1,0:T(2,128)} %pair_ref.1, f32[8,32,64]{2,1,0:T(8,128)} %start_hbm.1, f32[1,64]{1,0:T(1,128)} %bitcast.9, s32[2,256]{1,0:T(2,128)} %flag_ref.1), custom_call_target="tpu_custom_call" | custom-call | flops 20000000 | bytes 170256 | tf_op jit(solution)/shard_map/pallas_call | solution.py:513
  2.7 4.1 %collective-permute-start.2 = (f32[136,128]{1,0:T(8,128)}, f32[136,128]{1,0:T(8,128)S(1)}, u32[]{:S(2)}, u32[]{:S(2)}) collective-permute-start(f32[136,128]{1,0:T(8,128)} %get-tuple-element.31.refs_0_), channel_id=1, source_target_pairs={{0,4},{1,5},{2,6},{3,7},{4,0},{5,1},{6,2},{7,3},{8,12},{9,13},{10,... | collective-permute-start | bytes 208904 | tf_op jit(solution)/shard_map/ppermute | solution.py:529
  6.8 1.6 %collective-permute-start = (f32[136,128]{1,0:T(8,128)}, f32[136,128]{1,0:T(8,128)S(1)}, u32[]{:S(2)}, u32[]{:S(2)}) collective-permute-start(f32[136,128]{1,0:T(8,128)} %get-tuple-element.31.refs_0_), channel_id=1, source_target_pairs={{0,2},{1,3},{2,0},{3,1},{4,6},{5,7},{6,4},{7,5},{8,10},{9,11},{10,... | collective-permute-start | bytes 208904 | tf_op jit(solution)/shard_map/ppermute | solution.py:529
  9.1 1.0 %copy-done = bf16[8,2,64,256]{3,2,1,0:T(8,128)(2,1)S(1)} copy-done((bf16[8,2,64,256]{3,2,1,0:T(8,128)(2,1)S(1)}, bf16[8,2,64,256]{3,2,1,0:T(8,128)(2,1)}, u32[]{:S(2)}) %copy-start) | copy-done | bytes 524312
  10.1 1.0 %copy-done.1 = bf16[8,2,64,256]{3,2,1,0:T(8,128)(2,1)S(1)} copy-done((bf16[8,2,64,256]{3,2,1,0:T(8,128)(2,1)S(1)}, bf16[8,2,64,256]{3,2,1,0:T(8,128)(2,1)}, u32[]{:S(2)}) %copy-start.1) | copy-done | bytes 524312
  11.2 1.3 %shard_map.88 = (f32[8,16,16,128]{3,2,1,0:T(8,128)S(1)}, f32[8,16,16,128]{3,2,1,0:T(8,128)S(1)}, f32[256,128]{1,0:T(8,128)S(1)}, f32[256,128]{1,0:T(8,128)S(1)},...) custom-call(s32[2,2]{1,0:T(2,128)S(1)} %copy-done.4, s32[1,64]{1,0:T(1,128)S(1)} %bitcast.7, ...), custom_call_target="tpu_custom_call" | custom-call | flops 20000000 | bytes 100000 | tf_op jit(solution)/shard_map/pallas_call | solution.py:513
  14.3 2.2 %collective-permute-done.3.refs_4_ = f32[72,128]{1,0:T(8,128)S(1)} collective-permute-done((f32[72,128]{1,0:T(8,128)S(1)}, f32[72,128]{1,0:T(8,128)S(1)}, u32[]{:S(2)}, u32[]{:S(2)}) %collective-permute-start.3) | collective-permute-done | bytes 36896 | tf_op jit(solution)/shard_map/ppermute | solution.py:529
  17.9 2.5 %shard_map.90 = (f32[128,128]{1,0:T(8,128)S(1)}, f32[192,128]{1,0:T(8,128)S(1)}, f32[96,128]{1,0:T(8,128)S(1)}) custom-call(f32[136,128]{1,0:T(8,128)S(1)} %copy-done.2, f32[136,128]{1,0:T(8,128)S(1)} %shard_map.87.refs_1_, f32[136,128]{1,0:T(8,128)S(1)} %collective-permute-done.2.whole_ref.refs_2_, f32[64,128]{1,0:T(8,128)S(1)} %collective-permute-done.1.refs_1_.refs_3_, ...), custom_call_target="tpu_custom_call" | custom-call | flops 20000000 | bytes 3063808 | tf_op jit(solution)/shard_map/pallas_call | solution.py:513
  20.4 2.4 %collective-permute-start.10 = (f32[192,128]{1,0:T(8,128)S(1)}, f32[192,128]{1,0:T(8,128)S(1)}, u32[]{:S(2)}, u32[]{:S(2)}) collective-permute-start(f32[192,128]{1,0:T(8,128)S(1)} %get-tuple-element.38.refs_0_), channel_id=1, source_target_pairs={{0,4},{1,5},{2,6},{3,7},{4,0},{5,1},{6,2},{7,3},{8,12},{9,13},{10,... | collective-permute-start | bytes 294920 | tf_op jit(solution)/shard_map/ppermute | solution.py:529
  22.9 2.0 %collective-permute-start.9 = (f32[192,128]{1,0:T(8,128)S(1)}, f32[192,128]{1,0:T(8,128)S(1)}, u32[]{:S(2)}, u32[]{:S(2)}) collective-permute-start(f32[192,128]{1,0:T(8,128)S(1)} %get-tuple-element.38.refs_0_), channel_id=1, source_target_pairs={{0,2},{1,3},{2,0},{3,1},{4,6},{5,7},{6,4},{7,5},{8,10},{9,11},{10,... | collective-permute-start | bytes 294920 | tf_op jit(solution)/shard_map/ppermute | solution.py:529
  25.4 3.7 %collective-permute-done.10.whole_ref.refs_2_ = f32[192,128]{1,0:T(8,128)S(1)} collective-permute-done((f32[192,128]{1,0:T(8,128)S(1)}, f32[192,128]{1,0:T(8,128)S(1)}, u32[]{:S(2)}, u32[]{:S(2)}) %collective-permute-start.10) | collective-permute-done | bytes 98336 | tf_op jit(solution)/shard_map/ppermute | solution.py:529
  30.9 2.3 %collective-permute-done.12.refs_4_ = f32[96,128]{1,0:T(8,128)S(1)} collective-permute-done((f32[96,128]{1,0:T(8,128)S(1)}, f32[96,128]{1,0:T(8,128)S(1)}, u32[]{:S(2)}, u32[]{:S(2)}) %collective-permute-start.12) | collective-permute-done | bytes 49184 | tf_op jit(solution)/shard_map/ppermute | solution.py:529
  33.2 1.2 %collective-permute-done.17.refs_9_ = f32[96,128]{1,0:T(8,128)S(1)} collective-permute-done((f32[96,128]{1,0:T(8,128)S(1)}, f32[96,128]{1,0:T(8,128)S(1)}, u32[]{:S(2)}, u32[]{:S(2)}) %collective-permute-start.17) | collective-permute-done | bytes 49184 | tf_op jit(solution)/shard_map/ppermute | solution.py:554
  34.4 2.7 %shard_map.93 = (f32[128,256]{1,0:T(8,128)S(1)}, f32[192,128]{1,0:T(8,128)S(1)}, f32[96,128]{1,0:T(8,128)S(1)}) custom-call(f32[192,128]{1,0:T(8,128)S(1)} %get-tuple-element.38.refs_0_, f32[192,128]{1,0:T(8,128)S(1)} %collective-permute-done.9.refs_1_, f32[192,128]{1,0:T(8,128)S(1)} %collective-permute-done.10.whole_ref.refs_2_, ...), custom_call_target="tpu_custom_call" | custom-call | flops 20000000 | bytes 3915776 | tf_op jit(solution)/shard_map/pallas_call | solution.py:513
  37.5 1.8 %collective-permute-start.21 = (f32[144,128]{1,0:T(8,128)S(1)}, f32[144,128]{1,0:T(8,128)S(1)}, u32[]{:S(2)}, u32[]{:S(2)}) collective-permute-start(f32[144,128]{1,0:T(8,128)S(1)} %shard_map.94), channel_id=1, source_target_pairs={{0,8},{8,0},{16,24},{24,16},{1,9},{9,1},{17,25},{25,17},{2,10},{10... | collective-permute-start | bytes 221192 | tf_op jit(solution)/shard_map/ppermute | solution.py:569
  39.2 1.6 %collective-permute-start.19 = (f32[192,128]{1,0:T(8,128)S(1)}, f32[192,128]{1,0:T(8,128)S(1)}, u32[]{:S(2)}, u32[]{:S(2)}) collective-permute-start(f32[192,128]{1,0:T(8,128)S(1)} %get-tuple-element.46.refs_0_), channel_id=1, source_target_pairs={{0,4},{1,5},{2,6},{3,7},{4,0},{5,1},{6,2},{7,3},{8,12},{9,13},{10,... | collective-permute-start | bytes 294920 | tf_op jit(solution)/shard_map/ppermute | solution.py:529
  40.9 2.0 %collective-permute-start.18 = (f32[192,128]{1,0:T(8,128)S(1)}, f32[192,128]{1,0:T(8,128)S(1)}, u32[]{:S(2)}, u32[]{:S(2)}) collective-permute-start(f32[192,128]{1,0:T(8,128)S(1)} %get-tuple-element.46.refs_0_), channel_id=1, source_target_pairs={{0,2},{1,3},{2,0},{3,1},{4,6},{5,7},{6,4},{7,5},{8,10},{9,11},{10,... | collective-permute-start | bytes 294920 | tf_op jit(solution)/shard_map/ppermute | solution.py:529
  43.6 1.6 %collective-permute-start.23 = (f32[144,128]{1,0:T(8,128)S(1)}, f32[144,128]{1,0:T(8,128)S(1)}, u32[]{:S(2)}, u32[]{:S(2)}) collective-permute-start(f32[144,128]{1,0:T(8,128)S(1)} %add.6.one_ref), channel_id=1, source_target_pairs={{0,16},{8,24},{16,0},{24,8},{1,17},{9,25},{17,1},{25,9},{2,18},{10... | collective-permute-start | bytes 221192 | tf_op jit(solution)/shard_map/ppermute | solution.py:572
  45.2 2.6 %collective-permute-done.19.whole_ref.refs_2_ = f32[192,128]{1,0:T(8,128)S(1)} collective-permute-done((f32[192,128]{1,0:T(8,128)S(1)}, f32[192,128]{1,0:T(8,128)S(1)}, u32[]{:S(2)}, u32[]{:S(2)}) %collective-permute-start.19) | collective-permute-done | bytes 98336 | tf_op jit(solution)/shard_map/ppermute | solution.py:529
  49.5 1.4 %shard_map.96 = (f32[128,256]{1,0:T(8,128)S(1)}, f32[128,256]{1,0:T(8,128)S(1)}, f32[128,128]{1,0:T(8,128)S(1)}) custom-call(f32[144,128]{1,0:T(8,128)S(1)} %add.6.one_ref, f32[144,128]{1,0:T(8,128)S(1)} %collective-permute-done.23.two_ref, f32[128,256]{1,0:T(8,128)S(1)} %get-tuple-element.48.gains_ref, f32[256,128]{1,0:T(8,128)S(1)} %get-tuple-element.49.basis_ref.refs_15_), custom_call_target="tpu_custom_call" | custom-call | flops 20000000 | bytes 737280 | tf_op jit(solution)/shard_map/pallas_call | solution.py:513
  50.9 1.0 %collective-permute-done.22.refs_0_ = f32[96,128]{1,0:T(8,128)S(1)} collective-permute-done((f32[96,128]{1,0:T(8,128)S(1)}, f32[96,128]{1,0:T(8,128)S(1)}, u32[]{:S(2)}, u32[]{:S(2)}) %collective-permute-start.22) | collective-permute-done | bytes 49184 | tf_op jit(solution)/shard_map/ppermute | solution.py:529
  52.0 1.2 %collective-permute-done.28.refs_9_ = f32[96,128]{1,0:T(8,128)S(1)} collective-permute-done((f32[96,128]{1,0:T(8,128)S(1)}, f32[96,128]{1,0:T(8,128)S(1)}, u32[]{:S(2)}, u32[]{:S(2)}) %collective-permute-start.28) | collective-permute-done | bytes 49184 | tf_op jit(solution)/shard_map/ppermute | solution.py:554
  53.2 2.7 %shard_map.98 = (f32[128,256]{1,0:T(8,128)S(1)}, f32[192,128]{1,0:T(8,128)S(1)}, f32[96,128]{1,0:T(8,128)S(1)}) custom-call(f32[192,128]{1,0:T(8,128)S(1)} %get-tuple-element.46.refs_0_, f32[192,128]{1,0:T(8,128)S(1)} %collective-permute-done.18.refs_1_, f32[192,128]{1,0:T(8,128)S(1)} %collective-permute-done.19.whole_ref.refs_2_, ...), custom_call_target="tpu_custom_call" | custom-call | flops 20000000 | bytes 3915776 | tf_op jit(solution)/shard_map/pallas_call | solution.py:513
  56.8 1.9 %collective-permute-start.29 = (f32[192,128]{1,0:T(8,128)S(1)}, f32[192,128]{1,0:T(8,128)S(1)}, u32[]{:S(2)}, u32[]{:S(2)}) collective-permute-start(f32[192,128]{1,0:T(8,128)S(1)} %get-tuple-element.51.refs_0_), channel_id=1, source_target_pairs={{0,2},{1,3},{2,0},{3,1},{4,6},{5,7},{6,4},{7,5},{8,10},{9,11},{10,... | collective-permute-start | bytes 294920 | tf_op jit(solution)/shard_map/ppermute | solution.py:529
  59.5 1.5 %collective-permute-start.31 = (f32[96,128]{1,0:T(8,128)S(1)}, f32[96,128]{1,0:T(8,128)S(1)}, u32[]{:S(2)}, u32[]{:S(2)}) collective-permute-start(f32[96,128]{1,0:T(8,128)S(1)} %get-tuple-element.52), channel_id=1, source_target_pairs={{0,6},{1,7},{2,4},{3,5},{4,2},{5,3},{6,0},{7,1},{8,14},{9,15},{10,... | collective-permute-start | bytes 147464 | tf_op jit(solution)/shard_map/ppermute | solution.py:529
  61.0 2.2 %collective-permute-done.32.refs_0_ = f32[128,128]{1,0:T(8,128)S(1)} collective-permute-done((f32[128,128]{1,0:T(8,128)S(1)}, f32[128,128]{1,0:T(8,128)S(1)}, u32[]{:S(2)}, u32[]{:S(2)}) %collective-permute-start.32) | collective-permute-done | bytes 65568 | tf_op jit(solution)/shard_map/ppermute | solution.py:569
  63.3 1.6 %collective-permute-start.34 = (f32[128,128]{1,0:T(8,128)S(1)}, f32[128,128]{1,0:T(8,128)S(1)}, u32[]{:S(2)}, u32[]{:S(2)}) collective-permute-start(f32[128,128]{1,0:T(8,128)S(1)} %add.7.one_ref), channel_id=1, source_target_pairs={{0,16},{8,24},{16,0},{24,8},{1,17},{9,25},{17,1},{25,9},{2,18},{10... | collective-permute-start | bytes 196616 | tf_op jit(solution)/shard_map/ppermute | solution.py:572
  66.0 1.6 %collective-permute-done.34.two_ref = f32[128,128]{1,0:T(8,128)S(1)} collective-permute-done((f32[128,128]{1,0:T(8,128)S(1)}, f32[128,128]{1,0:T(8,128)S(1)}, u32[]{:S(2)}, u32[]{:S(2)}) %collective-permute-start.34) | collective-permute-done | bytes 65568 | tf_op jit(solution)/shard_map/ppermute | solution.py:572
  69.1 1.2 %collective-permute-done.39.refs_9_ = f32[96,128]{1,0:T(8,128)S(1)} collective-permute-done((f32[96,128]{1,0:T(8,128)S(1)}, f32[96,128]{1,0:T(8,128)S(1)}, u32[]{:S(2)}, u32[]{:S(2)}) %collective-permute-start.39) | collective-permute-done | bytes 49184 | tf_op jit(solution)/shard_map/ppermute | solution.py:554
  71.9 1.2 %collective-permute-start.41 = (f32[64,128]{1,0:T(8,128)S(1)}, f32[64,128]{1,0:T(8,128)S(1)}, u32[]{:S(2)}, u32[]{:S(2)}) collective-permute-start(f32[64,128]{1,0:T(8,128)S(1)} %get-tuple-element.59.refs_0_), channel_id=1, source_target_pairs={{0,16},{8,24},{16,0},{24,8},{1,17},{9,25},{17,1},{25,9},{2,18},{10... | collective-permute-start | bytes 98312 | tf_op jit(solution)/shard_map/ppermute | solution.py:561
  73.1 1.5 %collective-permute-start.40 = (f32[64,128]{1,0:T(8,128)S(1)}, f32[64,128]{1,0:T(8,128)S(1)}, u32[]{:S(2)}, u32[]{:S(2)}) collective-permute-start(f32[64,128]{1,0:T(8,128)S(1)} %get-tuple-element.59.refs_0_), channel_id=1, source_target_pairs={{0,8},{8,0},{16,24},{24,16},{1,9},{9,1},{17,25},{25,17},{2,10},{10... | collective-permute-start | bytes 98312 | tf_op jit(solution)/shard_map/ppermute | solution.py:561
  77.0 1.2 %shard_map.105 = f32[9,8,64]{2,1,0:T(8,128)} custom-call(f32[64,128]{1,0:T(8,128)S(1)} %get-tuple-element.59.refs_0_, f32[64,128]{1,0:T(8,128)S(1)} %collective-permute-done.40.refs_1_, f32[64,128]{1,0:T(8,128)S(1)} %collective-permute-done.41.refs_2_, f32[64,128]{1,0:T(8,128)S(1)} %collective-permute-done.42.refs_3_, ...), custom_call_target="tpu_custom_call" | custom-call | flops 20000000 | bytes 215040 | tf_op jit(solution)/shard_map/pallas_call | solution.py:513
  (88 shorter events, 17.2 us)
Async XLA Ops:
  2.7 9.8 %collective-permute-start.2 = (f32[136,128]{1,0:T(8,128)}, f32[136,128]{1,0:T(8,128)S(1)}, u32[]{:S(2)}, u32[]{:S(2)}) collective-permute-start(f32[136,128]{1,0:T(8,128)} %get-tuple-element.31.refs_0_), channel_id=1, source_target_pairs={{0,4},{1,5},{2,6},{3,7},{4,0},{5,1},{6,2},{7,3},{8,12},{9,13},{10,... | collective-permute-start | bytes 208904 | tf_op jit(solution)/shard_map/ppermute | solution.py:529
  6.8 7.5 %collective-permute-start = (f32[136,128]{1,0:T(8,128)}, f32[136,128]{1,0:T(8,128)S(1)}, u32[]{:S(2)}, u32[]{:S(2)}) collective-permute-start(f32[136,128]{1,0:T(8,128)} %get-tuple-element.31.refs_0_), channel_id=1, source_target_pairs={{0,2},{1,3},{2,0},{3,1},{4,6},{5,7},{6,4},{7,5},{8,10},{9,11},{10,... | collective-permute-start | bytes 208904 | tf_op jit(solution)/shard_map/ppermute | solution.py:529
  8.4 5.9 %collective-permute-start.1 = (f32[64,128]{1,0:T(8,128)}, f32[64,128]{1,0:T(8,128)S(1)}, u32[]{:S(2)}, u32[]{:S(2)}) collective-permute-start(f32[64,128]{1,0:T(8,128)} %get-tuple-element.32), channel_id=1, source_target_pairs={{0,6},{1,7},{2,4},{3,5},{4,2},{5,3},{6,0},{7,1},{8,14},{9,15},{10,... | collective-permute-start | bytes 98312 | tf_op jit(solution)/shard_map/ppermute | solution.py:529
  12.5 4.0 %collective-permute-start.3 = (f32[72,128]{1,0:T(8,128)S(1)}, f32[72,128]{1,0:T(8,128)S(1)}, u32[]{:S(2)}, u32[]{:S(2)}) collective-permute-start(f32[72,128]{1,0:T(8,128)S(1)} %shard_map.89), channel_id=1, source_target_pairs={{0,2},{1,3},{2,0},{3,1},{4,6},{5,7},{6,4},{7,5},{8,10},{9,11},{10,... | collective-permute-start | bytes 110600 | tf_op jit(solution)/shard_map/ppermute | solution.py:529
  13.5 4.4 %collective-permute-start.4 = (f32[136,128]{1,0:T(8,128)S(1)}, f32[136,128]{1,0:T(8,128)S(1)}, u32[]{:S(2)}, u32[]{:S(2)}) collective-permute-start(f32[136,128]{1,0:T(8,128)S(1)} %copy-done.2), channel_id=1, source_target_pairs={{0,1},{1,0},{2,3},{3,2},{4,5},{5,4},{6,7},{7,6},{8,9},{9,8},{10,11... | collective-permute-start | bytes 208904 | tf_op jit(solution)/shard_map/ppermute | solution.py:554
  13.5 4.4 %collective-permute-start.6 = (f32[136,128]{1,0:T(8,128)S(1)}, f32[136,128]{1,0:T(8,128)S(1)}, u32[]{:S(2)}, u32[]{:S(2)}) collective-permute-start(f32[136,128]{1,0:T(8,128)S(1)} %collective-permute-done.2.whole_ref.refs_2_), channel_id=1, source_target_pairs={{0,1},{1,0},{2,3},{3,2},{4,5},{5,4},{6,7},{7,6},{8,9},{9,8},{10,11... | collective-permute-start | bytes 208904 | tf_op jit(solution)/shard_map/ppermute | solution.py:554
  14.3 3.6 %collective-permute-start.5 = (f32[136,128]{1,0:T(8,128)S(1)}, f32[136,128]{1,0:T(8,128)S(1)}, u32[]{:S(2)}, u32[]{:S(2)}) collective-permute-start(f32[136,128]{1,0:T(8,128)S(1)} %shard_map.87.refs_1_), channel_id=1, source_target_pairs={{0,1},{1,0},{2,3},{3,2},{4,5},{5,4},{6,7},{7,6},{8,9},{9,8},{10,11... | collective-permute-start | bytes 208904 | tf_op jit(solution)/shard_map/ppermute | solution.py:554
  20.4 8.6 %collective-permute-start.10 = (f32[192,128]{1,0:T(8,128)S(1)}, f32[192,128]{1,0:T(8,128)S(1)}, u32[]{:S(2)}, u32[]{:S(2)}) collective-permute-start(f32[192,128]{1,0:T(8,128)S(1)} %get-tuple-element.38.refs_0_), channel_id=1, source_target_pairs={{0,4},{1,5},{2,6},{3,7},{4,0},{5,1},{6,2},{7,3},{8,12},{9,13},{10,... | collective-permute-start | bytes 294920 | tf_op jit(solution)/shard_map/ppermute | solution.py:529
  22.9 7.0 %collective-permute-start.9 = (f32[192,128]{1,0:T(8,128)S(1)}, f32[192,128]{1,0:T(8,128)S(1)}, u32[]{:S(2)}, u32[]{:S(2)}) collective-permute-start(f32[192,128]{1,0:T(8,128)S(1)} %get-tuple-element.38.refs_0_), channel_id=1, source_target_pairs={{0,2},{1,3},{2,0},{3,1},{4,6},{5,7},{6,4},{7,5},{8,10},{9,11},{10,... | collective-permute-start | bytes 294920 | tf_op jit(solution)/shard_map/ppermute | solution.py:529
  24.9 6.0 %collective-permute-start.11 = (f32[96,128]{1,0:T(8,128)S(1)}, f32[96,128]{1,0:T(8,128)S(1)}, u32[]{:S(2)}, u32[]{:S(2)}) collective-permute-start(f32[96,128]{1,0:T(8,128)S(1)} %get-tuple-element.39), channel_id=1, source_target_pairs={{0,6},{1,7},{2,4},{3,5},{4,2},{5,3},{6,0},{7,1},{8,14},{9,15},{10,... | collective-permute-start | bytes 147464 | tf_op jit(solution)/shard_map/ppermute | solution.py:529
  29.1 4.1 %collective-permute-start.12 = (f32[96,128]{1,0:T(8,128)S(1)}, f32[96,128]{1,0:T(8,128)S(1)}, u32[]{:S(2)}, u32[]{:S(2)}) collective-permute-start(f32[96,128]{1,0:T(8,128)S(1)} %shard_map.92), channel_id=1, source_target_pairs={{0,2},{1,3},{2,0},{3,1},{4,6},{5,7},{6,4},{7,5},{8,10},{9,11},{10,... | collective-permute-start | bytes 147464 | tf_op jit(solution)/shard_map/ppermute | solution.py:529
  29.4 3.8 %collective-permute-start.13 = (f32[192,128]{1,0:T(8,128)S(1)}, f32[192,128]{1,0:T(8,128)S(1)}, u32[]{:S(2)}, u32[]{:S(2)}) collective-permute-start(f32[192,128]{1,0:T(8,128)S(1)} %get-tuple-element.38.refs_0_), channel_id=1, source_target_pairs={{0,1},{1,0},{2,3},{3,2},{4,5},{5,4},{6,7},{7,6},{8,9},{9,8},{10,11... | collective-permute-start | bytes 294920 | tf_op jit(solution)/shard_map/ppermute | solution.py:554
  29.4 5.0 %collective-permute-start.15 = (f32[192,128]{1,0:T(8,128)S(1)}, f32[192,128]{1,0:T(8,128)S(1)}, u32[]{:S(2)}, u32[]{:S(2)}) collective-permute-start(f32[192,128]{1,0:T(8,128)S(1)} %collective-permute-done.10.whole_ref.refs_2_), channel_id=1, source_target_pairs={{0,1},{1,0},{2,3},{3,2},{4,5},{5,4},{6,7},{7,6},{8,9},{9,8},{10,11... | collective-permute-start | bytes 294920 | tf_op jit(solution)/shard_map/ppermute | solution.py:554
  29.9 4.5 %collective-permute-start.14 = (f32[192,128]{1,0:T(8,128)S(1)}, f32[192,128]{1,0:T(8,128)S(1)}, u32[]{:S(2)}, u32[]{:S(2)}) collective-permute-start(f32[192,128]{1,0:T(8,128)S(1)} %collective-permute-done.9.refs_1_), channel_id=1, source_target_pairs={{0,1},{1,0},{2,3},{3,2},{4,5},{5,4},{6,7},{7,6},{8,9},{9,8},{10,11... | collective-permute-start | bytes 294920 | tf_op jit(solution)/shard_map/ppermute | solution.py:554
  37.5 6.2 %collective-permute-start.21 = (f32[144,128]{1,0:T(8,128)S(1)}, f32[144,128]{1,0:T(8,128)S(1)}, u32[]{:S(2)}, u32[]{:S(2)}) collective-permute-start(f32[144,128]{1,0:T(8,128)S(1)} %shard_map.94), channel_id=1, source_target_pairs={{0,8},{8,0},{16,24},{24,16},{1,9},{9,1},{17,25},{25,17},{2,10},{10... | collective-permute-start | bytes 221192 | tf_op jit(solution)/shard_map/ppermute | solution.py:569
  39.2 8.6 %collective-permute-start.19 = (f32[192,128]{1,0:T(8,128)S(1)}, f32[192,128]{1,0:T(8,128)S(1)}, u32[]{:S(2)}, u32[]{:S(2)}) collective-permute-start(f32[192,128]{1,0:T(8,128)S(1)} %get-tuple-element.46.refs_0_), channel_id=1, source_target_pairs={{0,4},{1,5},{2,6},{3,7},{4,0},{5,1},{6,2},{7,3},{8,12},{9,13},{10,... | collective-permute-start | bytes 294920 | tf_op jit(solution)/shard_map/ppermute | solution.py:529
  40.9 8.0 %collective-permute-start.18 = (f32[192,128]{1,0:T(8,128)S(1)}, f32[192,128]{1,0:T(8,128)S(1)}, u32[]{:S(2)}, u32[]{:S(2)}) collective-permute-start(f32[192,128]{1,0:T(8,128)S(1)} %get-tuple-element.46.refs_0_), channel_id=1, source_target_pairs={{0,2},{1,3},{2,0},{3,1},{4,6},{5,7},{6,4},{7,5},{8,10},{9,11},{10,... | collective-permute-start | bytes 294920 | tf_op jit(solution)/shard_map/ppermute | solution.py:529
  42.9 6.0 %collective-permute-start.20 = (f32[96,128]{1,0:T(8,128)S(1)}, f32[96,128]{1,0:T(8,128)S(1)}, u32[]{:S(2)}, u32[]{:S(2)}) collective-permute-start(f32[96,128]{1,0:T(8,128)S(1)} %get-tuple-element.47), channel_id=1, source_target_pairs={{0,6},{1,7},{2,4},{3,5},{4,2},{5,3},{6,0},{7,1},{8,14},{9,15},{10,... | collective-permute-start | bytes 147464 | tf_op jit(solution)/shard_map/ppermute | solution.py:529
  43.6 5.8 %collective-permute-start.23 = (f32[144,128]{1,0:T(8,128)S(1)}, f32[144,128]{1,0:T(8,128)S(1)}, u32[]{:S(2)}, u32[]{:S(2)}) collective-permute-start(f32[144,128]{1,0:T(8,128)S(1)} %add.6.one_ref), channel_id=1, source_target_pairs={{0,16},{8,24},{16,0},{24,8},{1,17},{9,25},{17,1},{25,9},{2,18},{10... | collective-permute-start | bytes 221192 | tf_op jit(solution)/shard_map/ppermute | solution.py:572
  45.2 6.8 %collective-permute-start.24 = (f32[192,128]{1,0:T(8,128)S(1)}, f32[192,128]{1,0:T(8,128)S(1)}, u32[]{:S(2)}, u32[]{:S(2)}) collective-permute-start(f32[192,128]{1,0:T(8,128)S(1)} %get-tuple-element.46.refs_0_), channel_id=1, source_target_pairs={{0,1},{1,0},{2,3},{3,2},{4,5},{5,4},{6,7},{7,6},{8,9},{9,8},{10,11... | collective-permute-start | bytes 294920 | tf_op jit(solution)/shard_map/ppermute | solution.py:554
  47.9 4.1 %collective-permute-start.22 = (f32[96,128]{1,0:T(8,128)S(1)}, f32[96,128]{1,0:T(8,128)S(1)}, u32[]{:S(2)}, u32[]{:S(2)}) collective-permute-start(f32[96,128]{1,0:T(8,128)S(1)} %shard_map.95), channel_id=1, source_target_pairs={{0,2},{1,3},{2,0},{3,1},{4,6},{5,7},{6,4},{7,5},{8,10},{9,11},{10,... | collective-permute-start | bytes 147464 | tf_op jit(solution)/shard_map/ppermute | solution.py:529
  55.9 8.9 %collective-permute-start.30 = (f32[192,128]{1,0:T(8,128)S(1)}, f32[192,128]{1,0:T(8,128)S(1)}, u32[]{:S(2)}, u32[]{:S(2)}) collective-permute-start(f32[192,128]{1,0:T(8,128)S(1)} %get-tuple-element.51.refs_0_), channel_id=1, source_target_pairs={{0,4},{1,5},{2,6},{3,7},{4,0},{5,1},{6,2},{7,3},{8,12},{9,13},{10,... | collective-permute-start | bytes 294920 | tf_op jit(solution)/shard_map/ppermute | solution.py:529
  56.8 8.7 %collective-permute-start.29 = (f32[192,128]{1,0:T(8,128)S(1)}, f32[192,128]{1,0:T(8,128)S(1)}, u32[]{:S(2)}, u32[]{:S(2)}) collective-permute-start(f32[192,128]{1,0:T(8,128)S(1)} %get-tuple-element.51.refs_0_), channel_id=1, source_target_pairs={{0,2},{1,3},{2,0},{3,1},{4,6},{5,7},{6,4},{7,5},{8,10},{9,11},{10,... | collective-permute-start | bytes 294920 | tf_op jit(solution)/shard_map/ppermute | solution.py:529
  58.9 4.3 %collective-permute-start.32 = (f32[128,128]{1,0:T(8,128)S(1)}, f32[128,128]{1,0:T(8,128)S(1)}, u32[]{:S(2)}, u32[]{:S(2)}) collective-permute-start(f32[128,128]{1,0:T(8,128)S(1)} %shard_map.99), channel_id=1, source_target_pairs={{0,8},{8,0},{16,24},{24,16},{1,9},{9,1},{17,25},{25,17},{2,10},{10... | collective-permute-start | bytes 196616 | tf_op jit(solution)/shard_map/ppermute | solution.py:569
  59.5 6.0 %collective-permute-start.31 = (f32[96,128]{1,0:T(8,128)S(1)}, f32[96,128]{1,0:T(8,128)S(1)}, u32[]{:S(2)}, u32[]{:S(2)}) collective-permute-start(f32[96,128]{1,0:T(8,128)S(1)} %get-tuple-element.52), channel_id=1, source_target_pairs={{0,6},{1,7},{2,4},{3,5},{4,2},{5,3},{6,0},{7,1},{8,14},{9,15},{10,... | collective-permute-start | bytes 147464 | tf_op jit(solution)/shard_map/ppermute | solution.py:529
  63.3 4.3 %collective-permute-start.34 = (f32[128,128]{1,0:T(8,128)S(1)}, f32[128,128]{1,0:T(8,128)S(1)}, u32[]{:S(2)}, u32[]{:S(2)}) collective-permute-start(f32[128,128]{1,0:T(8,128)S(1)} %add.7.one_ref), channel_id=1, source_target_pairs={{0,16},{8,24},{16,0},{24,8},{1,17},{9,25},{17,1},{25,9},{2,18},{10... | collective-permute-start | bytes 196616 | tf_op jit(solution)/shard_map/ppermute | solution.py:572
  64.8 4.2 %collective-permute-start.35 = (f32[192,128]{1,0:T(8,128)S(1)}, f32[192,128]{1,0:T(8,128)S(1)}, u32[]{:S(2)}, u32[]{:S(2)}) collective-permute-start(f32[192,128]{1,0:T(8,128)S(1)} %get-tuple-element.51.refs_0_), channel_id=1, source_target_pairs={{0,1},{1,0},{2,3},{3,2},{4,5},{5,4},{6,7},{7,6},{8,9},{9,8},{10,11... | collective-permute-start | bytes 294920 | tf_op jit(solution)/shard_map/ppermute | solution.py:554
  64.9 4.2 %collective-permute-start.33 = (f32[96,128]{1,0:T(8,128)S(1)}, f32[96,128]{1,0:T(8,128)S(1)}, u32[]{:S(2)}, u32[]{:S(2)}) collective-permute-start(f32[96,128]{1,0:T(8,128)S(1)} %shard_map.100), channel_id=1, source_target_pairs={{0,2},{1,3},{2,0},{3,1},{4,6},{5,7},{6,4},{7,5},{8,10},{9,11},{10,... | collective-permute-start | bytes 147464 | tf_op jit(solution)/shard_map/ppermute | solution.py:529
  65.5 3.6 %collective-permute-start.36 = (f32[192,128]{1,0:T(8,128)S(1)}, f32[192,128]{1,0:T(8,128)S(1)}, u32[]{:S(2)}, u32[]{:S(2)}) collective-permute-start(f32[192,128]{1,0:T(8,128)S(1)} %collective-permute-done.29.refs_1_), channel_id=1, source_target_pairs={{0,1},{1,0},{2,3},{3,2},{4,5},{5,4},{6,7},{7,6},{8,9},{9,8},{10,11... | collective-permute-start | bytes 294920 | tf_op jit(solution)/shard_map/ppermute | solution.py:554
  71.0 5.1 %collective-permute-start.42 = (f32[64,128]{1,0:T(8,128)S(1)}, f32[64,128]{1,0:T(8,128)S(1)}, u32[]{:S(2)}, u32[]{:S(2)}) collective-permute-start(f32[64,128]{1,0:T(8,128)S(1)} %get-tuple-element.59.refs_0_), channel_id=1, source_target_pairs={{0,24},{8,16},{16,8},{24,0},{1,25},{9,17},{17,9},{25,1},{2,26},{10... | collective-permute-start | bytes 98312 | tf_op jit(solution)/shard_map/ppermute | solution.py:561
  71.9 4.3 %collective-permute-start.41 = (f32[64,128]{1,0:T(8,128)S(1)}, f32[64,128]{1,0:T(8,128)S(1)}, u32[]{:S(2)}, u32[]{:S(2)}) collective-permute-start(f32[64,128]{1,0:T(8,128)S(1)} %get-tuple-element.59.refs_0_), channel_id=1, source_target_pairs={{0,16},{8,24},{16,0},{24,8},{1,17},{9,25},{17,1},{25,9},{2,18},{10... | collective-permute-start | bytes 98312 | tf_op jit(solution)/shard_map/ppermute | solution.py:561
  73.1 3.9 %collective-permute-start.40 = (f32[64,128]{1,0:T(8,128)S(1)}, f32[64,128]{1,0:T(8,128)S(1)}, u32[]{:S(2)}, u32[]{:S(2)}) collective-permute-start(f32[64,128]{1,0:T(8,128)S(1)} %get-tuple-element.59.refs_0_), channel_id=1, source_target_pairs={{0,8},{8,0},{16,24},{24,16},{1,9},{9,1},{17,25},{25,17},{2,10},{10... | collective-permute-start | bytes 98312 | tf_op jit(solution)/shard_map/ppermute | solution.py:561
  (17 other events, 27.7 us)
where the time goes:
time: 78.5 us; the launch traced here: 78.2 us
  starting transfers between devices  32 us (41%)
  waiting for transfers between devices  25.3 us (32%)
  Pallas kernels  17.2 us (22%)
  local copies, waits for them, and re-layouts  2.78 us (4%)
  between operations  0.84 us (1%)
    ppermute x16, starting transfers between devices, along(): return lax.ppermute(y, 'base', [(d, d ^ 2 * k) for d in range(devices)])  20.2 us
    pallas_call x13, Pallas kernels, call(): pl.pallas_call(kernel, out_shape=shapes, in_specs=in_specs, out_specs=[vm...  17.2 us
    ppermute x16, waiting for transfers between devices, along(): return lax.ppermute(y, 'base', [(d, d ^ 2 * k) for d in range(devices)])  15.6 us
    ppermute x4, starting transfers between devices, sum_band(): lax.ppermute(x, 'band', [(d, d ^ step) for d in range(devices)])  5.55 us
    ppermute x20, waiting for transfers between devices, share_base(): lax.ppermute(y, 'base', [(d, d ^ 1) for d in range(devices)])  4.52 us
    ppermute x4, waiting for transfers between devices, sum_band(): lax.ppermute(x, 'band', [(d, d ^ step) for d in range(devices)])  3.8 us
    ppermute x3, starting transfers between devices, share_band(): lax.ppermute(x, 'band', [(d, d ^ k) for d in range(devices)])  3.55 us
    unnamed x12, local copies, waits for them, and re-layouts  2.78 us
  transfers between devices with their start and end apart: 43, of which 18 were waited for; matrix products, arithmetic and copies ran while one was open for 0% of the time, Pallas kernels for 6%

commit v1 on v0

--- a/solution.py
+++ b/solution.py
@@ -20,6 +20,8 @@
 
 GAIN_ROWS = 8 * BLOCK
 TERM_ROWS = 12 * BLOCK
+PRODUCTS = 48
+CROSS = ((0, 1), (0, 2), (0, 3), (1, 2), (1, 3), (2, 3))
 
 
 def nt(left, right, **kw):
@@ -46,65 +48,75 @@
     return lax.broadcasted_iota(jnp.int32, shape, axis)
 
 
-def mul(a, b):
+def add(terms):
+    total = None
+    for sign, x, y in terms:
+        if total is None:
+            total = x * y if sign > 0 else -(x * y)
+        else:
+            total = total + x * y if sign > 0 else total - x * y
+    return total
+
+
+def apply_gains(pairs, gains, turned):
     re, im = [], []
     for r in range(2):
         for c in range(2):
-            re.append(
-                (a[2 * r] * b[c] + a[2 * r + 1] * b[2 + c])
-                - (a[4 + 2 * r] * b[4 + c] + a[5 + 2 * r] * b[6 + c])
-            )
-            im.append(
-                (a[2 * r] * b[4 + c] + a[2 * r + 1] * b[6 + c])
-                + (a[4 + 2 * r] * b[c] + a[5 + 2 * r] * b[2 + c])
-            )
+            to_re, to_im = [], []
+            for k in range(2):
+                for n in range(2):
+                    x_re, x_im = pairs(k, r, n, c) if turned else pairs(r, k, c, n)
+                    g_re, g_im = gains[2 * k + n], gains[4 + 2 * k + n]
+                    sign = -1 if turned else 1
+                    to_re += [(1, x_re, g_re), (-sign, x_im, g_im)]
+                    to_im += [(1, x_re, g_im), (sign, x_im, g_re)]
+            re.append(add(to_re))
+            im.append(add(to_im))
     return re + im
 
 
-def mul_herm(a, b):
-    re, im = [], []
+def square(gains):
+    return [
+        add([(1, gains[n], gains[n]) for n in (0, 2, 4, 6)]),
+        add([(1, gains[n], gains[n]) for n in (1, 3, 5, 7)]),
+        add([(1, gains[n], gains[n + 1]) for n in (0, 2, 4, 6)]),
+        add([(1, gains[0], gains[5]), (-1, gains[4], gains[1])])
+        + add([(1, gains[2], gains[7]), (-1, gains[6], gains[3])]),
+    ]
+
+
+def outer_first(own, cross, q):
+    out = []
     for r in range(2):
-        for c in range(2):
-            re.append(
-                (a[2 * r] * b[2 * c] + a[2 * r + 1] * b[2 * c + 1])
-                + (a[4 + 2 * r] * b[4 + 2 * c] + a[5 + 2 * r] * b[5 + 2 * c])
-            )
-            im.append(
-                (a[4 + 2 * r] * b[2 * c] + a[5 + 2 * r] * b[2 * c + 1])
-                - (a[2 * r] * b[4 + 2 * c] + a[2 * r + 1] * b[5 + 2 * c])
-            )
-    return re + im
-
-
-def herm_mul(a, b):
-    re, im = [], []
-    for r in range(2):
-        for c in range(2):
-            re.append(
-                (a[r] * b[c] + a[2 + r] * b[2 + c]) + (a[4 + r] * b[4 + c] + a[6 + r] * b[6 + c])
-            )
-            im.append(
-                (a[r] * b[4 + c] + a[2 + r] * b[6 + c]) - (a[4 + r] * b[c] + a[6 + r] * b[2 + c])
-            )
-    return re + im
-
-
-def outer_rows(c):
-    return [
-        (c[0] * c[0] + c[1] * c[1]) + (c[4] * c[4] + c[5] * c[5]),
-        (c[2] * c[2] + c[3] * c[3]) + (c[6] * c[6] + c[7] * c[7]),
-        (c[0] * c[2] + c[1] * c[3]) + (c[4] * c[6] + c[5] * c[7]),
-        (c[4] * c[2] + c[5] * c[3]) - (c[0] * c[6] + c[1] * c[7]),
-    ]
-
-
-def outer_columns(d):
-    return [
-        (d[0] * d[0] + d[2] * d[2]) + (d[4] * d[4] + d[6] * d[6]),
-        (d[1] * d[1] + d[3] * d[3]) + (d[5] * d[5] + d[7] * d[7]),
-        (d[0] * d[1] + d[2] * d[3]) + (d[4] * d[5] + d[6] * d[7]),
-        (d[0] * d[5] + d[2] * d[7]) - (d[4] * d[1] + d[6] * d[3]),
-    ]
+        x_re, x_im = cross(r, 0, r, 1)
+        twice = add([(1, x_re, q[2]), (-1, x_im, q[3])])
+        out.append(add([(1, own[r][0], q[0]), (1, own[r][1], q[1])]) + (twice + twice))
+    (a_re, a_im), (b_re, b_im) = cross(0, 0, 1, 0), cross(0, 1, 1, 1)
+    (c_re, c_im), (d_re, d_im) = cross(0, 0, 1, 1), cross(0, 1, 1, 0)
+    out.append(
+        add([(1, a_re, q[0]), (1, b_re, q[1]), (1, c_re + d_re, q[2]), (-1, c_im - d_im, q[3])])
+    )
+    out.append(
+        add([(1, a_im, q[0]), (1, b_im, q[1]), (1, c_im + d_im, q[2]), (1, c_re - d_re, q[3])])
+    )
+    return out
+
+
+def outer_second(own, cross, q):
+    out = []
+    for c in range(2):
+        x_re, x_im = cross(0, c, 1, c)
+        twice = add([(1, x_re, q[2]), (1, x_im, q[3])])
+        out.append(add([(1, own[0][c], q[0]), (1, own[1][c], q[1])]) + (twice + twice))
+    (a_re, a_im), (b_re, b_im) = cross(0, 0, 0, 1), cross(1, 0, 1, 1)
+    (c_re, c_im), (d_re, d_im) = cross(0, 0, 1, 1), cross(0, 1, 1, 0)
+    out.append(
+        add([(1, a_re, q[0]), (1, b_re, q[1]), (1, c_re + d_re, q[2]), (1, c_im + d_im, q[3])])
+    )
+    out.append(
+        add([(-1, a_im, q[0]), (-1, b_im, q[1]), (1, c_re - d_re, q[3]), (-1, c_im - d_im, q[2])])
+    )
+    return out
 
 
 def slot_key(index, pairs, scale, intervals):
@@ -143,7 +155,7 @@
 
 
 def greet_kernel(
-    blocks, intervals, pair_hbm, start_hbm, penalty_hbm, flag_hbm, out_ref, top_ref, pair_ref, start_ref,
+    blocks, intervals, pair_hbm, start_hbm, penalty_hbm, flag_hbm, out_ref, pair_ref, start_ref,
     penalty_ref, flag_ref, sems
 ):
     copies = [
@@ -194,17 +206,25 @@
         plane = jnp.where(here, jnp.concatenate([plane] * (LANES // intervals), 0), 0.0)
         high = plane.astype(BF16)
         low = (plane - high.astype(F32)).astype(BF16)
-        plane = nt(place, high) + nt(place, low)
-        out_ref[m * BLOCK : (m + 1) * BLOCK, :] = plane
-        if (m + 1) * BLOCK <= top_ref.shape[0]:
-            top_ref[m * BLOCK : (m + 1) * BLOCK, :] = plane
+        out_ref[m * BLOCK : (m + 1) * BLOCK, :] = nt(place, high) + nt(place, low)
 
 
 def prepare_kernel(
-    blocks, intervals, bands, pair_ref, chan_ref, vis_ref, model_ref, flag_ref, vt_ref, mt_ref,
-    key_ref, at_ref, basis_ref, chans_ref, expand_ref
+    blocks, intervals, bands, pair_hbm, chan_hbm, flag_hbm, vis_hbm, model_hbm, prod_ref, key_ref,
+    at_ref, basis_ref, chans_ref, pair_ref, chan_ref, flag_ref, vis_ref, model_ref, mt_ref, sems
 ):
     planes, width, cells = vis_ref.shape
+    moves = [(pair_hbm, pair_ref), (chan_hbm, chan_ref), (flag_hbm, flag_ref)]
+    for source, target in ((model_hbm, model_ref), (vis_hbm, vis_ref)):
+        moves += [(source.at[m], target.at[m]) for m in range(planes)]
+    copies = [
+        pltpu.make_async_copy(source, target, sems.at[n])
+        for n, (source, target) in enumerate(moves)
+    ]
+    for copy in copies[: 3 + planes]:
+        copy.start()
+    for copy in copies[:3]:
+        copy.wait()
     pairs = scalar_pairs(pair_ref)
     tiles = len(pairs)
     channels = width // tiles
@@ -232,38 +252,44 @@
     for order in range(NPOLY):
         basis = jnp.where(lane % KPAD == order, terms[order], basis)
     basis_ref[...] = jnp.where(row // intervals == lane // KPAD, basis, 0.0)
-    row = iota((LANES, 2 * width), 0)
-    lane = iota((LANES, 2 * width), 1)
-    wide = jnp.concatenate([local] * (2 * tiles), 1)
-    expand = (row // intervals == lane // channels) & (row % intervals == wide)
-    expand_ref[...] = expand.astype(BF16)
+    lanes = 2 * tiles * intervals
+    row = iota((lanes, 2 * width), 0)
+    lane = iota((lanes, 2 * width), 1)
+    at = jnp.concatenate([local] * (2 * tiles), 1)
+    fold = ((row // intervals == lane // channels) & (row % intervals == at)).astype(BF16)
     ident = (iota((cells, cells), 0) == iota((cells, cells), 1)).astype(BF16)
     rows = cell_weights(pairs, flag_ref[...].astype(F32))
     weight = jnp.concatenate([jnp.broadcast_to(w, (channels, cells)) for w in rows], 0)
+    half = cells // 2
+
+    def put(at, product):
+        beside = jnp.concatenate([product[:half], product[half:]], 1)
+        prod_ref[at] = pick(beside, fold).reshape(prod_ref.shape[1:])
+
+    order = [4 * (m % 2) + m // 2 for m in range(planes)]
     for m in range(planes):
-        vt_ref[m] = nt(ident, vis_ref[m]).reshape(BLOCK, BLOCK, width)
+        copies[3 + m].wait()
+        copies[3 + planes + order[m]].start()
         masked = (model_ref[m].astype(F32) * weight).astype(BF16)
-        mt_ref[m] = nt(ident, masked).reshape(BLOCK, BLOCK, width)
+        mt_ref[m] = nt(ident, masked)
+    for x in range(4):
+        put(32 + x, mt_ref[x] * mt_ref[x] + mt_ref[4 + x] * mt_ref[4 + x])
+    for n, (x, y) in enumerate(CROSS):
+        x_re, x_im, y_re, y_im = mt_ref[x], mt_ref[4 + x], mt_ref[y], mt_ref[4 + y]
+        put(36 + n, x_re * y_re + x_im * y_im)
+        put(42 + n, x_im * y_re - x_re * y_im)
+    for x in range(4):
+        copies[3 + planes + x].wait()
+        copies[3 + planes + 4 + x].wait()
+        v_re, v_im = nt(ident, vis_ref[x]), nt(ident, vis_ref[4 + x])
+        for y in range(4):
+            m_re, m_im = mt_ref[y], mt_ref[4 + y]
+            put(4 * x + y, v_re * m_re + v_im * m_im)
+            put(16 + 4 * x + y, v_im * m_re - v_re * m_im)
 
 
 def tie_kernel(*refs):
     pass
-
-
-def hand_on_kernel(whole_ref, *refs):
-    out_ref = refs[-1]
-    out_ref[...] = whole_ref[whole_ref.shape[0] - out_ref.shape[0] :, :]
-
-
-def hand_on(whole, rows, others):
-    vmem = pl.BlockSpec(memory_space=pltpu.VMEM)
-    return pl.pallas_call(
-        hand_on_kernel,
-        out_shape=jax.ShapeDtypeStruct((rows, whole.shape[1]), whole.dtype),
-        in_specs=[vmem] + [pl.BlockSpec(memory_space=pl.ANY)] * len(others),
-        out_specs=vmem,
-        compiler_params=pltpu.CompilerParams(vmem_limit_bytes=1024 * 1024),
-    )(whole, *others)
 
 
 def after(values, others):
@@ -278,42 +304,61 @@
     )(*values, *others)
 
 
-def normal_terms(gains, vt_ref, mt_ref, expand, first_s, second_s, a_s, b_s):
-    wide = pick(gains, expand, nn)
-    width = wide.shape[1] // 2
-    first_s[...] = wide[:, :width].reshape(8, BLOCK, width)
-    second_s[...] = wide[:, width:].reshape(8, BLOCK, width)
+def normal_terms(gains, prod_ref, first_s, second_s, a_s, out_ref):
     half = BLOCK // 2
+    low = iota((half, LANES), 1) < LANES // 2
+
+    def swap(x):
+        return pltpu.roll(x, LANES // 2, 1)
+
+    first, second = [], [[], []]
+    for m in range(8):
+        part = [gains[m * BLOCK + h * half : m * BLOCK + (h + 1) * half] for h in range(2)]
+        first.append(jnp.where(low, part[0], swap(part[1])))
+        for h in range(2):
+            second[h].append(jnp.where(low, swap(part[h]), part[h]))
+    for n, x in enumerate(first + square(first)):
+        first_s[n] = x
+    for h in range(2):
+        for n, x in enumerate(second[h] + square(second[h])):
+            second_s[h, n] = x
 
     def step(i, totals):
         partial = None
         new = []
-        first = [first_s[m, pl.ds(i, 1), :] for m in range(8)]
-        vis_all = [vt_ref[m, i].astype(F32) for m in range(8)]
-        mdl_all = [mt_ref[m, i].astype(F32) for m in range(8)]
+        one = [first_s[n, pl.ds(i, 1), :] for n in range(12)]
         for h in range(2):
-            at = slice(h * half, (h + 1) * half)
-            vis = [x[at] for x in vis_all]
-            mdl = [x[at] for x in mdl_all]
-            second = [second_s[m, at, :] for m in range(8)]
-            along = mul_herm(mdl, second)
-            terms = mul_herm(vis, along) + outer_rows(along)
+            two = [second_s[h, n] for n in range(12)]
+
+            def load(n):
+                return prod_ref[n, i, h * half : (h + 1) * half, :]
+
+            def pairs(r, k, c, n):
+                at = (2 * r + k) * 4 + 2 * c + n
+                return load(at), load(16 + at)
+
+            def cross(r, k, c, n):
+                at = CROSS.index((2 * r + k, 2 * c + n))
+                return load(36 + at), load(42 + at)
+
+            own = [[load(32 + 2 * r + k) for k in range(2)] for r in range(2)]
+            terms = apply_gains(pairs, two[:8], False) + outer_first(own, cross, two[8:])
             partial = terms if partial is None else [x + y for x, y in zip(partial, terms)]
-            back = mul(first, mdl)
-            terms = herm_mul(vis, back) + outer_columns(back)
+            terms = apply_gains(pairs, one[:8], True) + outer_second(own, cross, one[8:])
             new += [x + y for x, y in zip(totals[12 * h : 12 * (h + 1)], terms)]
         for k in range(12):
             a_s[k, pl.ds(i, 1), :] = jnp.sum(partial[k], 0, keepdims=True)
         return tuple(new)
 
-    zero = jnp.zeros((half, width), F32)
-    totals = lax.fori_loop(0, BLOCK, step, (zero,) * 24)
-    for h in range(2):
-        for k in range(12):
-            b_s[k, h * half : (h + 1) * half, :] = totals[12 * h + k]
-    return jnp.concatenate(
-        [a_s[...].reshape(TERM_ROWS, width), b_s[...].reshape(TERM_ROWS, width)], 1
-    )
+    zero = jnp.zeros((half, LANES), F32)
+    totals = lax.fori_loop(0, half, step, (zero,) * 24)
+    for k in range(12):
+        mine = a_s[k]
+        for h in range(2):
+            other = totals[12 * h + k]
+            other = other + swap(other)
+            at = k * BLOCK + h * half
+            out_ref[at : at + half, :] = jnp.where(low, swap(mine) if h else mine, other)
 
 
 def key_match(rows, lanes):
@@ -321,30 +366,22 @@
     return (jnp.concatenate([rows] * count, 1) == lanes).astype(BF16)
 
 
-def beside(refs, form):
-    refs = list(refs)
-    pieces = []
-    for parts in form:
-        part = [refs.pop(0)[...] for _ in range(parts)]
-        pieces.append(part[0] if parts == 1 else jnp.concatenate(part, 0))
-    return jnp.concatenate(pieces, 1), refs
-
-
-def first_kernel(form, *refs):
-    every, refs = beside(refs, form)
-    key_ref, expand_ref, vt_ref, mt_ref, gains_ref, out_ref, top_ref = refs[:7]
-    scratch = refs[7:]
+def beside(refs, count):
+    return jnp.concatenate([p[...] for p in refs[:count]], 1), refs[count:]
+
+
+def first_kernel(count, *refs):
+    every, refs = beside(refs, count)
+    key_ref, prod_ref, gains_ref, out_ref = refs[:4]
+    scratch = refs[4:]
     select = key_match(key_ref[:LANES, :], every[GAIN_ROWS + 1 : GAIN_ROWS + 2])
     gains = pick(every[:GAIN_ROWS], select)
     gains_ref[...] = gains
-    expand = expand_ref[...]
-    terms = pick(normal_terms(gains, vt_ref, mt_ref, expand, *scratch), expand)
-    out_ref[...] = terms
-    top_ref[...] = terms[: top_ref.shape[0]]
-
-
-def state_kernel(form, blocks, intervals, *refs):
-    every, refs = beside(refs, form)
+    normal_terms(gains, prod_ref, *scratch, out_ref)
+
+
+def state_kernel(count, blocks, intervals, *refs):
+    every, refs = beside(refs, count)
     key_ref, at_ref, gains_ref, chans_ref, z_ref, pen_ref, scale_ref, select_ref = refs
     rows = every[GAIN_ROWS:]
     z_ref[:, :LANES] = gains_ref[...]
@@ -381,18 +418,14 @@
     return jnp.concatenate(out, 0)
 
 
-def step_kernel(form, *refs):
-    every, refs = beside(refs, form)
-    select_ref, z_ref, pen_ref, scale_ref, expand_ref, vt_ref, mt_ref = refs[:7]
-    gains_ref, out_ref, top_ref = refs[7:10]
-    scratch = refs[10:]
+def step_kernel(count, *refs):
+    every, refs = beside(refs, count)
+    select_ref, z_ref, pen_ref, scale_ref, prod_ref, gains_ref, out_ref = refs[:7]
+    scratch = refs[7:]
     normal = pick(every, select_ref[...])
     gains = solve(normal, scale_ref[...], pen_ref[...], z_ref[...])
     gains_ref[...] = gains
-    expand = expand_ref[...]
-    terms = pick(normal_terms(gains[:, :LANES], vt_ref, mt_ref, expand, *scratch), expand)
-    out_ref[...] = terms
-    top_ref[...] = terms[: top_ref.shape[0]]
+    normal_terms(gains[:, :LANES], prod_ref, *scratch, out_ref)
 
 
 def first_total_kernel(gains_ref, basis_ref, out_ref):
@@ -458,8 +491,8 @@
     settle(total, inverse_ref[...], basis_ref, gains, z_ref, dual_ref)
 
 
-def last_kernel(form, *refs):
-    every, refs = beside(refs, form)
+def last_kernel(count, *refs):
+    every, refs = beside(refs, count)
     select_ref, z_ref, pen_ref, scale_ref, dual_ref, basis_ref, gains_ref, out_ref = refs
     own = slice(LANES, 2 * LANES)
     normal = pick(every, select_ref[own, :])
@@ -493,66 +526,46 @@
     coeff = nn(band_total(refs[:bands]), inverse_ref[...], precision=HIGH)
     owned = blocks * BLOCK
     place = (iota((KPAD, LANES), 0) == iota((KPAD, LANES), 1) % KPAD).astype(BF16)
+    parts = []
     for m in range(8):
         first = (m // 4) * (LANES // 2 // KPAD)
         here = iota((owned, LANES), 0) // BLOCK == iota((owned, LANES), 1) // KPAD - first
         part = coeff[(m % 4) * BLOCK : (m % 4 + 1) * BLOCK]
-        part = jnp.where(here, jnp.concatenate([part] * blocks, 0), 0.0)
-        out_ref[:, m, :] = turn(place, part)[:NPOLY]
-
-
-def call(kernel, operands, shapes, scratch=(), smem=0, held=False, flops=20_000_000, moved=None):
+        parts.append(jnp.where(here, jnp.concatenate([part] * blocks, 0), 0.0))
+    turned = turn(place, jnp.concatenate(parts, 0))
+    for m in range(8):
+        out_ref[:, m, :] = turned[:NPOLY, m * owned : (m + 1) * owned]
+
+
+def call(kernel, operands, shapes, scratch=(), hbm=False, flops=20_000_000):
     vmem = pl.BlockSpec(memory_space=pltpu.VMEM)
-    in_specs = [pl.BlockSpec(memory_space=pltpu.SMEM)] * smem + [vmem] * (len(operands) - smem)
-    params = pltpu.CompilerParams(vmem_limit_bytes=12 * 1024 * 1024)
-    if held:
-        in_specs = [pl.BlockSpec(memory_space=pl.ANY)] * len(operands)
-        params = pltpu.CompilerParams()
-    if moved is None:
-        moved = sum(x.size * x.dtype.itemsize for x in (*operands, *shapes))
+    in_specs = [vmem] * len(operands)
+    moved = sum(x.size * x.dtype.itemsize for x in (*operands, *shapes))
+    if hbm:
+        in_specs = [pl.BlockSpec(memory_space=pltpu.HBM)] * len(operands)
+        operands = [pltpu.with_memory_space_constraint(x, pltpu.HBM) for x in operands]
     return pl.pallas_call(
         kernel,
         out_shape=shapes,
         in_specs=in_specs,
         out_specs=[vmem] * len(shapes),
         scratch_shapes=list(scratch),
-        compiler_params=params,
+        compiler_params=pltpu.CompilerParams(vmem_limit_bytes=14 * 1024 * 1024),
         cost_estimate=pl.CostEstimate(flops=flops, bytes_accessed=moved, transcendentals=0),
     )(*operands)
 
 
-def share_base(x, top, early=(), late=(), first=False):
+def share_base(x, last=(), ties=(2,)):
     devices = lax.axis_size("base")
-    chips = devices // 2
-
-    def along(y, k):
-        return lax.ppermute(y, "base", [(d, d ^ (2 * k)) for d in range(devices)])
-
-    if chips == 4:
-        two = along(x, 2)
-        far = along(top, 3)
-        one = along(x, 1)
-        rest = along(hand_on(two, x.shape[0] - top.shape[0], early), 1)
-        if first:
-            (one,) = after([one], (far,))
-        if late:
-            (rest,) = after([rest], late)
-        mine, form = [x, one, two, far, rest], [1, 1, 1, 2]
-    else:
-        mine = {0: x}
-        step = chips // 2
-        while step:
-            for k in sorted(mine):
-                mine[k + step] = along(mine[k], step)
-            if early:
-                (mine[step],) = after([mine[step]], early)
-                early = ()
-            step //= 2
-        if late:
-            (mine[chips - 1],) = after([mine[chips - 1]], late)
-        mine, form = [mine[k] for k in sorted(mine)], [1] * chips
+    mine = [x] + [
+        lax.ppermute(x, "base", [(d, d ^ (2 * k)) for d in range(devices)])
+        for k in range(1, devices // 2)
+    ]
+    if last:
+        for k, y in zip(ties, after([mine[k] for k in ties], last)):
+            mine[k] = y
     other = [lax.ppermute(y, "base", [(d, d ^ 1) for d in range(devices)]) for y in mine]
-    return mine + other, form + form
+    return mine + other
 
 
 def share_band(x):
@@ -564,12 +577,11 @@
 
 def sum_band(x):
     devices = lax.axis_size("band")
-    step, came = 1, []
+    step = 1
     while 2 * step < devices:
-        came.append(lax.ppermute(x, "band", [(d, d ^ step) for d in range(devices)]))
-        x = x + came[-1]
+        x = x + lax.ppermute(x, "band", [(d, d ^ step) for d in range(devices)])
         step = 2 * step
-    return (x, lax.ppermute(x, "band", [(d, d ^ step) for d in range(devices)])), came[:1]
+    return x, lax.ppermute(x, "band", [(d, d ^ step) for d in range(devices)])
 
 
 def on_device(visibilities, model, start_gains, penalty, pairs, flags, chan_band):
@@ -587,14 +599,13 @@
     wide = shape(GAIN_ROWS, 2 * LANES)
     narrow = shape(GAIN_ROWS, LANES)
     single = shape(BLOCK, 2 * LANES)
-    messages = [shape(TERM_ROWS, LANES), shape(TERM_ROWS // 2, LANES)]
+    terms = shape(TERM_ROWS, LANES)
     square = shape(2 * LANES, LANES)
-    planes = shape(8, BLOCK, BLOCK, width)
-
-    greeting, top = call(
+
+    (greeting,) = call(
         functools.partial(greet_kernel, blocks, intervals),
         (pairs, start_gains, penalty.reshape(1, owned), flags),
-        [shape(GAIN_ROWS + 8, LANES), shape(GAIN_ROWS // 2, LANES)],
+        [shape(GAIN_ROWS + 8, LANES)],
         [
             pltpu.SMEM(pairs.shape, jnp.int32),
             pltpu.VMEM(start_gains.shape, F32),
@@ -602,66 +613,76 @@
             pltpu.VMEM(flags.shape, jnp.int32),
             pltpu.SemaphoreType.DMA((4,)),
         ],
-        held=True,
-    )
-    vt, mt, keys, at, basis, chans, expand = call(
+        hbm=True,
+    )
+    products, keys, at, basis, chans = call(
         functools.partial(prepare_kernel, blocks, intervals, bands),
         (
             pairs,
             chan_band.reshape(1, channels),
+            flags,
             visibilities.reshape(8, width, cells),
             model.reshape(8, width, cells),
-            flags,
         ),
         [
-            planes,
-            planes,
+            shape(PRODUCTS, BLOCK // 2, BLOCK, 2 * tiles * intervals),
             square,
             square,
             square,
             shape(8, 2 * LANES),
-            shape(LANES, 2 * width, dtype=BF16),
         ],
-        smem=1,
-        moved=100_000,
-    )
-    greetings, form = share_base(greeting, top, early=(chans,), first=True)
-    scratch = [pltpu.VMEM((8, BLOCK, width), F32)] * 2 + [pltpu.VMEM((12, BLOCK, width), F32)] * 2
-
-    gains, *message = call(
-        functools.partial(first_kernel, form),
-        (*greetings, keys, expand, vt, mt),
-        [narrow, *messages],
+        [
+            pltpu.SMEM(pairs.shape, jnp.int32),
+            pltpu.VMEM((1, channels), jnp.int32),
+            pltpu.VMEM(flags.shape, jnp.int32),
+            *[pltpu.VMEM((8, width, cells), BF16)] * 2,
+            pltpu.VMEM((8, cells, width), F32),
+            pltpu.SemaphoreType.DMA((19,)),
+        ],
+        hbm=True,
+        flops=2_000_000_000,
+    )
+    greetings = share_base(greeting, last=(chans,))
+    scratch = [
+        pltpu.VMEM((12, BLOCK // 2, LANES), F32),
+        pltpu.VMEM((2, 12, BLOCK // 2, LANES), F32),
+        pltpu.VMEM((12, BLOCK // 2, LANES), F32),
+    ]
+
+    gains, message = call(
+        functools.partial(first_kernel, count),
+        (*greetings, keys, products),
+        [narrow, terms],
         scratch,
     )
     z, pen, scale, select = call(
-        functools.partial(state_kernel, form, blocks, intervals),
+        functools.partial(state_kernel, count, blocks, intervals),
         (*greetings, keys, at, gains, chans),
         [wide, single, single, shape(2 * LANES, count * LANES, dtype=BF16)],
     )
-    pieces, form = share_base(*message, early=(scale,))
-    gains, *message = call(
-        functools.partial(step_kernel, form),
-        (*pieces, select, z, pen, scale, expand, vt, mt),
-        [wide, *messages],
+    pieces = share_base(message, last=(scale,))
+    gains, message = call(
+        functools.partial(step_kernel, count),
+        (*pieces, select, z, pen, scale, products),
+        [wide, terms],
         scratch,
     )
     (part,) = call(first_total_kernel, (gains, basis), [shape(GAIN_ROWS + KPAD, LANES)])
-    parts, came = sum_band(part)
-    z, dual, inverse = call(first_consensus_kernel, (*parts, gains, basis), [wide, wide, narrow])
-    pieces, form = share_base(*message, early=came, late=(z,))
-    gains, *message = call(
-        functools.partial(step_kernel, form),
-        (*pieces, select, z, pen, scale, expand, vt, mt),
-        [wide, *messages],
+    z, dual, inverse = call(
+        first_consensus_kernel, (*sum_band(part), gains, basis), [wide, wide, narrow]
+    )
+    pieces = share_base(message, last=(z,), ties=(1, 2))
+    gains, message = call(
+        functools.partial(step_kernel, count),
+        (*pieces, select, z, pen, scale, products),
+        [wide, terms],
         scratch,
     )
     (part,) = call(total_kernel, (gains, dual, basis), [narrow])
-    parts, came = sum_band(part)
-    z, dual = call(consensus_kernel, (*parts, gains, dual, basis, inverse), [wide, wide])
-    pieces, form = share_base(*message, early=came, late=(z,))
+    z, dual = call(consensus_kernel, (*sum_band(part), gains, dual, basis, inverse), [wide, wide])
+    pieces = share_base(message, last=(z,), ties=(1, 2))
     gains, part = call(
-        functools.partial(last_kernel, form),
+        functools.partial(last_kernel, count),
         (*pieces, select, z, pen, scale, dual, basis),
         [narrow, shape(GAIN_ROWS // 2, LANES)],
     )

time: 78.5 us -> 71.9 us (0.916)
  local copies, waits for them, and re-layouts: 2.78 us -> 0 us
  waiting for transfers between devices: 25.3 us -> 22.7 us
  starting transfers between devices: 32 us -> 30.2 us
  Pallas kernels: 17.2 us -> 18.1 us
    ppermute x20 -> x16, waiting for transfers between devices: 19.4 us -> 15.9 us  [the longest x12 12.6 us: share_base(): lax.ppermute(x, 'base', [(d, d ^ 2 * k) for d in range(devices)])]
    unnamed x12 -> x0, local copies, waits for them, and re-layouts: 2.78 us -> none
    ppermute x20 -> x16, starting transfers between devices: 25.8 us -> 23.9 us  [the longest x12 18.5 us: share_base(): lax.ppermute(x, 'base', [(d, d ^ 2 * k) for d in range(devices)])]
    ppermute x3, waiting for transfers between devices: 1.44 us -> 2.4 us  [share_band(): lax.ppermute(x, 'band', [(d, d ^ k) for d in range(devices)])]
    pallas_call x13, Pallas kernels: 17.2 us -> 18.1 us  [call(): pl.pallas_call(kernel, out_shape=shapes, in_specs=in_specs, out_specs=[vm...]
    ppermute x20 -> x16, waiting for transfers between devices: 4.52 us -> 4.36 us  [share_base(): lax.ppermute(y, 'base', [(d, d ^ 1) for d in range(devices)])]
    ppermute x20 -> x16, starting transfers between devices: 2.65 us -> 2.71 us  [share_base(): lax.ppermute(y, 'base', [(d, d ^ 1) for d in range(devices)])]
  transfers between devices with their start and end apart: 43 -> 35, of which waited for: 18 -> 20; matrix products, arithmetic and copies ran while one was open for 0% -> 0% of each run, Pallas kernels for 6% -> 13%
where the time goes in v1:
time: 71.9 us; the launch traced here: 71.8 us
  starting transfers between devices  30.2 us (42%)
  waiting for transfers between devices  22.7 us (32%)
  Pallas kernels  18.1 us (25%)
  between operations  0.77 us (1%)
    ppermute x12, starting transfers between devices, share_base(): lax.ppermute(x, 'base', [(d, d ^ 2 * k) for d in range(devices)])  18.5 us
    pallas_call x13, Pallas kernels, call(): pl.pallas_call(kernel, out_shape=shapes, in_specs=in_specs, out_specs=[vm...  18.1 us
    ppermute x12, waiting for transfers between devices, share_base(): lax.ppermute(x, 'base', [(d, d ^ 2 * k) for d in range(devices)])  12.6 us
    ppermute x16, waiting for transfers between devices, share_base(): lax.ppermute(y, 'base', [(d, d ^ 1) for d in range(devices)])  4.36 us
    ppermute x3, starting transfers between devices, share_band(): lax.ppermute(x, 'band', [(d, d ^ k) for d in range(devices)])  3.57 us
    ppermute x2, waiting for transfers between devices, sum_band(): return (x, lax.ppermute(x, 'band', [(d, d ^ step) for d in range(devices)]))  3.37 us
    ppermute x2, starting transfers between devices, sum_band(): return (x, lax.ppermute(x, 'band', [(d, d ^ step) for d in range(devices)]))  3.18 us
    ppermute x16, starting transfers between devices, share_base(): lax.ppermute(y, 'base', [(d, d ^ 1) for d in range(devices)])  2.71 us
  transfers between devices with their start and end apart: 35, of which 20 were waited for; matrix products, arithmetic and copies ran while one was open for 0% of the time, Pallas kernels for 13%

profile of v1, /device:TPU:0, one launch (start us, length us, event | category | flops | bytes accessed | tf_op | source)
XLA Modules:
  0.0 71.8 jit_solution(7936305760704732151)
XLA Ops:
  0.6 1.4 %shard_map.86.refs_0_ = f32[136,128]{1,0:T(8,128)S(1)} custom-call(s32[2,2]{1,0:T(2,128)} %pair_hbm.3, f32[8,32,64]{2,1,0:T(8,128)} %start_hbm.1, f32[1,64]{1,0:T(1,128)} %bitcast.6, s32[2,256]{1,0:T(2,128)} %flag_hbm.3), custom_call_target="tpu_custom_call" | custom-call | flops 20000000 | bytes 137488 | tf_op jit(solution)/shard_map/pallas_call | solution.py:547
  2.6 4.7 %collective-permute-start.2 = (f32[136,128]{1,0:T(8,128)S(1)}, f32[136,128]{1,0:T(8,128)S(1)}, u32[]{:S(2)}, u32[]{:S(2)}) collective-permute-start(f32[136,128]{1,0:T(8,128)S(1)} %shard_map.86.refs_0_), channel_id=1, source_target_pairs={{0,6},{1,7},{2,4},{3,5},{4,2},{5,3},{6,0},{7,1},{8,14},{9,15},{10,... | collective-permute-start | bytes 208904 | tf_op jit(solution)/shard_map/ppermute | solution.py:561
  7.9 6.2 %shard_map.87 = (f32[48,8,16,128]{3,2,1,0:T(8,128)S(1)}, f32[256,128]{1,0:T(8,128)S(1)}, f32[256,128]{1,0:T(8,128)S(1)}, f32[256,128]{1,0:T(8,128)S(1)}, f32[8,256]{1,0:T(8,128)S(1)}) custom-call(s32[2,2]{1,0:T(2,128)} %pair_hbm.3, s32[1,64]{1,0:T(1,128)} %bitcast.9, s32[2,256]{1,0:T(2,128)} %flag_hbm.3, bf16[8,128,256]{2,1,0:T(8,128)(2,1)} %bitcast.7, ...), custom_call_target="tpu_custom_call" | custom-call | flops 2000000000 | bytes 4598032 | tf_op jit(solution)/shard_map/pallas_call | solution.py:547
  14.8 0.7 collective-permute-done.6.refs_7_
  15.9 1.4 %shard_map.89 = (f32[128,128]{1,0:T(8,128)S(1)}, f32[192,128]{1,0:T(8,128)S(1)}) custom-call(f32[136,128]{1,0:T(8,128)S(1)} %shard_map.86.refs_0_, f32[136,128]{1,0:T(8,128)S(1)} %collective-permute-done.refs_1_, f32[136,128]{1,0:T(8,128)S(1)} %shard_map.88.refs_2_, f32[136,128]{1,0:T(8,128)S(1)} %collective-permute-done.2.refs_3_, ...), custom_call_target="tpu_custom_call" | custom-call | flops 20000000 | bytes 3997696 | tf_op jit(solution)/shard_map/pallas_call | solution.py:547
  17.3 2.3 %collective-permute-start.8 = (f32[192,128]{1,0:T(8,128)S(1)}, f32[192,128]{1,0:T(8,128)S(1)}, u32[]{:S(2)}, u32[]{:S(2)}) collective-permute-start(f32[192,128]{1,0:T(8,128)S(1)} %get-tuple-element.31.refs_0_), channel_id=1, source_target_pairs={{0,4},{1,5},{2,6},{3,7},{4,0},{5,1},{6,2},{7,3},{8,12},{9,13},{10,... | collective-permute-start | bytes 294920 | tf_op jit(solution)/shard_map/ppermute | solution.py:561
  19.7 1.5 %collective-permute-start.9 = (f32[192,128]{1,0:T(8,128)S(1)}, f32[192,128]{1,0:T(8,128)S(1)}, u32[]{:S(2)}, u32[]{:S(2)}) collective-permute-start(f32[192,128]{1,0:T(8,128)S(1)} %get-tuple-element.31.refs_0_), channel_id=1, source_target_pairs={{0,6},{1,7},{2,4},{3,5},{4,2},{5,3},{6,0},{7,1},{8,14},{9,15},{10,... | collective-permute-start | bytes 294920 | tf_op jit(solution)/shard_map/ppermute | solution.py:561
  22.2 6.0 %collective-permute-done.8.refs_0_ = f32[192,128]{1,0:T(8,128)S(1)} collective-permute-done((f32[192,128]{1,0:T(8,128)S(1)}, f32[192,128]{1,0:T(8,128)S(1)}, u32[]{:S(2)}, u32[]{:S(2)}) %collective-permute-start.8) | collective-permute-done | bytes 98336 | tf_op jit(solution)/shard_map/ppermute | solution.py:561
  28.8 0.8 %collective-permute-done.13.refs_7_ = f32[192,128]{1,0:T(8,128)S(1)} collective-permute-done((f32[192,128]{1,0:T(8,128)S(1)}, f32[192,128]{1,0:T(8,128)S(1)}, u32[]{:S(2)}, u32[]{:S(2)}) %collective-permute-start.13) | collective-permute-done | bytes 98336 | tf_op jit(solution)/shard_map/ppermute | solution.py:567
  30.1 1.6 %shard_map.92 = (f32[128,256]{1,0:T(8,128)S(1)}, f32[192,128]{1,0:T(8,128)S(1)}) custom-call(f32[192,128]{1,0:T(8,128)S(1)} %get-tuple-element.31.refs_0_, f32[192,128]{1,0:T(8,128)S(1)} %collective-permute-done.7.refs_1_, f32[192,128]{1,0:T(8,128)S(1)} %shard_map.91.refs_2_, f32[192,128]{1,0:T(8,128)S(1)} %collective-permute-done.9.refs_3_, ...), custom_call_target="tpu_custom_call" | custom-call | flops 20000000 | bytes 4849664 | tf_op jit(solution)/shard_map/pallas_call | solution.py:547
  32.0 1.7 %collective-permute-start.16 = (f32[144,128]{1,0:T(8,128)S(1)}, f32[144,128]{1,0:T(8,128)S(1)}, u32[]{:S(2)}, u32[]{:S(2)}) collective-permute-start(f32[144,128]{1,0:T(8,128)S(1)} %shard_map.93), channel_id=1, source_target_pairs={{0,8},{8,0},{16,24},{24,16},{1,9},{9,1},{17,25},{25,17},{2,10},{10... | collective-permute-start | bytes 221192 | tf_op jit(solution)/shard_map/ppermute | solution.py:582
  33.7 3.0 %collective-permute-start.18 = (f32[192,128]{1,0:T(8,128)S(1)}, f32[192,128]{1,0:T(8,128)S(1)}, u32[]{:S(2)}, u32[]{:S(2)}) collective-permute-start(f32[192,128]{1,0:T(8,128)S(1)} %get-tuple-element.38.refs_0_), channel_id=1, source_target_pairs={{0,6},{1,7},{2,4},{3,5},{4,2},{5,3},{6,0},{7,1},{8,14},{9,15},{10,... | collective-permute-start | bytes 294920 | tf_op jit(solution)/shard_map/ppermute | solution.py:561
  36.7 1.4 %collective-permute-start.14 = (f32[192,128]{1,0:T(8,128)S(1)}, f32[192,128]{1,0:T(8,128)S(1)}, u32[]{:S(2)}, u32[]{:S(2)}) collective-permute-start(f32[192,128]{1,0:T(8,128)S(1)} %get-tuple-element.38.refs_0_), channel_id=1, source_target_pairs={{0,2},{1,3},{2,0},{3,1},{4,6},{5,7},{6,4},{7,5},{8,10},{9,11},{10,... | collective-permute-start | bytes 294920 | tf_op jit(solution)/shard_map/ppermute | solution.py:561
  38.1 1.6 %collective-permute-start.17 = (f32[144,128]{1,0:T(8,128)S(1)}, f32[144,128]{1,0:T(8,128)S(1)}, u32[]{:S(2)}, u32[]{:S(2)}) collective-permute-start(f32[144,128]{1,0:T(8,128)S(1)} %add.6.one_ref), channel_id=1, source_target_pairs={{0,16},{8,24},{16,0},{24,8},{1,17},{9,25},{17,1},{25,9},{2,18},{10... | collective-permute-start | bytes 221192 | tf_op jit(solution)/shard_map/ppermute | solution.py:584
  39.7 0.6 collective-permute-done.18.refs_3_
  40.4 2.2 %collective-permute-done.17.two_ref = f32[144,128]{1,0:T(8,128)S(1)} collective-permute-done((f32[144,128]{1,0:T(8,128)S(1)}, f32[144,128]{1,0:T(8,128)S(1)}, u32[]{:S(2)}, u32[]{:S(2)}) %collective-permute-start.17) | collective-permute-done | bytes 73760 | tf_op jit(solution)/shard_map/ppermute | solution.py:584
  42.5 1.5 %shard_map.94 = (f32[128,256]{1,0:T(8,128)S(1)}, f32[128,256]{1,0:T(8,128)S(1)}, f32[128,128]{1,0:T(8,128)S(1)}) custom-call(f32[144,128]{1,0:T(8,128)S(1)} %add.6.one_ref, f32[144,128]{1,0:T(8,128)S(1)} %collective-permute-done.17.two_ref, f32[128,256]{1,0:T(8,128)S(1)} %get-tuple-element.39.gains_ref, f32[256,128]{1,0:T(8,128)S(1)} %get-tuple-element.40.basis_ref.refs_13_), custom_call_target="tpu_custom_call" | custom-call | flops 20000000 | bytes 737280 | tf_op jit(solution)/shard_map/pallas_call | solution.py:547
  44.0 2.0 %collective-permute-done.15.refs_1_ = f32[192,128]{1,0:T(8,128)S(1)} collective-permute-done((f32[192,128]{1,0:T(8,128)S(1)}, f32[192,128]{1,0:T(8,128)S(1)}, u32[]{:S(2)}, u32[]{:S(2)}) %collective-permute-start.15) | collective-permute-done | bytes 98336 | tf_op jit(solution)/shard_map/ppermute | solution.py:561
  46.6 0.8 %collective-permute-done.20.refs_5_ = f32[192,128]{1,0:T(8,128)S(1)} collective-permute-done((f32[192,128]{1,0:T(8,128)S(1)}, f32[192,128]{1,0:T(8,128)S(1)}, u32[]{:S(2)}, u32[]{:S(2)}) %collective-permute-start.20) | collective-permute-done | bytes 98336 | tf_op jit(solution)/shard_map/ppermute | solution.py:567
  47.5 1.6 %shard_map.96 = (f32[128,256]{1,0:T(8,128)S(1)}, f32[192,128]{1,0:T(8,128)S(1)}) custom-call(f32[192,128]{1,0:T(8,128)S(1)} %get-tuple-element.38.refs_0_, f32[192,128]{1,0:T(8,128)S(1)} %get-tuple-element.42.refs_1_, f32[192,128]{1,0:T(8,128)S(1)} %get-tuple-element.43.refs_2_, f32[192,128]{1,0:T(8,128)S(1)} %collective-permute-done.18.refs_3_, ...), custom_call_target="tpu_custom_call" | custom-call | flops 20000000 | bytes 4849664 | tf_op jit(solution)/shard_map/pallas_call | solution.py:547
  49.9 2.6 %collective-permute-start.27 = (f32[192,128]{1,0:T(8,128)S(1)}, f32[192,128]{1,0:T(8,128)S(1)}, u32[]{:S(2)}, u32[]{:S(2)}) collective-permute-start(f32[192,128]{1,0:T(8,128)S(1)} %get-tuple-element.44.refs_0_), channel_id=1, source_target_pairs={{0,6},{1,7},{2,4},{3,5},{4,2},{5,3},{6,0},{7,1},{8,14},{9,15},{10,... | collective-permute-start | bytes 294920 | tf_op jit(solution)/shard_map/ppermute | solution.py:561
  52.6 1.7 %collective-permute-start.23 = (f32[192,128]{1,0:T(8,128)S(1)}, f32[192,128]{1,0:T(8,128)S(1)}, u32[]{:S(2)}, u32[]{:S(2)}) collective-permute-start(f32[192,128]{1,0:T(8,128)S(1)} %get-tuple-element.44.refs_0_), channel_id=1, source_target_pairs={{0,2},{1,3},{2,0},{3,1},{4,6},{5,7},{6,4},{7,5},{8,10},{9,11},{10,... | collective-permute-start | bytes 294920 | tf_op jit(solution)/shard_map/ppermute | solution.py:561
  54.4 1.6 %collective-permute-start.26 = (f32[128,128]{1,0:T(8,128)S(1)}, f32[128,128]{1,0:T(8,128)S(1)}, u32[]{:S(2)}, u32[]{:S(2)}) collective-permute-start(f32[128,128]{1,0:T(8,128)S(1)} %add.7.one_ref), channel_id=1, source_target_pairs={{0,16},{8,24},{16,0},{24,8},{1,17},{9,25},{17,1},{25,9},{2,18},{10... | collective-permute-start | bytes 196616 | tf_op jit(solution)/shard_map/ppermute | solution.py:584
  55.9 1.5 %collective-permute-done.27.refs_3_ = f32[192,128]{1,0:T(8,128)S(1)} collective-permute-done((f32[192,128]{1,0:T(8,128)S(1)}, f32[192,128]{1,0:T(8,128)S(1)}, u32[]{:S(2)}, u32[]{:S(2)}) %collective-permute-start.27) | collective-permute-done | bytes 98336 | tf_op jit(solution)/shard_map/ppermute | solution.py:561
  57.5 1.2 %collective-permute-done.26.two_ref = f32[128,128]{1,0:T(8,128)S(1)} collective-permute-done((f32[128,128]{1,0:T(8,128)S(1)}, f32[128,128]{1,0:T(8,128)S(1)}, u32[]{:S(2)}, u32[]{:S(2)}) %collective-permute-start.26) | collective-permute-done | bytes 65568 | tf_op jit(solution)/shard_map/ppermute | solution.py:584
  59.2 2.2 %collective-permute-done.24.refs_1_ = f32[192,128]{1,0:T(8,128)S(1)} collective-permute-done((f32[192,128]{1,0:T(8,128)S(1)}, f32[192,128]{1,0:T(8,128)S(1)}, u32[]{:S(2)}, u32[]{:S(2)}) %collective-permute-start.24) | collective-permute-done | bytes 98336 | tf_op jit(solution)/shard_map/ppermute | solution.py:561
  61.9 0.8 %collective-permute-done.29.refs_5_ = f32[192,128]{1,0:T(8,128)S(1)} collective-permute-done((f32[192,128]{1,0:T(8,128)S(1)}, f32[192,128]{1,0:T(8,128)S(1)}, u32[]{:S(2)}, u32[]{:S(2)}) %collective-permute-start.29) | collective-permute-done | bytes 98336 | tf_op jit(solution)/shard_map/ppermute | solution.py:567
  62.9 0.7 shard_map.100
  63.6 2.5 %collective-permute-start.34 = (f32[64,128]{1,0:T(8,128)S(1)}, f32[64,128]{1,0:T(8,128)S(1)}, u32[]{:S(2)}, u32[]{:S(2)}) collective-permute-start(f32[64,128]{1,0:T(8,128)S(1)} %get-tuple-element.53.refs_0_), channel_id=1, source_target_pairs={{0,24},{8,16},{16,8},{24,0},{1,25},{9,17},{17,9},{25,1},{2,26},{10... | collective-permute-start | bytes 98312 | tf_op jit(solution)/shard_map/ppermute | solution.py:574
  67.2 1.0 %shard_map.101 = f32[8,32,64]{2,1,0:T(8,128)} custom-call(f32[128,128]{1,0:T(8,128)S(1)} %get-tuple-element.52.gains_ref), custom_call_target="tpu_custom_call" | custom-call | flops 20000000 | bytes 131072 | tf_op jit(solution)/shard_map/pallas_call | solution.py:547
  68.5 1.6 %collective-permute-done.33.refs_2_ = f32[64,128]{1,0:T(8,128)S(1)} collective-permute-done((f32[64,128]{1,0:T(8,128)S(1)}, f32[64,128]{1,0:T(8,128)S(1)}, u32[]{:S(2)}, u32[]{:S(2)}) %collective-permute-start.33) | collective-permute-done | bytes 32800 | tf_op jit(solution)/shard_map/ppermute | solution.py:574
  70.5 1.2 %shard_map.102 = f32[9,8,64]{2,1,0:T(8,128)} custom-call(f32[64,128]{1,0:T(8,128)S(1)} %get-tuple-element.53.refs_0_, f32[64,128]{1,0:T(8,128)S(1)} %collective-permute-done.32.refs_1_, f32[64,128]{1,0:T(8,128)S(1)} %collective-permute-done.33.refs_2_, f32[64,128]{1,0:T(8,128)S(1)} %collective-permute-done.34.refs_3_, ...), custom_call_target="tpu_custom_call" | custom-call | flops 20000000 | bytes 215040 | tf_op jit(solution)/shard_map/pallas_call | solution.py:547
  (57 shorter events, 9.3 us)
Async XLA Ops:
  2.1 12.7 %collective-permute-start.3 = (f32[136,128]{1,0:T(8,128)S(1)}, f32[136,128]{1,0:T(8,128)S(1)}, u32[]{:S(2)}, u32[]{:S(2)}) collective-permute-start(f32[136,128]{1,0:T(8,128)S(1)} %shard_map.86.refs_0_), channel_id=1, source_target_pairs={{0,1},{1,0},{2,3},{3,2},{4,5},{5,4},{6,7},{7,6},{8,9},{9,8},{10,11... | collective-permute-start | bytes 208904 | tf_op jit(solution)/shard_map/ppermute | solution.py:567
  2.6 11.5 %collective-permute-start.2 = (f32[136,128]{1,0:T(8,128)S(1)}, f32[136,128]{1,0:T(8,128)S(1)}, u32[]{:S(2)}, u32[]{:S(2)}) collective-permute-start(f32[136,128]{1,0:T(8,128)S(1)} %shard_map.86.refs_0_), channel_id=1, source_target_pairs={{0,6},{1,7},{2,4},{3,5},{4,2},{5,3},{6,0},{7,1},{8,14},{9,15},{10,... | collective-permute-start | bytes 208904 | tf_op jit(solution)/shard_map/ppermute | solution.py:561
  7.3 7.4 %collective-permute-start.1 = (f32[136,128]{1,0:T(8,128)S(1)}, f32[136,128]{1,0:T(8,128)S(1)}, u32[]{:S(2)}, u32[]{:S(2)}) collective-permute-start(f32[136,128]{1,0:T(8,128)S(1)} %shard_map.86.refs_0_), channel_id=1, source_target_pairs={{0,4},{1,5},{2,6},{3,7},{4,0},{5,1},{6,2},{7,3},{8,12},{9,13},{10,... | collective-permute-start | bytes 208904 | tf_op jit(solution)/shard_map/ppermute | solution.py:561
  7.3 6.9 %collective-permute-start = (f32[136,128]{1,0:T(8,128)S(1)}, f32[136,128]{1,0:T(8,128)S(1)}, u32[]{:S(2)}, u32[]{:S(2)}) collective-permute-start(f32[136,128]{1,0:T(8,128)S(1)} %shard_map.86.refs_0_), channel_id=1, source_target_pairs={{0,2},{1,3},{2,0},{3,1},{4,6},{5,7},{6,4},{7,5},{8,10},{9,11},{10,... | collective-permute-start | bytes 208904 | tf_op jit(solution)/shard_map/ppermute | solution.py:561
  14.1 1.3 %collective-permute-start.6 = (f32[136,128]{1,0:T(8,128)S(1)}, f32[136,128]{1,0:T(8,128)S(1)}, u32[]{:S(2)}, u32[]{:S(2)}) collective-permute-start(f32[136,128]{1,0:T(8,128)S(1)} %collective-permute-done.2.refs_3_), channel_id=1, source_target_pairs={{0,1},{1,0},{2,3},{3,2},{4,5},{5,4},{6,7},{7,6},{8,9},{9,8},{10,11... | collective-permute-start | bytes 208904 | tf_op jit(solution)/shard_map/ppermute | solution.py:567
  14.2 1.4 %collective-permute-start.4 = (f32[136,128]{1,0:T(8,128)S(1)}, f32[136,128]{1,0:T(8,128)S(1)}, u32[]{:S(2)}, u32[]{:S(2)}) collective-permute-start(f32[136,128]{1,0:T(8,128)S(1)} %collective-permute-done.refs_1_), channel_id=1, source_target_pairs={{0,1},{1,0},{2,3},{3,2},{4,5},{5,4},{6,7},{7,6},{8,9},{9,8},{10,11... | collective-permute-start | bytes 208904 | tf_op jit(solution)/shard_map/ppermute | solution.py:567
  17.3 10.9 %collective-permute-start.8 = (f32[192,128]{1,0:T(8,128)S(1)}, f32[192,128]{1,0:T(8,128)S(1)}, u32[]{:S(2)}, u32[]{:S(2)}) collective-permute-start(f32[192,128]{1,0:T(8,128)S(1)} %get-tuple-element.31.refs_0_), channel_id=1, source_target_pairs={{0,4},{1,5},{2,6},{3,7},{4,0},{5,1},{6,2},{7,3},{8,12},{9,13},{10,... | collective-permute-start | bytes 294920 | tf_op jit(solution)/shard_map/ppermute | solution.py:561
  19.7 8.5 %collective-permute-start.9 = (f32[192,128]{1,0:T(8,128)S(1)}, f32[192,128]{1,0:T(8,128)S(1)}, u32[]{:S(2)}, u32[]{:S(2)}) collective-permute-start(f32[192,128]{1,0:T(8,128)S(1)} %get-tuple-element.31.refs_0_), channel_id=1, source_target_pairs={{0,6},{1,7},{2,4},{3,5},{4,2},{5,3},{6,0},{7,1},{8,14},{9,15},{10,... | collective-permute-start | bytes 294920 | tf_op jit(solution)/shard_map/ppermute | solution.py:561
  21.2 7.6 %collective-permute-start.7 = (f32[192,128]{1,0:T(8,128)S(1)}, f32[192,128]{1,0:T(8,128)S(1)}, u32[]{:S(2)}, u32[]{:S(2)}) collective-permute-start(f32[192,128]{1,0:T(8,128)S(1)} %get-tuple-element.31.refs_0_), channel_id=1, source_target_pairs={{0,2},{1,3},{2,0},{3,1},{4,6},{5,7},{6,4},{7,5},{8,10},{9,11},{10,... | collective-permute-start | bytes 294920 | tf_op jit(solution)/shard_map/ppermute | solution.py:561
  21.7 7.1 %collective-permute-start.10 = (f32[192,128]{1,0:T(8,128)S(1)}, f32[192,128]{1,0:T(8,128)S(1)}, u32[]{:S(2)}, u32[]{:S(2)}) collective-permute-start(f32[192,128]{1,0:T(8,128)S(1)} %get-tuple-element.31.refs_0_), channel_id=1, source_target_pairs={{0,1},{1,0},{2,3},{3,2},{4,5},{5,4},{6,7},{7,6},{8,9},{9,8},{10,11... | collective-permute-start | bytes 294920 | tf_op jit(solution)/shard_map/ppermute | solution.py:567
  28.2 1.5 %collective-permute-start.12 = (f32[192,128]{1,0:T(8,128)S(1)}, f32[192,128]{1,0:T(8,128)S(1)}, u32[]{:S(2)}, u32[]{:S(2)}) collective-permute-start(f32[192,128]{1,0:T(8,128)S(1)} %shard_map.91.refs_2_), channel_id=1, source_target_pairs={{0,1},{1,0},{2,3},{3,2},{4,5},{5,4},{6,7},{7,6},{8,9},{9,8},{10,11... | collective-permute-start | bytes 294920 | tf_op jit(solution)/shard_map/ppermute | solution.py:567
  28.2 1.5 %collective-permute-start.13 = (f32[192,128]{1,0:T(8,128)S(1)}, f32[192,128]{1,0:T(8,128)S(1)}, u32[]{:S(2)}, u32[]{:S(2)}) collective-permute-start(f32[192,128]{1,0:T(8,128)S(1)} %collective-permute-done.9.refs_3_), channel_id=1, source_target_pairs={{0,1},{1,0},{2,3},{3,2},{4,5},{5,4},{6,7},{7,6},{8,9},{9,8},{10,11... | collective-permute-start | bytes 294920 | tf_op jit(solution)/shard_map/ppermute | solution.py:567
  32.0 6.1 %collective-permute-start.16 = (f32[144,128]{1,0:T(8,128)S(1)}, f32[144,128]{1,0:T(8,128)S(1)}, u32[]{:S(2)}, u32[]{:S(2)}) collective-permute-start(f32[144,128]{1,0:T(8,128)S(1)} %shard_map.93), channel_id=1, source_target_pairs={{0,8},{8,0},{16,24},{24,16},{1,9},{9,1},{17,25},{25,17},{2,10},{10... | collective-permute-start | bytes 221192 | tf_op jit(solution)/shard_map/ppermute | solution.py:582
  33.7 6.6 %collective-permute-start.18 = (f32[192,128]{1,0:T(8,128)S(1)}, f32[192,128]{1,0:T(8,128)S(1)}, u32[]{:S(2)}, u32[]{:S(2)}) collective-permute-start(f32[192,128]{1,0:T(8,128)S(1)} %get-tuple-element.38.refs_0_), channel_id=1, source_target_pairs={{0,6},{1,7},{2,4},{3,5},{4,2},{5,3},{6,0},{7,1},{8,14},{9,15},{10,... | collective-permute-start | bytes 294920 | tf_op jit(solution)/shard_map/ppermute | solution.py:561
  36.7 9.3 %collective-permute-start.15 = (f32[192,128]{1,0:T(8,128)S(1)}, f32[192,128]{1,0:T(8,128)S(1)}, u32[]{:S(2)}, u32[]{:S(2)}) collective-permute-start(f32[192,128]{1,0:T(8,128)S(1)} %get-tuple-element.38.refs_0_), channel_id=1, source_target_pairs={{0,4},{1,5},{2,6},{3,7},{4,0},{5,1},{6,2},{7,3},{8,12},{9,13},{10,... | collective-permute-start | bytes 294920 | tf_op jit(solution)/shard_map/ppermute | solution.py:561
  36.7 9.3 %collective-permute-start.14 = (f32[192,128]{1,0:T(8,128)S(1)}, f32[192,128]{1,0:T(8,128)S(1)}, u32[]{:S(2)}, u32[]{:S(2)}) collective-permute-start(f32[192,128]{1,0:T(8,128)S(1)} %get-tuple-element.38.refs_0_), channel_id=1, source_target_pairs={{0,2},{1,3},{2,0},{3,1},{4,6},{5,7},{6,4},{7,5},{8,10},{9,11},{10,... | collective-permute-start | bytes 294920 | tf_op jit(solution)/shard_map/ppermute | solution.py:561
  38.1 4.4 %collective-permute-start.17 = (f32[144,128]{1,0:T(8,128)S(1)}, f32[144,128]{1,0:T(8,128)S(1)}, u32[]{:S(2)}, u32[]{:S(2)}) collective-permute-start(f32[144,128]{1,0:T(8,128)S(1)} %add.6.one_ref), channel_id=1, source_target_pairs={{0,16},{8,24},{16,0},{24,8},{1,17},{9,25},{17,1},{25,9},{2,18},{10... | collective-permute-start | bytes 221192 | tf_op jit(solution)/shard_map/ppermute | solution.py:584
  39.7 6.9 %collective-permute-start.19 = (f32[192,128]{1,0:T(8,128)S(1)}, f32[192,128]{1,0:T(8,128)S(1)}, u32[]{:S(2)}, u32[]{:S(2)}) collective-permute-start(f32[192,128]{1,0:T(8,128)S(1)} %get-tuple-element.38.refs_0_), channel_id=1, source_target_pairs={{0,1},{1,0},{2,3},{3,2},{4,5},{5,4},{6,7},{7,6},{8,9},{9,8},{10,11... | collective-permute-start | bytes 294920 | tf_op jit(solution)/shard_map/ppermute | solution.py:567
  40.4 6.2 %collective-permute-start.22 = (f32[192,128]{1,0:T(8,128)S(1)}, f32[192,128]{1,0:T(8,128)S(1)}, u32[]{:S(2)}, u32[]{:S(2)}) collective-permute-start(f32[192,128]{1,0:T(8,128)S(1)} %collective-permute-done.18.refs_3_), channel_id=1, source_target_pairs={{0,1},{1,0},{2,3},{3,2},{4,5},{5,4},{6,7},{7,6},{8,9},{9,8},{10,11... | collective-permute-start | bytes 294920 | tf_op jit(solution)/shard_map/ppermute | solution.py:567
  46.0 1.3 %collective-permute-start.20 = (f32[192,128]{1,0:T(8,128)S(1)}, f32[192,128]{1,0:T(8,128)S(1)}, u32[]{:S(2)}, u32[]{:S(2)}) collective-permute-start(f32[192,128]{1,0:T(8,128)S(1)} %get-tuple-element.42.refs_1_), channel_id=1, source_target_pairs={{0,1},{1,0},{2,3},{3,2},{4,5},{5,4},{6,7},{7,6},{8,9},{9,8},{10,11... | collective-permute-start | bytes 294920 | tf_op jit(solution)/shard_map/ppermute | solution.py:567
  46.1 1.5 %collective-permute-start.21 = (f32[192,128]{1,0:T(8,128)S(1)}, f32[192,128]{1,0:T(8,128)S(1)}, u32[]{:S(2)}, u32[]{:S(2)}) collective-permute-start(f32[192,128]{1,0:T(8,128)S(1)} %get-tuple-element.43.refs_2_), channel_id=1, source_target_pairs={{0,1},{1,0},{2,3},{3,2},{4,5},{5,4},{6,7},{7,6},{8,9},{9,8},{10,11... | collective-permute-start | bytes 294920 | tf_op jit(solution)/shard_map/ppermute | solution.py:567
  49.3 5.0 %collective-permute-start.25 = (f32[128,128]{1,0:T(8,128)S(1)}, f32[128,128]{1,0:T(8,128)S(1)}, u32[]{:S(2)}, u32[]{:S(2)}) collective-permute-start(f32[128,128]{1,0:T(8,128)S(1)} %shard_map.97), channel_id=1, source_target_pairs={{0,8},{8,0},{16,24},{24,16},{1,9},{9,1},{17,25},{25,17},{2,10},{10... | collective-permute-start | bytes 196616 | tf_op jit(solution)/shard_map/ppermute | solution.py:582
  49.9 7.5 %collective-permute-start.27 = (f32[192,128]{1,0:T(8,128)S(1)}, f32[192,128]{1,0:T(8,128)S(1)}, u32[]{:S(2)}, u32[]{:S(2)}) collective-permute-start(f32[192,128]{1,0:T(8,128)S(1)} %get-tuple-element.44.refs_0_), channel_id=1, source_target_pairs={{0,6},{1,7},{2,4},{3,5},{4,2},{5,3},{6,0},{7,1},{8,14},{9,15},{10,... | collective-permute-start | bytes 294920 | tf_op jit(solution)/shard_map/ppermute | solution.py:561
  52.6 8.8 %collective-permute-start.24 = (f32[192,128]{1,0:T(8,128)S(1)}, f32[192,128]{1,0:T(8,128)S(1)}, u32[]{:S(2)}, u32[]{:S(2)}) collective-permute-start(f32[192,128]{1,0:T(8,128)S(1)} %get-tuple-element.44.refs_0_), channel_id=1, source_target_pairs={{0,4},{1,5},{2,6},{3,7},{4,0},{5,1},{6,2},{7,3},{8,12},{9,13},{10,... | collective-permute-start | bytes 294920 | tf_op jit(solution)/shard_map/ppermute | solution.py:561
  52.6 8.8 %collective-permute-start.23 = (f32[192,128]{1,0:T(8,128)S(1)}, f32[192,128]{1,0:T(8,128)S(1)}, u32[]{:S(2)}, u32[]{:S(2)}) collective-permute-start(f32[192,128]{1,0:T(8,128)S(1)} %get-tuple-element.44.refs_0_), channel_id=1, source_target_pairs={{0,2},{1,3},{2,0},{3,1},{4,6},{5,7},{6,4},{7,5},{8,10},{9,11},{10,... | collective-permute-start | bytes 294920 | tf_op jit(solution)/shard_map/ppermute | solution.py:561
  54.4 4.3 %collective-permute-start.26 = (f32[128,128]{1,0:T(8,128)S(1)}, f32[128,128]{1,0:T(8,128)S(1)}, u32[]{:S(2)}, u32[]{:S(2)}) collective-permute-start(f32[128,128]{1,0:T(8,128)S(1)} %add.7.one_ref), channel_id=1, source_target_pairs={{0,16},{8,24},{16,0},{24,8},{1,17},{9,25},{17,1},{25,9},{2,18},{10... | collective-permute-start | bytes 196616 | tf_op jit(solution)/shard_map/ppermute | solution.py:584
  55.9 6.0 %collective-permute-start.28 = (f32[192,128]{1,0:T(8,128)S(1)}, f32[192,128]{1,0:T(8,128)S(1)}, u32[]{:S(2)}, u32[]{:S(2)}) collective-permute-start(f32[192,128]{1,0:T(8,128)S(1)} %get-tuple-element.44.refs_0_), channel_id=1, source_target_pairs={{0,1},{1,0},{2,3},{3,2},{4,5},{5,4},{6,7},{7,6},{8,9},{9,8},{10,11... | collective-permute-start | bytes 294920 | tf_op jit(solution)/shard_map/ppermute | solution.py:567
  57.5 4.5 %collective-permute-start.31 = (f32[192,128]{1,0:T(8,128)S(1)}, f32[192,128]{1,0:T(8,128)S(1)}, u32[]{:S(2)}, u32[]{:S(2)}) collective-permute-start(f32[192,128]{1,0:T(8,128)S(1)} %collective-permute-done.27.refs_3_), channel_id=1, source_target_pairs={{0,1},{1,0},{2,3},{3,2},{4,5},{5,4},{6,7},{7,6},{8,9},{9,8},{10,11... | collective-permute-start | bytes 294920 | tf_op jit(solution)/shard_map/ppermute | solution.py:567
  61.4 1.5 %collective-permute-start.30 = (f32[192,128]{1,0:T(8,128)S(1)}, f32[192,128]{1,0:T(8,128)S(1)}, u32[]{:S(2)}, u32[]{:S(2)}) collective-permute-start(f32[192,128]{1,0:T(8,128)S(1)} %get-tuple-element.50.refs_2_), channel_id=1, source_target_pairs={{0,1},{1,0},{2,3},{3,2},{4,5},{5,4},{6,7},{7,6},{8,9},{9,8},{10,11... | collective-permute-start | bytes 294920 | tf_op jit(solution)/shard_map/ppermute | solution.py:567
  63.6 4.9 %collective-permute-start.34 = (f32[64,128]{1,0:T(8,128)S(1)}, f32[64,128]{1,0:T(8,128)S(1)}, u32[]{:S(2)}, u32[]{:S(2)}) collective-permute-start(f32[64,128]{1,0:T(8,128)S(1)} %get-tuple-element.53.refs_0_), channel_id=1, source_target_pairs={{0,24},{8,16},{16,8},{24,0},{1,25},{9,17},{17,9},{25,1},{2,26},{10... | collective-permute-start | bytes 98312 | tf_op jit(solution)/shard_map/ppermute | solution.py:574
  66.1 3.9 %collective-permute-start.33 = (f32[64,128]{1,0:T(8,128)S(1)}, f32[64,128]{1,0:T(8,128)S(1)}, u32[]{:S(2)}, u32[]{:S(2)}) collective-permute-start(f32[64,128]{1,0:T(8,128)S(1)} %get-tuple-element.53.refs_0_), channel_id=1, source_target_pairs={{0,16},{8,24},{16,0},{24,8},{1,17},{9,25},{17,1},{25,9},{2,18},{10... | collective-permute-start | bytes 98312 | tf_op jit(solution)/shard_map/ppermute | solution.py:574
  66.6 3.9 %collective-permute-start.32 = (f32[64,128]{1,0:T(8,128)S(1)}, f32[64,128]{1,0:T(8,128)S(1)}, u32[]{:S(2)}, u32[]{:S(2)}) collective-permute-start(f32[64,128]{1,0:T(8,128)S(1)} %get-tuple-element.53.refs_0_), channel_id=1, source_target_pairs={{0,8},{8,0},{16,24},{24,16},{1,9},{9,1},{17,25},{25,17},{2,10},{10... | collective-permute-start | bytes 98312 | tf_op jit(solution)/shard_map/ppermute | solution.py:574
  (3 other events, 3.9 us)

commit v2 on v1

--- a/solution.py
+++ b/solution.py
@@ -214,16 +214,20 @@
     at_ref, basis_ref, chans_ref, pair_ref, chan_ref, flag_ref, vis_ref, model_ref, mt_ref, sems
 ):
     planes, width, cells = vis_ref.shape
-    moves = [(pair_hbm, pair_ref), (chan_hbm, chan_ref), (flag_hbm, flag_ref)]
-    for source, target in ((model_hbm, model_ref), (vis_hbm, vis_ref)):
-        moves += [(source.at[m], target.at[m]) for m in range(planes)]
+    moves = [
+        (model_hbm, model_ref),
+        (vis_hbm, vis_ref),
+        (pair_hbm, pair_ref),
+        (chan_hbm, chan_ref),
+        (flag_hbm, flag_ref),
+    ]
     copies = [
         pltpu.make_async_copy(source, target, sems.at[n])
         for n, (source, target) in enumerate(moves)
     ]
-    for copy in copies[: 3 + planes]:
+    for copy in copies:
         copy.start()
-    for copy in copies[:3]:
+    for copy in copies[2:]:
         copy.wait()
     pairs = scalar_pairs(pair_ref)
     tiles = len(pairs)
@@ -266,10 +270,8 @@
         beside = jnp.concatenate([product[:half], product[half:]], 1)
         prod_ref[at] = pick(beside, fold).reshape(prod_ref.shape[1:])
 
-    order = [4 * (m % 2) + m // 2 for m in range(planes)]
+    copies[0].wait()
     for m in range(planes):
-        copies[3 + m].wait()
-        copies[3 + planes + order[m]].start()
         masked = (model_ref[m].astype(F32) * weight).astype(BF16)
         mt_ref[m] = nt(ident, masked)
     for x in range(4):
@@ -278,9 +280,8 @@
         x_re, x_im, y_re, y_im = mt_ref[x], mt_ref[4 + x], mt_ref[y], mt_ref[4 + y]
         put(36 + n, x_re * y_re + x_im * y_im)
         put(42 + n, x_im * y_re - x_re * y_im)
+    copies[1].wait()
     for x in range(4):
-        copies[3 + planes + x].wait()
-        copies[3 + planes + 4 + x].wait()
         v_re, v_im = nt(ident, vis_ref[x]), nt(ident, vis_ref[4 + x])
         for y in range(4):
             m_re, m_im = mt_ref[y], mt_ref[4 + y]
@@ -292,7 +293,7 @@
     pass
 
 
-def after(values, others):
+def after(values, others, flops=0):
     place = pl.BlockSpec(memory_space=pl.ANY)
     return pl.pallas_call(
         tie_kernel,
@@ -301,6 +302,7 @@
         out_specs=[place] * len(values),
         input_output_aliases={n: n for n in range(len(values))},
         compiler_params=pltpu.CompilerParams(vmem_limit_bytes=1024 * 1024),
+        cost_estimate=pl.CostEstimate(flops=flops, bytes_accessed=0, transcendentals=0),
     )(*values, *others)
 
 
@@ -351,7 +353,7 @@
         return tuple(new)
 
     zero = jnp.zeros((half, LANES), F32)
-    totals = lax.fori_loop(0, half, step, (zero,) * 24)
+    totals = lax.fori_loop(0, half, step, (zero,) * 24, unroll=2)
     for k in range(12):
         mine = a_s[k]
         for h in range(2):
@@ -555,12 +557,14 @@
     )(*operands)
 
 
-def share_base(x, last=(), ties=(2,)):
+def share_base(x, last=(), ties=(2,), ahead=False):
     devices = lax.axis_size("base")
     mine = [x] + [
         lax.ppermute(x, "base", [(d, d ^ (2 * k)) for d in range(devices)])
         for k in range(1, devices // 2)
     ]
+    if ahead:
+        mine[3:] = after(mine[3:], (), flops=5_000_000_000)
     if last:
         for k, y in zip(ties, after([mine[k] for k in ties], last)):
             mine[k] = y
@@ -637,7 +641,7 @@
             pltpu.VMEM(flags.shape, jnp.int32),
             *[pltpu.VMEM((8, width, cells), BF16)] * 2,
             pltpu.VMEM((8, cells, width), F32),
-            pltpu.SemaphoreType.DMA((19,)),
+            pltpu.SemaphoreType.DMA((5,)),
         ],
         hbm=True,
         flops=2_000_000_000,
@@ -671,7 +675,7 @@
     z, dual, inverse = call(
         first_consensus_kernel, (*sum_band(part), gains, basis), [wide, wide, narrow]
     )
-    pieces = share_base(message, last=(z,), ties=(1, 2))
+    pieces = share_base(message, last=(z,), ties=(1, 2), ahead=True)
     gains, message = call(
         functools.partial(step_kernel, count),
         (*pieces, select, z, pen, scale, products),
@@ -680,7 +684,7 @@
     )
     (part,) = call(total_kernel, (gains, dual, basis), [narrow])
     z, dual = call(consensus_kernel, (*sum_band(part), gains, dual, basis, inverse), [wide, wide])
-    pieces = share_base(message, last=(z,), ties=(1, 2))
+    pieces = share_base(message, last=(z,), ties=(1, 2), ahead=True)
     gains, part = call(
         functools.partial(last_kernel, count),
         (*pieces, select, z, pen, scale, dual, basis),

time: 71.9 us -> 68.7 us (0.955)
  Pallas kernels: 18.1 us -> 16.2 us
  waiting for transfers between devices: 22.7 us -> 21 us
    ppermute x12, waiting for transfers between devices: 12.6 us -> 7.59 us  [share_base(): lax.ppermute(x, 'base', [(d, d ^ 2 * k) for d in range(devices)])]
    ppermute x2, waiting for transfers between devices: 3.37 us -> 5.57 us  [sum_band(): return (x, lax.ppermute(x, 'band', [(d, d ^ step) for d in range(devices)]))]
    pallas_call x13, Pallas kernels: 18.1 us -> 16.2 us  [call(): pl.pallas_call(kernel, out_shape=shapes, in_specs=in_specs, out_specs=[vm...]
    ppermute x2, waiting for transfers between devices: 0.01 us -> 1.11 us  [sum_band(): x = x + lax.ppermute(x, 'band', [(d, d ^ step) for d in range(devices)])]
    ppermute x2, starting transfers between devices: 2.3 us -> 3.11 us  [sum_band(): x = x + lax.ppermute(x, 'band', [(d, d ^ step) for d in range(devices)])]
  transfers between devices with their start and end apart: 35 -> 35, of which waited for: 20 -> 18; matrix products, arithmetic and copies ran while one was open for 0% -> 0% of each run, Pallas kernels for 13% -> 13%
where the time goes in v2:
time: 68.7 us; the launch traced here: 68.6 us
  starting transfers between devices  30.6 us (45%)
  waiting for transfers between devices  21 us (31%)
  Pallas kernels  16.2 us (24%)
  between operations  0.8 us (1%)
    ppermute x12, starting transfers between devices, share_base(): lax.ppermute(x, 'base', [(d, d ^ 2 * k) for d in range(devices)])  18 us
    pallas_call x13, Pallas kernels, call(): pl.pallas_call(kernel, out_shape=shapes, in_specs=in_specs, out_specs=[vm...  16.2 us
    ppermute x12, waiting for transfers between devices, share_base(): lax.ppermute(x, 'base', [(d, d ^ 2 * k) for d in range(devices)])  7.59 us
    ppermute x2, waiting for transfers between devices, sum_band(): return (x, lax.ppermute(x, 'band', [(d, d ^ step) for d in range(devices)]))  5.57 us
    ppermute x16, waiting for transfers between devices, share_base(): lax.ppermute(y, 'base', [(d, d ^ 1) for d in range(devices)])  4.39 us
    ppermute x3, starting transfers between devices, share_band(): lax.ppermute(x, 'band', [(d, d ^ k) for d in range(devices)])  3.55 us
    ppermute x2, starting transfers between devices, sum_band(): return (x, lax.ppermute(x, 'band', [(d, d ^ step) for d in range(devices)]))  3.17 us
    ppermute x2, starting transfers between devices, sum_band(): x = x + lax.ppermute(x, 'band', [(d, d ^ step) for d in range(devices)])  3.11 us
  transfers between devices with their start and end apart: 35, of which 18 were waited for; matrix products, arithmetic and copies ran while one was open for 0% of the time, Pallas kernels for 13%

profile of v2, /device:TPU:0, one launch (start us, length us, event | category | flops | bytes accessed | tf_op | source)
XLA Modules:
  0.0 68.6 jit_solution(4072996222057195698)
XLA Ops:
  0.6 1.4 %shard_map.86.refs_0_ = f32[136,128]{1,0:T(8,128)S(1)} custom-call(s32[2,2]{1,0:T(2,128)} %pair_hbm.3, f32[8,32,64]{2,1,0:T(8,128)} %start_hbm.1, f32[1,64]{1,0:T(1,128)} %bitcast.6, s32[2,256]{1,0:T(2,128)} %flag_hbm.3), custom_call_target="tpu_custom_call" | custom-call | flops 20000000 | bytes 137488 | tf_op jit(solution)/shard_map/pallas_call | solution.py:549
  2.6 4.7 %collective-permute-start.2 = (f32[136,128]{1,0:T(8,128)S(1)}, f32[136,128]{1,0:T(8,128)S(1)}, u32[]{:S(2)}, u32[]{:S(2)}) collective-permute-start(f32[136,128]{1,0:T(8,128)S(1)} %shard_map.86.refs_0_), channel_id=1, source_target_pairs={{0,6},{1,7},{2,4},{3,5},{4,2},{5,3},{6,0},{7,1},{8,14},{9,15},{10,... | collective-permute-start | bytes 208904 | tf_op jit(solution)/shard_map/ppermute | solution.py:563
  7.3 0.6 collective-permute-start
  7.9 4.6 %shard_map.87 = (f32[48,8,16,128]{3,2,1,0:T(8,128)S(1)}, f32[256,128]{1,0:T(8,128)S(1)}, f32[256,128]{1,0:T(8,128)S(1)}, f32[256,128]{1,0:T(8,128)S(1)}, f32[8,256]{1,0:T(8,128)S(1)}) custom-call(s32[2,2]{1,0:T(2,128)} %pair_hbm.3, s32[1,64]{1,0:T(1,128)} %bitcast.9, s32[2,256]{1,0:T(2,128)} %flag_hbm.3, bf16[8,128,256]{2,1,0:T(8,128)(2,1)} %bitcast.7, ...), custom_call_target="tpu_custom_call" | custom-call | flops 2000000000 | bytes 4598032 | tf_op jit(solution)/shard_map/pallas_call | solution.py:549
  14.0 0.9 %collective-permute-done.5.refs_6_ = f32[136,128]{1,0:T(8,128)S(1)} collective-permute-done((f32[136,128]{1,0:T(8,128)S(1)}, f32[136,128]{1,0:T(8,128)S(1)}, u32[]{:S(2)}, u32[]{:S(2)}) %collective-permute-start.5) | collective-permute-done | bytes 69664 | tf_op jit(solution)/shard_map/ppermute | solution.py:571
  14.9 1.3 %shard_map.89 = (f32[128,128]{1,0:T(8,128)S(1)}, f32[192,128]{1,0:T(8,128)S(1)}) custom-call(f32[136,128]{1,0:T(8,128)S(1)} %shard_map.86.refs_0_, f32[136,128]{1,0:T(8,128)S(1)} %collective-permute-done.refs_1_, f32[136,128]{1,0:T(8,128)S(1)} %shard_map.88.refs_2_, f32[136,128]{1,0:T(8,128)S(1)} %collective-permute-done.2.refs_3_, ...), custom_call_target="tpu_custom_call" | custom-call | flops 20000000 | bytes 3997696 | tf_op jit(solution)/shard_map/pallas_call | solution.py:549
  16.3 1.8 %collective-permute-start.8 = (f32[192,128]{1,0:T(8,128)S(1)}, f32[192,128]{1,0:T(8,128)S(1)}, u32[]{:S(2)}, u32[]{:S(2)}) collective-permute-start(f32[192,128]{1,0:T(8,128)S(1)} %get-tuple-element.31.refs_0_), channel_id=1, source_target_pairs={{0,4},{1,5},{2,6},{3,7},{4,0},{5,1},{6,2},{7,3},{8,12},{9,13},{10,... | collective-permute-start | bytes 294920 | tf_op jit(solution)/shard_map/ppermute | solution.py:563
  18.0 1.9 %collective-permute-start.9 = (f32[192,128]{1,0:T(8,128)S(1)}, f32[192,128]{1,0:T(8,128)S(1)}, u32[]{:S(2)}, u32[]{:S(2)}) collective-permute-start(f32[192,128]{1,0:T(8,128)S(1)} %get-tuple-element.31.refs_0_), channel_id=1, source_target_pairs={{0,6},{1,7},{2,4},{3,5},{4,2},{5,3},{6,0},{7,1},{8,14},{9,15},{10,... | collective-permute-start | bytes 294920 | tf_op jit(solution)/shard_map/ppermute | solution.py:563
  20.6 6.5 %collective-permute-done.8.refs_0_ = f32[192,128]{1,0:T(8,128)S(1)} collective-permute-done((f32[192,128]{1,0:T(8,128)S(1)}, f32[192,128]{1,0:T(8,128)S(1)}, u32[]{:S(2)}, u32[]{:S(2)}) %collective-permute-start.8) | collective-permute-done | bytes 98336 | tf_op jit(solution)/shard_map/ppermute | solution.py:563
  27.7 0.9 %collective-permute-done.13.refs_7_ = f32[192,128]{1,0:T(8,128)S(1)} collective-permute-done((f32[192,128]{1,0:T(8,128)S(1)}, f32[192,128]{1,0:T(8,128)S(1)}, u32[]{:S(2)}, u32[]{:S(2)}) %collective-permute-start.13) | collective-permute-done | bytes 98336 | tf_op jit(solution)/shard_map/ppermute | solution.py:571
  29.0 1.5 %shard_map.92 = (f32[128,256]{1,0:T(8,128)S(1)}, f32[192,128]{1,0:T(8,128)S(1)}) custom-call(f32[192,128]{1,0:T(8,128)S(1)} %get-tuple-element.31.refs_0_, f32[192,128]{1,0:T(8,128)S(1)} %collective-permute-done.7.refs_1_, f32[192,128]{1,0:T(8,128)S(1)} %shard_map.91.refs_2_, f32[192,128]{1,0:T(8,128)S(1)} %collective-permute-done.9.refs_3_, ...), custom_call_target="tpu_custom_call" | custom-call | flops 20000000 | bytes 4849664 | tf_op jit(solution)/shard_map/pallas_call | solution.py:549
  30.4 2.7 %collective-permute-start.18 = (f32[192,128]{1,0:T(8,128)S(1)}, f32[192,128]{1,0:T(8,128)S(1)}, u32[]{:S(2)}, u32[]{:S(2)}) collective-permute-start(f32[192,128]{1,0:T(8,128)S(1)} %get-tuple-element.38.refs_0_), channel_id=1, source_target_pairs={{0,6},{1,7},{2,4},{3,5},{4,2},{5,3},{6,0},{7,1},{8,14},{9,15},{10,... | collective-permute-start | bytes 294920 | tf_op jit(solution)/shard_map/ppermute | solution.py:563
  33.5 1.6 %collective-permute-start.16 = (f32[144,128]{1,0:T(8,128)S(1)}, f32[144,128]{1,0:T(8,128)S(1)}, u32[]{:S(2)}, u32[]{:S(2)}) collective-permute-start(f32[144,128]{1,0:T(8,128)S(1)} %shard_map.93), channel_id=1, source_target_pairs={{0,8},{8,0},{16,24},{24,16},{1,9},{9,1},{17,25},{25,17},{2,10},{10... | collective-permute-start | bytes 221192 | tf_op jit(solution)/shard_map/ppermute | solution.py:586
  35.3 1.4 %collective-permute-start.14 = (f32[192,128]{1,0:T(8,128)S(1)}, f32[192,128]{1,0:T(8,128)S(1)}, u32[]{:S(2)}, u32[]{:S(2)}) collective-permute-start(f32[192,128]{1,0:T(8,128)S(1)} %get-tuple-element.38.refs_0_), channel_id=1, source_target_pairs={{0,2},{1,3},{2,0},{3,1},{4,6},{5,7},{6,4},{7,5},{8,10},{9,11},{10,... | collective-permute-start | bytes 294920 | tf_op jit(solution)/shard_map/ppermute | solution.py:563
  36.8 1.1 %collective-permute-done.16 = f32[144,128]{1,0:T(8,128)S(1)} collective-permute-done((f32[144,128]{1,0:T(8,128)S(1)}, f32[144,128]{1,0:T(8,128)S(1)}, u32[]{:S(2)}, u32[]{:S(2)}) %collective-permute-start.16) | collective-permute-done | bytes 73760 | tf_op jit(solution)/shard_map/ppermute | solution.py:586
  37.9 1.6 %collective-permute-start.17 = (f32[144,128]{1,0:T(8,128)S(1)}, f32[144,128]{1,0:T(8,128)S(1)}, u32[]{:S(2)}, u32[]{:S(2)}) collective-permute-start(f32[144,128]{1,0:T(8,128)S(1)} %add.6.one_ref), channel_id=1, source_target_pairs={{0,16},{8,24},{16,0},{24,8},{1,17},{9,25},{17,1},{25,9},{2,18},{10... | collective-permute-start | bytes 221192 | tf_op jit(solution)/shard_map/ppermute | solution.py:588
  39.5 2.8 %collective-permute-done.17.two_ref = f32[144,128]{1,0:T(8,128)S(1)} collective-permute-done((f32[144,128]{1,0:T(8,128)S(1)}, f32[144,128]{1,0:T(8,128)S(1)}, u32[]{:S(2)}, u32[]{:S(2)}) %collective-permute-start.17) | collective-permute-done | bytes 73760 | tf_op jit(solution)/shard_map/ppermute | solution.py:588
  42.3 1.5 %shard_map.94 = (f32[128,256]{1,0:T(8,128)S(1)}, f32[128,256]{1,0:T(8,128)S(1)}, f32[128,128]{1,0:T(8,128)S(1)}) custom-call(f32[144,128]{1,0:T(8,128)S(1)} %add.6.one_ref, f32[144,128]{1,0:T(8,128)S(1)} %collective-permute-done.17.two_ref, f32[128,256]{1,0:T(8,128)S(1)} %get-tuple-element.39.gains_ref, f32[256,128]{1,0:T(8,128)S(1)} %get-tuple-element.40.basis_ref.refs_13_), custom_call_target="tpu_custom_call" | custom-call | flops 20000000 | bytes 737280 | tf_op jit(solution)/shard_map/pallas_call | solution.py:549
  44.4 0.8 %collective-permute-done.20.refs_5_ = f32[192,128]{1,0:T(8,128)S(1)} collective-permute-done((f32[192,128]{1,0:T(8,128)S(1)}, f32[192,128]{1,0:T(8,128)S(1)}, u32[]{:S(2)}, u32[]{:S(2)}) %collective-permute-start.20) | collective-permute-done | bytes 98336 | tf_op jit(solution)/shard_map/ppermute | solution.py:571
  45.3 1.5 %shard_map.97 = (f32[128,256]{1,0:T(8,128)S(1)}, f32[192,128]{1,0:T(8,128)S(1)}) custom-call(f32[192,128]{1,0:T(8,128)S(1)} %get-tuple-element.38.refs_0_, f32[192,128]{1,0:T(8,128)S(1)} %get-tuple-element.42.refs_1_, f32[192,128]{1,0:T(8,128)S(1)} %get-tuple-element.43.refs_2_, f32[192,128]{1,0:T(8,128)S(1)} %shard_map.96.refs_3_, ...), custom_call_target="tpu_custom_call" | custom-call | flops 20000000 | bytes 4849664 | tf_op jit(solution)/shard_map/pallas_call | solution.py:549
  46.8 1.7 %collective-permute-start.27 = (f32[192,128]{1,0:T(8,128)S(1)}, f32[192,128]{1,0:T(8,128)S(1)}, u32[]{:S(2)}, u32[]{:S(2)}) collective-permute-start(f32[192,128]{1,0:T(8,128)S(1)} %get-tuple-element.44.refs_0_), channel_id=1, source_target_pairs={{0,6},{1,7},{2,4},{3,5},{4,2},{5,3},{6,0},{7,1},{8,14},{9,15},{10,... | collective-permute-start | bytes 294920 | tf_op jit(solution)/shard_map/ppermute | solution.py:563
  48.7 1.6 %collective-permute-start.25 = (f32[128,128]{1,0:T(8,128)S(1)}, f32[128,128]{1,0:T(8,128)S(1)}, u32[]{:S(2)}, u32[]{:S(2)}) collective-permute-start(f32[128,128]{1,0:T(8,128)S(1)} %shard_map.98), channel_id=1, source_target_pairs={{0,8},{8,0},{16,24},{24,16},{1,9},{9,1},{17,25},{25,17},{2,10},{10... | collective-permute-start | bytes 196616 | tf_op jit(solution)/shard_map/ppermute | solution.py:586
  50.8 2.3 %collective-permute-start.23 = (f32[192,128]{1,0:T(8,128)S(1)}, f32[192,128]{1,0:T(8,128)S(1)}, u32[]{:S(2)}, u32[]{:S(2)}) collective-permute-start(f32[192,128]{1,0:T(8,128)S(1)} %get-tuple-element.44.refs_0_), channel_id=1, source_target_pairs={{0,2},{1,3},{2,0},{3,1},{4,6},{5,7},{6,4},{7,5},{8,10},{9,11},{10,... | collective-permute-start | bytes 294920 | tf_op jit(solution)/shard_map/ppermute | solution.py:563
  53.1 1.6 %collective-permute-start.26 = (f32[128,128]{1,0:T(8,128)S(1)}, f32[128,128]{1,0:T(8,128)S(1)}, u32[]{:S(2)}, u32[]{:S(2)}) collective-permute-start(f32[128,128]{1,0:T(8,128)S(1)} %add.7.one_ref), channel_id=1, source_target_pairs={{0,16},{8,24},{16,0},{24,8},{1,17},{9,25},{17,1},{25,9},{2,18},{10... | collective-permute-start | bytes 196616 | tf_op jit(solution)/shard_map/ppermute | solution.py:588
  54.7 2.7 %collective-permute-done.26.two_ref = f32[128,128]{1,0:T(8,128)S(1)} collective-permute-done((f32[128,128]{1,0:T(8,128)S(1)}, f32[128,128]{1,0:T(8,128)S(1)}, u32[]{:S(2)}, u32[]{:S(2)}) %collective-permute-start.26) | collective-permute-done | bytes 65568 | tf_op jit(solution)/shard_map/ppermute | solution.py:588
  58.9 0.8 %collective-permute-done.29.refs_5_ = f32[192,128]{1,0:T(8,128)S(1)} collective-permute-done((f32[192,128]{1,0:T(8,128)S(1)}, f32[192,128]{1,0:T(8,128)S(1)}, u32[]{:S(2)}, u32[]{:S(2)}) %collective-permute-start.29) | collective-permute-done | bytes 98336 | tf_op jit(solution)/shard_map/ppermute | solution.py:571
  59.8 0.7 %shard_map.102 = (f32[128,128]{1,0:T(8,128)S(1)}, f32[64,128]{1,0:T(8,128)S(1)}) custom-call(f32[192,128]{1,0:T(8,128)S(1)} %get-tuple-element.44.refs_0_, f32[192,128]{1,0:T(8,128)S(1)} %get-tuple-element.49.refs_1_, f32[192,128]{1,0:T(8,128)S(1)} %get-tuple-element.50.refs_2_, f32[192,128]{1,0:T(8,128)S(1)} %shard_map.101.refs_3_, ...), custom_call_target="tpu_custom_call" | custom-call | flops 20000000 | bytes 1835008 | tf_op jit(solution)/shard_map/pallas_call | solution.py:549
  60.5 2.4 %collective-permute-start.34 = (f32[64,128]{1,0:T(8,128)S(1)}, f32[64,128]{1,0:T(8,128)S(1)}, u32[]{:S(2)}, u32[]{:S(2)}) collective-permute-start(f32[64,128]{1,0:T(8,128)S(1)} %get-tuple-element.53.refs_0_), channel_id=1, source_target_pairs={{0,24},{8,16},{16,8},{24,0},{1,25},{9,17},{17,9},{25,1},{2,26},{10... | collective-permute-start | bytes 98312 | tf_op jit(solution)/shard_map/ppermute | solution.py:578
  63.5 0.6 collective-permute-start.32
  64.1 1.0 %shard_map.103 = f32[8,32,64]{2,1,0:T(8,128)} custom-call(f32[128,128]{1,0:T(8,128)S(1)} %get-tuple-element.52.gains_ref), custom_call_target="tpu_custom_call" | custom-call | flops 20000000 | bytes 131072 | tf_op jit(solution)/shard_map/pallas_call | solution.py:549
  65.4 1.5 %collective-permute-done.33.refs_2_ = f32[64,128]{1,0:T(8,128)S(1)} collective-permute-done((f32[64,128]{1,0:T(8,128)S(1)}, f32[64,128]{1,0:T(8,128)S(1)}, u32[]{:S(2)}, u32[]{:S(2)}) %collective-permute-start.33) | collective-permute-done | bytes 32800 | tf_op jit(solution)/shard_map/ppermute | solution.py:578
  67.4 1.2 %shard_map.104 = f32[9,8,64]{2,1,0:T(8,128)} custom-call(f32[64,128]{1,0:T(8,128)S(1)} %get-tuple-element.53.refs_0_, f32[64,128]{1,0:T(8,128)S(1)} %collective-permute-done.32.refs_1_, f32[64,128]{1,0:T(8,128)S(1)} %collective-permute-done.33.refs_2_, f32[64,128]{1,0:T(8,128)S(1)} %collective-permute-done.34.refs_3_, ...), custom_call_target="tpu_custom_call" | custom-call | flops 20000000 | bytes 215040 | tf_op jit(solution)/shard_map/pallas_call | solution.py:549
  (59 shorter events, 8.6 us)
Async XLA Ops:
  2.1 11.6 %collective-permute-start.3 = (f32[136,128]{1,0:T(8,128)S(1)}, f32[136,128]{1,0:T(8,128)S(1)}, u32[]{:S(2)}, u32[]{:S(2)}) collective-permute-start(f32[136,128]{1,0:T(8,128)S(1)} %shard_map.86.refs_0_), channel_id=1, source_target_pairs={{0,1},{1,0},{2,3},{3,2},{4,5},{5,4},{6,7},{7,6},{8,9},{9,8},{10,11... | collective-permute-start | bytes 208904 | tf_op jit(solution)/shard_map/ppermute | solution.py:571
  2.6 9.9 %collective-permute-start.2 = (f32[136,128]{1,0:T(8,128)S(1)}, f32[136,128]{1,0:T(8,128)S(1)}, u32[]{:S(2)}, u32[]{:S(2)}) collective-permute-start(f32[136,128]{1,0:T(8,128)S(1)} %shard_map.86.refs_0_), channel_id=1, source_target_pairs={{0,6},{1,7},{2,4},{3,5},{4,2},{5,3},{6,0},{7,1},{8,14},{9,15},{10,... | collective-permute-start | bytes 208904 | tf_op jit(solution)/shard_map/ppermute | solution.py:563
  7.3 6.4 %collective-permute-start.1 = (f32[136,128]{1,0:T(8,128)S(1)}, f32[136,128]{1,0:T(8,128)S(1)}, u32[]{:S(2)}, u32[]{:S(2)}) collective-permute-start(f32[136,128]{1,0:T(8,128)S(1)} %shard_map.86.refs_0_), channel_id=1, source_target_pairs={{0,4},{1,5},{2,6},{3,7},{4,0},{5,1},{6,2},{7,3},{8,12},{9,13},{10,... | collective-permute-start | bytes 208904 | tf_op jit(solution)/shard_map/ppermute | solution.py:563
  7.3 5.3 %collective-permute-start = (f32[136,128]{1,0:T(8,128)S(1)}, f32[136,128]{1,0:T(8,128)S(1)}, u32[]{:S(2)}, u32[]{:S(2)}) collective-permute-start(f32[136,128]{1,0:T(8,128)S(1)} %shard_map.86.refs_0_), channel_id=1, source_target_pairs={{0,2},{1,3},{2,0},{3,1},{4,6},{5,7},{6,4},{7,5},{8,10},{9,11},{10,... | collective-permute-start | bytes 208904 | tf_op jit(solution)/shard_map/ppermute | solution.py:563
  12.5 1.3 %collective-permute-start.6 = (f32[136,128]{1,0:T(8,128)S(1)}, f32[136,128]{1,0:T(8,128)S(1)}, u32[]{:S(2)}, u32[]{:S(2)}) collective-permute-start(f32[136,128]{1,0:T(8,128)S(1)} %collective-permute-done.2.refs_3_), channel_id=1, source_target_pairs={{0,1},{1,0},{2,3},{3,2},{4,5},{5,4},{6,7},{7,6},{8,9},{9,8},{10,11... | collective-permute-start | bytes 208904 | tf_op jit(solution)/shard_map/ppermute | solution.py:571
  12.6 1.4 %collective-permute-start.4 = (f32[136,128]{1,0:T(8,128)S(1)}, f32[136,128]{1,0:T(8,128)S(1)}, u32[]{:S(2)}, u32[]{:S(2)}) collective-permute-start(f32[136,128]{1,0:T(8,128)S(1)} %collective-permute-done.refs_1_), channel_id=1, source_target_pairs={{0,1},{1,0},{2,3},{3,2},{4,5},{5,4},{6,7},{7,6},{8,9},{9,8},{10,11... | collective-permute-start | bytes 208904 | tf_op jit(solution)/shard_map/ppermute | solution.py:571
  16.3 10.9 %collective-permute-start.8 = (f32[192,128]{1,0:T(8,128)S(1)}, f32[192,128]{1,0:T(8,128)S(1)}, u32[]{:S(2)}, u32[]{:S(2)}) collective-permute-start(f32[192,128]{1,0:T(8,128)S(1)} %get-tuple-element.31.refs_0_), channel_id=1, source_target_pairs={{0,4},{1,5},{2,6},{3,7},{4,0},{5,1},{6,2},{7,3},{8,12},{9,13},{10,... | collective-permute-start | bytes 294920 | tf_op jit(solution)/shard_map/ppermute | solution.py:563
  18.0 9.1 %collective-permute-start.9 = (f32[192,128]{1,0:T(8,128)S(1)}, f32[192,128]{1,0:T(8,128)S(1)}, u32[]{:S(2)}, u32[]{:S(2)}) collective-permute-start(f32[192,128]{1,0:T(8,128)S(1)} %get-tuple-element.31.refs_0_), channel_id=1, source_target_pairs={{0,6},{1,7},{2,4},{3,5},{4,2},{5,3},{6,0},{7,1},{8,14},{9,15},{10,... | collective-permute-start | bytes 294920 | tf_op jit(solution)/shard_map/ppermute | solution.py:563
  20.0 7.7 %collective-permute-start.7 = (f32[192,128]{1,0:T(8,128)S(1)}, f32[192,128]{1,0:T(8,128)S(1)}, u32[]{:S(2)}, u32[]{:S(2)}) collective-permute-start(f32[192,128]{1,0:T(8,128)S(1)} %get-tuple-element.31.refs_0_), channel_id=1, source_target_pairs={{0,2},{1,3},{2,0},{3,1},{4,6},{5,7},{6,4},{7,5},{8,10},{9,11},{10,... | collective-permute-start | bytes 294920 | tf_op jit(solution)/shard_map/ppermute | solution.py:563
  20.1 7.6 %collective-permute-start.10 = (f32[192,128]{1,0:T(8,128)S(1)}, f32[192,128]{1,0:T(8,128)S(1)}, u32[]{:S(2)}, u32[]{:S(2)}) collective-permute-start(f32[192,128]{1,0:T(8,128)S(1)} %get-tuple-element.31.refs_0_), channel_id=1, source_target_pairs={{0,1},{1,0},{2,3},{3,2},{4,5},{5,4},{6,7},{7,6},{8,9},{9,8},{10,11... | collective-permute-start | bytes 294920 | tf_op jit(solution)/shard_map/ppermute | solution.py:571
  27.1 1.5 %collective-permute-start.12 = (f32[192,128]{1,0:T(8,128)S(1)}, f32[192,128]{1,0:T(8,128)S(1)}, u32[]{:S(2)}, u32[]{:S(2)}) collective-permute-start(f32[192,128]{1,0:T(8,128)S(1)} %shard_map.91.refs_2_), channel_id=1, source_target_pairs={{0,1},{1,0},{2,3},{3,2},{4,5},{5,4},{6,7},{7,6},{8,9},{9,8},{10,11... | collective-permute-start | bytes 294920 | tf_op jit(solution)/shard_map/ppermute | solution.py:571
  27.1 1.5 %collective-permute-start.13 = (f32[192,128]{1,0:T(8,128)S(1)}, f32[192,128]{1,0:T(8,128)S(1)}, u32[]{:S(2)}, u32[]{:S(2)}) collective-permute-start(f32[192,128]{1,0:T(8,128)S(1)} %collective-permute-done.9.refs_3_), channel_id=1, source_target_pairs={{0,1},{1,0},{2,3},{3,2},{4,5},{5,4},{6,7},{7,6},{8,9},{9,8},{10,11... | collective-permute-start | bytes 294920 | tf_op jit(solution)/shard_map/ppermute | solution.py:571
  30.4 9.0 %collective-permute-start.18 = (f32[192,128]{1,0:T(8,128)S(1)}, f32[192,128]{1,0:T(8,128)S(1)}, u32[]{:S(2)}, u32[]{:S(2)}) collective-permute-start(f32[192,128]{1,0:T(8,128)S(1)} %get-tuple-element.38.refs_0_), channel_id=1, source_target_pairs={{0,6},{1,7},{2,4},{3,5},{4,2},{5,3},{6,0},{7,1},{8,14},{9,15},{10,... | collective-permute-start | bytes 294920 | tf_op jit(solution)/shard_map/ppermute | solution.py:563
  33.5 4.4 %collective-permute-start.16 = (f32[144,128]{1,0:T(8,128)S(1)}, f32[144,128]{1,0:T(8,128)S(1)}, u32[]{:S(2)}, u32[]{:S(2)}) collective-permute-start(f32[144,128]{1,0:T(8,128)S(1)} %shard_map.93), channel_id=1, source_target_pairs={{0,8},{8,0},{16,24},{24,16},{1,9},{9,1},{17,25},{25,17},{2,10},{10... | collective-permute-start | bytes 221192 | tf_op jit(solution)/shard_map/ppermute | solution.py:586
  35.0 9.4 %collective-permute-start.19 = (f32[192,128]{1,0:T(8,128)S(1)}, f32[192,128]{1,0:T(8,128)S(1)}, u32[]{:S(2)}, u32[]{:S(2)}) collective-permute-start(f32[192,128]{1,0:T(8,128)S(1)} %get-tuple-element.38.refs_0_), channel_id=1, source_target_pairs={{0,1},{1,0},{2,3},{3,2},{4,5},{5,4},{6,7},{7,6},{8,9},{9,8},{10,11... | collective-permute-start | bytes 294920 | tf_op jit(solution)/shard_map/ppermute | solution.py:571
  35.0 8.8 %collective-permute-start.15 = (f32[192,128]{1,0:T(8,128)S(1)}, f32[192,128]{1,0:T(8,128)S(1)}, u32[]{:S(2)}, u32[]{:S(2)}) collective-permute-start(f32[192,128]{1,0:T(8,128)S(1)} %get-tuple-element.38.refs_0_), channel_id=1, source_target_pairs={{0,4},{1,5},{2,6},{3,7},{4,0},{5,1},{6,2},{7,3},{8,12},{9,13},{10,... | collective-permute-start | bytes 294920 | tf_op jit(solution)/shard_map/ppermute | solution.py:563
  35.3 8.4 %collective-permute-start.14 = (f32[192,128]{1,0:T(8,128)S(1)}, f32[192,128]{1,0:T(8,128)S(1)}, u32[]{:S(2)}, u32[]{:S(2)}) collective-permute-start(f32[192,128]{1,0:T(8,128)S(1)} %get-tuple-element.38.refs_0_), channel_id=1, source_target_pairs={{0,2},{1,3},{2,0},{3,1},{4,6},{5,7},{6,4},{7,5},{8,10},{9,11},{10,... | collective-permute-start | bytes 294920 | tf_op jit(solution)/shard_map/ppermute | solution.py:563
  37.9 4.4 %collective-permute-start.17 = (f32[144,128]{1,0:T(8,128)S(1)}, f32[144,128]{1,0:T(8,128)S(1)}, u32[]{:S(2)}, u32[]{:S(2)}) collective-permute-start(f32[144,128]{1,0:T(8,128)S(1)} %add.6.one_ref), channel_id=1, source_target_pairs={{0,16},{8,24},{16,0},{24,8},{1,17},{9,25},{17,1},{25,9},{2,18},{10... | collective-permute-start | bytes 221192 | tf_op jit(solution)/shard_map/ppermute | solution.py:588
  39.5 4.9 %collective-permute-start.22 = (f32[192,128]{1,0:T(8,128)S(1)}, f32[192,128]{1,0:T(8,128)S(1)}, u32[]{:S(2)}, u32[]{:S(2)}) collective-permute-start(f32[192,128]{1,0:T(8,128)S(1)} %shard_map.96.refs_3_), channel_id=1, source_target_pairs={{0,1},{1,0},{2,3},{3,2},{4,5},{5,4},{6,7},{7,6},{8,9},{9,8},{10,11... | collective-permute-start | bytes 294920 | tf_op jit(solution)/shard_map/ppermute | solution.py:571
  43.8 1.4 %collective-permute-start.20 = (f32[192,128]{1,0:T(8,128)S(1)}, f32[192,128]{1,0:T(8,128)S(1)}, u32[]{:S(2)}, u32[]{:S(2)}) collective-permute-start(f32[192,128]{1,0:T(8,128)S(1)} %get-tuple-element.42.refs_1_), channel_id=1, source_target_pairs={{0,1},{1,0},{2,3},{3,2},{4,5},{5,4},{6,7},{7,6},{8,9},{9,8},{10,11... | collective-permute-start | bytes 294920 | tf_op jit(solution)/shard_map/ppermute | solution.py:571
  43.9 1.4 %collective-permute-start.21 = (f32[192,128]{1,0:T(8,128)S(1)}, f32[192,128]{1,0:T(8,128)S(1)}, u32[]{:S(2)}, u32[]{:S(2)}) collective-permute-start(f32[192,128]{1,0:T(8,128)S(1)} %get-tuple-element.43.refs_2_), channel_id=1, source_target_pairs={{0,1},{1,0},{2,3},{3,2},{4,5},{5,4},{6,7},{7,6},{8,9},{9,8},{10,11... | collective-permute-start | bytes 294920 | tf_op jit(solution)/shard_map/ppermute | solution.py:571
  46.8 7.9 %collective-permute-start.27 = (f32[192,128]{1,0:T(8,128)S(1)}, f32[192,128]{1,0:T(8,128)S(1)}, u32[]{:S(2)}, u32[]{:S(2)}) collective-permute-start(f32[192,128]{1,0:T(8,128)S(1)} %get-tuple-element.44.refs_0_), channel_id=1, source_target_pairs={{0,6},{1,7},{2,4},{3,5},{4,2},{5,3},{6,0},{7,1},{8,14},{9,15},{10,... | collective-permute-start | bytes 294920 | tf_op jit(solution)/shard_map/ppermute | solution.py:563
  48.7 4.3 %collective-permute-start.25 = (f32[128,128]{1,0:T(8,128)S(1)}, f32[128,128]{1,0:T(8,128)S(1)}, u32[]{:S(2)}, u32[]{:S(2)}) collective-permute-start(f32[128,128]{1,0:T(8,128)S(1)} %shard_map.98), channel_id=1, source_target_pairs={{0,8},{8,0},{16,24},{24,16},{1,9},{9,1},{17,25},{25,17},{2,10},{10... | collective-permute-start | bytes 196616 | tf_op jit(solution)/shard_map/ppermute | solution.py:586
  50.3 8.6 %collective-permute-start.28 = (f32[192,128]{1,0:T(8,128)S(1)}, f32[192,128]{1,0:T(8,128)S(1)}, u32[]{:S(2)}, u32[]{:S(2)}) collective-permute-start(f32[192,128]{1,0:T(8,128)S(1)} %get-tuple-element.44.refs_0_), channel_id=1, source_target_pairs={{0,1},{1,0},{2,3},{3,2},{4,5},{5,4},{6,7},{7,6},{8,9},{9,8},{10,11... | collective-permute-start | bytes 294920 | tf_op jit(solution)/shard_map/ppermute | solution.py:571
  50.3 8.1 %collective-permute-start.24 = (f32[192,128]{1,0:T(8,128)S(1)}, f32[192,128]{1,0:T(8,128)S(1)}, u32[]{:S(2)}, u32[]{:S(2)}) collective-permute-start(f32[192,128]{1,0:T(8,128)S(1)} %get-tuple-element.44.refs_0_), channel_id=1, source_target_pairs={{0,4},{1,5},{2,6},{3,7},{4,0},{5,1},{6,2},{7,3},{8,12},{9,13},{10,... | collective-permute-start | bytes 294920 | tf_op jit(solution)/shard_map/ppermute | solution.py:563
  50.8 7.6 %collective-permute-start.23 = (f32[192,128]{1,0:T(8,128)S(1)}, f32[192,128]{1,0:T(8,128)S(1)}, u32[]{:S(2)}, u32[]{:S(2)}) collective-permute-start(f32[192,128]{1,0:T(8,128)S(1)} %get-tuple-element.44.refs_0_), channel_id=1, source_target_pairs={{0,2},{1,3},{2,0},{3,1},{4,6},{5,7},{6,4},{7,5},{8,10},{9,11},{10,... | collective-permute-start | bytes 294920 | tf_op jit(solution)/shard_map/ppermute | solution.py:563
  53.1 4.3 %collective-permute-start.26 = (f32[128,128]{1,0:T(8,128)S(1)}, f32[128,128]{1,0:T(8,128)S(1)}, u32[]{:S(2)}, u32[]{:S(2)}) collective-permute-start(f32[128,128]{1,0:T(8,128)S(1)} %add.7.one_ref), channel_id=1, source_target_pairs={{0,16},{8,24},{16,0},{24,8},{1,17},{9,25},{17,1},{25,9},{2,18},{10... | collective-permute-start | bytes 196616 | tf_op jit(solution)/shard_map/ppermute | solution.py:588
  54.7 4.2 %collective-permute-start.31 = (f32[192,128]{1,0:T(8,128)S(1)}, f32[192,128]{1,0:T(8,128)S(1)}, u32[]{:S(2)}, u32[]{:S(2)}) collective-permute-start(f32[192,128]{1,0:T(8,128)S(1)} %shard_map.101.refs_3_), channel_id=1, source_target_pairs={{0,1},{1,0},{2,3},{3,2},{4,5},{5,4},{6,7},{7,6},{8,9},{9,8},{10,11... | collective-permute-start | bytes 294920 | tf_op jit(solution)/shard_map/ppermute | solution.py:571
  58.4 1.5 %collective-permute-start.30 = (f32[192,128]{1,0:T(8,128)S(1)}, f32[192,128]{1,0:T(8,128)S(1)}, u32[]{:S(2)}, u32[]{:S(2)}) collective-permute-start(f32[192,128]{1,0:T(8,128)S(1)} %get-tuple-element.50.refs_2_), channel_id=1, source_target_pairs={{0,1},{1,0},{2,3},{3,2},{4,5},{5,4},{6,7},{7,6},{8,9},{9,8},{10,11... | collective-permute-start | bytes 294920 | tf_op jit(solution)/shard_map/ppermute | solution.py:571
  60.5 4.9 %collective-permute-start.34 = (f32[64,128]{1,0:T(8,128)S(1)}, f32[64,128]{1,0:T(8,128)S(1)}, u32[]{:S(2)}, u32[]{:S(2)}) collective-permute-start(f32[64,128]{1,0:T(8,128)S(1)} %get-tuple-element.53.refs_0_), channel_id=1, source_target_pairs={{0,24},{8,16},{16,8},{24,0},{1,25},{9,17},{17,9},{25,1},{2,26},{10... | collective-permute-start | bytes 98312 | tf_op jit(solution)/shard_map/ppermute | solution.py:578
  63.0 3.9 %collective-permute-start.33 = (f32[64,128]{1,0:T(8,128)S(1)}, f32[64,128]{1,0:T(8,128)S(1)}, u32[]{:S(2)}, u32[]{:S(2)}) collective-permute-start(f32[64,128]{1,0:T(8,128)S(1)} %get-tuple-element.53.refs_0_), channel_id=1, source_target_pairs={{0,16},{8,24},{16,0},{24,8},{1,17},{9,25},{17,1},{25,9},{2,18},{10... | collective-permute-start | bytes 98312 | tf_op jit(solution)/shard_map/ppermute | solution.py:578
  63.5 3.9 %collective-permute-start.32 = (f32[64,128]{1,0:T(8,128)S(1)}, f32[64,128]{1,0:T(8,128)S(1)}, u32[]{:S(2)}, u32[]{:S(2)}) collective-permute-start(f32[64,128]{1,0:T(8,128)S(1)} %get-tuple-element.53.refs_0_), channel_id=1, source_target_pairs={{0,8},{8,0},{16,24},{24,16},{1,9},{9,1},{17,25},{25,17},{2,10},{10... | collective-permute-start | bytes 98312 | tf_op jit(solution)/shard_map/ppermute | solution.py:578
  (3 other events, 3.9 us)

commit v3 on v2

--- a/solution.py
+++ b/solution.py
@@ -353,7 +353,7 @@
         return tuple(new)
 
     zero = jnp.zeros((half, LANES), F32)
-    totals = lax.fori_loop(0, half, step, (zero,) * 24, unroll=2)
+    totals = lax.fori_loop(0, half, step, (zero,) * 24, unroll=4)
     for k in range(12):
         mine = a_s[k]
         for h in range(2):
@@ -384,7 +384,11 @@
 
 def state_kernel(count, blocks, intervals, *refs):
     every, refs = beside(refs, count)
-    key_ref, at_ref, gains_ref, chans_ref, z_ref, pen_ref, scale_ref, select_ref = refs
+    key_ref, at_ref, gains_ref, chans_ref, basis_ref = refs[:5]
+    z_ref, pen_ref, scale_ref, select_ref, turned_ref = refs[5:]
+    place = (iota((KPAD, LANES), 0) == iota((KPAD, LANES), 1) % KPAD).astype(BF16)
+    for n, piece in enumerate(split(turn(place, basis_ref[LANES:, :]))):
+        turned_ref[n * KPAD : (n + 1) * KPAD, :] = piece
     rows = every[GAIN_ROWS:]
     z_ref[:, :LANES] = gains_ref[...]
     z_ref[:, LANES:] = every[:GAIN_ROWS, :LANES]
@@ -445,16 +449,44 @@
     out_ref[...] = nn(gains_ref[...] + dual_ref[...], basis_ref[...], precision=HIGH)
 
 
+def inverse_of_three(d):
+    def minor(r, c):
+        (r0, r1), (c0, c1) = [[k for k in range(3) if k != n] for n in (r, c)]
+        value = d[r0][c0] * d[r1][c1] - d[r0][c1] * d[r1][c0]
+        return value if (r + c) % 2 == 0 else -value
+
+    minors = [[minor(r, c) for c in range(3)] for r in range(3)]
+    over = 1.0 / (d[0][0] * minors[0][0] + d[0][1] * minors[0][1] + d[0][2] * minors[0][2])
+    return [[minors[c][r] * over for c in range(3)] for r in range(3)]
+
+
 def invert(gram):
     row, lane = iota(gram.shape, 0), iota(gram.shape, 1)
     inner = (row < NPOLY) & (lane < NPOLY)
     work = jnp.where(inner, gram + jnp.where(row == lane, ridge, 0.0), 0.0)
-    for p in range(NPOLY):
-        here = lane == p
-        column = jnp.sum(jnp.where(here, work, 0.0), 1, keepdims=True)
-        over = 1.0 / column[p : p + 1]
-        pivot = jnp.where(here[:1], over, work[p : p + 1] * over)
-        work = jnp.where(row == p, pivot, jnp.where(here, 0.0, work) - column * pivot)
+    lanes = iota((1, gram.shape[1]), 1)
+    for p in range(0, NPOLY, 3):
+        rows = [work[p + a : p + a + 1] for a in range(3)]
+        block = inverse_of_three(
+            [
+                [jnp.broadcast_to(rows[a][:, p + b : p + b + 1], lanes.shape) for b in range(3)]
+                for a in range(3)
+            ]
+        )
+        columns = [work[:, p + b : p + b + 1] for b in range(3)]
+        here = (lane >= p) & (lane < p + 3)
+        rows = [jnp.where(here[:1], 0.0, x) for x in rows]
+        pivots = []
+        for a in range(3):
+            pivot = block[a][0] * rows[0] + block[a][1] * rows[1] + block[a][2] * rows[2]
+            for b in range(3):
+                pivot = jnp.where(lanes == p + b, block[a][b], pivot)
+            pivots.append(pivot)
+        work = jnp.where(here, 0.0, work)
+        for b in range(3):
+            work = work - columns[b] * pivots[b]
+        for a in range(3):
+            work = jnp.where(row == p + a, pivots[a], work)
     return work
 
 
@@ -493,17 +525,30 @@
     settle(total, inverse_ref[...], basis_ref, gains, z_ref, dual_ref)
 
 
-def last_kernel(count, *refs):
+def last_kernel(count, blocks, intervals, *refs):
     every, refs = beside(refs, count)
-    select_ref, z_ref, pen_ref, scale_ref, dual_ref, basis_ref, gains_ref, out_ref = refs
+    select_ref, z_ref, pen_ref, scale_ref, dual_ref, turned_ref, gains_ref, out_ref = refs
     own = slice(LANES, 2 * LANES)
     normal = pick(every, select_ref[own, :])
     gains = solve(normal, scale_ref[:, own], pen_ref[:, own], z_ref[:, own])
     gains_ref[...] = gains
-    total = nn(gains + dual_ref[:, own], basis_ref[own, :], precision=HIGH)
-    half = GAIN_ROWS // 2
-    low = iota((half, LANES), 1) < LANES // 2
-    out_ref[...] = jnp.where(low, pltpu.roll(total[:half], LANES // 2, 1), total[half:])
+    owned = blocks * BLOCK
+    here = iota((owned, LANES), 0) // BLOCK == iota((owned, LANES), 1) // intervals
+    summed = gains + dual_ref[:, own]
+    parts = [summed[m * BLOCK : (m + 1) * BLOCK] for m in range(8)]
+    parts = [jnp.where(here, jnp.concatenate([x] * blocks, 0), 0.0) for x in parts]
+    high, mid, low = split(jnp.concatenate(parts, 0))
+    turned = turned_ref[...]
+    first, second = nt(turned, high), nt(turned[: 2 * KPAD], mid)
+    small = first[2 * KPAD :] + second[KPAD:] + nt(turned[:KPAD], low)
+    total = first[:KPAD] + ((first[KPAD : 2 * KPAD] + second[:KPAD]) + small)
+    chunks = total.shape[1] // LANES
+    for c in range(chunks):
+        lanes = slice(c * LANES, (c + 1) * LANES)
+        out_ref[8 * c : 8 * c + 8, :] = total[:8, lanes]
+        out_ref[8 * chunks + c : 8 * chunks + c + 1, :] = total[8:9, lanes]
+    rest = 9 * chunks
+    out_ref[rest:, :] = jnp.zeros((out_ref.shape[0] - rest, LANES), F32)
 
 
 def gains_kernel(blocks, intervals, gains_ref, out_ref):
@@ -515,28 +560,29 @@
         out_ref[m] = turn(place, jnp.where(here, jnp.concatenate([part] * blocks, 0), 0.0))
 
 
-def turn(place, values):
+def split(values):
     high = values.astype(BF16)
     rest = values - high.astype(F32)
     mid = rest.astype(BF16)
-    low = (rest - mid.astype(F32)).astype(BF16)
+    return high, mid, (rest - mid.astype(F32)).astype(BF16)
+
+
+def turn(place, values):
+    high, mid, low = split(values)
     return (nt(place, high) + nt(place, mid)) + nt(place, low)
 
 
-def coefficient_kernel(bands, blocks, *refs):
+def coefficient_kernel(bands, *refs):
     inverse_ref, out_ref = refs[bands:]
-    coeff = nn(band_total(refs[:bands]), inverse_ref[...], precision=HIGH)
-    owned = blocks * BLOCK
-    place = (iota((KPAD, LANES), 0) == iota((KPAD, LANES), 1) % KPAD).astype(BF16)
-    parts = []
+    total = band_total(refs[:bands])
+    owned = out_ref.shape[2]
+    chunks = 8 * owned // LANES
+    inverse = inverse_ref[:KPAD, :KPAD]
+    eight = jnp.concatenate([total[8 * c : 8 * c + 8] for c in range(chunks)], 1)
+    ninth = jnp.concatenate([total[8 * chunks + c : 8 * chunks + c + 1] for c in range(chunks)], 1)
+    coeff = nn(inverse[:, :8], eight, precision=HIGH) + inverse[:, 8:9] * ninth
     for m in range(8):
-        first = (m // 4) * (LANES // 2 // KPAD)
-        here = iota((owned, LANES), 0) // BLOCK == iota((owned, LANES), 1) // KPAD - first
-        part = coeff[(m % 4) * BLOCK : (m % 4 + 1) * BLOCK]
-        parts.append(jnp.where(here, jnp.concatenate([part] * blocks, 0), 0.0))
-    turned = turn(place, jnp.concatenate(parts, 0))
-    for m in range(8):
-        out_ref[:, m, :] = turned[:NPOLY, m * owned : (m + 1) * owned]
+        out_ref[:, m, :] = coeff[:NPOLY, m * owned : (m + 1) * owned]
 
 
 def call(kernel, operands, shapes, scratch=(), hbm=False, flops=20_000_000):
@@ -659,12 +705,18 @@
         [narrow, terms],
         scratch,
     )
-    z, pen, scale, select = call(
+    z, pen, scale, select, turned = call(
         functools.partial(state_kernel, count, blocks, intervals),
-        (*greetings, keys, at, gains, chans),
-        [wide, single, single, shape(2 * LANES, count * LANES, dtype=BF16)],
-    )
-    pieces = share_base(message, last=(scale,))
+        (*greetings, keys, at, gains, chans, basis),
+        [
+            wide,
+            single,
+            single,
+            shape(2 * LANES, count * LANES, dtype=BF16),
+            shape(3 * KPAD, LANES, dtype=BF16),
+        ],
+    )
+    pieces = share_base(message, last=(scale,), ahead=True)
     gains, message = call(
         functools.partial(step_kernel, count),
         (*pieces, select, z, pen, scale, products),
@@ -685,10 +737,11 @@
     (part,) = call(total_kernel, (gains, dual, basis), [narrow])
     z, dual = call(consensus_kernel, (*sum_band(part), gains, dual, basis, inverse), [wide, wide])
     pieces = share_base(message, last=(z,), ties=(1, 2), ahead=True)
+    chunks = 8 * owned // LANES
     gains, part = call(
-        functools.partial(last_kernel, count),
-        (*pieces, select, z, pen, scale, dual, basis),
-        [narrow, shape(GAIN_ROWS // 2, LANES)],
+        functools.partial(last_kernel, count, blocks, intervals),
+        (*pieces, select, z, pen, scale, dual, turned),
+        [narrow, shape(8 * chunks + -(-chunks // 8) * 8, LANES)],
     )
     parts = share_band(part)
     (out,) = call(
@@ -697,7 +750,7 @@
         [shape(8, intervals, owned)],
     )
     (coefficients,) = call(
-        functools.partial(coefficient_kernel, bands, blocks),
+        functools.partial(coefficient_kernel, bands),
         (*parts, inverse),
         [shape(NPOLY, 8, owned)],
     )

time: 68.7 us -> 68.1 us (level)
  Pallas kernels: 16.2 us -> 15.4 us
    pallas_call x13, Pallas kernels: 16.2 us -> 15.4 us  [call(): pl.pallas_call(kernel, out_shape=shapes, in_specs=in_specs, out_specs=[vm...]
  transfers between devices with their start and end apart: 35 -> 35, of which waited for: 18 -> 20; matrix products, arithmetic and copies ran while one was open for 0% -> 0% of each run, Pallas kernels for 13% -> 12%
where the time goes in v3:
time: 68.1 us; the launch traced here: 67.9 us
  starting transfers between devices  31.2 us (46%)
  waiting for transfers between devices  20.5 us (30%)
  Pallas kernels  15.4 us (23%)
  between operations  0.81 us (1%)
    ppermute x12, starting transfers between devices, share_base(): lax.ppermute(x, 'base', [(d, d ^ 2 * k) for d in range(devices)])  18.7 us
    pallas_call x13, Pallas kernels, call(): pl.pallas_call(kernel, out_shape=shapes, in_specs=in_specs, out_specs=[vm...  15.4 us
    ppermute x12, waiting for transfers between devices, share_base(): lax.ppermute(x, 'base', [(d, d ^ 2 * k) for d in range(devices)])  7.93 us
    ppermute x2, waiting for transfers between devices, sum_band(): return (x, lax.ppermute(x, 'band', [(d, d ^ step) for d in range(devices)]))  5.57 us
    ppermute x16, waiting for transfers between devices, share_base(): lax.ppermute(y, 'base', [(d, d ^ 1) for d in range(devices)])  4.08 us
    ppermute x3, starting transfers between devices, share_band(): lax.ppermute(x, 'band', [(d, d ^ k) for d in range(devices)])  3.53 us
    ppermute x2, starting transfers between devices, sum_band(): return (x, lax.ppermute(x, 'band', [(d, d ^ step) for d in range(devices)]))  3.17 us
    ppermute x2, starting transfers between devices, sum_band(): x = x + lax.ppermute(x, 'band', [(d, d ^ step) for d in range(devices)])  3.09 us
  transfers between devices with their start and end apart: 35, of which 20 were waited for; matrix products, arithmetic and copies ran while one was open for 0% of the time, Pallas kernels for 12%

profile of v3, /device:TPU:0, one launch (start us, length us, event | category | flops | bytes accessed | tf_op | source)
XLA Modules:
  0.0 67.9 jit_solution(532374935099760498)
XLA Ops:
  0.6 1.4 %shard_map.86.refs_0_ = f32[136,128]{1,0:T(8,128)S(1)} custom-call(s32[2,2]{1,0:T(2,128)} %pair_hbm.3, f32[8,32,64]{2,1,0:T(8,128)} %start_hbm.1, f32[1,64]{1,0:T(1,128)} %bitcast.6, s32[2,256]{1,0:T(2,128)} %flag_hbm.3), custom_call_target="tpu_custom_call" | custom-call | flops 20000000 | bytes 137488 | tf_op jit(solution)/shard_map/pallas_call | solution.py:595
  2.6 4.7 %collective-permute-start.2 = (f32[136,128]{1,0:T(8,128)S(1)}, f32[136,128]{1,0:T(8,128)S(1)}, u32[]{:S(2)}, u32[]{:S(2)}) collective-permute-start(f32[136,128]{1,0:T(8,128)S(1)} %shard_map.86.refs_0_), channel_id=1, source_target_pairs={{0,6},{1,7},{2,4},{3,5},{4,2},{5,3},{6,0},{7,1},{8,14},{9,15},{10,... | collective-permute-start | bytes 208904 | tf_op jit(solution)/shard_map/ppermute | solution.py:609
  7.3 0.6 collective-permute-start
  7.9 4.6 %shard_map.87 = (f32[48,8,16,128]{3,2,1,0:T(8,128)S(1)}, f32[256,128]{1,0:T(8,128)S(1)}, f32[256,128]{1,0:T(8,128)S(1)}, f32[256,128]{1,0:T(8,128)S(1)}, f32[8,256]{1,0:T(8,128)S(1)}) custom-call(s32[2,2]{1,0:T(2,128)} %pair_hbm.3, s32[1,64]{1,0:T(1,128)} %bitcast.9, s32[2,256]{1,0:T(2,128)} %flag_hbm.3, bf16[8,128,256]{2,1,0:T(8,128)(2,1)} %bitcast.7, ...), custom_call_target="tpu_custom_call" | custom-call | flops 2000000000 | bytes 4598032 | tf_op jit(solution)/shard_map/pallas_call | solution.py:595
  14.0 0.9 %collective-permute-done.5.refs_6_ = f32[136,128]{1,0:T(8,128)S(1)} collective-permute-done((f32[136,128]{1,0:T(8,128)S(1)}, f32[136,128]{1,0:T(8,128)S(1)}, u32[]{:S(2)}, u32[]{:S(2)}) %collective-permute-start.5) | collective-permute-done | bytes 69664 | tf_op jit(solution)/shard_map/ppermute | solution.py:617
  14.9 1.3 %shard_map.89 = (f32[128,128]{1,0:T(8,128)S(1)}, f32[192,128]{1,0:T(8,128)S(1)}) custom-call(f32[136,128]{1,0:T(8,128)S(1)} %shard_map.86.refs_0_, f32[136,128]{1,0:T(8,128)S(1)} %collective-permute-done.refs_1_, f32[136,128]{1,0:T(8,128)S(1)} %shard_map.88.refs_2_, f32[136,128]{1,0:T(8,128)S(1)} %collective-permute-done.2.refs_3_, ...), custom_call_target="tpu_custom_call" | custom-call | flops 20000000 | bytes 3997696 | tf_op jit(solution)/shard_map/pallas_call | solution.py:595
  16.2 3.2 %collective-permute-start.9 = (f32[192,128]{1,0:T(8,128)S(1)}, f32[192,128]{1,0:T(8,128)S(1)}, u32[]{:S(2)}, u32[]{:S(2)}) collective-permute-start(f32[192,128]{1,0:T(8,128)S(1)} %get-tuple-element.32.refs_0_), channel_id=1, source_target_pairs={{0,6},{1,7},{2,4},{3,5},{4,2},{5,3},{6,0},{7,1},{8,14},{9,15},{10,... | collective-permute-start | bytes 294920 | tf_op jit(solution)/shard_map/ppermute | solution.py:609
  19.5 1.2 %collective-permute-start.7 = (f32[192,128]{1,0:T(8,128)S(1)}, f32[192,128]{1,0:T(8,128)S(1)}, u32[]{:S(2)}, u32[]{:S(2)}) collective-permute-start(f32[192,128]{1,0:T(8,128)S(1)} %get-tuple-element.32.refs_0_), channel_id=1, source_target_pairs={{0,2},{1,3},{2,0},{3,1},{4,6},{5,7},{6,4},{7,5},{8,10},{9,11},{10,... | collective-permute-start | bytes 294920 | tf_op jit(solution)/shard_map/ppermute | solution.py:609
  21.2 2.6 %collective-permute-done.9.refs_0_ = f32[192,128]{1,0:T(8,128)S(1)} collective-permute-done((f32[192,128]{1,0:T(8,128)S(1)}, f32[192,128]{1,0:T(8,128)S(1)}, u32[]{:S(2)}, u32[]{:S(2)}) %collective-permute-start.9) | collective-permute-done | bytes 98336 | tf_op jit(solution)/shard_map/ppermute | solution.py:609
  23.9 4.6 %collective-permute-done.8.refs_0_ = f32[192,128]{1,0:T(8,128)S(1)} collective-permute-done((f32[192,128]{1,0:T(8,128)S(1)}, f32[192,128]{1,0:T(8,128)S(1)}, u32[]{:S(2)}, u32[]{:S(2)}) %collective-permute-start.8) | collective-permute-done | bytes 98336 | tf_op jit(solution)/shard_map/ppermute | solution.py:609
  28.9 0.8 %collective-permute-done.12.refs_6_ = f32[192,128]{1,0:T(8,128)S(1)} collective-permute-done((f32[192,128]{1,0:T(8,128)S(1)}, f32[192,128]{1,0:T(8,128)S(1)}, u32[]{:S(2)}, u32[]{:S(2)}) %collective-permute-start.12) | collective-permute-done | bytes 98336 | tf_op jit(solution)/shard_map/ppermute | solution.py:617
  29.9 1.5 %shard_map.93 = (f32[128,256]{1,0:T(8,128)S(1)}, f32[192,128]{1,0:T(8,128)S(1)}) custom-call(f32[192,128]{1,0:T(8,128)S(1)} %get-tuple-element.32.refs_0_, f32[192,128]{1,0:T(8,128)S(1)} %collective-permute-done.7.refs_1_, f32[192,128]{1,0:T(8,128)S(1)} %shard_map.91.refs_2_, f32[192,128]{1,0:T(8,128)S(1)} %shard_map.92.refs_3_, ...), custom_call_target="tpu_custom_call" | custom-call | flops 20000000 | bytes 4849664 | tf_op jit(solution)/shard_map/pallas_call | solution.py:595
  31.3 2.0 %collective-permute-start.18 = (f32[192,128]{1,0:T(8,128)S(1)}, f32[192,128]{1,0:T(8,128)S(1)}, u32[]{:S(2)}, u32[]{:S(2)}) collective-permute-start(f32[192,128]{1,0:T(8,128)S(1)} %get-tuple-element.40.refs_0_), channel_id=1, source_target_pairs={{0,6},{1,7},{2,4},{3,5},{4,2},{5,3},{6,0},{7,1},{8,14},{9,15},{10,... | collective-permute-start | bytes 294920 | tf_op jit(solution)/shard_map/ppermute | solution.py:609
  33.7 1.5 %collective-permute-start.16 = (f32[144,128]{1,0:T(8,128)S(1)}, f32[144,128]{1,0:T(8,128)S(1)}, u32[]{:S(2)}, u32[]{:S(2)}) collective-permute-start(f32[144,128]{1,0:T(8,128)S(1)} %shard_map.94), channel_id=1, source_target_pairs={{0,8},{8,0},{16,24},{24,16},{1,9},{9,1},{17,25},{25,17},{2,10},{10... | collective-permute-start | bytes 221192 | tf_op jit(solution)/shard_map/ppermute | solution.py:632
  35.2 2.4 %collective-permute-start.14 = (f32[192,128]{1,0:T(8,128)S(1)}, f32[192,128]{1,0:T(8,128)S(1)}, u32[]{:S(2)}, u32[]{:S(2)}) collective-permute-start(f32[192,128]{1,0:T(8,128)S(1)} %get-tuple-element.40.refs_0_), channel_id=1, source_target_pairs={{0,2},{1,3},{2,0},{3,1},{4,6},{5,7},{6,4},{7,5},{8,10},{9,11},{10,... | collective-permute-start | bytes 294920 | tf_op jit(solution)/shard_map/ppermute | solution.py:609
  38.1 1.6 %collective-permute-start.17 = (f32[144,128]{1,0:T(8,128)S(1)}, f32[144,128]{1,0:T(8,128)S(1)}, u32[]{:S(2)}, u32[]{:S(2)}) collective-permute-start(f32[144,128]{1,0:T(8,128)S(1)} %add.6.one_ref), channel_id=1, source_target_pairs={{0,16},{8,24},{16,0},{24,8},{1,17},{9,25},{17,1},{25,9},{2,18},{10... | collective-permute-start | bytes 221192 | tf_op jit(solution)/shard_map/ppermute | solution.py:634
  39.7 2.8 %collective-permute-done.17.two_ref = f32[144,128]{1,0:T(8,128)S(1)} collective-permute-done((f32[144,128]{1,0:T(8,128)S(1)}, f32[144,128]{1,0:T(8,128)S(1)}, u32[]{:S(2)}, u32[]{:S(2)}) %collective-permute-start.17) | collective-permute-done | bytes 73760 | tf_op jit(solution)/shard_map/ppermute | solution.py:634
  42.5 1.0 %shard_map.95 = (f32[128,256]{1,0:T(8,128)S(1)}, f32[128,256]{1,0:T(8,128)S(1)}, f32[128,128]{1,0:T(8,128)S(1)}) custom-call(f32[144,128]{1,0:T(8,128)S(1)} %add.6.one_ref, f32[144,128]{1,0:T(8,128)S(1)} %collective-permute-done.17.two_ref, f32[128,256]{1,0:T(8,128)S(1)} %get-tuple-element.41.gains_ref, f32[256,128]{1,0:T(8,128)S(1)} %get-tuple-element.35.refs_12_.basis_ref), custom_call_target="tpu_custom_call" | custom-call | flops 20000000 | bytes 737280 | tf_op jit(solution)/shard_map/pallas_call | solution.py:595
  44.1 0.8 %collective-permute-done.20.refs_5_ = f32[192,128]{1,0:T(8,128)S(1)} collective-permute-done((f32[192,128]{1,0:T(8,128)S(1)}, f32[192,128]{1,0:T(8,128)S(1)}, u32[]{:S(2)}, u32[]{:S(2)}) %collective-permute-start.20) | collective-permute-done | bytes 98336 | tf_op jit(solution)/shard_map/ppermute | solution.py:617
  45.1 1.4 %shard_map.98 = (f32[128,256]{1,0:T(8,128)S(1)}, f32[192,128]{1,0:T(8,128)S(1)}) custom-call(f32[192,128]{1,0:T(8,128)S(1)} %get-tuple-element.40.refs_0_, f32[192,128]{1,0:T(8,128)S(1)} %get-tuple-element.43.refs_1_, f32[192,128]{1,0:T(8,128)S(1)} %get-tuple-element.44.refs_2_, f32[192,128]{1,0:T(8,128)S(1)} %shard_map.97.refs_3_, ...), custom_call_target="tpu_custom_call" | custom-call | flops 20000000 | bytes 4849664 | tf_op jit(solution)/shard_map/pallas_call | solution.py:595
  46.5 2.0 %collective-permute-start.27 = (f32[192,128]{1,0:T(8,128)S(1)}, f32[192,128]{1,0:T(8,128)S(1)}, u32[]{:S(2)}, u32[]{:S(2)}) collective-permute-start(f32[192,128]{1,0:T(8,128)S(1)} %get-tuple-element.45.refs_0_), channel_id=1, source_target_pairs={{0,6},{1,7},{2,4},{3,5},{4,2},{5,3},{6,0},{7,1},{8,14},{9,15},{10,... | collective-permute-start | bytes 294920 | tf_op jit(solution)/shard_map/ppermute | solution.py:609
  48.8 1.5 %collective-permute-start.25 = (f32[128,128]{1,0:T(8,128)S(1)}, f32[128,128]{1,0:T(8,128)S(1)}, u32[]{:S(2)}, u32[]{:S(2)}) collective-permute-start(f32[128,128]{1,0:T(8,128)S(1)} %shard_map.99), channel_id=1, source_target_pairs={{0,8},{8,0},{16,24},{24,16},{1,9},{9,1},{17,25},{25,17},{2,10},{10... | collective-permute-start | bytes 196616 | tf_op jit(solution)/shard_map/ppermute | solution.py:632
  50.3 2.5 %collective-permute-start.23 = (f32[192,128]{1,0:T(8,128)S(1)}, f32[192,128]{1,0:T(8,128)S(1)}, u32[]{:S(2)}, u32[]{:S(2)}) collective-permute-start(f32[192,128]{1,0:T(8,128)S(1)} %get-tuple-element.45.refs_0_), channel_id=1, source_target_pairs={{0,2},{1,3},{2,0},{3,1},{4,6},{5,7},{6,4},{7,5},{8,10},{9,11},{10,... | collective-permute-start | bytes 294920 | tf_op jit(solution)/shard_map/ppermute | solution.py:609
  53.1 1.6 %collective-permute-start.26 = (f32[128,128]{1,0:T(8,128)S(1)}, f32[128,128]{1,0:T(8,128)S(1)}, u32[]{:S(2)}, u32[]{:S(2)}) collective-permute-start(f32[128,128]{1,0:T(8,128)S(1)} %add.7.one_ref), channel_id=1, source_target_pairs={{0,16},{8,24},{16,0},{24,8},{1,17},{9,25},{17,1},{25,9},{2,18},{10... | collective-permute-start | bytes 196616 | tf_op jit(solution)/shard_map/ppermute | solution.py:634
  54.7 2.7 %collective-permute-done.26.two_ref = f32[128,128]{1,0:T(8,128)S(1)} collective-permute-done((f32[128,128]{1,0:T(8,128)S(1)}, f32[128,128]{1,0:T(8,128)S(1)}, u32[]{:S(2)}, u32[]{:S(2)}) %collective-permute-start.26) | collective-permute-done | bytes 65568 | tf_op jit(solution)/shard_map/ppermute | solution.py:634
  58.6 0.8 %collective-permute-done.29.refs_5_ = f32[192,128]{1,0:T(8,128)S(1)} collective-permute-done((f32[192,128]{1,0:T(8,128)S(1)}, f32[192,128]{1,0:T(8,128)S(1)}, u32[]{:S(2)}, u32[]{:S(2)}) %collective-permute-start.29) | collective-permute-done | bytes 98336 | tf_op jit(solution)/shard_map/ppermute | solution.py:617
  59.6 0.8 %shard_map.103 = (f32[128,128]{1,0:T(8,128)S(1)}, f32[40,128]{1,0:T(8,128)S(1)}) custom-call(f32[192,128]{1,0:T(8,128)S(1)} %get-tuple-element.45.refs_0_, f32[192,128]{1,0:T(8,128)S(1)} %get-tuple-element.50.refs_1_, f32[192,128]{1,0:T(8,128)S(1)} %get-tuple-element.51.refs_2_, f32[192,128]{1,0:T(8,128)S(1)} %shard_map.102.refs_3_, ...), custom_call_target="tpu_custom_call" | custom-call | flops 20000000 | bytes 1703936 | tf_op jit(solution)/shard_map/pallas_call | solution.py:595
  60.3 2.4 %collective-permute-start.34 = (f32[40,128]{1,0:T(8,128)S(1)}, f32[40,128]{1,0:T(8,128)S(1)}, u32[]{:S(2)}, u32[]{:S(2)}) collective-permute-start(f32[40,128]{1,0:T(8,128)S(1)} %get-tuple-element.55.refs_0_), channel_id=1, source_target_pairs={{0,24},{8,16},{16,8},{24,0},{1,25},{9,17},{17,9},{25,1},{2,26},{10... | collective-permute-start | bytes 61448 | tf_op jit(solution)/shard_map/ppermute | solution.py:624
  63.2 0.6 collective-permute-start.32
  63.9 1.0 %shard_map.104 = f32[8,32,64]{2,1,0:T(8,128)} custom-call(f32[128,128]{1,0:T(8,128)S(1)} %get-tuple-element.54.gains_ref), custom_call_target="tpu_custom_call" | custom-call | flops 20000000 | bytes 131072 | tf_op jit(solution)/shard_map/pallas_call | solution.py:595
  65.1 1.5 %collective-permute-done.33.refs_2_ = f32[40,128]{1,0:T(8,128)S(1)} collective-permute-done((f32[40,128]{1,0:T(8,128)S(1)}, f32[40,128]{1,0:T(8,128)S(1)}, u32[]{:S(2)}, u32[]{:S(2)}) %collective-permute-start.33) | collective-permute-done | bytes 20512 | tf_op jit(solution)/shard_map/ppermute | solution.py:624
  67.0 0.9 %shard_map.105 = f32[9,8,64]{2,1,0:T(8,128)} custom-call(f32[40,128]{1,0:T(8,128)S(1)} %get-tuple-element.55.refs_0_, f32[40,128]{1,0:T(8,128)S(1)} %collective-permute-done.32.refs_1_, f32[40,128]{1,0:T(8,128)S(1)} %collective-permute-done.33.refs_2_, f32[40,128]{1,0:T(8,128)S(1)} %collective-permute-done.34.refs_3_, ...), custom_call_target="tpu_custom_call" | custom-call | flops 20000000 | bytes 165888 | tf_op jit(solution)/shard_map/pallas_call | solution.py:595
  (60 shorter events, 7.8 us)
Async XLA Ops:
  2.1 11.6 %collective-permute-start.3 = (f32[136,128]{1,0:T(8,128)S(1)}, f32[136,128]{1,0:T(8,128)S(1)}, u32[]{:S(2)}, u32[]{:S(2)}) collective-permute-start(f32[136,128]{1,0:T(8,128)S(1)} %shard_map.86.refs_0_), channel_id=1, source_target_pairs={{0,1},{1,0},{2,3},{3,2},{4,5},{5,4},{6,7},{7,6},{8,9},{9,8},{10,11... | collective-permute-start | bytes 208904 | tf_op jit(solution)/shard_map/ppermute | solution.py:617
  2.6 9.9 %collective-permute-start.2 = (f32[136,128]{1,0:T(8,128)S(1)}, f32[136,128]{1,0:T(8,128)S(1)}, u32[]{:S(2)}, u32[]{:S(2)}) collective-permute-start(f32[136,128]{1,0:T(8,128)S(1)} %shard_map.86.refs_0_), channel_id=1, source_target_pairs={{0,6},{1,7},{2,4},{3,5},{4,2},{5,3},{6,0},{7,1},{8,14},{9,15},{10,... | collective-permute-start | bytes 208904 | tf_op jit(solution)/shard_map/ppermute | solution.py:609
  7.3 6.4 %collective-permute-start.1 = (f32[136,128]{1,0:T(8,128)S(1)}, f32[136,128]{1,0:T(8,128)S(1)}, u32[]{:S(2)}, u32[]{:S(2)}) collective-permute-start(f32[136,128]{1,0:T(8,128)S(1)} %shard_map.86.refs_0_), channel_id=1, source_target_pairs={{0,4},{1,5},{2,6},{3,7},{4,0},{5,1},{6,2},{7,3},{8,12},{9,13},{10,... | collective-permute-start | bytes 208904 | tf_op jit(solution)/shard_map/ppermute | solution.py:609
  7.3 5.3 %collective-permute-start = (f32[136,128]{1,0:T(8,128)S(1)}, f32[136,128]{1,0:T(8,128)S(1)}, u32[]{:S(2)}, u32[]{:S(2)}) collective-permute-start(f32[136,128]{1,0:T(8,128)S(1)} %shard_map.86.refs_0_), channel_id=1, source_target_pairs={{0,2},{1,3},{2,0},{3,1},{4,6},{5,7},{6,4},{7,5},{8,10},{9,11},{10,... | collective-permute-start | bytes 208904 | tf_op jit(solution)/shard_map/ppermute | solution.py:609
  12.5 1.3 %collective-permute-start.6 = (f32[136,128]{1,0:T(8,128)S(1)}, f32[136,128]{1,0:T(8,128)S(1)}, u32[]{:S(2)}, u32[]{:S(2)}) collective-permute-start(f32[136,128]{1,0:T(8,128)S(1)} %collective-permute-done.2.refs_3_), channel_id=1, source_target_pairs={{0,1},{1,0},{2,3},{3,2},{4,5},{5,4},{6,7},{7,6},{8,9},{9,8},{10,11... | collective-permute-start | bytes 208904 | tf_op jit(solution)/shard_map/ppermute | solution.py:617
  12.6 1.4 %collective-permute-start.4 = (f32[136,128]{1,0:T(8,128)S(1)}, f32[136,128]{1,0:T(8,128)S(1)}, u32[]{:S(2)}, u32[]{:S(2)}) collective-permute-start(f32[136,128]{1,0:T(8,128)S(1)} %collective-permute-done.refs_1_), channel_id=1, source_target_pairs={{0,1},{1,0},{2,3},{3,2},{4,5},{5,4},{6,7},{7,6},{8,9},{9,8},{10,11... | collective-permute-start | bytes 208904 | tf_op jit(solution)/shard_map/ppermute | solution.py:617
  16.2 7.6 %collective-permute-start.9 = (f32[192,128]{1,0:T(8,128)S(1)}, f32[192,128]{1,0:T(8,128)S(1)}, u32[]{:S(2)}, u32[]{:S(2)}) collective-permute-start(f32[192,128]{1,0:T(8,128)S(1)} %get-tuple-element.32.refs_0_), channel_id=1, source_target_pairs={{0,6},{1,7},{2,4},{3,5},{4,2},{5,3},{6,0},{7,1},{8,14},{9,15},{10,... | collective-permute-start | bytes 294920 | tf_op jit(solution)/shard_map/ppermute | solution.py:609
  19.5 9.4 %collective-permute-start.10 = (f32[192,128]{1,0:T(8,128)S(1)}, f32[192,128]{1,0:T(8,128)S(1)}, u32[]{:S(2)}, u32[]{:S(2)}) collective-permute-start(f32[192,128]{1,0:T(8,128)S(1)} %get-tuple-element.32.refs_0_), channel_id=1, source_target_pairs={{0,1},{1,0},{2,3},{3,2},{4,5},{5,4},{6,7},{7,6},{8,9},{9,8},{10,11... | collective-permute-start | bytes 294920 | tf_op jit(solution)/shard_map/ppermute | solution.py:617
  19.5 8.9 %collective-permute-start.8 = (f32[192,128]{1,0:T(8,128)S(1)}, f32[192,128]{1,0:T(8,128)S(1)}, u32[]{:S(2)}, u32[]{:S(2)}) collective-permute-start(f32[192,128]{1,0:T(8,128)S(1)} %get-tuple-element.32.refs_0_), channel_id=1, source_target_pairs={{0,4},{1,5},{2,6},{3,7},{4,0},{5,1},{6,2},{7,3},{8,12},{9,13},{10,... | collective-permute-start | bytes 294920 | tf_op jit(solution)/shard_map/ppermute | solution.py:609
  19.5 8.9 %collective-permute-start.7 = (f32[192,128]{1,0:T(8,128)S(1)}, f32[192,128]{1,0:T(8,128)S(1)}, u32[]{:S(2)}, u32[]{:S(2)}) collective-permute-start(f32[192,128]{1,0:T(8,128)S(1)} %get-tuple-element.32.refs_0_), channel_id=1, source_target_pairs={{0,2},{1,3},{2,0},{3,1},{4,6},{5,7},{6,4},{7,5},{8,10},{9,11},{10,... | collective-permute-start | bytes 294920 | tf_op jit(solution)/shard_map/ppermute | solution.py:609
  23.9 5.1 %collective-permute-start.13 = (f32[192,128]{1,0:T(8,128)S(1)}, f32[192,128]{1,0:T(8,128)S(1)}, u32[]{:S(2)}, u32[]{:S(2)}) collective-permute-start(f32[192,128]{1,0:T(8,128)S(1)} %shard_map.92.refs_3_), channel_id=1, source_target_pairs={{0,1},{1,0},{2,3},{3,2},{4,5},{5,4},{6,7},{7,6},{8,9},{9,8},{10,11... | collective-permute-start | bytes 294920 | tf_op jit(solution)/shard_map/ppermute | solution.py:617
  28.4 1.5 %collective-permute-start.11 = (f32[192,128]{1,0:T(8,128)S(1)}, f32[192,128]{1,0:T(8,128)S(1)}, u32[]{:S(2)}, u32[]{:S(2)}) collective-permute-start(f32[192,128]{1,0:T(8,128)S(1)} %collective-permute-done.7.refs_1_), channel_id=1, source_target_pairs={{0,1},{1,0},{2,3},{3,2},{4,5},{5,4},{6,7},{7,6},{8,9},{9,8},{10,11... | collective-permute-start | bytes 294920 | tf_op jit(solution)/shard_map/ppermute | solution.py:617
  31.3 8.4 %collective-permute-start.18 = (f32[192,128]{1,0:T(8,128)S(1)}, f32[192,128]{1,0:T(8,128)S(1)}, u32[]{:S(2)}, u32[]{:S(2)}) collective-permute-start(f32[192,128]{1,0:T(8,128)S(1)} %get-tuple-element.40.refs_0_), channel_id=1, source_target_pairs={{0,6},{1,7},{2,4},{3,5},{4,2},{5,3},{6,0},{7,1},{8,14},{9,15},{10,... | collective-permute-start | bytes 294920 | tf_op jit(solution)/shard_map/ppermute | solution.py:609
  33.7 4.4 %collective-permute-start.16 = (f32[144,128]{1,0:T(8,128)S(1)}, f32[144,128]{1,0:T(8,128)S(1)}, u32[]{:S(2)}, u32[]{:S(2)}) collective-permute-start(f32[144,128]{1,0:T(8,128)S(1)} %shard_map.94), channel_id=1, source_target_pairs={{0,8},{8,0},{16,24},{24,16},{1,9},{9,1},{17,25},{25,17},{2,10},{10... | collective-permute-start | bytes 221192 | tf_op jit(solution)/shard_map/ppermute | solution.py:632
  35.2 8.9 %collective-permute-start.19 = (f32[192,128]{1,0:T(8,128)S(1)}, f32[192,128]{1,0:T(8,128)S(1)}, u32[]{:S(2)}, u32[]{:S(2)}) collective-permute-start(f32[192,128]{1,0:T(8,128)S(1)} %get-tuple-element.40.refs_0_), channel_id=1, source_target_pairs={{0,1},{1,0},{2,3},{3,2},{4,5},{5,4},{6,7},{7,6},{8,9},{9,8},{10,11... | collective-permute-start | bytes 294920 | tf_op jit(solution)/shard_map/ppermute | solution.py:617
  35.2 8.3 %collective-permute-start.15 = (f32[192,128]{1,0:T(8,128)S(1)}, f32[192,128]{1,0:T(8,128)S(1)}, u32[]{:S(2)}, u32[]{:S(2)}) collective-permute-start(f32[192,128]{1,0:T(8,128)S(1)} %get-tuple-element.40.refs_0_), channel_id=1, source_target_pairs={{0,4},{1,5},{2,6},{3,7},{4,0},{5,1},{6,2},{7,3},{8,12},{9,13},{10,... | collective-permute-start | bytes 294920 | tf_op jit(solution)/shard_map/ppermute | solution.py:609
  35.2 8.3 %collective-permute-start.14 = (f32[192,128]{1,0:T(8,128)S(1)}, f32[192,128]{1,0:T(8,128)S(1)}, u32[]{:S(2)}, u32[]{:S(2)}) collective-permute-start(f32[192,128]{1,0:T(8,128)S(1)} %get-tuple-element.40.refs_0_), channel_id=1, source_target_pairs={{0,2},{1,3},{2,0},{3,1},{4,6},{5,7},{6,4},{7,5},{8,10},{9,11},{10,... | collective-permute-start | bytes 294920 | tf_op jit(solution)/shard_map/ppermute | solution.py:609
  38.1 4.4 %collective-permute-start.17 = (f32[144,128]{1,0:T(8,128)S(1)}, f32[144,128]{1,0:T(8,128)S(1)}, u32[]{:S(2)}, u32[]{:S(2)}) collective-permute-start(f32[144,128]{1,0:T(8,128)S(1)} %add.6.one_ref), channel_id=1, source_target_pairs={{0,16},{8,24},{16,0},{24,8},{1,17},{9,25},{17,1},{25,9},{2,18},{10... | collective-permute-start | bytes 221192 | tf_op jit(solution)/shard_map/ppermute | solution.py:634
  39.7 4.4 %collective-permute-start.22 = (f32[192,128]{1,0:T(8,128)S(1)}, f32[192,128]{1,0:T(8,128)S(1)}, u32[]{:S(2)}, u32[]{:S(2)}) collective-permute-start(f32[192,128]{1,0:T(8,128)S(1)} %shard_map.97.refs_3_), channel_id=1, source_target_pairs={{0,1},{1,0},{2,3},{3,2},{4,5},{5,4},{6,7},{7,6},{8,9},{9,8},{10,11... | collective-permute-start | bytes 294920 | tf_op jit(solution)/shard_map/ppermute | solution.py:617
  43.5 1.4 %collective-permute-start.20 = (f32[192,128]{1,0:T(8,128)S(1)}, f32[192,128]{1,0:T(8,128)S(1)}, u32[]{:S(2)}, u32[]{:S(2)}) collective-permute-start(f32[192,128]{1,0:T(8,128)S(1)} %get-tuple-element.43.refs_1_), channel_id=1, source_target_pairs={{0,1},{1,0},{2,3},{3,2},{4,5},{5,4},{6,7},{7,6},{8,9},{9,8},{10,11... | collective-permute-start | bytes 294920 | tf_op jit(solution)/shard_map/ppermute | solution.py:617
  43.6 1.4 %collective-permute-start.21 = (f32[192,128]{1,0:T(8,128)S(1)}, f32[192,128]{1,0:T(8,128)S(1)}, u32[]{:S(2)}, u32[]{:S(2)}) collective-permute-start(f32[192,128]{1,0:T(8,128)S(1)} %get-tuple-element.44.refs_2_), channel_id=1, source_target_pairs={{0,1},{1,0},{2,3},{3,2},{4,5},{5,4},{6,7},{7,6},{8,9},{9,8},{10,11... | collective-permute-start | bytes 294920 | tf_op jit(solution)/shard_map/ppermute | solution.py:617
  46.5 8.2 %collective-permute-start.27 = (f32[192,128]{1,0:T(8,128)S(1)}, f32[192,128]{1,0:T(8,128)S(1)}, u32[]{:S(2)}, u32[]{:S(2)}) collective-permute-start(f32[192,128]{1,0:T(8,128)S(1)} %get-tuple-element.45.refs_0_), channel_id=1, source_target_pairs={{0,6},{1,7},{2,4},{3,5},{4,2},{5,3},{6,0},{7,1},{8,14},{9,15},{10,... | collective-permute-start | bytes 294920 | tf_op jit(solution)/shard_map/ppermute | solution.py:609
  48.8 4.3 %collective-permute-start.25 = (f32[128,128]{1,0:T(8,128)S(1)}, f32[128,128]{1,0:T(8,128)S(1)}, u32[]{:S(2)}, u32[]{:S(2)}) collective-permute-start(f32[128,128]{1,0:T(8,128)S(1)} %shard_map.99), channel_id=1, source_target_pairs={{0,8},{8,0},{16,24},{24,16},{1,9},{9,1},{17,25},{25,17},{2,10},{10... | collective-permute-start | bytes 196616 | tf_op jit(solution)/shard_map/ppermute | solution.py:632
  50.3 8.3 %collective-permute-start.28 = (f32[192,128]{1,0:T(8,128)S(1)}, f32[192,128]{1,0:T(8,128)S(1)}, u32[]{:S(2)}, u32[]{:S(2)}) collective-permute-start(f32[192,128]{1,0:T(8,128)S(1)} %get-tuple-element.45.refs_0_), channel_id=1, source_target_pairs={{0,1},{1,0},{2,3},{3,2},{4,5},{5,4},{6,7},{7,6},{8,9},{9,8},{10,11... | collective-permute-start | bytes 294920 | tf_op jit(solution)/shard_map/ppermute | solution.py:617
  50.3 7.6 %collective-permute-start.24 = (f32[192,128]{1,0:T(8,128)S(1)}, f32[192,128]{1,0:T(8,128)S(1)}, u32[]{:S(2)}, u32[]{:S(2)}) collective-permute-start(f32[192,128]{1,0:T(8,128)S(1)} %get-tuple-element.45.refs_0_), channel_id=1, source_target_pairs={{0,4},{1,5},{2,6},{3,7},{4,0},{5,1},{6,2},{7,3},{8,12},{9,13},{10,... | collective-permute-start | bytes 294920 | tf_op jit(solution)/shard_map/ppermute | solution.py:609
  50.3 7.8 %collective-permute-start.23 = (f32[192,128]{1,0:T(8,128)S(1)}, f32[192,128]{1,0:T(8,128)S(1)}, u32[]{:S(2)}, u32[]{:S(2)}) collective-permute-start(f32[192,128]{1,0:T(8,128)S(1)} %get-tuple-element.45.refs_0_), channel_id=1, source_target_pairs={{0,2},{1,3},{2,0},{3,1},{4,6},{5,7},{6,4},{7,5},{8,10},{9,11},{10,... | collective-permute-start | bytes 294920 | tf_op jit(solution)/shard_map/ppermute | solution.py:609
  53.1 4.3 %collective-permute-start.26 = (f32[128,128]{1,0:T(8,128)S(1)}, f32[128,128]{1,0:T(8,128)S(1)}, u32[]{:S(2)}, u32[]{:S(2)}) collective-permute-start(f32[128,128]{1,0:T(8,128)S(1)} %add.7.one_ref), channel_id=1, source_target_pairs={{0,16},{8,24},{16,0},{24,8},{1,17},{9,25},{17,1},{25,9},{2,18},{10... | collective-permute-start | bytes 196616 | tf_op jit(solution)/shard_map/ppermute | solution.py:634
  54.7 3.9 %collective-permute-start.31 = (f32[192,128]{1,0:T(8,128)S(1)}, f32[192,128]{1,0:T(8,128)S(1)}, u32[]{:S(2)}, u32[]{:S(2)}) collective-permute-start(f32[192,128]{1,0:T(8,128)S(1)} %shard_map.102.refs_3_), channel_id=1, source_target_pairs={{0,1},{1,0},{2,3},{3,2},{4,5},{5,4},{6,7},{7,6},{8,9},{9,8},{10,11... | collective-permute-start | bytes 294920 | tf_op jit(solution)/shard_map/ppermute | solution.py:617
  58.1 1.5 %collective-permute-start.30 = (f32[192,128]{1,0:T(8,128)S(1)}, f32[192,128]{1,0:T(8,128)S(1)}, u32[]{:S(2)}, u32[]{:S(2)}) collective-permute-start(f32[192,128]{1,0:T(8,128)S(1)} %get-tuple-element.51.refs_2_), channel_id=1, source_target_pairs={{0,1},{1,0},{2,3},{3,2},{4,5},{5,4},{6,7},{7,6},{8,9},{9,8},{10,11... | collective-permute-start | bytes 294920 | tf_op jit(solution)/shard_map/ppermute | solution.py:617
  60.3 4.7 %collective-permute-start.34 = (f32[40,128]{1,0:T(8,128)S(1)}, f32[40,128]{1,0:T(8,128)S(1)}, u32[]{:S(2)}, u32[]{:S(2)}) collective-permute-start(f32[40,128]{1,0:T(8,128)S(1)} %get-tuple-element.55.refs_0_), channel_id=1, source_target_pairs={{0,24},{8,16},{16,8},{24,0},{1,25},{9,17},{17,9},{25,1},{2,26},{10... | collective-permute-start | bytes 61448 | tf_op jit(solution)/shard_map/ppermute | solution.py:624
  62.7 3.8 %collective-permute-start.33 = (f32[40,128]{1,0:T(8,128)S(1)}, f32[40,128]{1,0:T(8,128)S(1)}, u32[]{:S(2)}, u32[]{:S(2)}) collective-permute-start(f32[40,128]{1,0:T(8,128)S(1)} %get-tuple-element.55.refs_0_), channel_id=1, source_target_pairs={{0,16},{8,24},{16,0},{24,8},{1,17},{9,25},{17,1},{25,9},{2,18},{10... | collective-permute-start | bytes 61448 | tf_op jit(solution)/shard_map/ppermute | solution.py:624
  63.2 3.8 %collective-permute-start.32 = (f32[40,128]{1,0:T(8,128)S(1)}, f32[40,128]{1,0:T(8,128)S(1)}, u32[]{:S(2)}, u32[]{:S(2)}) collective-permute-start(f32[40,128]{1,0:T(8,128)S(1)} %get-tuple-element.55.refs_0_), channel_id=1, source_target_pairs={{0,8},{8,0},{16,24},{24,16},{1,9},{9,1},{17,25},{25,17},{2,10},{10... | collective-permute-start | bytes 61448 | tf_op jit(solution)/shard_map/ppermute | solution.py:624
  (3 other events, 3.9 us)

commit v4 on v3

--- a/solution.py
+++ b/solution.py
@@ -716,7 +716,7 @@
             shape(3 * KPAD, LANES, dtype=BF16),
         ],
     )
-    pieces = share_base(message, last=(scale,), ahead=True)
+    pieces = share_base(message, last=(scale,), ties=(1, 2))
     gains, message = call(
         functools.partial(step_kernel, count),
         (*pieces, select, z, pen, scale, products),

time: 68.1 us -> 67.8 us (level)
  transfers between devices with their start and end apart: 35 -> 35, of which waited for: 20 -> 21; matrix products, arithmetic and copies ran while one was open for 0% -> 0% of each run, Pallas kernels for 12% -> 12%
where the time goes in v4:
time: 67.8 us; the launch traced here: 67.6 us
  starting transfers between devices  31.1 us (46%)
  waiting for transfers between devices  20.3 us (30%)
  Pallas kernels  15.4 us (23%)
  between operations  0.78 us (1%)
    ppermute x12, starting transfers between devices, share_base(): lax.ppermute(x, 'base', [(d, d ^ 2 * k) for d in range(devices)])  18.7 us
    pallas_call x13, Pallas kernels, call(): pl.pallas_call(kernel, out_shape=shapes, in_specs=in_specs, out_specs=[vm...  15.4 us
    ppermute x12, waiting for transfers between devices, share_base(): lax.ppermute(x, 'base', [(d, d ^ 2 * k) for d in range(devices)])  7.42 us
    ppermute x2, waiting for transfers between devices, sum_band(): return (x, lax.ppermute(x, 'band', [(d, d ^ step) for d in range(devices)]))  5.57 us
    ppermute x16, waiting for transfers between devices, share_base(): lax.ppermute(y, 'base', [(d, d ^ 1) for d in range(devices)])  4.08 us
    ppermute x3, starting transfers between devices, share_band(): lax.ppermute(x, 'band', [(d, d ^ k) for d in range(devices)])  3.53 us
    ppermute x2, starting transfers between devices, sum_band(): return (x, lax.ppermute(x, 'band', [(d, d ^ step) for d in range(devices)]))  3.16 us
    ppermute x2, starting transfers between devices, sum_band(): x = x + lax.ppermute(x, 'band', [(d, d ^ step) for d in range(devices)])  3.12 us
  transfers between devices with their start and end apart: 35, of which 21 were waited for; matrix products, arithmetic and copies ran while one was open for 0% of the time, Pallas kernels for 12%

profile of v4, /device:TPU:0, one launch (start us, length us, event | category | flops | bytes accessed | tf_op | source)
XLA Modules:
  0.0 67.6 jit_solution(14586513694697009055)
XLA Ops:
  0.6 1.4 %shard_map.86.refs_0_ = f32[136,128]{1,0:T(8,128)S(1)} custom-call(s32[2,2]{1,0:T(2,128)} %pair_hbm.3, f32[8,32,64]{2,1,0:T(8,128)} %start_hbm.1, f32[1,64]{1,0:T(1,128)} %bitcast.6, s32[2,256]{1,0:T(2,128)} %flag_hbm.3), custom_call_target="tpu_custom_call" | custom-call | flops 20000000 | bytes 137488 | tf_op jit(solution)/shard_map/pallas_call | solution.py:595
  2.6 4.7 %collective-permute-start.2 = (f32[136,128]{1,0:T(8,128)S(1)}, f32[136,128]{1,0:T(8,128)S(1)}, u32[]{:S(2)}, u32[]{:S(2)}) collective-permute-start(f32[136,128]{1,0:T(8,128)S(1)} %shard_map.86.refs_0_), channel_id=1, source_target_pairs={{0,6},{1,7},{2,4},{3,5},{4,2},{5,3},{6,0},{7,1},{8,14},{9,15},{10,... | collective-permute-start | bytes 208904 | tf_op jit(solution)/shard_map/ppermute | solution.py:609
  7.9 4.6 %shard_map.87 = (f32[48,8,16,128]{3,2,1,0:T(8,128)S(1)}, f32[256,128]{1,0:T(8,128)S(1)}, f32[256,128]{1,0:T(8,128)S(1)}, f32[256,128]{1,0:T(8,128)S(1)}, f32[8,256]{1,0:T(8,128)S(1)}) custom-call(s32[2,2]{1,0:T(2,128)} %pair_hbm.3, s32[1,64]{1,0:T(1,128)} %bitcast.9, s32[2,256]{1,0:T(2,128)} %flag_hbm.3, bf16[8,128,256]{2,1,0:T(8,128)(2,1)} %bitcast.7, ...), custom_call_target="tpu_custom_call" | custom-call | flops 2000000000 | bytes 4598032 | tf_op jit(solution)/shard_map/pallas_call | solution.py:595
  14.0 0.9 %collective-permute-done.5.refs_6_ = f32[136,128]{1,0:T(8,128)S(1)} collective-permute-done((f32[136,128]{1,0:T(8,128)S(1)}, f32[136,128]{1,0:T(8,128)S(1)}, u32[]{:S(2)}, u32[]{:S(2)}) %collective-permute-start.5) | collective-permute-done | bytes 69664 | tf_op jit(solution)/shard_map/ppermute | solution.py:617
  14.9 1.3 %shard_map.89 = (f32[128,128]{1,0:T(8,128)S(1)}, f32[192,128]{1,0:T(8,128)S(1)}) custom-call(f32[136,128]{1,0:T(8,128)S(1)} %shard_map.86.refs_0_, f32[136,128]{1,0:T(8,128)S(1)} %collective-permute-done.refs_1_, f32[136,128]{1,0:T(8,128)S(1)} %shard_map.88.refs_2_, f32[136,128]{1,0:T(8,128)S(1)} %collective-permute-done.2.refs_3_, ...), custom_call_target="tpu_custom_call" | custom-call | flops 20000000 | bytes 3997696 | tf_op jit(solution)/shard_map/pallas_call | solution.py:595
  16.2 1.8 %collective-permute-start.8 = (f32[192,128]{1,0:T(8,128)S(1)}, f32[192,128]{1,0:T(8,128)S(1)}, u32[]{:S(2)}, u32[]{:S(2)}) collective-permute-start(f32[192,128]{1,0:T(8,128)S(1)} %get-tuple-element.34.refs_0_), channel_id=1, source_target_pairs={{0,4},{1,5},{2,6},{3,7},{4,0},{5,1},{6,2},{7,3},{8,12},{9,13},{10,... | collective-permute-start | bytes 294920 | tf_op jit(solution)/shard_map/ppermute | solution.py:609
  18.0 2.0 %collective-permute-start.7 = (f32[192,128]{1,0:T(8,128)S(1)}, f32[192,128]{1,0:T(8,128)S(1)}, u32[]{:S(2)}, u32[]{:S(2)}) collective-permute-start(f32[192,128]{1,0:T(8,128)S(1)} %get-tuple-element.34.refs_0_), channel_id=1, source_target_pairs={{0,2},{1,3},{2,0},{3,1},{4,6},{5,7},{6,4},{7,5},{8,10},{9,11},{10,... | collective-permute-start | bytes 294920 | tf_op jit(solution)/shard_map/ppermute | solution.py:609
  21.2 4.1 %collective-permute-done.8.refs_1_ = f32[192,128]{1,0:T(8,128)S(1)} collective-permute-done((f32[192,128]{1,0:T(8,128)S(1)}, f32[192,128]{1,0:T(8,128)S(1)}, u32[]{:S(2)}, u32[]{:S(2)}) %collective-permute-start.8) | collective-permute-done | bytes 98336 | tf_op jit(solution)/shard_map/ppermute | solution.py:609
  25.3 2.0 %collective-permute-done.9.refs_3_ = f32[192,128]{1,0:T(8,128)S(1)} collective-permute-done((f32[192,128]{1,0:T(8,128)S(1)}, f32[192,128]{1,0:T(8,128)S(1)}, u32[]{:S(2)}, u32[]{:S(2)}) %collective-permute-start.9) | collective-permute-done | bytes 98336 | tf_op jit(solution)/shard_map/ppermute | solution.py:609
  27.9 0.8 %collective-permute-done.13.refs_7_ = f32[192,128]{1,0:T(8,128)S(1)} collective-permute-done((f32[192,128]{1,0:T(8,128)S(1)}, f32[192,128]{1,0:T(8,128)S(1)}, u32[]{:S(2)}, u32[]{:S(2)}) %collective-permute-start.13) | collective-permute-done | bytes 98336 | tf_op jit(solution)/shard_map/ppermute | solution.py:617
  28.8 1.4 %shard_map.92 = (f32[128,256]{1,0:T(8,128)S(1)}, f32[192,128]{1,0:T(8,128)S(1)}) custom-call(f32[192,128]{1,0:T(8,128)S(1)} %get-tuple-element.34.refs_0_, f32[192,128]{1,0:T(8,128)S(1)} %get-tuple-element.39.refs_1_, f32[192,128]{1,0:T(8,128)S(1)} %get-tuple-element.40.refs_2_, f32[192,128]{1,0:T(8,128)S(1)} %collective-permute-done.9.refs_3_, ...), custom_call_target="tpu_custom_call" | custom-call | flops 20000000 | bytes 4849664 | tf_op jit(solution)/shard_map/pallas_call | solution.py:595
  30.3 1.7 %collective-permute-start.18 = (f32[192,128]{1,0:T(8,128)S(1)}, f32[192,128]{1,0:T(8,128)S(1)}, u32[]{:S(2)}, u32[]{:S(2)}) collective-permute-start(f32[192,128]{1,0:T(8,128)S(1)} %get-tuple-element.44.refs_0_), channel_id=1, source_target_pairs={{0,6},{1,7},{2,4},{3,5},{4,2},{5,3},{6,0},{7,1},{8,14},{9,15},{10,... | collective-permute-start | bytes 294920 | tf_op jit(solution)/shard_map/ppermute | solution.py:609
  32.3 1.6 %collective-permute-start.16 = (f32[144,128]{1,0:T(8,128)S(1)}, f32[144,128]{1,0:T(8,128)S(1)}, u32[]{:S(2)}, u32[]{:S(2)}) collective-permute-start(f32[144,128]{1,0:T(8,128)S(1)} %shard_map.93), channel_id=1, source_target_pairs={{0,8},{8,0},{16,24},{24,16},{1,9},{9,1},{17,25},{25,17},{2,10},{10... | collective-permute-start | bytes 221192 | tf_op jit(solution)/shard_map/ppermute | solution.py:632
  33.9 1.4 %collective-permute-start.15 = (f32[192,128]{1,0:T(8,128)S(1)}, f32[192,128]{1,0:T(8,128)S(1)}, u32[]{:S(2)}, u32[]{:S(2)}) collective-permute-start(f32[192,128]{1,0:T(8,128)S(1)} %get-tuple-element.44.refs_0_), channel_id=1, source_target_pairs={{0,4},{1,5},{2,6},{3,7},{4,0},{5,1},{6,2},{7,3},{8,12},{9,13},{10,... | collective-permute-start | bytes 294920 | tf_op jit(solution)/shard_map/ppermute | solution.py:609
  35.3 1.3 %collective-permute-start.14 = (f32[192,128]{1,0:T(8,128)S(1)}, f32[192,128]{1,0:T(8,128)S(1)}, u32[]{:S(2)}, u32[]{:S(2)}) collective-permute-start(f32[192,128]{1,0:T(8,128)S(1)} %get-tuple-element.44.refs_0_), channel_id=1, source_target_pairs={{0,2},{1,3},{2,0},{3,1},{4,6},{5,7},{6,4},{7,5},{8,10},{9,11},{10,... | collective-permute-start | bytes 294920 | tf_op jit(solution)/shard_map/ppermute | solution.py:609
  36.7 1.6 %collective-permute-start.17 = (f32[144,128]{1,0:T(8,128)S(1)}, f32[144,128]{1,0:T(8,128)S(1)}, u32[]{:S(2)}, u32[]{:S(2)}) collective-permute-start(f32[144,128]{1,0:T(8,128)S(1)} %add.6.one_ref), channel_id=1, source_target_pairs={{0,16},{8,24},{16,0},{24,8},{1,17},{9,25},{17,1},{25,9},{2,18},{10... | collective-permute-start | bytes 221192 | tf_op jit(solution)/shard_map/ppermute | solution.py:634
  38.3 2.8 %collective-permute-done.17.two_ref = f32[144,128]{1,0:T(8,128)S(1)} collective-permute-done((f32[144,128]{1,0:T(8,128)S(1)}, f32[144,128]{1,0:T(8,128)S(1)}, u32[]{:S(2)}, u32[]{:S(2)}) %collective-permute-start.17) | collective-permute-done | bytes 73760 | tf_op jit(solution)/shard_map/ppermute | solution.py:634
  41.2 1.0 %shard_map.94 = (f32[128,256]{1,0:T(8,128)S(1)}, f32[128,256]{1,0:T(8,128)S(1)}, f32[128,128]{1,0:T(8,128)S(1)}) custom-call(f32[144,128]{1,0:T(8,128)S(1)} %add.6.one_ref, f32[144,128]{1,0:T(8,128)S(1)} %collective-permute-done.17.two_ref, f32[128,256]{1,0:T(8,128)S(1)} %get-tuple-element.45.gains_ref, f32[256,128]{1,0:T(8,128)S(1)} %get-tuple-element.37.refs_12_.basis_ref), custom_call_target="tpu_custom_call" | custom-call | flops 20000000 | bytes 737280 | tf_op jit(solution)/shard_map/pallas_call | solution.py:595
  43.3 0.8 %collective-permute-done.20.refs_5_ = f32[192,128]{1,0:T(8,128)S(1)} collective-permute-done((f32[192,128]{1,0:T(8,128)S(1)}, f32[192,128]{1,0:T(8,128)S(1)}, u32[]{:S(2)}, u32[]{:S(2)}) %collective-permute-start.20) | collective-permute-done | bytes 98336 | tf_op jit(solution)/shard_map/ppermute | solution.py:617
  44.2 1.4 %shard_map.97 = (f32[128,256]{1,0:T(8,128)S(1)}, f32[192,128]{1,0:T(8,128)S(1)}) custom-call(f32[192,128]{1,0:T(8,128)S(1)} %get-tuple-element.44.refs_0_, f32[192,128]{1,0:T(8,128)S(1)} %get-tuple-element.47.refs_1_, f32[192,128]{1,0:T(8,128)S(1)} %get-tuple-element.48.refs_2_, f32[192,128]{1,0:T(8,128)S(1)} %shard_map.96.refs_3_, ...), custom_call_target="tpu_custom_call" | custom-call | flops 20000000 | bytes 4849664 | tf_op jit(solution)/shard_map/pallas_call | solution.py:595
  45.7 2.5 %collective-permute-start.27 = (f32[192,128]{1,0:T(8,128)S(1)}, f32[192,128]{1,0:T(8,128)S(1)}, u32[]{:S(2)}, u32[]{:S(2)}) collective-permute-start(f32[192,128]{1,0:T(8,128)S(1)} %get-tuple-element.49.refs_0_), channel_id=1, source_target_pairs={{0,6},{1,7},{2,4},{3,5},{4,2},{5,3},{6,0},{7,1},{8,14},{9,15},{10,... | collective-permute-start | bytes 294920 | tf_op jit(solution)/shard_map/ppermute | solution.py:609
  48.4 1.6 %collective-permute-start.25 = (f32[128,128]{1,0:T(8,128)S(1)}, f32[128,128]{1,0:T(8,128)S(1)}, u32[]{:S(2)}, u32[]{:S(2)}) collective-permute-start(f32[128,128]{1,0:T(8,128)S(1)} %shard_map.98), channel_id=1, source_target_pairs={{0,8},{8,0},{16,24},{24,16},{1,9},{9,1},{17,25},{25,17},{2,10},{10... | collective-permute-start | bytes 196616 | tf_op jit(solution)/shard_map/ppermute | solution.py:632
  50.2 1.8 %collective-permute-start.23 = (f32[192,128]{1,0:T(8,128)S(1)}, f32[192,128]{1,0:T(8,128)S(1)}, u32[]{:S(2)}, u32[]{:S(2)}) collective-permute-start(f32[192,128]{1,0:T(8,128)S(1)} %get-tuple-element.49.refs_0_), channel_id=1, source_target_pairs={{0,2},{1,3},{2,0},{3,1},{4,6},{5,7},{6,4},{7,5},{8,10},{9,11},{10,... | collective-permute-start | bytes 294920 | tf_op jit(solution)/shard_map/ppermute | solution.py:609
  52.0 0.8 %collective-permute-done.25 = f32[128,128]{1,0:T(8,128)S(1)} collective-permute-done((f32[128,128]{1,0:T(8,128)S(1)}, f32[128,128]{1,0:T(8,128)S(1)}, u32[]{:S(2)}, u32[]{:S(2)}) %collective-permute-start.25) | collective-permute-done | bytes 65568 | tf_op jit(solution)/shard_map/ppermute | solution.py:632
  52.8 1.6 %collective-permute-start.26 = (f32[128,128]{1,0:T(8,128)S(1)}, f32[128,128]{1,0:T(8,128)S(1)}, u32[]{:S(2)}, u32[]{:S(2)}) collective-permute-start(f32[128,128]{1,0:T(8,128)S(1)} %add.7.one_ref), channel_id=1, source_target_pairs={{0,16},{8,24},{16,0},{24,8},{1,17},{9,25},{17,1},{25,9},{2,18},{10... | collective-permute-start | bytes 196616 | tf_op jit(solution)/shard_map/ppermute | solution.py:634
  54.4 2.7 %collective-permute-done.26.two_ref = f32[128,128]{1,0:T(8,128)S(1)} collective-permute-done((f32[128,128]{1,0:T(8,128)S(1)}, f32[128,128]{1,0:T(8,128)S(1)}, u32[]{:S(2)}, u32[]{:S(2)}) %collective-permute-start.26) | collective-permute-done | bytes 65568 | tf_op jit(solution)/shard_map/ppermute | solution.py:634
  58.2 0.8 %collective-permute-done.29.refs_5_ = f32[192,128]{1,0:T(8,128)S(1)} collective-permute-done((f32[192,128]{1,0:T(8,128)S(1)}, f32[192,128]{1,0:T(8,128)S(1)}, u32[]{:S(2)}, u32[]{:S(2)}) %collective-permute-start.29) | collective-permute-done | bytes 98336 | tf_op jit(solution)/shard_map/ppermute | solution.py:617
  59.2 0.8 %shard_map.102 = (f32[128,128]{1,0:T(8,128)S(1)}, f32[40,128]{1,0:T(8,128)S(1)}) custom-call(f32[192,128]{1,0:T(8,128)S(1)} %get-tuple-element.49.refs_0_, f32[192,128]{1,0:T(8,128)S(1)} %get-tuple-element.54.refs_1_, f32[192,128]{1,0:T(8,128)S(1)} %get-tuple-element.55.refs_2_, f32[192,128]{1,0:T(8,128)S(1)} %shard_map.101.refs_3_, ...), custom_call_target="tpu_custom_call" | custom-call | flops 20000000 | bytes 1703936 | tf_op jit(solution)/shard_map/pallas_call | solution.py:595
  59.9 2.5 %collective-permute-start.34 = (f32[40,128]{1,0:T(8,128)S(1)}, f32[40,128]{1,0:T(8,128)S(1)}, u32[]{:S(2)}, u32[]{:S(2)}) collective-permute-start(f32[40,128]{1,0:T(8,128)S(1)} %get-tuple-element.59.refs_0_), channel_id=1, source_target_pairs={{0,24},{8,16},{16,8},{24,0},{1,25},{9,17},{17,9},{25,1},{2,26},{10... | collective-permute-start | bytes 61448 | tf_op jit(solution)/shard_map/ppermute | solution.py:624
  63.5 1.0 %shard_map.103 = f32[8,32,64]{2,1,0:T(8,128)} custom-call(f32[128,128]{1,0:T(8,128)S(1)} %get-tuple-element.58.gains_ref), custom_call_target="tpu_custom_call" | custom-call | flops 20000000 | bytes 131072 | tf_op jit(solution)/shard_map/pallas_call | solution.py:595
  64.7 1.5 %collective-permute-done.33.refs_2_ = f32[40,128]{1,0:T(8,128)S(1)} collective-permute-done((f32[40,128]{1,0:T(8,128)S(1)}, f32[40,128]{1,0:T(8,128)S(1)}, u32[]{:S(2)}, u32[]{:S(2)}) %collective-permute-start.33) | collective-permute-done | bytes 20512 | tf_op jit(solution)/shard_map/ppermute | solution.py:624
  66.7 0.9 %shard_map.104 = f32[9,8,64]{2,1,0:T(8,128)} custom-call(f32[40,128]{1,0:T(8,128)S(1)} %get-tuple-element.59.refs_0_, f32[40,128]{1,0:T(8,128)S(1)} %collective-permute-done.32.refs_1_, f32[40,128]{1,0:T(8,128)S(1)} %collective-permute-done.33.refs_2_, f32[40,128]{1,0:T(8,128)S(1)} %collective-permute-done.34.refs_3_, ...), custom_call_target="tpu_custom_call" | custom-call | flops 20000000 | bytes 165888 | tf_op jit(solution)/shard_map/pallas_call | solution.py:595
  (59 shorter events, 9.7 us)
Async XLA Ops:
  2.1 11.6 %collective-permute-start.3 = (f32[136,128]{1,0:T(8,128)S(1)}, f32[136,128]{1,0:T(8,128)S(1)}, u32[]{:S(2)}, u32[]{:S(2)}) collective-permute-start(f32[136,128]{1,0:T(8,128)S(1)} %shard_map.86.refs_0_), channel_id=1, source_target_pairs={{0,1},{1,0},{2,3},{3,2},{4,5},{5,4},{6,7},{7,6},{8,9},{9,8},{10,11... | collective-permute-start | bytes 208904 | tf_op jit(solution)/shard_map/ppermute | solution.py:617
  2.6 9.9 %collective-permute-start.2 = (f32[136,128]{1,0:T(8,128)S(1)}, f32[136,128]{1,0:T(8,128)S(1)}, u32[]{:S(2)}, u32[]{:S(2)}) collective-permute-start(f32[136,128]{1,0:T(8,128)S(1)} %shard_map.86.refs_0_), channel_id=1, source_target_pairs={{0,6},{1,7},{2,4},{3,5},{4,2},{5,3},{6,0},{7,1},{8,14},{9,15},{10,... | collective-permute-start | bytes 208904 | tf_op jit(solution)/shard_map/ppermute | solution.py:609
  7.3 6.4 %collective-permute-start.1 = (f32[136,128]{1,0:T(8,128)S(1)}, f32[136,128]{1,0:T(8,128)S(1)}, u32[]{:S(2)}, u32[]{:S(2)}) collective-permute-start(f32[136,128]{1,0:T(8,128)S(1)} %shard_map.86.refs_0_), channel_id=1, source_target_pairs={{0,4},{1,5},{2,6},{3,7},{4,0},{5,1},{6,2},{7,3},{8,12},{9,13},{10,... | collective-permute-start | bytes 208904 | tf_op jit(solution)/shard_map/ppermute | solution.py:609
  7.3 5.3 %collective-permute-start = (f32[136,128]{1,0:T(8,128)S(1)}, f32[136,128]{1,0:T(8,128)S(1)}, u32[]{:S(2)}, u32[]{:S(2)}) collective-permute-start(f32[136,128]{1,0:T(8,128)S(1)} %shard_map.86.refs_0_), channel_id=1, source_target_pairs={{0,2},{1,3},{2,0},{3,1},{4,6},{5,7},{6,4},{7,5},{8,10},{9,11},{10,... | collective-permute-start | bytes 208904 | tf_op jit(solution)/shard_map/ppermute | solution.py:609
  12.5 1.3 %collective-permute-start.6 = (f32[136,128]{1,0:T(8,128)S(1)}, f32[136,128]{1,0:T(8,128)S(1)}, u32[]{:S(2)}, u32[]{:S(2)}) collective-permute-start(f32[136,128]{1,0:T(8,128)S(1)} %collective-permute-done.2.refs_3_), channel_id=1, source_target_pairs={{0,1},{1,0},{2,3},{3,2},{4,5},{5,4},{6,7},{7,6},{8,9},{9,8},{10,11... | collective-permute-start | bytes 208904 | tf_op jit(solution)/shard_map/ppermute | solution.py:617
  12.6 1.4 %collective-permute-start.4 = (f32[136,128]{1,0:T(8,128)S(1)}, f32[136,128]{1,0:T(8,128)S(1)}, u32[]{:S(2)}, u32[]{:S(2)}) collective-permute-start(f32[136,128]{1,0:T(8,128)S(1)} %collective-permute-done.refs_1_), channel_id=1, source_target_pairs={{0,1},{1,0},{2,3},{3,2},{4,5},{5,4},{6,7},{7,6},{8,9},{9,8},{10,11... | collective-permute-start | bytes 208904 | tf_op jit(solution)/shard_map/ppermute | solution.py:617
  16.2 9.1 %collective-permute-start.8 = (f32[192,128]{1,0:T(8,128)S(1)}, f32[192,128]{1,0:T(8,128)S(1)}, u32[]{:S(2)}, u32[]{:S(2)}) collective-permute-start(f32[192,128]{1,0:T(8,128)S(1)} %get-tuple-element.34.refs_0_), channel_id=1, source_target_pairs={{0,4},{1,5},{2,6},{3,7},{4,0},{5,1},{6,2},{7,3},{8,12},{9,13},{10,... | collective-permute-start | bytes 294920 | tf_op jit(solution)/shard_map/ppermute | solution.py:609
  18.0 7.3 %collective-permute-start.7 = (f32[192,128]{1,0:T(8,128)S(1)}, f32[192,128]{1,0:T(8,128)S(1)}, u32[]{:S(2)}, u32[]{:S(2)}) collective-permute-start(f32[192,128]{1,0:T(8,128)S(1)} %get-tuple-element.34.refs_0_), channel_id=1, source_target_pairs={{0,2},{1,3},{2,0},{3,1},{4,6},{5,7},{6,4},{7,5},{8,10},{9,11},{10,... | collective-permute-start | bytes 294920 | tf_op jit(solution)/shard_map/ppermute | solution.py:609
  20.1 7.3 %collective-permute-start.9 = (f32[192,128]{1,0:T(8,128)S(1)}, f32[192,128]{1,0:T(8,128)S(1)}, u32[]{:S(2)}, u32[]{:S(2)}) collective-permute-start(f32[192,128]{1,0:T(8,128)S(1)} %get-tuple-element.34.refs_0_), channel_id=1, source_target_pairs={{0,6},{1,7},{2,4},{3,5},{4,2},{5,3},{6,0},{7,1},{8,14},{9,15},{10,... | collective-permute-start | bytes 294920 | tf_op jit(solution)/shard_map/ppermute | solution.py:609
  20.7 7.2 %collective-permute-start.10 = (f32[192,128]{1,0:T(8,128)S(1)}, f32[192,128]{1,0:T(8,128)S(1)}, u32[]{:S(2)}, u32[]{:S(2)}) collective-permute-start(f32[192,128]{1,0:T(8,128)S(1)} %get-tuple-element.34.refs_0_), channel_id=1, source_target_pairs={{0,1},{1,0},{2,3},{3,2},{4,5},{5,4},{6,7},{7,6},{8,9},{9,8},{10,11... | collective-permute-start | bytes 294920 | tf_op jit(solution)/shard_map/ppermute | solution.py:617
  25.3 3.3 %collective-permute-start.11 = (f32[192,128]{1,0:T(8,128)S(1)}, f32[192,128]{1,0:T(8,128)S(1)}, u32[]{:S(2)}, u32[]{:S(2)}) collective-permute-start(f32[192,128]{1,0:T(8,128)S(1)} %get-tuple-element.39.refs_1_), channel_id=1, source_target_pairs={{0,1},{1,0},{2,3},{3,2},{4,5},{5,4},{6,7},{7,6},{8,9},{9,8},{10,11... | collective-permute-start | bytes 294920 | tf_op jit(solution)/shard_map/ppermute | solution.py:617
  27.4 1.5 %collective-permute-start.12 = (f32[192,128]{1,0:T(8,128)S(1)}, f32[192,128]{1,0:T(8,128)S(1)}, u32[]{:S(2)}, u32[]{:S(2)}) collective-permute-start(f32[192,128]{1,0:T(8,128)S(1)} %get-tuple-element.40.refs_2_), channel_id=1, source_target_pairs={{0,1},{1,0},{2,3},{3,2},{4,5},{5,4},{6,7},{7,6},{8,9},{9,8},{10,11... | collective-permute-start | bytes 294920 | tf_op jit(solution)/shard_map/ppermute | solution.py:617
  30.3 8.1 %collective-permute-start.18 = (f32[192,128]{1,0:T(8,128)S(1)}, f32[192,128]{1,0:T(8,128)S(1)}, u32[]{:S(2)}, u32[]{:S(2)}) collective-permute-start(f32[192,128]{1,0:T(8,128)S(1)} %get-tuple-element.44.refs_0_), channel_id=1, source_target_pairs={{0,6},{1,7},{2,4},{3,5},{4,2},{5,3},{6,0},{7,1},{8,14},{9,15},{10,... | collective-permute-start | bytes 294920 | tf_op jit(solution)/shard_map/ppermute | solution.py:609
  32.3 4.4 %collective-permute-start.16 = (f32[144,128]{1,0:T(8,128)S(1)}, f32[144,128]{1,0:T(8,128)S(1)}, u32[]{:S(2)}, u32[]{:S(2)}) collective-permute-start(f32[144,128]{1,0:T(8,128)S(1)} %shard_map.93), channel_id=1, source_target_pairs={{0,8},{8,0},{16,24},{24,16},{1,9},{9,1},{17,25},{25,17},{2,10},{10... | collective-permute-start | bytes 221192 | tf_op jit(solution)/shard_map/ppermute | solution.py:632
  33.9 9.4 %collective-permute-start.19 = (f32[192,128]{1,0:T(8,128)S(1)}, f32[192,128]{1,0:T(8,128)S(1)}, u32[]{:S(2)}, u32[]{:S(2)}) collective-permute-start(f32[192,128]{1,0:T(8,128)S(1)} %get-tuple-element.44.refs_0_), channel_id=1, source_target_pairs={{0,1},{1,0},{2,3},{3,2},{4,5},{5,4},{6,7},{7,6},{8,9},{9,8},{10,11... | collective-permute-start | bytes 294920 | tf_op jit(solution)/shard_map/ppermute | solution.py:617
  33.9 8.9 %collective-permute-start.15 = (f32[192,128]{1,0:T(8,128)S(1)}, f32[192,128]{1,0:T(8,128)S(1)}, u32[]{:S(2)}, u32[]{:S(2)}) collective-permute-start(f32[192,128]{1,0:T(8,128)S(1)} %get-tuple-element.44.refs_0_), channel_id=1, source_target_pairs={{0,4},{1,5},{2,6},{3,7},{4,0},{5,1},{6,2},{7,3},{8,12},{9,13},{10,... | collective-permute-start | bytes 294920 | tf_op jit(solution)/shard_map/ppermute | solution.py:609
  35.3 7.5 %collective-permute-start.14 = (f32[192,128]{1,0:T(8,128)S(1)}, f32[192,128]{1,0:T(8,128)S(1)}, u32[]{:S(2)}, u32[]{:S(2)}) collective-permute-start(f32[192,128]{1,0:T(8,128)S(1)} %get-tuple-element.44.refs_0_), channel_id=1, source_target_pairs={{0,2},{1,3},{2,0},{3,1},{4,6},{5,7},{6,4},{7,5},{8,10},{9,11},{10,... | collective-permute-start | bytes 294920 | tf_op jit(solution)/shard_map/ppermute | solution.py:609
  36.7 4.4 %collective-permute-start.17 = (f32[144,128]{1,0:T(8,128)S(1)}, f32[144,128]{1,0:T(8,128)S(1)}, u32[]{:S(2)}, u32[]{:S(2)}) collective-permute-start(f32[144,128]{1,0:T(8,128)S(1)} %add.6.one_ref), channel_id=1, source_target_pairs={{0,16},{8,24},{16,0},{24,8},{1,17},{9,25},{17,1},{25,9},{2,18},{10... | collective-permute-start | bytes 221192 | tf_op jit(solution)/shard_map/ppermute | solution.py:634
  38.3 4.9 %collective-permute-start.22 = (f32[192,128]{1,0:T(8,128)S(1)}, f32[192,128]{1,0:T(8,128)S(1)}, u32[]{:S(2)}, u32[]{:S(2)}) collective-permute-start(f32[192,128]{1,0:T(8,128)S(1)} %shard_map.96.refs_3_), channel_id=1, source_target_pairs={{0,1},{1,0},{2,3},{3,2},{4,5},{5,4},{6,7},{7,6},{8,9},{9,8},{10,11... | collective-permute-start | bytes 294920 | tf_op jit(solution)/shard_map/ppermute | solution.py:617
  42.7 1.3 %collective-permute-start.20 = (f32[192,128]{1,0:T(8,128)S(1)}, f32[192,128]{1,0:T(8,128)S(1)}, u32[]{:S(2)}, u32[]{:S(2)}) collective-permute-start(f32[192,128]{1,0:T(8,128)S(1)} %get-tuple-element.47.refs_1_), channel_id=1, source_target_pairs={{0,1},{1,0},{2,3},{3,2},{4,5},{5,4},{6,7},{7,6},{8,9},{9,8},{10,11... | collective-permute-start | bytes 294920 | tf_op jit(solution)/shard_map/ppermute | solution.py:617
  42.7 1.5 %collective-permute-start.21 = (f32[192,128]{1,0:T(8,128)S(1)}, f32[192,128]{1,0:T(8,128)S(1)}, u32[]{:S(2)}, u32[]{:S(2)}) collective-permute-start(f32[192,128]{1,0:T(8,128)S(1)} %get-tuple-element.48.refs_2_), channel_id=1, source_target_pairs={{0,1},{1,0},{2,3},{3,2},{4,5},{5,4},{6,7},{7,6},{8,9},{9,8},{10,11... | collective-permute-start | bytes 294920 | tf_op jit(solution)/shard_map/ppermute | solution.py:617
  45.7 8.7 %collective-permute-start.27 = (f32[192,128]{1,0:T(8,128)S(1)}, f32[192,128]{1,0:T(8,128)S(1)}, u32[]{:S(2)}, u32[]{:S(2)}) collective-permute-start(f32[192,128]{1,0:T(8,128)S(1)} %get-tuple-element.49.refs_0_), channel_id=1, source_target_pairs={{0,6},{1,7},{2,4},{3,5},{4,2},{5,3},{6,0},{7,1},{8,14},{9,15},{10,... | collective-permute-start | bytes 294920 | tf_op jit(solution)/shard_map/ppermute | solution.py:609
  48.4 4.3 %collective-permute-start.25 = (f32[128,128]{1,0:T(8,128)S(1)}, f32[128,128]{1,0:T(8,128)S(1)}, u32[]{:S(2)}, u32[]{:S(2)}) collective-permute-start(f32[128,128]{1,0:T(8,128)S(1)} %shard_map.98), channel_id=1, source_target_pairs={{0,8},{8,0},{16,24},{24,16},{1,9},{9,1},{17,25},{25,17},{2,10},{10... | collective-permute-start | bytes 196616 | tf_op jit(solution)/shard_map/ppermute | solution.py:632
  50.0 8.2 %collective-permute-start.28 = (f32[192,128]{1,0:T(8,128)S(1)}, f32[192,128]{1,0:T(8,128)S(1)}, u32[]{:S(2)}, u32[]{:S(2)}) collective-permute-start(f32[192,128]{1,0:T(8,128)S(1)} %get-tuple-element.49.refs_0_), channel_id=1, source_target_pairs={{0,1},{1,0},{2,3},{3,2},{4,5},{5,4},{6,7},{7,6},{8,9},{9,8},{10,11... | collective-permute-start | bytes 294920 | tf_op jit(solution)/shard_map/ppermute | solution.py:617
  50.0 7.7 %collective-permute-start.24 = (f32[192,128]{1,0:T(8,128)S(1)}, f32[192,128]{1,0:T(8,128)S(1)}, u32[]{:S(2)}, u32[]{:S(2)}) collective-permute-start(f32[192,128]{1,0:T(8,128)S(1)} %get-tuple-element.49.refs_0_), channel_id=1, source_target_pairs={{0,4},{1,5},{2,6},{3,7},{4,0},{5,1},{6,2},{7,3},{8,12},{9,13},{10,... | collective-permute-start | bytes 294920 | tf_op jit(solution)/shard_map/ppermute | solution.py:609
  50.2 7.5 %collective-permute-start.23 = (f32[192,128]{1,0:T(8,128)S(1)}, f32[192,128]{1,0:T(8,128)S(1)}, u32[]{:S(2)}, u32[]{:S(2)}) collective-permute-start(f32[192,128]{1,0:T(8,128)S(1)} %get-tuple-element.49.refs_0_), channel_id=1, source_target_pairs={{0,2},{1,3},{2,0},{3,1},{4,6},{5,7},{6,4},{7,5},{8,10},{9,11},{10,... | collective-permute-start | bytes 294920 | tf_op jit(solution)/shard_map/ppermute | solution.py:609
  52.8 4.3 %collective-permute-start.26 = (f32[128,128]{1,0:T(8,128)S(1)}, f32[128,128]{1,0:T(8,128)S(1)}, u32[]{:S(2)}, u32[]{:S(2)}) collective-permute-start(f32[128,128]{1,0:T(8,128)S(1)} %add.7.one_ref), channel_id=1, source_target_pairs={{0,16},{8,24},{16,0},{24,8},{1,17},{9,25},{17,1},{25,9},{2,18},{10... | collective-permute-start | bytes 196616 | tf_op jit(solution)/shard_map/ppermute | solution.py:634
  54.4 3.9 %collective-permute-start.31 = (f32[192,128]{1,0:T(8,128)S(1)}, f32[192,128]{1,0:T(8,128)S(1)}, u32[]{:S(2)}, u32[]{:S(2)}) collective-permute-start(f32[192,128]{1,0:T(8,128)S(1)} %shard_map.101.refs_3_), channel_id=1, source_target_pairs={{0,1},{1,0},{2,3},{3,2},{4,5},{5,4},{6,7},{7,6},{8,9},{9,8},{10,11... | collective-permute-start | bytes 294920 | tf_op jit(solution)/shard_map/ppermute | solution.py:617
  57.7 1.4 %collective-permute-start.30 = (f32[192,128]{1,0:T(8,128)S(1)}, f32[192,128]{1,0:T(8,128)S(1)}, u32[]{:S(2)}, u32[]{:S(2)}) collective-permute-start(f32[192,128]{1,0:T(8,128)S(1)} %get-tuple-element.55.refs_2_), channel_id=1, source_target_pairs={{0,1},{1,0},{2,3},{3,2},{4,5},{5,4},{6,7},{7,6},{8,9},{9,8},{10,11... | collective-permute-start | bytes 294920 | tf_op jit(solution)/shard_map/ppermute | solution.py:617
  59.9 4.7 %collective-permute-start.34 = (f32[40,128]{1,0:T(8,128)S(1)}, f32[40,128]{1,0:T(8,128)S(1)}, u32[]{:S(2)}, u32[]{:S(2)}) collective-permute-start(f32[40,128]{1,0:T(8,128)S(1)} %get-tuple-element.59.refs_0_), channel_id=1, source_target_pairs={{0,24},{8,16},{16,8},{24,0},{1,25},{9,17},{17,9},{25,1},{2,26},{10... | collective-permute-start | bytes 61448 | tf_op jit(solution)/shard_map/ppermute | solution.py:624
  62.4 3.8 %collective-permute-start.33 = (f32[40,128]{1,0:T(8,128)S(1)}, f32[40,128]{1,0:T(8,128)S(1)}, u32[]{:S(2)}, u32[]{:S(2)}) collective-permute-start(f32[40,128]{1,0:T(8,128)S(1)} %get-tuple-element.59.refs_0_), channel_id=1, source_target_pairs={{0,16},{8,24},{16,0},{24,8},{1,17},{9,25},{17,1},{25,9},{2,18},{10... | collective-permute-start | bytes 61448 | tf_op jit(solution)/shard_map/ppermute | solution.py:624
  62.9 3.8 %collective-permute-start.32 = (f32[40,128]{1,0:T(8,128)S(1)}, f32[40,128]{1,0:T(8,128)S(1)}, u32[]{:S(2)}, u32[]{:S(2)}) collective-permute-start(f32[40,128]{1,0:T(8,128)S(1)} %get-tuple-element.59.refs_0_), channel_id=1, source_target_pairs={{0,8},{8,0},{16,24},{24,16},{1,9},{9,1},{17,25},{25,17},{2,10},{10... | collective-permute-start | bytes 61448 | tf_op jit(solution)/shard_map/ppermute | solution.py:624
  (3 other events, 3.9 us)

commit v5 on v4

--- a/solution.py
+++ b/solution.py
@@ -155,7 +155,7 @@
 
 
 def greet_kernel(
-    blocks, intervals, pair_hbm, start_hbm, penalty_hbm, flag_hbm, out_ref, pair_ref, start_ref,
+    blocks, intervals, pair_hbm, start_hbm, penalty_hbm, flag_hbm, out_ref, again_ref, pair_ref, start_ref,
     penalty_ref, flag_ref, sems
 ):
     copies = [
@@ -207,6 +207,7 @@
         high = plane.astype(BF16)
         low = (plane - high.astype(F32)).astype(BF16)
         out_ref[m * BLOCK : (m + 1) * BLOCK, :] = nt(place, high) + nt(place, low)
+    again_ref[...] = out_ref[...]
 
 
 def prepare_kernel(
@@ -603,18 +604,21 @@
     )(*operands)
 
 
-def share_base(x, last=(), ties=(2,), ahead=False):
+def share_base(x, last=(), ties=(2,), ahead=False, again=None):
     devices = lax.axis_size("base")
     mine = [x] + [
         lax.ppermute(x, "base", [(d, d ^ (2 * k)) for d in range(devices)])
         for k in range(1, devices // 2)
     ]
     if ahead:
-        mine[3:] = after(mine[3:], (), flops=5_000_000_000)
+        mine[2:3] = after(mine[2:3], (), flops=5_000_000_000)
     if last:
         for k, y in zip(ties, after([mine[k] for k in ties], last)):
             mine[k] = y
-    other = [lax.ppermute(y, "base", [(d, d ^ 1) for d in range(devices)]) for y in mine]
+    sent = list(mine)
+    if again is not None:
+        (sent[0],) = after([again], last)
+    other = [lax.ppermute(y, "base", [(d, d ^ 1) for d in range(devices)]) for y in sent]
     return mine + other
 
 
@@ -652,10 +656,10 @@
     terms = shape(TERM_ROWS, LANES)
     square = shape(2 * LANES, LANES)
 
-    (greeting,) = call(
+    greeting, again = call(
         functools.partial(greet_kernel, blocks, intervals),
         (pairs, start_gains, penalty.reshape(1, owned), flags),
-        [shape(GAIN_ROWS + 8, LANES)],
+        [shape(GAIN_ROWS + 8, LANES)] * 2,
         [
             pltpu.SMEM(pairs.shape, jnp.int32),
             pltpu.VMEM(start_gains.shape, F32),
@@ -692,7 +696,7 @@
         hbm=True,
         flops=2_000_000_000,
     )
-    greetings = share_base(greeting, last=(chans,))
+    greetings = share_base(greeting, last=(chans,), again=again)
     scratch = [
         pltpu.VMEM((12, BLOCK // 2, LANES), F32),
         pltpu.VMEM((2, 12, BLOCK // 2, LANES), F32),
@@ -727,7 +731,7 @@
     z, dual, inverse = call(
         first_consensus_kernel, (*sum_band(part), gains, basis), [wide, wide, narrow]
     )
-    pieces = share_base(message, last=(z,), ties=(1, 2), ahead=True)
+    pieces = share_base(message, last=(z,), ties=(3,), ahead=True)
     gains, message = call(
         functools.partial(step_kernel, count),
         (*pieces, select, z, pen, scale, products),
@@ -736,7 +740,7 @@
     )
     (part,) = call(total_kernel, (gains, dual, basis), [narrow])
     z, dual = call(consensus_kernel, (*sum_band(part), gains, dual, basis, inverse), [wide, wide])
-    pieces = share_base(message, last=(z,), ties=(1, 2), ahead=True)
+    pieces = share_base(message, last=(z,), ties=(3,), ahead=True)
     chunks = 8 * owned // LANES
     gains, part = call(
         functools.partial(last_kernel, count, blocks, intervals),

time: 67.8 us -> 69.1 us (1.019)
  waiting for transfers between devices: 20.3 us -> 22.5 us
  starting transfers between devices: 31.1 us -> 30.1 us
    ppermute x12, waiting for transfers between devices: 7.42 us -> 13.9 us  [share_base(): lax.ppermute(x, 'base', [(d, d ^ 2 * k) for d in range(devices)])]
    ppermute x2, waiting for transfers between devices: 5.57 us -> 0.01 us  [sum_band(): return (x, lax.ppermute(x, 'band', [(d, d ^ step) for d in range(devices)]))]
    ppermute x2, waiting for transfers between devices: 0.91 us -> 3.33 us  [sum_band(): x = x + lax.ppermute(x, 'band', [(d, d ^ step) for d in range(devices)])]
    ppermute x2, starting transfers between devices: 3.12 us -> 2.16 us  [sum_band(): x = x + lax.ppermute(x, 'band', [(d, d ^ step) for d in range(devices)])]
    ppermute x3, waiting for transfers between devices: 2.26 us -> 1.54 us  [share_band(): lax.ppermute(x, 'band', [(d, d ^ k) for d in range(devices)])]
  transfers between devices with their start and end apart: 35 -> 35, of which waited for: 21 -> 19; matrix products, arithmetic and copies ran while one was open for 0% -> 0% of each run, Pallas kernels for 12% -> 12%
where the time goes in v5:
time: 69.1 us; the launch traced here: 68.9 us
  starting transfers between devices  30.1 us (44%)
  waiting for transfers between devices  22.5 us (33%)
  Pallas kernels  15.5 us (22%)
  between operations  0.8 us (1%)
    ppermute x12, starting transfers between devices, share_base(): lax.ppermute(x, 'base', [(d, d ^ 2 * k) for d in range(devices)])  18.5 us
    pallas_call x13, Pallas kernels, call(): pl.pallas_call(kernel, out_shape=shapes, in_specs=in_specs, out_specs=[vm...  15.4 us
    ppermute x12, waiting for transfers between devices, share_base(): lax.ppermute(x, 'base', [(d, d ^ 2 * k) for d in range(devices)])  13.9 us
    ppermute x16, waiting for transfers between devices, share_base(): lax.ppermute(y, 'base', [(d, d ^ 1) for d in range(devices)])  3.73 us
    ppermute x3, starting transfers between devices, share_band(): lax.ppermute(x, 'band', [(d, d ^ k) for d in range(devices)])  3.53 us
    ppermute x2, waiting for transfers between devices, sum_band(): x = x + lax.ppermute(x, 'band', [(d, d ^ step) for d in range(devices)])  3.33 us
    ppermute x2, starting transfers between devices, sum_band(): return (x, lax.ppermute(x, 'band', [(d, d ^ step) for d in range(devices)]))  3.18 us
    ppermute x16, starting transfers between devices, share_base(): lax.ppermute(y, 'base', [(d, d ^ 1) for d in range(devices)])  2.74 us
  transfers between devices with their start and end apart: 35, of which 19 were waited for; matrix products, arithmetic and copies ran while one was open for 0% of the time, Pallas kernels for 12%

profile of v5, /device:TPU:0, one launch (start us, length us, event | category | flops | bytes accessed | tf_op | source)
XLA Modules:
  0.0 68.9 jit_solution(16884889501567453239)
XLA Ops:
  0.6 1.4 %shard_map.86 = (f32[136,128]{1,0:T(8,128)S(1)}, f32[136,128]{1,0:T(8,128)S(1)}) custom-call(s32[2,2]{1,0:T(2,128)} %pair_hbm.3, f32[8,32,64]{2,1,0:T(8,128)} %start_hbm.1, f32[1,64]{1,0:T(1,128)} %bitcast.6, s32[2,256]{1,0:T(2,128)} %flag_hbm.3), custom_call_target="tpu_custom_call" | custom-call | flops 20000000 | bytes 207120 | tf_op jit(solution)/shard_map/pallas_call | solution.py:596
  2.1 5.1 %collective-permute-start.2 = (f32[136,128]{1,0:T(8,128)S(1)}, f32[136,128]{1,0:T(8,128)S(1)}, u32[]{:S(2)}, u32[]{:S(2)}) collective-permute-start(f32[136,128]{1,0:T(8,128)S(1)} %get-tuple-element.29.refs_0_), channel_id=1, source_target_pairs={{0,6},{1,7},{2,4},{3,5},{4,2},{5,3},{6,0},{7,1},{8,14},{9,15},{10,... | collective-permute-start | bytes 208904 | tf_op jit(solution)/shard_map/ppermute | solution.py:610
  7.8 4.6 %shard_map.87 = (f32[48,8,16,128]{3,2,1,0:T(8,128)S(1)}, f32[256,128]{1,0:T(8,128)S(1)}, f32[256,128]{1,0:T(8,128)S(1)}, f32[256,128]{1,0:T(8,128)S(1)}, f32[8,256]{1,0:T(8,128)S(1)}) custom-call(s32[2,2]{1,0:T(2,128)} %pair_hbm.3, s32[1,64]{1,0:T(1,128)} %bitcast.9, s32[2,256]{1,0:T(2,128)} %flag_hbm.3, bf16[8,128,256]{2,1,0:T(8,128)(2,1)} %bitcast.7, ...), custom_call_target="tpu_custom_call" | custom-call | flops 2000000000 | bytes 4598032 | tf_op jit(solution)/shard_map/pallas_call | solution.py:596
  14.4 1.3 %shard_map.90 = (f32[128,128]{1,0:T(8,128)S(1)}, f32[192,128]{1,0:T(8,128)S(1)}) custom-call(f32[136,128]{1,0:T(8,128)S(1)} %get-tuple-element.29.refs_0_, f32[136,128]{1,0:T(8,128)S(1)} %collective-permute-done.refs_1_, f32[136,128]{1,0:T(8,128)S(1)} %shard_map.88.refs_2_, f32[136,128]{1,0:T(8,128)S(1)} %collective-permute-done.2.refs_3_, ...), custom_call_target="tpu_custom_call" | custom-call | flops 20000000 | bytes 3997696 | tf_op jit(solution)/shard_map/pallas_call | solution.py:596
  15.8 2.4 %collective-permute-start.8 = (f32[192,128]{1,0:T(8,128)S(1)}, f32[192,128]{1,0:T(8,128)S(1)}, u32[]{:S(2)}, u32[]{:S(2)}) collective-permute-start(f32[192,128]{1,0:T(8,128)S(1)} %get-tuple-element.34.refs_0_), channel_id=1, source_target_pairs={{0,4},{1,5},{2,6},{3,7},{4,0},{5,1},{6,2},{7,3},{8,12},{9,13},{10,... | collective-permute-start | bytes 294920 | tf_op jit(solution)/shard_map/ppermute | solution.py:610
  18.1 2.0 %collective-permute-start.7 = (f32[192,128]{1,0:T(8,128)S(1)}, f32[192,128]{1,0:T(8,128)S(1)}, u32[]{:S(2)}, u32[]{:S(2)}) collective-permute-start(f32[192,128]{1,0:T(8,128)S(1)} %get-tuple-element.34.refs_0_), channel_id=1, source_target_pairs={{0,2},{1,3},{2,0},{3,1},{4,6},{5,7},{6,4},{7,5},{8,10},{9,11},{10,... | collective-permute-start | bytes 294920 | tf_op jit(solution)/shard_map/ppermute | solution.py:610
  20.7 3.7 %collective-permute-done.8.refs_1_ = f32[192,128]{1,0:T(8,128)S(1)} collective-permute-done((f32[192,128]{1,0:T(8,128)S(1)}, f32[192,128]{1,0:T(8,128)S(1)}, u32[]{:S(2)}, u32[]{:S(2)}) %collective-permute-start.8) | collective-permute-done | bytes 98336 | tf_op jit(solution)/shard_map/ppermute | solution.py:610
  24.4 2.8 %collective-permute-done.9.refs_3_ = f32[192,128]{1,0:T(8,128)S(1)} collective-permute-done((f32[192,128]{1,0:T(8,128)S(1)}, f32[192,128]{1,0:T(8,128)S(1)}, u32[]{:S(2)}, u32[]{:S(2)}) %collective-permute-start.9) | collective-permute-done | bytes 98336 | tf_op jit(solution)/shard_map/ppermute | solution.py:610
  27.8 0.8 %collective-permute-done.13.refs_7_ = f32[192,128]{1,0:T(8,128)S(1)} collective-permute-done((f32[192,128]{1,0:T(8,128)S(1)}, f32[192,128]{1,0:T(8,128)S(1)}, u32[]{:S(2)}, u32[]{:S(2)}) %collective-permute-start.13) | collective-permute-done | bytes 98336 | tf_op jit(solution)/shard_map/ppermute | solution.py:621
  28.7 1.5 %shard_map.93 = (f32[128,256]{1,0:T(8,128)S(1)}, f32[192,128]{1,0:T(8,128)S(1)}) custom-call(f32[192,128]{1,0:T(8,128)S(1)} %get-tuple-element.34.refs_0_, f32[192,128]{1,0:T(8,128)S(1)} %get-tuple-element.39.refs_1_, f32[192,128]{1,0:T(8,128)S(1)} %get-tuple-element.40.refs_2_, f32[192,128]{1,0:T(8,128)S(1)} %collective-permute-done.9.refs_3_, ...), custom_call_target="tpu_custom_call" | custom-call | flops 20000000 | bytes 4849664 | tf_op jit(solution)/shard_map/pallas_call | solution.py:596
  30.2 3.2 %collective-permute-start.15 = (f32[192,128]{1,0:T(8,128)S(1)}, f32[192,128]{1,0:T(8,128)S(1)}, u32[]{:S(2)}, u32[]{:S(2)}) collective-permute-start(f32[192,128]{1,0:T(8,128)S(1)} %get-tuple-element.44.refs_0_), channel_id=1, source_target_pairs={{0,4},{1,5},{2,6},{3,7},{4,0},{5,1},{6,2},{7,3},{8,12},{9,13},{10,... | collective-permute-start | bytes 294920 | tf_op jit(solution)/shard_map/ppermute | solution.py:610
  33.7 1.6 %collective-permute-start.17 = (f32[144,128]{1,0:T(8,128)S(1)}, f32[144,128]{1,0:T(8,128)S(1)}, u32[]{:S(2)}, u32[]{:S(2)}) collective-permute-start(f32[144,128]{1,0:T(8,128)S(1)} %shard_map.95), channel_id=1, source_target_pairs={{0,8},{8,0},{16,24},{24,16},{1,9},{9,1},{17,25},{25,17},{2,10},{10... | collective-permute-start | bytes 221192 | tf_op jit(solution)/shard_map/ppermute | solution.py:636
  35.3 0.8 %collective-permute-start.16 = (f32[192,128]{1,0:T(8,128)S(1)}, f32[192,128]{1,0:T(8,128)S(1)}, u32[]{:S(2)}, u32[]{:S(2)}) collective-permute-start(f32[192,128]{1,0:T(8,128)S(1)} %get-tuple-element.44.refs_0_), channel_id=1, source_target_pairs={{0,6},{1,7},{2,4},{3,5},{4,2},{5,3},{6,0},{7,1},{8,14},{9,15},{10,... | collective-permute-start | bytes 294920 | tf_op jit(solution)/shard_map/ppermute | solution.py:610
  36.0 2.1 %collective-permute-done.17 = f32[144,128]{1,0:T(8,128)S(1)} collective-permute-done((f32[144,128]{1,0:T(8,128)S(1)}, f32[144,128]{1,0:T(8,128)S(1)}, u32[]{:S(2)}, u32[]{:S(2)}) %collective-permute-start.17) | collective-permute-done | bytes 73760 | tf_op jit(solution)/shard_map/ppermute | solution.py:636
  38.1 1.6 %collective-permute-start.18 = (f32[144,128]{1,0:T(8,128)S(1)}, f32[144,128]{1,0:T(8,128)S(1)}, u32[]{:S(2)}, u32[]{:S(2)}) collective-permute-start(f32[144,128]{1,0:T(8,128)S(1)} %add.6.one_ref), channel_id=1, source_target_pairs={{0,16},{8,24},{16,0},{24,8},{1,17},{9,25},{17,1},{25,9},{2,18},{10... | collective-permute-start | bytes 221192 | tf_op jit(solution)/shard_map/ppermute | solution.py:638
  39.7 3.5 %collective-permute-done.14.refs_1_ = f32[192,128]{1,0:T(8,128)S(1)} collective-permute-done((f32[192,128]{1,0:T(8,128)S(1)}, f32[192,128]{1,0:T(8,128)S(1)}, u32[]{:S(2)}, u32[]{:S(2)}) %collective-permute-start.14) | collective-permute-done | bytes 98336 | tf_op jit(solution)/shard_map/ppermute | solution.py:610
  43.2 1.0 %shard_map.96 = (f32[128,256]{1,0:T(8,128)S(1)}, f32[128,256]{1,0:T(8,128)S(1)}, f32[128,128]{1,0:T(8,128)S(1)}) custom-call(f32[144,128]{1,0:T(8,128)S(1)} %add.6.one_ref, f32[144,128]{1,0:T(8,128)S(1)} %collective-permute-done.18.two_ref, f32[128,256]{1,0:T(8,128)S(1)} %get-tuple-element.45.gains_ref, f32[256,128]{1,0:T(8,128)S(1)} %get-tuple-element.37.refs_12_.basis_ref), custom_call_target="tpu_custom_call" | custom-call | flops 20000000 | bytes 737280 | tf_op jit(solution)/shard_map/pallas_call | solution.py:596
  44.8 0.9 %collective-permute-done.22.refs_7_ = f32[192,128]{1,0:T(8,128)S(1)} collective-permute-done((f32[192,128]{1,0:T(8,128)S(1)}, f32[192,128]{1,0:T(8,128)S(1)}, u32[]{:S(2)}, u32[]{:S(2)}) %collective-permute-start.22) | collective-permute-done | bytes 98336 | tf_op jit(solution)/shard_map/ppermute | solution.py:621
  45.7 1.4 %shard_map.98 = (f32[128,256]{1,0:T(8,128)S(1)}, f32[192,128]{1,0:T(8,128)S(1)}) custom-call(f32[192,128]{1,0:T(8,128)S(1)} %get-tuple-element.44.refs_0_, f32[192,128]{1,0:T(8,128)S(1)} %collective-permute-done.14.refs_1_, f32[192,128]{1,0:T(8,128)S(1)} %shard_map.94.refs_2_, f32[192,128]{1,0:T(8,128)S(1)} %shard_map.97.refs_3_, ...), custom_call_target="tpu_custom_call" | custom-call | flops 20000000 | bytes 4849664 | tf_op jit(solution)/shard_map/pallas_call | solution.py:596
  47.2 1.9 %collective-permute-start.24 = (f32[192,128]{1,0:T(8,128)S(1)}, f32[192,128]{1,0:T(8,128)S(1)}, u32[]{:S(2)}, u32[]{:S(2)}) collective-permute-start(f32[192,128]{1,0:T(8,128)S(1)} %get-tuple-element.47.refs_0_), channel_id=1, source_target_pairs={{0,4},{1,5},{2,6},{3,7},{4,0},{5,1},{6,2},{7,3},{8,12},{9,13},{10,... | collective-permute-start | bytes 294920 | tf_op jit(solution)/shard_map/ppermute | solution.py:610
  49.9 1.0 %collective-permute-start.25 = (f32[192,128]{1,0:T(8,128)S(1)}, f32[192,128]{1,0:T(8,128)S(1)}, u32[]{:S(2)}, u32[]{:S(2)}) collective-permute-start(f32[192,128]{1,0:T(8,128)S(1)} %get-tuple-element.47.refs_0_), channel_id=1, source_target_pairs={{0,6},{1,7},{2,4},{3,5},{4,2},{5,3},{6,0},{7,1},{8,14},{9,15},{10,... | collective-permute-start | bytes 294920 | tf_op jit(solution)/shard_map/ppermute | solution.py:610
  50.9 1.4 %collective-permute-start.23 = (f32[192,128]{1,0:T(8,128)S(1)}, f32[192,128]{1,0:T(8,128)S(1)}, u32[]{:S(2)}, u32[]{:S(2)}) collective-permute-start(f32[192,128]{1,0:T(8,128)S(1)} %get-tuple-element.47.refs_0_), channel_id=1, source_target_pairs={{0,2},{1,3},{2,0},{3,1},{4,6},{5,7},{6,4},{7,5},{8,10},{9,11},{10,... | collective-permute-start | bytes 294920 | tf_op jit(solution)/shard_map/ppermute | solution.py:610
  52.4 1.3 %collective-permute-done.26 = f32[128,128]{1,0:T(8,128)S(1)} collective-permute-done((f32[128,128]{1,0:T(8,128)S(1)}, f32[128,128]{1,0:T(8,128)S(1)}, u32[]{:S(2)}, u32[]{:S(2)}) %collective-permute-start.26) | collective-permute-done | bytes 65568 | tf_op jit(solution)/shard_map/ppermute | solution.py:636
  53.6 1.6 %collective-permute-start.27 = (f32[128,128]{1,0:T(8,128)S(1)}, f32[128,128]{1,0:T(8,128)S(1)}, u32[]{:S(2)}, u32[]{:S(2)}) collective-permute-start(f32[128,128]{1,0:T(8,128)S(1)} %add.7.one_ref), channel_id=1, source_target_pairs={{0,16},{8,24},{16,0},{24,8},{1,17},{9,25},{17,1},{25,9},{2,18},{10... | collective-permute-start | bytes 196616 | tf_op jit(solution)/shard_map/ppermute | solution.py:638
  55.2 1.7 %collective-permute-done.24.refs_0_ = f32[192,128]{1,0:T(8,128)S(1)} collective-permute-done((f32[192,128]{1,0:T(8,128)S(1)}, f32[192,128]{1,0:T(8,128)S(1)}, u32[]{:S(2)}, u32[]{:S(2)}) %collective-permute-start.24) | collective-permute-done | bytes 98336 | tf_op jit(solution)/shard_map/ppermute | solution.py:610
  56.9 2.2 %collective-permute-done.23.refs_1_ = f32[192,128]{1,0:T(8,128)S(1)} collective-permute-done((f32[192,128]{1,0:T(8,128)S(1)}, f32[192,128]{1,0:T(8,128)S(1)}, u32[]{:S(2)}, u32[]{:S(2)}) %collective-permute-start.23) | collective-permute-done | bytes 98336 | tf_op jit(solution)/shard_map/ppermute | solution.py:610
  60.5 0.8 %collective-permute-done.31.refs_7_ = f32[192,128]{1,0:T(8,128)S(1)} collective-permute-done((f32[192,128]{1,0:T(8,128)S(1)}, f32[192,128]{1,0:T(8,128)S(1)}, u32[]{:S(2)}, u32[]{:S(2)}) %collective-permute-start.31) | collective-permute-done | bytes 98336 | tf_op jit(solution)/shard_map/ppermute | solution.py:621
  61.2 0.8 %shard_map.103 = (f32[128,128]{1,0:T(8,128)S(1)}, f32[40,128]{1,0:T(8,128)S(1)}) custom-call(f32[192,128]{1,0:T(8,128)S(1)} %get-tuple-element.47.refs_0_, f32[192,128]{1,0:T(8,128)S(1)} %collective-permute-done.23.refs_1_, f32[192,128]{1,0:T(8,128)S(1)} %shard_map.99.refs_2_, f32[192,128]{1,0:T(8,128)S(1)} %shard_map.102.refs_3_, ...), custom_call_target="tpu_custom_call" | custom-call | flops 20000000 | bytes 1703936 | tf_op jit(solution)/shard_map/pallas_call | solution.py:596
  62.0 1.8 %collective-permute-start.34 = (f32[40,128]{1,0:T(8,128)S(1)}, f32[40,128]{1,0:T(8,128)S(1)}, u32[]{:S(2)}, u32[]{:S(2)}) collective-permute-start(f32[40,128]{1,0:T(8,128)S(1)} %get-tuple-element.55.refs_0_), channel_id=1, source_target_pairs={{0,24},{8,16},{16,8},{24,0},{1,25},{9,17},{17,9},{25,1},{2,26},{10... | collective-permute-start | bytes 61448 | tf_op jit(solution)/shard_map/ppermute | solution.py:628
  64.3 1.3 %collective-permute-start.32 = (f32[40,128]{1,0:T(8,128)S(1)}, f32[40,128]{1,0:T(8,128)S(1)}, u32[]{:S(2)}, u32[]{:S(2)}) collective-permute-start(f32[40,128]{1,0:T(8,128)S(1)} %get-tuple-element.55.refs_0_), channel_id=1, source_target_pairs={{0,8},{8,0},{16,24},{24,16},{1,9},{9,1},{17,25},{25,17},{2,10},{10... | collective-permute-start | bytes 61448 | tf_op jit(solution)/shard_map/ppermute | solution.py:628
  65.5 1.0 %shard_map.104 = f32[8,32,64]{2,1,0:T(8,128)} custom-call(f32[128,128]{1,0:T(8,128)S(1)} %get-tuple-element.54.gains_ref), custom_call_target="tpu_custom_call" | custom-call | flops 20000000 | bytes 131072 | tf_op jit(solution)/shard_map/pallas_call | solution.py:596
  68.0 0.9 %shard_map.105 = f32[9,8,64]{2,1,0:T(8,128)} custom-call(f32[40,128]{1,0:T(8,128)S(1)} %get-tuple-element.55.refs_0_, f32[40,128]{1,0:T(8,128)S(1)} %collective-permute-done.32.refs_1_, f32[40,128]{1,0:T(8,128)S(1)} %collective-permute-done.33.refs_2_, f32[40,128]{1,0:T(8,128)S(1)} %collective-permute-done.34.refs_3_, ...), custom_call_target="tpu_custom_call" | custom-call | flops 20000000 | bytes 165888 | tf_op jit(solution)/shard_map/pallas_call | solution.py:596
  (60 shorter events, 9.0 us)
Async XLA Ops:
  2.1 10.5 %collective-permute-start.2 = (f32[136,128]{1,0:T(8,128)S(1)}, f32[136,128]{1,0:T(8,128)S(1)}, u32[]{:S(2)}, u32[]{:S(2)}) collective-permute-start(f32[136,128]{1,0:T(8,128)S(1)} %get-tuple-element.29.refs_0_), channel_id=1, source_target_pairs={{0,6},{1,7},{2,4},{3,5},{4,2},{5,3},{6,0},{7,1},{8,14},{9,15},{10,... | collective-permute-start | bytes 208904 | tf_op jit(solution)/shard_map/ppermute | solution.py:610
  7.2 5.9 %collective-permute-start.1 = (f32[136,128]{1,0:T(8,128)S(1)}, f32[136,128]{1,0:T(8,128)S(1)}, u32[]{:S(2)}, u32[]{:S(2)}) collective-permute-start(f32[136,128]{1,0:T(8,128)S(1)} %get-tuple-element.29.refs_0_), channel_id=1, source_target_pairs={{0,4},{1,5},{2,6},{3,7},{4,0},{5,1},{6,2},{7,3},{8,12},{9,13},{10,... | collective-permute-start | bytes 208904 | tf_op jit(solution)/shard_map/ppermute | solution.py:610
  7.2 5.8 %collective-permute-start = (f32[136,128]{1,0:T(8,128)S(1)}, f32[136,128]{1,0:T(8,128)S(1)}, u32[]{:S(2)}, u32[]{:S(2)}) collective-permute-start(f32[136,128]{1,0:T(8,128)S(1)} %get-tuple-element.29.refs_0_), channel_id=1, source_target_pairs={{0,2},{1,3},{2,0},{3,1},{4,6},{5,7},{6,4},{7,5},{8,10},{9,11},{10,... | collective-permute-start | bytes 208904 | tf_op jit(solution)/shard_map/ppermute | solution.py:610
  12.4 1.3 %collective-permute-start.3 = (f32[136,128]{1,0:T(8,128)S(1)}, f32[136,128]{1,0:T(8,128)S(1)}, u32[]{:S(2)}, u32[]{:S(2)}) collective-permute-start(f32[136,128]{1,0:T(8,128)S(1)} %shard_map.89), channel_id=1, source_target_pairs={{0,1},{1,0},{2,3},{3,2},{4,5},{5,4},{6,7},{7,6},{8,9},{9,8},{10,11... | collective-permute-start | bytes 208904 | tf_op jit(solution)/shard_map/ppermute | solution.py:621
  12.5 1.4 %collective-permute-start.6 = (f32[136,128]{1,0:T(8,128)S(1)}, f32[136,128]{1,0:T(8,128)S(1)}, u32[]{:S(2)}, u32[]{:S(2)}) collective-permute-start(f32[136,128]{1,0:T(8,128)S(1)} %collective-permute-done.2.refs_3_), channel_id=1, source_target_pairs={{0,1},{1,0},{2,3},{3,2},{4,5},{5,4},{6,7},{7,6},{8,9},{9,8},{10,11... | collective-permute-start | bytes 208904 | tf_op jit(solution)/shard_map/ppermute | solution.py:621
  13.1 1.3 %collective-permute-start.5 = (f32[136,128]{1,0:T(8,128)S(1)}, f32[136,128]{1,0:T(8,128)S(1)}, u32[]{:S(2)}, u32[]{:S(2)}) collective-permute-start(f32[136,128]{1,0:T(8,128)S(1)} %shard_map.88.refs_2_), channel_id=1, source_target_pairs={{0,1},{1,0},{2,3},{3,2},{4,5},{5,4},{6,7},{7,6},{8,9},{9,8},{10,11... | collective-permute-start | bytes 208904 | tf_op jit(solution)/shard_map/ppermute | solution.py:621
  15.8 8.7 %collective-permute-start.8 = (f32[192,128]{1,0:T(8,128)S(1)}, f32[192,128]{1,0:T(8,128)S(1)}, u32[]{:S(2)}, u32[]{:S(2)}) collective-permute-start(f32[192,128]{1,0:T(8,128)S(1)} %get-tuple-element.34.refs_0_), channel_id=1, source_target_pairs={{0,4},{1,5},{2,6},{3,7},{4,0},{5,1},{6,2},{7,3},{8,12},{9,13},{10,... | collective-permute-start | bytes 294920 | tf_op jit(solution)/shard_map/ppermute | solution.py:610
  18.1 6.3 %collective-permute-start.7 = (f32[192,128]{1,0:T(8,128)S(1)}, f32[192,128]{1,0:T(8,128)S(1)}, u32[]{:S(2)}, u32[]{:S(2)}) collective-permute-start(f32[192,128]{1,0:T(8,128)S(1)} %get-tuple-element.34.refs_0_), channel_id=1, source_target_pairs={{0,2},{1,3},{2,0},{3,1},{4,6},{5,7},{6,4},{7,5},{8,10},{9,11},{10,... | collective-permute-start | bytes 294920 | tf_op jit(solution)/shard_map/ppermute | solution.py:610
  20.1 7.1 %collective-permute-start.9 = (f32[192,128]{1,0:T(8,128)S(1)}, f32[192,128]{1,0:T(8,128)S(1)}, u32[]{:S(2)}, u32[]{:S(2)}) collective-permute-start(f32[192,128]{1,0:T(8,128)S(1)} %get-tuple-element.34.refs_0_), channel_id=1, source_target_pairs={{0,6},{1,7},{2,4},{3,5},{4,2},{5,3},{6,0},{7,1},{8,14},{9,15},{10,... | collective-permute-start | bytes 294920 | tf_op jit(solution)/shard_map/ppermute | solution.py:610
  20.2 7.6 %collective-permute-start.10 = (f32[192,128]{1,0:T(8,128)S(1)}, f32[192,128]{1,0:T(8,128)S(1)}, u32[]{:S(2)}, u32[]{:S(2)}) collective-permute-start(f32[192,128]{1,0:T(8,128)S(1)} %get-tuple-element.34.refs_0_), channel_id=1, source_target_pairs={{0,1},{1,0},{2,3},{3,2},{4,5},{5,4},{6,7},{7,6},{8,9},{9,8},{10,11... | collective-permute-start | bytes 294920 | tf_op jit(solution)/shard_map/ppermute | solution.py:621
  24.4 4.1 %collective-permute-start.11 = (f32[192,128]{1,0:T(8,128)S(1)}, f32[192,128]{1,0:T(8,128)S(1)}, u32[]{:S(2)}, u32[]{:S(2)}) collective-permute-start(f32[192,128]{1,0:T(8,128)S(1)} %get-tuple-element.39.refs_1_), channel_id=1, source_target_pairs={{0,1},{1,0},{2,3},{3,2},{4,5},{5,4},{6,7},{7,6},{8,9},{9,8},{10,11... | collective-permute-start | bytes 294920 | tf_op jit(solution)/shard_map/ppermute | solution.py:621
  27.3 1.5 %collective-permute-start.12 = (f32[192,128]{1,0:T(8,128)S(1)}, f32[192,128]{1,0:T(8,128)S(1)}, u32[]{:S(2)}, u32[]{:S(2)}) collective-permute-start(f32[192,128]{1,0:T(8,128)S(1)} %get-tuple-element.40.refs_2_), channel_id=1, source_target_pairs={{0,1},{1,0},{2,3},{3,2},{4,5},{5,4},{6,7},{7,6},{8,9},{9,8},{10,11... | collective-permute-start | bytes 294920 | tf_op jit(solution)/shard_map/ppermute | solution.py:621
  30.2 9.6 %collective-permute-start.15 = (f32[192,128]{1,0:T(8,128)S(1)}, f32[192,128]{1,0:T(8,128)S(1)}, u32[]{:S(2)}, u32[]{:S(2)}) collective-permute-start(f32[192,128]{1,0:T(8,128)S(1)} %get-tuple-element.44.refs_0_), channel_id=1, source_target_pairs={{0,4},{1,5},{2,6},{3,7},{4,0},{5,1},{6,2},{7,3},{8,12},{9,13},{10,... | collective-permute-start | bytes 294920 | tf_op jit(solution)/shard_map/ppermute | solution.py:610
  33.7 4.4 %collective-permute-start.17 = (f32[144,128]{1,0:T(8,128)S(1)}, f32[144,128]{1,0:T(8,128)S(1)}, u32[]{:S(2)}, u32[]{:S(2)}) collective-permute-start(f32[144,128]{1,0:T(8,128)S(1)} %shard_map.95), channel_id=1, source_target_pairs={{0,8},{8,0},{16,24},{24,16},{1,9},{9,1},{17,25},{25,17},{2,10},{10... | collective-permute-start | bytes 221192 | tf_op jit(solution)/shard_map/ppermute | solution.py:636
  35.3 9.5 %collective-permute-start.19 = (f32[192,128]{1,0:T(8,128)S(1)}, f32[192,128]{1,0:T(8,128)S(1)}, u32[]{:S(2)}, u32[]{:S(2)}) collective-permute-start(f32[192,128]{1,0:T(8,128)S(1)} %get-tuple-element.44.refs_0_), channel_id=1, source_target_pairs={{0,1},{1,0},{2,3},{3,2},{4,5},{5,4},{6,7},{7,6},{8,9},{9,8},{10,11... | collective-permute-start | bytes 294920 | tf_op jit(solution)/shard_map/ppermute | solution.py:621
  35.3 8.9 %collective-permute-start.16 = (f32[192,128]{1,0:T(8,128)S(1)}, f32[192,128]{1,0:T(8,128)S(1)}, u32[]{:S(2)}, u32[]{:S(2)}) collective-permute-start(f32[192,128]{1,0:T(8,128)S(1)} %get-tuple-element.44.refs_0_), channel_id=1, source_target_pairs={{0,6},{1,7},{2,4},{3,5},{4,2},{5,3},{6,0},{7,1},{8,14},{9,15},{10,... | collective-permute-start | bytes 294920 | tf_op jit(solution)/shard_map/ppermute | solution.py:610
  36.0 7.2 %collective-permute-start.14 = (f32[192,128]{1,0:T(8,128)S(1)}, f32[192,128]{1,0:T(8,128)S(1)}, u32[]{:S(2)}, u32[]{:S(2)}) collective-permute-start(f32[192,128]{1,0:T(8,128)S(1)} %get-tuple-element.44.refs_0_), channel_id=1, source_target_pairs={{0,2},{1,3},{2,0},{3,1},{4,6},{5,7},{6,4},{7,5},{8,10},{9,11},{10,... | collective-permute-start | bytes 294920 | tf_op jit(solution)/shard_map/ppermute | solution.py:610
  38.1 5.1 %collective-permute-start.18 = (f32[144,128]{1,0:T(8,128)S(1)}, f32[144,128]{1,0:T(8,128)S(1)}, u32[]{:S(2)}, u32[]{:S(2)}) collective-permute-start(f32[144,128]{1,0:T(8,128)S(1)} %add.6.one_ref), channel_id=1, source_target_pairs={{0,16},{8,24},{16,0},{24,8},{1,17},{9,25},{17,1},{25,9},{2,18},{10... | collective-permute-start | bytes 221192 | tf_op jit(solution)/shard_map/ppermute | solution.py:638
  39.7 5.1 %collective-permute-start.21 = (f32[192,128]{1,0:T(8,128)S(1)}, f32[192,128]{1,0:T(8,128)S(1)}, u32[]{:S(2)}, u32[]{:S(2)}) collective-permute-start(f32[192,128]{1,0:T(8,128)S(1)} %shard_map.94.refs_2_), channel_id=1, source_target_pairs={{0,1},{1,0},{2,3},{3,2},{4,5},{5,4},{6,7},{7,6},{8,9},{9,8},{10,11... | collective-permute-start | bytes 294920 | tf_op jit(solution)/shard_map/ppermute | solution.py:621
  43.2 1.6 %collective-permute-start.20 = (f32[192,128]{1,0:T(8,128)S(1)}, f32[192,128]{1,0:T(8,128)S(1)}, u32[]{:S(2)}, u32[]{:S(2)}) collective-permute-start(f32[192,128]{1,0:T(8,128)S(1)} %collective-permute-done.14.refs_1_), channel_id=1, source_target_pairs={{0,1},{1,0},{2,3},{3,2},{4,5},{5,4},{6,7},{7,6},{8,9},{9,8},{10,11... | collective-permute-start | bytes 294920 | tf_op jit(solution)/shard_map/ppermute | solution.py:621
  44.2 1.5 %collective-permute-start.22 = (f32[192,128]{1,0:T(8,128)S(1)}, f32[192,128]{1,0:T(8,128)S(1)}, u32[]{:S(2)}, u32[]{:S(2)}) collective-permute-start(f32[192,128]{1,0:T(8,128)S(1)} %shard_map.97.refs_3_), channel_id=1, source_target_pairs={{0,1},{1,0},{2,3},{3,2},{4,5},{5,4},{6,7},{7,6},{8,9},{9,8},{10,11... | collective-permute-start | bytes 294920 | tf_op jit(solution)/shard_map/ppermute | solution.py:621
  47.2 9.7 %collective-permute-start.24 = (f32[192,128]{1,0:T(8,128)S(1)}, f32[192,128]{1,0:T(8,128)S(1)}, u32[]{:S(2)}, u32[]{:S(2)}) collective-permute-start(f32[192,128]{1,0:T(8,128)S(1)} %get-tuple-element.47.refs_0_), channel_id=1, source_target_pairs={{0,4},{1,5},{2,6},{3,7},{4,0},{5,1},{6,2},{7,3},{8,12},{9,13},{10,... | collective-permute-start | bytes 294920 | tf_op jit(solution)/shard_map/ppermute | solution.py:610
  49.3 4.3 %collective-permute-start.26 = (f32[128,128]{1,0:T(8,128)S(1)}, f32[128,128]{1,0:T(8,128)S(1)}, u32[]{:S(2)}, u32[]{:S(2)}) collective-permute-start(f32[128,128]{1,0:T(8,128)S(1)} %shard_map.100), channel_id=1, source_target_pairs={{0,8},{8,0},{16,24},{24,16},{1,9},{9,1},{17,25},{25,17},{2,10},{10... | collective-permute-start | bytes 196616 | tf_op jit(solution)/shard_map/ppermute | solution.py:636
  49.9 10.4 %collective-permute-start.28 = (f32[192,128]{1,0:T(8,128)S(1)}, f32[192,128]{1,0:T(8,128)S(1)}, u32[]{:S(2)}, u32[]{:S(2)}) collective-permute-start(f32[192,128]{1,0:T(8,128)S(1)} %get-tuple-element.47.refs_0_), channel_id=1, source_target_pairs={{0,1},{1,0},{2,3},{3,2},{4,5},{5,4},{6,7},{7,6},{8,9},{9,8},{10,11... | collective-permute-start | bytes 294920 | tf_op jit(solution)/shard_map/ppermute | solution.py:621
  49.9 9.8 %collective-permute-start.25 = (f32[192,128]{1,0:T(8,128)S(1)}, f32[192,128]{1,0:T(8,128)S(1)}, u32[]{:S(2)}, u32[]{:S(2)}) collective-permute-start(f32[192,128]{1,0:T(8,128)S(1)} %get-tuple-element.47.refs_0_), channel_id=1, source_target_pairs={{0,6},{1,7},{2,4},{3,5},{4,2},{5,3},{6,0},{7,1},{8,14},{9,15},{10,... | collective-permute-start | bytes 294920 | tf_op jit(solution)/shard_map/ppermute | solution.py:610
  50.9 8.2 %collective-permute-start.23 = (f32[192,128]{1,0:T(8,128)S(1)}, f32[192,128]{1,0:T(8,128)S(1)}, u32[]{:S(2)}, u32[]{:S(2)}) collective-permute-start(f32[192,128]{1,0:T(8,128)S(1)} %get-tuple-element.47.refs_0_), channel_id=1, source_target_pairs={{0,2},{1,3},{2,0},{3,1},{4,6},{5,7},{6,4},{7,5},{8,10},{9,11},{10,... | collective-permute-start | bytes 294920 | tf_op jit(solution)/shard_map/ppermute | solution.py:610
  53.6 5.6 %collective-permute-start.27 = (f32[128,128]{1,0:T(8,128)S(1)}, f32[128,128]{1,0:T(8,128)S(1)}, u32[]{:S(2)}, u32[]{:S(2)}) collective-permute-start(f32[128,128]{1,0:T(8,128)S(1)} %add.7.one_ref), channel_id=1, source_target_pairs={{0,16},{8,24},{16,0},{24,8},{1,17},{9,25},{17,1},{25,9},{2,18},{10... | collective-permute-start | bytes 196616 | tf_op jit(solution)/shard_map/ppermute | solution.py:638
  56.9 3.4 %collective-permute-start.30 = (f32[192,128]{1,0:T(8,128)S(1)}, f32[192,128]{1,0:T(8,128)S(1)}, u32[]{:S(2)}, u32[]{:S(2)}) collective-permute-start(f32[192,128]{1,0:T(8,128)S(1)} %shard_map.99.refs_2_), channel_id=1, source_target_pairs={{0,1},{1,0},{2,3},{3,2},{4,5},{5,4},{6,7},{7,6},{8,9},{9,8},{10,11... | collective-permute-start | bytes 294920 | tf_op jit(solution)/shard_map/ppermute | solution.py:621
  59.7 1.5 %collective-permute-start.31 = (f32[192,128]{1,0:T(8,128)S(1)}, f32[192,128]{1,0:T(8,128)S(1)}, u32[]{:S(2)}, u32[]{:S(2)}) collective-permute-start(f32[192,128]{1,0:T(8,128)S(1)} %shard_map.102.refs_3_), channel_id=1, source_target_pairs={{0,1},{1,0},{2,3},{3,2},{4,5},{5,4},{6,7},{7,6},{8,9},{9,8},{10,11... | collective-permute-start | bytes 294920 | tf_op jit(solution)/shard_map/ppermute | solution.py:621
  62.0 4.8 %collective-permute-start.34 = (f32[40,128]{1,0:T(8,128)S(1)}, f32[40,128]{1,0:T(8,128)S(1)}, u32[]{:S(2)}, u32[]{:S(2)}) collective-permute-start(f32[40,128]{1,0:T(8,128)S(1)} %get-tuple-element.55.refs_0_), channel_id=1, source_target_pairs={{0,24},{8,16},{16,8},{24,0},{1,25},{9,17},{17,9},{25,1},{2,26},{10... | collective-permute-start | bytes 61448 | tf_op jit(solution)/shard_map/ppermute | solution.py:628
  63.8 3.8 %collective-permute-start.33 = (f32[40,128]{1,0:T(8,128)S(1)}, f32[40,128]{1,0:T(8,128)S(1)}, u32[]{:S(2)}, u32[]{:S(2)}) collective-permute-start(f32[40,128]{1,0:T(8,128)S(1)} %get-tuple-element.55.refs_0_), channel_id=1, source_target_pairs={{0,16},{8,24},{16,0},{24,8},{1,17},{9,25},{17,1},{25,9},{2,18},{10... | collective-permute-start | bytes 61448 | tf_op jit(solution)/shard_map/ppermute | solution.py:628
  64.3 3.8 %collective-permute-start.32 = (f32[40,128]{1,0:T(8,128)S(1)}, f32[40,128]{1,0:T(8,128)S(1)}, u32[]{:S(2)}, u32[]{:S(2)}) collective-permute-start(f32[40,128]{1,0:T(8,128)S(1)} %get-tuple-element.55.refs_0_), channel_id=1, source_target_pairs={{0,8},{8,0},{16,24},{24,16},{1,9},{9,1},{17,25},{25,17},{2,10},{10... | collective-permute-start | bytes 61448 | tf_op jit(solution)/shard_map/ppermute | solution.py:628
  (3 other events, 3.9 us)

commit v6 on v4

--- a/solution.py
+++ b/solution.py
@@ -201,12 +201,16 @@
     copies[0].wait()
     place = (iota((BLOCK, owned), 0) == iota((BLOCK, owned), 1) % BLOCK).astype(BF16)
     here = iota((LANES, owned), 0) // intervals == iota((LANES, owned), 1) // BLOCK
+    parts = []
     for m in range(8):
-        plane = start_ref[m]
-        plane = jnp.where(here, jnp.concatenate([plane] * (LANES // intervals), 0), 0.0)
-        high = plane.astype(BF16)
-        low = (plane - high.astype(F32)).astype(BF16)
-        out_ref[m * BLOCK : (m + 1) * BLOCK, :] = nt(place, high) + nt(place, low)
+        plane = jnp.concatenate([start_ref[m]] * (LANES // intervals), 0)
+        parts.append(jnp.where(here, plane, 0.0))
+    parts = jnp.concatenate(parts, 0)
+    high = parts.astype(BF16)
+    low = (parts - high.astype(F32)).astype(BF16)
+    turned = nt(place, high) + nt(place, low)
+    for m in range(8):
+        out_ref[m * BLOCK : (m + 1) * BLOCK, :] = turned[:, m * LANES : (m + 1) * LANES]
 
 
 def prepare_kernel(
@@ -266,27 +270,24 @@
     weight = jnp.concatenate([jnp.broadcast_to(w, (channels, cells)) for w in rows], 0)
     half = cells // 2
 
-    def put(at, product):
-        beside = jnp.concatenate([product[:half], product[half:]], 1)
-        prod_ref[at] = pick(beside, fold).reshape(prod_ref.shape[1:])
+    def put(at, products):
+        beside = [jnp.concatenate([x[:half], x[half:]], 1) for x in products]
+        count = len(products)
+        shape = (count,) + prod_ref.shape[1:]
+        prod_ref[at : at + count] = pick(jnp.concatenate(beside, 0), fold).reshape(shape)
 
     copies[0].wait()
     for m in range(planes):
         masked = (model_ref[m].astype(F32) * weight).astype(BF16)
         mt_ref[m] = nt(ident, masked)
-    for x in range(4):
-        put(32 + x, mt_ref[x] * mt_ref[x] + mt_ref[4 + x] * mt_ref[4 + x])
-    for n, (x, y) in enumerate(CROSS):
-        x_re, x_im, y_re, y_im = mt_ref[x], mt_ref[4 + x], mt_ref[y], mt_ref[4 + y]
-        put(36 + n, x_re * y_re + x_im * y_im)
-        put(42 + n, x_im * y_re - x_re * y_im)
+    put(32, [mt_ref[x] * mt_ref[x] + mt_ref[4 + x] * mt_ref[4 + x] for x in range(4)])
+    put(36, [mt_ref[x] * mt_ref[y] + mt_ref[4 + x] * mt_ref[4 + y] for x, y in CROSS])
+    put(42, [mt_ref[4 + x] * mt_ref[y] - mt_ref[x] * mt_ref[4 + y] for x, y in CROSS])
     copies[1].wait()
     for x in range(4):
         v_re, v_im = nt(ident, vis_ref[x]), nt(ident, vis_ref[4 + x])
-        for y in range(4):
-            m_re, m_im = mt_ref[y], mt_ref[4 + y]
-            put(4 * x + y, v_re * m_re + v_im * m_im)
-            put(16 + 4 * x + y, v_im * m_re - v_re * m_im)
+        put(4 * x, [v_re * mt_ref[y] + v_im * mt_ref[4 + y] for y in range(4)])
+        put(16 + 4 * x, [v_im * mt_ref[y] - v_re * mt_ref[4 + y] for y in range(4)])
 
 
 def tie_kernel(*refs):

time: 67.8 us -> 67.9 us (level)
  no operation moved by 1% of the time
where the time goes in v6:
time: 67.9 us; the launch traced here: 67.7 us
  starting transfers between devices  31.2 us (46%)
  waiting for transfers between devices  20.2 us (30%)
  Pallas kernels  15.5 us (23%)
  between operations  0.78 us (1%)
    ppermute x12, starting transfers between devices, share_base(): lax.ppermute(x, 'base', [(d, d ^ 2 * k) for d in range(devices)])  18.7 us
    pallas_call x13, Pallas kernels, call(): pl.pallas_call(kernel, out_shape=shapes, in_specs=in_specs, out_specs=[vm...  15.5 us
    ppermute x12, waiting for transfers between devices, share_base(): lax.ppermute(x, 'base', [(d, d ^ 2 * k) for d in range(devices)])  7.15 us
    ppermute x2, waiting for transfers between devices, sum_band(): return (x, lax.ppermute(x, 'band', [(d, d ^ step) for d in range(devices)]))  5.55 us
    ppermute x16, waiting for transfers between devices, share_base(): lax.ppermute(y, 'base', [(d, d ^ 1) for d in range(devices)])  4.08 us
    ppermute x3, starting transfers between devices, share_band(): lax.ppermute(x, 'band', [(d, d ^ k) for d in range(devices)])  3.53 us
    ppermute x2, starting transfers between devices, sum_band(): return (x, lax.ppermute(x, 'band', [(d, d ^ step) for d in range(devices)]))  3.18 us
    ppermute x2, starting transfers between devices, sum_band(): x = x + lax.ppermute(x, 'band', [(d, d ^ step) for d in range(devices)])  3.12 us
  transfers between devices with their start and end apart: 35, of which 21 were waited for; matrix products, arithmetic and copies ran while one was open for 0% of the time, Pallas kernels for 12%

profile of v6, /device:TPU:0, one launch (start us, length us, event | category | flops | bytes accessed | tf_op | source)
XLA Modules:
  0.0 67.7 jit_solution(96544494352408745)
XLA Ops:
  0.6 1.3 %shard_map.86.refs_0_ = f32[136,128]{1,0:T(8,128)S(1)} custom-call(s32[2,2]{1,0:T(2,128)} %pair_hbm.3, f32[8,32,64]{2,1,0:T(8,128)} %start_hbm.1, f32[1,64]{1,0:T(1,128)} %bitcast.6, s32[2,256]{1,0:T(2,128)} %flag_hbm.3), custom_call_target="tpu_custom_call" | custom-call | flops 20000000 | bytes 137488 | tf_op jit(solution)/shard_map/pallas_call | solution.py:596
  2.5 4.7 %collective-permute-start.2 = (f32[136,128]{1,0:T(8,128)S(1)}, f32[136,128]{1,0:T(8,128)S(1)}, u32[]{:S(2)}, u32[]{:S(2)}) collective-permute-start(f32[136,128]{1,0:T(8,128)S(1)} %shard_map.86.refs_0_), channel_id=1, source_target_pairs={{0,6},{1,7},{2,4},{3,5},{4,2},{5,3},{6,0},{7,1},{8,14},{9,15},{10,... | collective-permute-start | bytes 208904 | tf_op jit(solution)/shard_map/ppermute | solution.py:610
  7.8 4.8 %shard_map.87 = (f32[48,8,16,128]{3,2,1,0:T(8,128)S(1)}, f32[256,128]{1,0:T(8,128)S(1)}, f32[256,128]{1,0:T(8,128)S(1)}, f32[256,128]{1,0:T(8,128)S(1)}, f32[8,256]{1,0:T(8,128)S(1)}) custom-call(s32[2,2]{1,0:T(2,128)} %pair_hbm.3, s32[1,64]{1,0:T(1,128)} %bitcast.9, s32[2,256]{1,0:T(2,128)} %flag_hbm.3, bf16[8,128,256]{2,1,0:T(8,128)(2,1)} %bitcast.7, ...), custom_call_target="tpu_custom_call" | custom-call | flops 2000000000 | bytes 4598032 | tf_op jit(solution)/shard_map/pallas_call | solution.py:596
  14.1 0.7 %collective-permute-done.5.refs_6_ = f32[136,128]{1,0:T(8,128)S(1)} collective-permute-done((f32[136,128]{1,0:T(8,128)S(1)}, f32[136,128]{1,0:T(8,128)S(1)}, u32[]{:S(2)}, u32[]{:S(2)}) %collective-permute-start.5) | collective-permute-done | bytes 69664 | tf_op jit(solution)/shard_map/ppermute | solution.py:618
  14.8 1.3 %shard_map.89 = (f32[128,128]{1,0:T(8,128)S(1)}, f32[192,128]{1,0:T(8,128)S(1)}) custom-call(f32[136,128]{1,0:T(8,128)S(1)} %shard_map.86.refs_0_, f32[136,128]{1,0:T(8,128)S(1)} %collective-permute-done.refs_1_, f32[136,128]{1,0:T(8,128)S(1)} %shard_map.88.refs_2_, f32[136,128]{1,0:T(8,128)S(1)} %collective-permute-done.2.refs_3_, ...), custom_call_target="tpu_custom_call" | custom-call | flops 20000000 | bytes 3997696 | tf_op jit(solution)/shard_map/pallas_call | solution.py:596
  16.1 2.0 %collective-permute-start.8 = (f32[192,128]{1,0:T(8,128)S(1)}, f32[192,128]{1,0:T(8,128)S(1)}, u32[]{:S(2)}, u32[]{:S(2)}) collective-permute-start(f32[192,128]{1,0:T(8,128)S(1)} %get-tuple-element.34.refs_0_), channel_id=1, source_target_pairs={{0,4},{1,5},{2,6},{3,7},{4,0},{5,1},{6,2},{7,3},{8,12},{9,13},{10,... | collective-permute-start | bytes 294920 | tf_op jit(solution)/shard_map/ppermute | solution.py:610
  18.1 2.0 %collective-permute-start.7 = (f32[192,128]{1,0:T(8,128)S(1)}, f32[192,128]{1,0:T(8,128)S(1)}, u32[]{:S(2)}, u32[]{:S(2)}) collective-permute-start(f32[192,128]{1,0:T(8,128)S(1)} %get-tuple-element.34.refs_0_), channel_id=1, source_target_pairs={{0,2},{1,3},{2,0},{3,1},{4,6},{5,7},{6,4},{7,5},{8,10},{9,11},{10,... | collective-permute-start | bytes 294920 | tf_op jit(solution)/shard_map/ppermute | solution.py:610
  21.1 4.1 %collective-permute-done.8.refs_1_ = f32[192,128]{1,0:T(8,128)S(1)} collective-permute-done((f32[192,128]{1,0:T(8,128)S(1)}, f32[192,128]{1,0:T(8,128)S(1)}, u32[]{:S(2)}, u32[]{:S(2)}) %collective-permute-start.8) | collective-permute-done | bytes 98336 | tf_op jit(solution)/shard_map/ppermute | solution.py:610
  25.2 2.0 %collective-permute-done.9.refs_3_ = f32[192,128]{1,0:T(8,128)S(1)} collective-permute-done((f32[192,128]{1,0:T(8,128)S(1)}, f32[192,128]{1,0:T(8,128)S(1)}, u32[]{:S(2)}, u32[]{:S(2)}) %collective-permute-start.9) | collective-permute-done | bytes 98336 | tf_op jit(solution)/shard_map/ppermute | solution.py:610
  27.8 0.8 %collective-permute-done.13.refs_7_ = f32[192,128]{1,0:T(8,128)S(1)} collective-permute-done((f32[192,128]{1,0:T(8,128)S(1)}, f32[192,128]{1,0:T(8,128)S(1)}, u32[]{:S(2)}, u32[]{:S(2)}) %collective-permute-start.13) | collective-permute-done | bytes 98336 | tf_op jit(solution)/shard_map/ppermute | solution.py:618
  28.7 1.4 %shard_map.92 = (f32[128,256]{1,0:T(8,128)S(1)}, f32[192,128]{1,0:T(8,128)S(1)}) custom-call(f32[192,128]{1,0:T(8,128)S(1)} %get-tuple-element.34.refs_0_, f32[192,128]{1,0:T(8,128)S(1)} %get-tuple-element.39.refs_1_, f32[192,128]{1,0:T(8,128)S(1)} %get-tuple-element.40.refs_2_, f32[192,128]{1,0:T(8,128)S(1)} %collective-permute-done.9.refs_3_, ...), custom_call_target="tpu_custom_call" | custom-call | flops 20000000 | bytes 4849664 | tf_op jit(solution)/shard_map/pallas_call | solution.py:596
  30.1 1.9 %collective-permute-start.18 = (f32[192,128]{1,0:T(8,128)S(1)}, f32[192,128]{1,0:T(8,128)S(1)}, u32[]{:S(2)}, u32[]{:S(2)}) collective-permute-start(f32[192,128]{1,0:T(8,128)S(1)} %get-tuple-element.44.refs_0_), channel_id=1, source_target_pairs={{0,6},{1,7},{2,4},{3,5},{4,2},{5,3},{6,0},{7,1},{8,14},{9,15},{10,... | collective-permute-start | bytes 294920 | tf_op jit(solution)/shard_map/ppermute | solution.py:610
  32.4 1.6 %collective-permute-start.16 = (f32[144,128]{1,0:T(8,128)S(1)}, f32[144,128]{1,0:T(8,128)S(1)}, u32[]{:S(2)}, u32[]{:S(2)}) collective-permute-start(f32[144,128]{1,0:T(8,128)S(1)} %shard_map.93), channel_id=1, source_target_pairs={{0,8},{8,0},{16,24},{24,16},{1,9},{9,1},{17,25},{25,17},{2,10},{10... | collective-permute-start | bytes 221192 | tf_op jit(solution)/shard_map/ppermute | solution.py:633
  34.0 1.2 %collective-permute-start.15 = (f32[192,128]{1,0:T(8,128)S(1)}, f32[192,128]{1,0:T(8,128)S(1)}, u32[]{:S(2)}, u32[]{:S(2)}) collective-permute-start(f32[192,128]{1,0:T(8,128)S(1)} %get-tuple-element.44.refs_0_), channel_id=1, source_target_pairs={{0,4},{1,5},{2,6},{3,7},{4,0},{5,1},{6,2},{7,3},{8,12},{9,13},{10,... | collective-permute-start | bytes 294920 | tf_op jit(solution)/shard_map/ppermute | solution.py:610
  35.2 1.3 %collective-permute-start.14 = (f32[192,128]{1,0:T(8,128)S(1)}, f32[192,128]{1,0:T(8,128)S(1)}, u32[]{:S(2)}, u32[]{:S(2)}) collective-permute-start(f32[192,128]{1,0:T(8,128)S(1)} %get-tuple-element.44.refs_0_), channel_id=1, source_target_pairs={{0,2},{1,3},{2,0},{3,1},{4,6},{5,7},{6,4},{7,5},{8,10},{9,11},{10,... | collective-permute-start | bytes 294920 | tf_op jit(solution)/shard_map/ppermute | solution.py:610
  36.9 1.6 %collective-permute-start.17 = (f32[144,128]{1,0:T(8,128)S(1)}, f32[144,128]{1,0:T(8,128)S(1)}, u32[]{:S(2)}, u32[]{:S(2)}) collective-permute-start(f32[144,128]{1,0:T(8,128)S(1)} %add.6.one_ref), channel_id=1, source_target_pairs={{0,16},{8,24},{16,0},{24,8},{1,17},{9,25},{17,1},{25,9},{2,18},{10... | collective-permute-start | bytes 221192 | tf_op jit(solution)/shard_map/ppermute | solution.py:635
  38.5 2.8 %collective-permute-done.17.two_ref = f32[144,128]{1,0:T(8,128)S(1)} collective-permute-done((f32[144,128]{1,0:T(8,128)S(1)}, f32[144,128]{1,0:T(8,128)S(1)}, u32[]{:S(2)}, u32[]{:S(2)}) %collective-permute-start.17) | collective-permute-done | bytes 73760 | tf_op jit(solution)/shard_map/ppermute | solution.py:635
  41.3 1.0 %shard_map.94 = (f32[128,256]{1,0:T(8,128)S(1)}, f32[128,256]{1,0:T(8,128)S(1)}, f32[128,128]{1,0:T(8,128)S(1)}) custom-call(f32[144,128]{1,0:T(8,128)S(1)} %add.6.one_ref, f32[144,128]{1,0:T(8,128)S(1)} %collective-permute-done.17.two_ref, f32[128,256]{1,0:T(8,128)S(1)} %get-tuple-element.45.gains_ref, f32[256,128]{1,0:T(8,128)S(1)} %get-tuple-element.37.refs_12_.basis_ref), custom_call_target="tpu_custom_call" | custom-call | flops 20000000 | bytes 737280 | tf_op jit(solution)/shard_map/pallas_call | solution.py:596
  43.3 0.8 %collective-permute-done.20.refs_5_ = f32[192,128]{1,0:T(8,128)S(1)} collective-permute-done((f32[192,128]{1,0:T(8,128)S(1)}, f32[192,128]{1,0:T(8,128)S(1)}, u32[]{:S(2)}, u32[]{:S(2)}) %collective-permute-start.20) | collective-permute-done | bytes 98336 | tf_op jit(solution)/shard_map/ppermute | solution.py:618
  44.3 1.5 %shard_map.97 = (f32[128,256]{1,0:T(8,128)S(1)}, f32[192,128]{1,0:T(8,128)S(1)}) custom-call(f32[192,128]{1,0:T(8,128)S(1)} %get-tuple-element.44.refs_0_, f32[192,128]{1,0:T(8,128)S(1)} %get-tuple-element.47.refs_1_, f32[192,128]{1,0:T(8,128)S(1)} %get-tuple-element.48.refs_2_, f32[192,128]{1,0:T(8,128)S(1)} %shard_map.96.refs_3_, ...), custom_call_target="tpu_custom_call" | custom-call | flops 20000000 | bytes 4849664 | tf_op jit(solution)/shard_map/pallas_call | solution.py:596
  45.7 2.5 %collective-permute-start.27 = (f32[192,128]{1,0:T(8,128)S(1)}, f32[192,128]{1,0:T(8,128)S(1)}, u32[]{:S(2)}, u32[]{:S(2)}) collective-permute-start(f32[192,128]{1,0:T(8,128)S(1)} %get-tuple-element.49.refs_0_), channel_id=1, source_target_pairs={{0,6},{1,7},{2,4},{3,5},{4,2},{5,3},{6,0},{7,1},{8,14},{9,15},{10,... | collective-permute-start | bytes 294920 | tf_op jit(solution)/shard_map/ppermute | solution.py:610
  48.5 1.6 %collective-permute-start.25 = (f32[128,128]{1,0:T(8,128)S(1)}, f32[128,128]{1,0:T(8,128)S(1)}, u32[]{:S(2)}, u32[]{:S(2)}) collective-permute-start(f32[128,128]{1,0:T(8,128)S(1)} %shard_map.98), channel_id=1, source_target_pairs={{0,8},{8,0},{16,24},{24,16},{1,9},{9,1},{17,25},{25,17},{2,10},{10... | collective-permute-start | bytes 196616 | tf_op jit(solution)/shard_map/ppermute | solution.py:633
  50.3 1.7 %collective-permute-start.23 = (f32[192,128]{1,0:T(8,128)S(1)}, f32[192,128]{1,0:T(8,128)S(1)}, u32[]{:S(2)}, u32[]{:S(2)}) collective-permute-start(f32[192,128]{1,0:T(8,128)S(1)} %get-tuple-element.49.refs_0_), channel_id=1, source_target_pairs={{0,2},{1,3},{2,0},{3,1},{4,6},{5,7},{6,4},{7,5},{8,10},{9,11},{10,... | collective-permute-start | bytes 294920 | tf_op jit(solution)/shard_map/ppermute | solution.py:610
  52.0 0.8 %collective-permute-done.25 = f32[128,128]{1,0:T(8,128)S(1)} collective-permute-done((f32[128,128]{1,0:T(8,128)S(1)}, f32[128,128]{1,0:T(8,128)S(1)}, u32[]{:S(2)}, u32[]{:S(2)}) %collective-permute-start.25) | collective-permute-done | bytes 65568 | tf_op jit(solution)/shard_map/ppermute | solution.py:633
  52.9 1.6 %collective-permute-start.26 = (f32[128,128]{1,0:T(8,128)S(1)}, f32[128,128]{1,0:T(8,128)S(1)}, u32[]{:S(2)}, u32[]{:S(2)}) collective-permute-start(f32[128,128]{1,0:T(8,128)S(1)} %add.7.one_ref), channel_id=1, source_target_pairs={{0,16},{8,24},{16,0},{24,8},{1,17},{9,25},{17,1},{25,9},{2,18},{10... | collective-permute-start | bytes 196616 | tf_op jit(solution)/shard_map/ppermute | solution.py:635
  54.5 2.7 %collective-permute-done.26.two_ref = f32[128,128]{1,0:T(8,128)S(1)} collective-permute-done((f32[128,128]{1,0:T(8,128)S(1)}, f32[128,128]{1,0:T(8,128)S(1)}, u32[]{:S(2)}, u32[]{:S(2)}) %collective-permute-start.26) | collective-permute-done | bytes 65568 | tf_op jit(solution)/shard_map/ppermute | solution.py:635
  58.3 0.8 %collective-permute-done.29.refs_5_ = f32[192,128]{1,0:T(8,128)S(1)} collective-permute-done((f32[192,128]{1,0:T(8,128)S(1)}, f32[192,128]{1,0:T(8,128)S(1)}, u32[]{:S(2)}, u32[]{:S(2)}) %collective-permute-start.29) | collective-permute-done | bytes 98336 | tf_op jit(solution)/shard_map/ppermute | solution.py:618
  59.3 0.8 %shard_map.102 = (f32[128,128]{1,0:T(8,128)S(1)}, f32[40,128]{1,0:T(8,128)S(1)}) custom-call(f32[192,128]{1,0:T(8,128)S(1)} %get-tuple-element.49.refs_0_, f32[192,128]{1,0:T(8,128)S(1)} %get-tuple-element.54.refs_1_, f32[192,128]{1,0:T(8,128)S(1)} %get-tuple-element.55.refs_2_, f32[192,128]{1,0:T(8,128)S(1)} %shard_map.101.refs_3_, ...), custom_call_target="tpu_custom_call" | custom-call | flops 20000000 | bytes 1703936 | tf_op jit(solution)/shard_map/pallas_call | solution.py:596
  60.0 2.5 %collective-permute-start.34 = (f32[40,128]{1,0:T(8,128)S(1)}, f32[40,128]{1,0:T(8,128)S(1)}, u32[]{:S(2)}, u32[]{:S(2)}) collective-permute-start(f32[40,128]{1,0:T(8,128)S(1)} %get-tuple-element.59.refs_0_), channel_id=1, source_target_pairs={{0,24},{8,16},{16,8},{24,0},{1,25},{9,17},{17,9},{25,1},{2,26},{10... | collective-permute-start | bytes 61448 | tf_op jit(solution)/shard_map/ppermute | solution.py:625
  63.6 1.0 %shard_map.103 = f32[8,32,64]{2,1,0:T(8,128)} custom-call(f32[128,128]{1,0:T(8,128)S(1)} %get-tuple-element.58.gains_ref), custom_call_target="tpu_custom_call" | custom-call | flops 20000000 | bytes 131072 | tf_op jit(solution)/shard_map/pallas_call | solution.py:596
  64.8 1.5 %collective-permute-done.33.refs_2_ = f32[40,128]{1,0:T(8,128)S(1)} collective-permute-done((f32[40,128]{1,0:T(8,128)S(1)}, f32[40,128]{1,0:T(8,128)S(1)}, u32[]{:S(2)}, u32[]{:S(2)}) %collective-permute-start.33) | collective-permute-done | bytes 20512 | tf_op jit(solution)/shard_map/ppermute | solution.py:625
  66.8 0.9 %shard_map.104 = f32[9,8,64]{2,1,0:T(8,128)} custom-call(f32[40,128]{1,0:T(8,128)S(1)} %get-tuple-element.59.refs_0_, f32[40,128]{1,0:T(8,128)S(1)} %collective-permute-done.32.refs_1_, f32[40,128]{1,0:T(8,128)S(1)} %collective-permute-done.33.refs_2_, f32[40,128]{1,0:T(8,128)S(1)} %collective-permute-done.34.refs_3_, ...), custom_call_target="tpu_custom_call" | custom-call | flops 20000000 | bytes 165888 | tf_op jit(solution)/shard_map/pallas_call | solution.py:596
  (59 shorter events, 9.7 us)
Async XLA Ops:
  1.9 11.6 %collective-permute-start.3 = (f32[136,128]{1,0:T(8,128)S(1)}, f32[136,128]{1,0:T(8,128)S(1)}, u32[]{:S(2)}, u32[]{:S(2)}) collective-permute-start(f32[136,128]{1,0:T(8,128)S(1)} %shard_map.86.refs_0_), channel_id=1, source_target_pairs={{0,1},{1,0},{2,3},{3,2},{4,5},{5,4},{6,7},{7,6},{8,9},{9,8},{10,11... | collective-permute-start | bytes 208904 | tf_op jit(solution)/shard_map/ppermute | solution.py:618
  2.5 10.2 %collective-permute-start.2 = (f32[136,128]{1,0:T(8,128)S(1)}, f32[136,128]{1,0:T(8,128)S(1)}, u32[]{:S(2)}, u32[]{:S(2)}) collective-permute-start(f32[136,128]{1,0:T(8,128)S(1)} %shard_map.86.refs_0_), channel_id=1, source_target_pairs={{0,6},{1,7},{2,4},{3,5},{4,2},{5,3},{6,0},{7,1},{8,14},{9,15},{10,... | collective-permute-start | bytes 208904 | tf_op jit(solution)/shard_map/ppermute | solution.py:610
  7.1 6.4 %collective-permute-start.1 = (f32[136,128]{1,0:T(8,128)S(1)}, f32[136,128]{1,0:T(8,128)S(1)}, u32[]{:S(2)}, u32[]{:S(2)}) collective-permute-start(f32[136,128]{1,0:T(8,128)S(1)} %shard_map.86.refs_0_), channel_id=1, source_target_pairs={{0,4},{1,5},{2,6},{3,7},{4,0},{5,1},{6,2},{7,3},{8,12},{9,13},{10,... | collective-permute-start | bytes 208904 | tf_op jit(solution)/shard_map/ppermute | solution.py:610
  7.1 5.6 %collective-permute-start = (f32[136,128]{1,0:T(8,128)S(1)}, f32[136,128]{1,0:T(8,128)S(1)}, u32[]{:S(2)}, u32[]{:S(2)}) collective-permute-start(f32[136,128]{1,0:T(8,128)S(1)} %shard_map.86.refs_0_), channel_id=1, source_target_pairs={{0,2},{1,3},{2,0},{3,1},{4,6},{5,7},{6,4},{7,5},{8,10},{9,11},{10,... | collective-permute-start | bytes 208904 | tf_op jit(solution)/shard_map/ppermute | solution.py:610
  12.6 1.3 %collective-permute-start.6 = (f32[136,128]{1,0:T(8,128)S(1)}, f32[136,128]{1,0:T(8,128)S(1)}, u32[]{:S(2)}, u32[]{:S(2)}) collective-permute-start(f32[136,128]{1,0:T(8,128)S(1)} %collective-permute-done.2.refs_3_), channel_id=1, source_target_pairs={{0,1},{1,0},{2,3},{3,2},{4,5},{5,4},{6,7},{7,6},{8,9},{9,8},{10,11... | collective-permute-start | bytes 208904 | tf_op jit(solution)/shard_map/ppermute | solution.py:618
  12.7 1.4 %collective-permute-start.4 = (f32[136,128]{1,0:T(8,128)S(1)}, f32[136,128]{1,0:T(8,128)S(1)}, u32[]{:S(2)}, u32[]{:S(2)}) collective-permute-start(f32[136,128]{1,0:T(8,128)S(1)} %collective-permute-done.refs_1_), channel_id=1, source_target_pairs={{0,1},{1,0},{2,3},{3,2},{4,5},{5,4},{6,7},{7,6},{8,9},{9,8},{10,11... | collective-permute-start | bytes 208904 | tf_op jit(solution)/shard_map/ppermute | solution.py:618
  16.1 9.1 %collective-permute-start.8 = (f32[192,128]{1,0:T(8,128)S(1)}, f32[192,128]{1,0:T(8,128)S(1)}, u32[]{:S(2)}, u32[]{:S(2)}) collective-permute-start(f32[192,128]{1,0:T(8,128)S(1)} %get-tuple-element.34.refs_0_), channel_id=1, source_target_pairs={{0,4},{1,5},{2,6},{3,7},{4,0},{5,1},{6,2},{7,3},{8,12},{9,13},{10,... | collective-permute-start | bytes 294920 | tf_op jit(solution)/shard_map/ppermute | solution.py:610
  18.1 7.1 %collective-permute-start.7 = (f32[192,128]{1,0:T(8,128)S(1)}, f32[192,128]{1,0:T(8,128)S(1)}, u32[]{:S(2)}, u32[]{:S(2)}) collective-permute-start(f32[192,128]{1,0:T(8,128)S(1)} %get-tuple-element.34.refs_0_), channel_id=1, source_target_pairs={{0,2},{1,3},{2,0},{3,1},{4,6},{5,7},{6,4},{7,5},{8,10},{9,11},{10,... | collective-permute-start | bytes 294920 | tf_op jit(solution)/shard_map/ppermute | solution.py:610
  20.2 7.1 %collective-permute-start.9 = (f32[192,128]{1,0:T(8,128)S(1)}, f32[192,128]{1,0:T(8,128)S(1)}, u32[]{:S(2)}, u32[]{:S(2)}) collective-permute-start(f32[192,128]{1,0:T(8,128)S(1)} %get-tuple-element.34.refs_0_), channel_id=1, source_target_pairs={{0,6},{1,7},{2,4},{3,5},{4,2},{5,3},{6,0},{7,1},{8,14},{9,15},{10,... | collective-permute-start | bytes 294920 | tf_op jit(solution)/shard_map/ppermute | solution.py:610
  20.6 7.2 %collective-permute-start.10 = (f32[192,128]{1,0:T(8,128)S(1)}, f32[192,128]{1,0:T(8,128)S(1)}, u32[]{:S(2)}, u32[]{:S(2)}) collective-permute-start(f32[192,128]{1,0:T(8,128)S(1)} %get-tuple-element.34.refs_0_), channel_id=1, source_target_pairs={{0,1},{1,0},{2,3},{3,2},{4,5},{5,4},{6,7},{7,6},{8,9},{9,8},{10,11... | collective-permute-start | bytes 294920 | tf_op jit(solution)/shard_map/ppermute | solution.py:618
  25.2 3.3 %collective-permute-start.11 = (f32[192,128]{1,0:T(8,128)S(1)}, f32[192,128]{1,0:T(8,128)S(1)}, u32[]{:S(2)}, u32[]{:S(2)}) collective-permute-start(f32[192,128]{1,0:T(8,128)S(1)} %get-tuple-element.39.refs_1_), channel_id=1, source_target_pairs={{0,1},{1,0},{2,3},{3,2},{4,5},{5,4},{6,7},{7,6},{8,9},{9,8},{10,11... | collective-permute-start | bytes 294920 | tf_op jit(solution)/shard_map/ppermute | solution.py:618
  27.2 1.5 %collective-permute-start.12 = (f32[192,128]{1,0:T(8,128)S(1)}, f32[192,128]{1,0:T(8,128)S(1)}, u32[]{:S(2)}, u32[]{:S(2)}) collective-permute-start(f32[192,128]{1,0:T(8,128)S(1)} %get-tuple-element.40.refs_2_), channel_id=1, source_target_pairs={{0,1},{1,0},{2,3},{3,2},{4,5},{5,4},{6,7},{7,6},{8,9},{9,8},{10,11... | collective-permute-start | bytes 294920 | tf_op jit(solution)/shard_map/ppermute | solution.py:618
  30.1 8.3 %collective-permute-start.18 = (f32[192,128]{1,0:T(8,128)S(1)}, f32[192,128]{1,0:T(8,128)S(1)}, u32[]{:S(2)}, u32[]{:S(2)}) collective-permute-start(f32[192,128]{1,0:T(8,128)S(1)} %get-tuple-element.44.refs_0_), channel_id=1, source_target_pairs={{0,6},{1,7},{2,4},{3,5},{4,2},{5,3},{6,0},{7,1},{8,14},{9,15},{10,... | collective-permute-start | bytes 294920 | tf_op jit(solution)/shard_map/ppermute | solution.py:610
  32.4 4.4 %collective-permute-start.16 = (f32[144,128]{1,0:T(8,128)S(1)}, f32[144,128]{1,0:T(8,128)S(1)}, u32[]{:S(2)}, u32[]{:S(2)}) collective-permute-start(f32[144,128]{1,0:T(8,128)S(1)} %shard_map.93), channel_id=1, source_target_pairs={{0,8},{8,0},{16,24},{24,16},{1,9},{9,1},{17,25},{25,17},{2,10},{10... | collective-permute-start | bytes 221192 | tf_op jit(solution)/shard_map/ppermute | solution.py:633
  34.0 9.4 %collective-permute-start.19 = (f32[192,128]{1,0:T(8,128)S(1)}, f32[192,128]{1,0:T(8,128)S(1)}, u32[]{:S(2)}, u32[]{:S(2)}) collective-permute-start(f32[192,128]{1,0:T(8,128)S(1)} %get-tuple-element.44.refs_0_), channel_id=1, source_target_pairs={{0,1},{1,0},{2,3},{3,2},{4,5},{5,4},{6,7},{7,6},{8,9},{9,8},{10,11... | collective-permute-start | bytes 294920 | tf_op jit(solution)/shard_map/ppermute | solution.py:618
  34.0 8.8 %collective-permute-start.15 = (f32[192,128]{1,0:T(8,128)S(1)}, f32[192,128]{1,0:T(8,128)S(1)}, u32[]{:S(2)}, u32[]{:S(2)}) collective-permute-start(f32[192,128]{1,0:T(8,128)S(1)} %get-tuple-element.44.refs_0_), channel_id=1, source_target_pairs={{0,4},{1,5},{2,6},{3,7},{4,0},{5,1},{6,2},{7,3},{8,12},{9,13},{10,... | collective-permute-start | bytes 294920 | tf_op jit(solution)/shard_map/ppermute | solution.py:610
  35.2 7.7 %collective-permute-start.14 = (f32[192,128]{1,0:T(8,128)S(1)}, f32[192,128]{1,0:T(8,128)S(1)}, u32[]{:S(2)}, u32[]{:S(2)}) collective-permute-start(f32[192,128]{1,0:T(8,128)S(1)} %get-tuple-element.44.refs_0_), channel_id=1, source_target_pairs={{0,2},{1,3},{2,0},{3,1},{4,6},{5,7},{6,4},{7,5},{8,10},{9,11},{10,... | collective-permute-start | bytes 294920 | tf_op jit(solution)/shard_map/ppermute | solution.py:610
  36.9 4.4 %collective-permute-start.17 = (f32[144,128]{1,0:T(8,128)S(1)}, f32[144,128]{1,0:T(8,128)S(1)}, u32[]{:S(2)}, u32[]{:S(2)}) collective-permute-start(f32[144,128]{1,0:T(8,128)S(1)} %add.6.one_ref), channel_id=1, source_target_pairs={{0,16},{8,24},{16,0},{24,8},{1,17},{9,25},{17,1},{25,9},{2,18},{10... | collective-permute-start | bytes 221192 | tf_op jit(solution)/shard_map/ppermute | solution.py:635
  38.4 4.9 %collective-permute-start.22 = (f32[192,128]{1,0:T(8,128)S(1)}, f32[192,128]{1,0:T(8,128)S(1)}, u32[]{:S(2)}, u32[]{:S(2)}) collective-permute-start(f32[192,128]{1,0:T(8,128)S(1)} %shard_map.96.refs_3_), channel_id=1, source_target_pairs={{0,1},{1,0},{2,3},{3,2},{4,5},{5,4},{6,7},{7,6},{8,9},{9,8},{10,11... | collective-permute-start | bytes 294920 | tf_op jit(solution)/shard_map/ppermute | solution.py:618
  42.8 1.5 %collective-permute-start.21 = (f32[192,128]{1,0:T(8,128)S(1)}, f32[192,128]{1,0:T(8,128)S(1)}, u32[]{:S(2)}, u32[]{:S(2)}) collective-permute-start(f32[192,128]{1,0:T(8,128)S(1)} %get-tuple-element.48.refs_2_), channel_id=1, source_target_pairs={{0,1},{1,0},{2,3},{3,2},{4,5},{5,4},{6,7},{7,6},{8,9},{9,8},{10,11... | collective-permute-start | bytes 294920 | tf_op jit(solution)/shard_map/ppermute | solution.py:618
  45.7 8.7 %collective-permute-start.27 = (f32[192,128]{1,0:T(8,128)S(1)}, f32[192,128]{1,0:T(8,128)S(1)}, u32[]{:S(2)}, u32[]{:S(2)}) collective-permute-start(f32[192,128]{1,0:T(8,128)S(1)} %get-tuple-element.49.refs_0_), channel_id=1, source_target_pairs={{0,6},{1,7},{2,4},{3,5},{4,2},{5,3},{6,0},{7,1},{8,14},{9,15},{10,... | collective-permute-start | bytes 294920 | tf_op jit(solution)/shard_map/ppermute | solution.py:610
  48.5 4.3 %collective-permute-start.25 = (f32[128,128]{1,0:T(8,128)S(1)}, f32[128,128]{1,0:T(8,128)S(1)}, u32[]{:S(2)}, u32[]{:S(2)}) collective-permute-start(f32[128,128]{1,0:T(8,128)S(1)} %shard_map.98), channel_id=1, source_target_pairs={{0,8},{8,0},{16,24},{24,16},{1,9},{9,1},{17,25},{25,17},{2,10},{10... | collective-permute-start | bytes 196616 | tf_op jit(solution)/shard_map/ppermute | solution.py:633
  50.1 8.2 %collective-permute-start.28 = (f32[192,128]{1,0:T(8,128)S(1)}, f32[192,128]{1,0:T(8,128)S(1)}, u32[]{:S(2)}, u32[]{:S(2)}) collective-permute-start(f32[192,128]{1,0:T(8,128)S(1)} %get-tuple-element.49.refs_0_), channel_id=1, source_target_pairs={{0,1},{1,0},{2,3},{3,2},{4,5},{5,4},{6,7},{7,6},{8,9},{9,8},{10,11... | collective-permute-start | bytes 294920 | tf_op jit(solution)/shard_map/ppermute | solution.py:618
  50.1 7.7 %collective-permute-start.24 = (f32[192,128]{1,0:T(8,128)S(1)}, f32[192,128]{1,0:T(8,128)S(1)}, u32[]{:S(2)}, u32[]{:S(2)}) collective-permute-start(f32[192,128]{1,0:T(8,128)S(1)} %get-tuple-element.49.refs_0_), channel_id=1, source_target_pairs={{0,4},{1,5},{2,6},{3,7},{4,0},{5,1},{6,2},{7,3},{8,12},{9,13},{10,... | collective-permute-start | bytes 294920 | tf_op jit(solution)/shard_map/ppermute | solution.py:610
  50.3 7.5 %collective-permute-start.23 = (f32[192,128]{1,0:T(8,128)S(1)}, f32[192,128]{1,0:T(8,128)S(1)}, u32[]{:S(2)}, u32[]{:S(2)}) collective-permute-start(f32[192,128]{1,0:T(8,128)S(1)} %get-tuple-element.49.refs_0_), channel_id=1, source_target_pairs={{0,2},{1,3},{2,0},{3,1},{4,6},{5,7},{6,4},{7,5},{8,10},{9,11},{10,... | collective-permute-start | bytes 294920 | tf_op jit(solution)/shard_map/ppermute | solution.py:610
  52.9 4.3 %collective-permute-start.26 = (f32[128,128]{1,0:T(8,128)S(1)}, f32[128,128]{1,0:T(8,128)S(1)}, u32[]{:S(2)}, u32[]{:S(2)}) collective-permute-start(f32[128,128]{1,0:T(8,128)S(1)} %add.7.one_ref), channel_id=1, source_target_pairs={{0,16},{8,24},{16,0},{24,8},{1,17},{9,25},{17,1},{25,9},{2,18},{10... | collective-permute-start | bytes 196616 | tf_op jit(solution)/shard_map/ppermute | solution.py:635
  54.5 3.9 %collective-permute-start.31 = (f32[192,128]{1,0:T(8,128)S(1)}, f32[192,128]{1,0:T(8,128)S(1)}, u32[]{:S(2)}, u32[]{:S(2)}) collective-permute-start(f32[192,128]{1,0:T(8,128)S(1)} %shard_map.101.refs_3_), channel_id=1, source_target_pairs={{0,1},{1,0},{2,3},{3,2},{4,5},{5,4},{6,7},{7,6},{8,9},{9,8},{10,11... | collective-permute-start | bytes 294920 | tf_op jit(solution)/shard_map/ppermute | solution.py:618
  57.8 1.3 %collective-permute-start.29 = (f32[192,128]{1,0:T(8,128)S(1)}, f32[192,128]{1,0:T(8,128)S(1)}, u32[]{:S(2)}, u32[]{:S(2)}) collective-permute-start(f32[192,128]{1,0:T(8,128)S(1)} %get-tuple-element.54.refs_1_), channel_id=1, source_target_pairs={{0,1},{1,0},{2,3},{3,2},{4,5},{5,4},{6,7},{7,6},{8,9},{9,8},{10,11... | collective-permute-start | bytes 294920 | tf_op jit(solution)/shard_map/ppermute | solution.py:618
  57.8 1.4 %collective-permute-start.30 = (f32[192,128]{1,0:T(8,128)S(1)}, f32[192,128]{1,0:T(8,128)S(1)}, u32[]{:S(2)}, u32[]{:S(2)}) collective-permute-start(f32[192,128]{1,0:T(8,128)S(1)} %get-tuple-element.55.refs_2_), channel_id=1, source_target_pairs={{0,1},{1,0},{2,3},{3,2},{4,5},{5,4},{6,7},{7,6},{8,9},{9,8},{10,11... | collective-permute-start | bytes 294920 | tf_op jit(solution)/shard_map/ppermute | solution.py:618
  60.0 4.7 %collective-permute-start.34 = (f32[40,128]{1,0:T(8,128)S(1)}, f32[40,128]{1,0:T(8,128)S(1)}, u32[]{:S(2)}, u32[]{:S(2)}) collective-permute-start(f32[40,128]{1,0:T(8,128)S(1)} %get-tuple-element.59.refs_0_), channel_id=1, source_target_pairs={{0,24},{8,16},{16,8},{24,0},{1,25},{9,17},{17,9},{25,1},{2,26},{10... | collective-permute-start | bytes 61448 | tf_op jit(solution)/shard_map/ppermute | solution.py:625
  62.5 3.8 %collective-permute-start.33 = (f32[40,128]{1,0:T(8,128)S(1)}, f32[40,128]{1,0:T(8,128)S(1)}, u32[]{:S(2)}, u32[]{:S(2)}) collective-permute-start(f32[40,128]{1,0:T(8,128)S(1)} %get-tuple-element.59.refs_0_), channel_id=1, source_target_pairs={{0,16},{8,24},{16,0},{24,8},{1,17},{9,25},{17,1},{25,9},{2,18},{10... | collective-permute-start | bytes 61448 | tf_op jit(solution)/shard_map/ppermute | solution.py:625
  63.0 3.8 %collective-permute-start.32 = (f32[40,128]{1,0:T(8,128)S(1)}, f32[40,128]{1,0:T(8,128)S(1)}, u32[]{:S(2)}, u32[]{:S(2)}) collective-permute-start(f32[40,128]{1,0:T(8,128)S(1)} %get-tuple-element.59.refs_0_), channel_id=1, source_target_pairs={{0,8},{8,0},{16,24},{24,16},{1,9},{9,1},{17,25},{25,17},{2,10},{10... | collective-permute-start | bytes 61448 | tf_op jit(solution)/shard_map/ppermute | solution.py:625
  (3 other events, 3.9 us)

commit v7 on v4

--- a/solution.py
+++ b/solution.py
@@ -201,12 +201,16 @@
     copies[0].wait()
     place = (iota((BLOCK, owned), 0) == iota((BLOCK, owned), 1) % BLOCK).astype(BF16)
     here = iota((LANES, owned), 0) // intervals == iota((LANES, owned), 1) // BLOCK
+    parts = []
     for m in range(8):
-        plane = start_ref[m]
-        plane = jnp.where(here, jnp.concatenate([plane] * (LANES // intervals), 0), 0.0)
-        high = plane.astype(BF16)
-        low = (plane - high.astype(F32)).astype(BF16)
-        out_ref[m * BLOCK : (m + 1) * BLOCK, :] = nt(place, high) + nt(place, low)
+        plane = jnp.concatenate([start_ref[m]] * (LANES // intervals), 0)
+        parts.append(jnp.where(here, plane, 0.0))
+    parts = jnp.concatenate(parts, 0)
+    high = parts.astype(BF16)
+    low = (parts - high.astype(F32)).astype(BF16)
+    turned = nt(place, high) + nt(place, low)
+    for m in range(8):
+        out_ref[m * BLOCK : (m + 1) * BLOCK, :] = turned[:, m * LANES : (m + 1) * LANES]
 
 
 def prepare_kernel(
@@ -225,7 +229,7 @@
         pltpu.make_async_copy(source, target, sems.at[n])
         for n, (source, target) in enumerate(moves)
     ]
-    for copy in copies:
+    for copy in copies[:1] + copies[2:]:
         copy.start()
     for copy in copies[2:]:
         copy.wait()
@@ -271,6 +275,7 @@
         prod_ref[at] = pick(beside, fold).reshape(prod_ref.shape[1:])
 
     copies[0].wait()
+    copies[1].start()
     for m in range(planes):
         masked = (model_ref[m].astype(F32) * weight).astype(BF16)
         mt_ref[m] = nt(ident, masked)
@@ -692,7 +697,7 @@
         hbm=True,
         flops=2_000_000_000,
     )
-    greetings = share_base(greeting, last=(chans,))
+    greetings = share_base(greeting, last=(chans,), ties=(1, 2))
     scratch = [
         pltpu.VMEM((12, BLOCK // 2, LANES), F32),
         pltpu.VMEM((2, 12, BLOCK // 2, LANES), F32),

time: 67.8 us -> 67.8 us (level)
  transfers between devices with their start and end apart: 35 -> 35, of which waited for: 21 -> 19; matrix products, arithmetic and copies ran while one was open for 0% -> 0% of each run, Pallas kernels for 12% -> 12%
where the time goes in v7:
time: 67.8 us; the launch traced here: 67.6 us
  starting transfers between devices  31.2 us (46%)
  waiting for transfers between devices  20.5 us (30%)
  Pallas kernels  15.1 us (22%)
  between operations  0.76 us (1%)
    ppermute x12, starting transfers between devices, share_base(): lax.ppermute(x, 'base', [(d, d ^ 2 * k) for d in range(devices)])  18.7 us
    pallas_call x13, Pallas kernels, call(): pl.pallas_call(kernel, out_shape=shapes, in_specs=in_specs, out_specs=[vm...  15.1 us
    ppermute x12, waiting for transfers between devices, share_base(): lax.ppermute(x, 'base', [(d, d ^ 2 * k) for d in range(devices)])  7.8 us
    ppermute x2, waiting for transfers between devices, sum_band(): return (x, lax.ppermute(x, 'band', [(d, d ^ step) for d in range(devices)]))  5.57 us
    ppermute x16, waiting for transfers between devices, share_base(): lax.ppermute(y, 'base', [(d, d ^ 1) for d in range(devices)])  4.02 us
    ppermute x3, starting transfers between devices, share_band(): lax.ppermute(x, 'band', [(d, d ^ k) for d in range(devices)])  3.53 us
    ppermute x2, starting transfers between devices, sum_band(): return (x, lax.ppermute(x, 'band', [(d, d ^ step) for d in range(devices)]))  3.17 us
    ppermute x2, starting transfers between devices, sum_band(): x = x + lax.ppermute(x, 'band', [(d, d ^ step) for d in range(devices)])  3.11 us
  transfers between devices with their start and end apart: 35, of which 19 were waited for; matrix products, arithmetic and copies ran while one was open for 0% of the time, Pallas kernels for 12%

profile of v7, /device:TPU:0, one launch (start us, length us, event | category | flops | bytes accessed | tf_op | source)
XLA Modules:
  0.0 67.6 jit_solution(6877458440750688093)
XLA Ops:
  0.6 1.3 %shard_map.86.refs_0_ = f32[136,128]{1,0:T(8,128)S(1)} custom-call(s32[2,2]{1,0:T(2,128)} %pair_hbm.3, f32[8,32,64]{2,1,0:T(8,128)} %start_hbm.1, f32[1,64]{1,0:T(1,128)} %bitcast.6, s32[2,256]{1,0:T(2,128)} %flag_hbm.3), custom_call_target="tpu_custom_call" | custom-call | flops 20000000 | bytes 137488 | tf_op jit(solution)/shard_map/pallas_call | solution.py:600
  2.5 4.7 %collective-permute-start.2 = (f32[136,128]{1,0:T(8,128)S(1)}, f32[136,128]{1,0:T(8,128)S(1)}, u32[]{:S(2)}, u32[]{:S(2)}) collective-permute-start(f32[136,128]{1,0:T(8,128)S(1)} %shard_map.86.refs_0_), channel_id=1, source_target_pairs={{0,6},{1,7},{2,4},{3,5},{4,2},{5,3},{6,0},{7,1},{8,14},{9,15},{10,... | collective-permute-start | bytes 208904 | tf_op jit(solution)/shard_map/ppermute | solution.py:614
  7.8 4.4 %shard_map.87 = (f32[48,8,16,128]{3,2,1,0:T(8,128)S(1)}, f32[256,128]{1,0:T(8,128)S(1)}, f32[256,128]{1,0:T(8,128)S(1)}, f32[256,128]{1,0:T(8,128)S(1)}, f32[8,256]{1,0:T(8,128)S(1)}) custom-call(s32[2,2]{1,0:T(2,128)} %pair_hbm.3, s32[1,64]{1,0:T(1,128)} %bitcast.9, s32[2,256]{1,0:T(2,128)} %flag_hbm.3, bf16[8,128,256]{2,1,0:T(8,128)(2,1)} %bitcast.7, ...), custom_call_target="tpu_custom_call" | custom-call | flops 2000000000 | bytes 4598032 | tf_op jit(solution)/shard_map/pallas_call | solution.py:600
  12.2 1.3 %collective-permute-done.1.refs_1_ = f32[136,128]{1,0:T(8,128)S(1)} collective-permute-done((f32[136,128]{1,0:T(8,128)S(1)}, f32[136,128]{1,0:T(8,128)S(1)}, u32[]{:S(2)}, u32[]{:S(2)}) %collective-permute-start.1) | collective-permute-done | bytes 69664 | tf_op jit(solution)/shard_map/ppermute | solution.py:614
  14.1 0.8 %collective-permute-done.6.refs_7_ = f32[136,128]{1,0:T(8,128)S(1)} collective-permute-done((f32[136,128]{1,0:T(8,128)S(1)}, f32[136,128]{1,0:T(8,128)S(1)}, u32[]{:S(2)}, u32[]{:S(2)}) %collective-permute-start.6) | collective-permute-done | bytes 69664 | tf_op jit(solution)/shard_map/ppermute | solution.py:622
  15.3 1.3 %shard_map.89 = (f32[128,128]{1,0:T(8,128)S(1)}, f32[192,128]{1,0:T(8,128)S(1)}) custom-call(f32[136,128]{1,0:T(8,128)S(1)} %shard_map.86.refs_0_, f32[136,128]{1,0:T(8,128)S(1)} %get-tuple-element.34.refs_1_, f32[136,128]{1,0:T(8,128)S(1)} %get-tuple-element.35.refs_2_, f32[136,128]{1,0:T(8,128)S(1)} %collective-permute-done.2.refs_3_, ...), custom_call_target="tpu_custom_call" | custom-call | flops 20000000 | bytes 3997696 | tf_op jit(solution)/shard_map/pallas_call | solution.py:600
  16.6 1.1 %collective-permute-start.8 = (f32[192,128]{1,0:T(8,128)S(1)}, f32[192,128]{1,0:T(8,128)S(1)}, u32[]{:S(2)}, u32[]{:S(2)}) collective-permute-start(f32[192,128]{1,0:T(8,128)S(1)} %get-tuple-element.38.refs_0_), channel_id=1, source_target_pairs={{0,4},{1,5},{2,6},{3,7},{4,0},{5,1},{6,2},{7,3},{8,12},{9,13},{10,... | collective-permute-start | bytes 294920 | tf_op jit(solution)/shard_map/ppermute | solution.py:614
  17.8 2.0 %collective-permute-start.7 = (f32[192,128]{1,0:T(8,128)S(1)}, f32[192,128]{1,0:T(8,128)S(1)}, u32[]{:S(2)}, u32[]{:S(2)}) collective-permute-start(f32[192,128]{1,0:T(8,128)S(1)} %get-tuple-element.38.refs_0_), channel_id=1, source_target_pairs={{0,2},{1,3},{2,0},{3,1},{4,6},{5,7},{6,4},{7,5},{8,10},{9,11},{10,... | collective-permute-start | bytes 294920 | tf_op jit(solution)/shard_map/ppermute | solution.py:614
  19.8 1.3 %collective-permute-start.9 = (f32[192,128]{1,0:T(8,128)S(1)}, f32[192,128]{1,0:T(8,128)S(1)}, u32[]{:S(2)}, u32[]{:S(2)}) collective-permute-start(f32[192,128]{1,0:T(8,128)S(1)} %get-tuple-element.38.refs_0_), channel_id=1, source_target_pairs={{0,6},{1,7},{2,4},{3,5},{4,2},{5,3},{6,0},{7,1},{8,14},{9,15},{10,... | collective-permute-start | bytes 294920 | tf_op jit(solution)/shard_map/ppermute | solution.py:614
  21.6 4.4 %collective-permute-done.8.refs_1_ = f32[192,128]{1,0:T(8,128)S(1)} collective-permute-done((f32[192,128]{1,0:T(8,128)S(1)}, f32[192,128]{1,0:T(8,128)S(1)}, u32[]{:S(2)}, u32[]{:S(2)}) %collective-permute-start.8) | collective-permute-done | bytes 98336 | tf_op jit(solution)/shard_map/ppermute | solution.py:614
  26.0 1.4 %collective-permute-done.9.refs_3_ = f32[192,128]{1,0:T(8,128)S(1)} collective-permute-done((f32[192,128]{1,0:T(8,128)S(1)}, f32[192,128]{1,0:T(8,128)S(1)}, u32[]{:S(2)}, u32[]{:S(2)}) %collective-permute-start.9) | collective-permute-done | bytes 98336 | tf_op jit(solution)/shard_map/ppermute | solution.py:614
  27.9 0.8 %collective-permute-done.13.refs_7_ = f32[192,128]{1,0:T(8,128)S(1)} collective-permute-done((f32[192,128]{1,0:T(8,128)S(1)}, f32[192,128]{1,0:T(8,128)S(1)}, u32[]{:S(2)}, u32[]{:S(2)}) %collective-permute-start.13) | collective-permute-done | bytes 98336 | tf_op jit(solution)/shard_map/ppermute | solution.py:622
  28.9 1.4 %shard_map.92 = (f32[128,256]{1,0:T(8,128)S(1)}, f32[192,128]{1,0:T(8,128)S(1)}) custom-call(f32[192,128]{1,0:T(8,128)S(1)} %get-tuple-element.38.refs_0_, f32[192,128]{1,0:T(8,128)S(1)} %get-tuple-element.43.refs_1_, f32[192,128]{1,0:T(8,128)S(1)} %get-tuple-element.44.refs_2_, f32[192,128]{1,0:T(8,128)S(1)} %collective-permute-done.9.refs_3_, ...), custom_call_target="tpu_custom_call" | custom-call | flops 20000000 | bytes 4849664 | tf_op jit(solution)/shard_map/pallas_call | solution.py:600
  30.3 2.0 %collective-permute-start.18 = (f32[192,128]{1,0:T(8,128)S(1)}, f32[192,128]{1,0:T(8,128)S(1)}, u32[]{:S(2)}, u32[]{:S(2)}) collective-permute-start(f32[192,128]{1,0:T(8,128)S(1)} %get-tuple-element.48.refs_0_), channel_id=1, source_target_pairs={{0,6},{1,7},{2,4},{3,5},{4,2},{5,3},{6,0},{7,1},{8,14},{9,15},{10,... | collective-permute-start | bytes 294920 | tf_op jit(solution)/shard_map/ppermute | solution.py:614
  32.7 1.6 %collective-permute-start.16 = (f32[144,128]{1,0:T(8,128)S(1)}, f32[144,128]{1,0:T(8,128)S(1)}, u32[]{:S(2)}, u32[]{:S(2)}) collective-permute-start(f32[144,128]{1,0:T(8,128)S(1)} %shard_map.93), channel_id=1, source_target_pairs={{0,8},{8,0},{16,24},{24,16},{1,9},{9,1},{17,25},{25,17},{2,10},{10... | collective-permute-start | bytes 221192 | tf_op jit(solution)/shard_map/ppermute | solution.py:637
  34.2 1.5 %collective-permute-start.15 = (f32[192,128]{1,0:T(8,128)S(1)}, f32[192,128]{1,0:T(8,128)S(1)}, u32[]{:S(2)}, u32[]{:S(2)}) collective-permute-start(f32[192,128]{1,0:T(8,128)S(1)} %get-tuple-element.48.refs_0_), channel_id=1, source_target_pairs={{0,4},{1,5},{2,6},{3,7},{4,0},{5,1},{6,2},{7,3},{8,12},{9,13},{10,... | collective-permute-start | bytes 294920 | tf_op jit(solution)/shard_map/ppermute | solution.py:614
  35.7 1.0 %collective-permute-start.14 = (f32[192,128]{1,0:T(8,128)S(1)}, f32[192,128]{1,0:T(8,128)S(1)}, u32[]{:S(2)}, u32[]{:S(2)}) collective-permute-start(f32[192,128]{1,0:T(8,128)S(1)} %get-tuple-element.48.refs_0_), channel_id=1, source_target_pairs={{0,2},{1,3},{2,0},{3,1},{4,6},{5,7},{6,4},{7,5},{8,10},{9,11},{10,... | collective-permute-start | bytes 294920 | tf_op jit(solution)/shard_map/ppermute | solution.py:614
  37.1 1.6 %collective-permute-start.17 = (f32[144,128]{1,0:T(8,128)S(1)}, f32[144,128]{1,0:T(8,128)S(1)}, u32[]{:S(2)}, u32[]{:S(2)}) collective-permute-start(f32[144,128]{1,0:T(8,128)S(1)} %add.6.one_ref), channel_id=1, source_target_pairs={{0,16},{8,24},{16,0},{24,8},{1,17},{9,25},{17,1},{25,9},{2,18},{10... | collective-permute-start | bytes 221192 | tf_op jit(solution)/shard_map/ppermute | solution.py:639
  38.7 2.8 %collective-permute-done.17.two_ref = f32[144,128]{1,0:T(8,128)S(1)} collective-permute-done((f32[144,128]{1,0:T(8,128)S(1)}, f32[144,128]{1,0:T(8,128)S(1)}, u32[]{:S(2)}, u32[]{:S(2)}) %collective-permute-start.17) | collective-permute-done | bytes 73760 | tf_op jit(solution)/shard_map/ppermute | solution.py:639
  41.5 1.0 %shard_map.94 = (f32[128,256]{1,0:T(8,128)S(1)}, f32[128,256]{1,0:T(8,128)S(1)}, f32[128,128]{1,0:T(8,128)S(1)}) custom-call(f32[144,128]{1,0:T(8,128)S(1)} %add.6.one_ref, f32[144,128]{1,0:T(8,128)S(1)} %collective-permute-done.17.two_ref, f32[128,256]{1,0:T(8,128)S(1)} %get-tuple-element.49.gains_ref, f32[256,128]{1,0:T(8,128)S(1)} %get-tuple-element.41.refs_12_.basis_ref), custom_call_target="tpu_custom_call" | custom-call | flops 20000000 | bytes 737280 | tf_op jit(solution)/shard_map/pallas_call | solution.py:600
  43.7 0.8 %collective-permute-done.20.refs_5_ = f32[192,128]{1,0:T(8,128)S(1)} collective-permute-done((f32[192,128]{1,0:T(8,128)S(1)}, f32[192,128]{1,0:T(8,128)S(1)}, u32[]{:S(2)}, u32[]{:S(2)}) %collective-permute-start.20) | collective-permute-done | bytes 98336 | tf_op jit(solution)/shard_map/ppermute | solution.py:622
  44.6 1.4 %shard_map.97 = (f32[128,256]{1,0:T(8,128)S(1)}, f32[192,128]{1,0:T(8,128)S(1)}) custom-call(f32[192,128]{1,0:T(8,128)S(1)} %get-tuple-element.48.refs_0_, f32[192,128]{1,0:T(8,128)S(1)} %get-tuple-element.51.refs_1_, f32[192,128]{1,0:T(8,128)S(1)} %get-tuple-element.52.refs_2_, f32[192,128]{1,0:T(8,128)S(1)} %shard_map.96.refs_3_, ...), custom_call_target="tpu_custom_call" | custom-call | flops 20000000 | bytes 4849664 | tf_op jit(solution)/shard_map/pallas_call | solution.py:600
  46.1 2.1 %collective-permute-start.27 = (f32[192,128]{1,0:T(8,128)S(1)}, f32[192,128]{1,0:T(8,128)S(1)}, u32[]{:S(2)}, u32[]{:S(2)}) collective-permute-start(f32[192,128]{1,0:T(8,128)S(1)} %get-tuple-element.53.refs_0_), channel_id=1, source_target_pairs={{0,6},{1,7},{2,4},{3,5},{4,2},{5,3},{6,0},{7,1},{8,14},{9,15},{10,... | collective-permute-start | bytes 294920 | tf_op jit(solution)/shard_map/ppermute | solution.py:614
  48.4 1.6 %collective-permute-start.25 = (f32[128,128]{1,0:T(8,128)S(1)}, f32[128,128]{1,0:T(8,128)S(1)}, u32[]{:S(2)}, u32[]{:S(2)}) collective-permute-start(f32[128,128]{1,0:T(8,128)S(1)} %shard_map.98), channel_id=1, source_target_pairs={{0,8},{8,0},{16,24},{24,16},{1,9},{9,1},{17,25},{25,17},{2,10},{10... | collective-permute-start | bytes 196616 | tf_op jit(solution)/shard_map/ppermute | solution.py:637
  50.0 2.4 %collective-permute-start.23 = (f32[192,128]{1,0:T(8,128)S(1)}, f32[192,128]{1,0:T(8,128)S(1)}, u32[]{:S(2)}, u32[]{:S(2)}) collective-permute-start(f32[192,128]{1,0:T(8,128)S(1)} %get-tuple-element.53.refs_0_), channel_id=1, source_target_pairs={{0,2},{1,3},{2,0},{3,1},{4,6},{5,7},{6,4},{7,5},{8,10},{9,11},{10,... | collective-permute-start | bytes 294920 | tf_op jit(solution)/shard_map/ppermute | solution.py:614
  52.7 1.6 %collective-permute-start.26 = (f32[128,128]{1,0:T(8,128)S(1)}, f32[128,128]{1,0:T(8,128)S(1)}, u32[]{:S(2)}, u32[]{:S(2)}) collective-permute-start(f32[128,128]{1,0:T(8,128)S(1)} %add.7.one_ref), channel_id=1, source_target_pairs={{0,16},{8,24},{16,0},{24,8},{1,17},{9,25},{17,1},{25,9},{2,18},{10... | collective-permute-start | bytes 196616 | tf_op jit(solution)/shard_map/ppermute | solution.py:639
  54.3 2.7 %collective-permute-done.26.two_ref = f32[128,128]{1,0:T(8,128)S(1)} collective-permute-done((f32[128,128]{1,0:T(8,128)S(1)}, f32[128,128]{1,0:T(8,128)S(1)}, u32[]{:S(2)}, u32[]{:S(2)}) %collective-permute-start.26) | collective-permute-done | bytes 65568 | tf_op jit(solution)/shard_map/ppermute | solution.py:639
  58.2 0.8 %collective-permute-done.29.refs_5_ = f32[192,128]{1,0:T(8,128)S(1)} collective-permute-done((f32[192,128]{1,0:T(8,128)S(1)}, f32[192,128]{1,0:T(8,128)S(1)}, u32[]{:S(2)}, u32[]{:S(2)}) %collective-permute-start.29) | collective-permute-done | bytes 98336 | tf_op jit(solution)/shard_map/ppermute | solution.py:622
  59.9 2.5 %collective-permute-start.34 = (f32[40,128]{1,0:T(8,128)S(1)}, f32[40,128]{1,0:T(8,128)S(1)}, u32[]{:S(2)}, u32[]{:S(2)}) collective-permute-start(f32[40,128]{1,0:T(8,128)S(1)} %get-tuple-element.63.refs_0_), channel_id=1, source_target_pairs={{0,24},{8,16},{16,8},{24,0},{1,25},{9,17},{17,9},{25,1},{2,26},{10... | collective-permute-start | bytes 61448 | tf_op jit(solution)/shard_map/ppermute | solution.py:629
  63.4 1.0 %shard_map.103 = f32[8,32,64]{2,1,0:T(8,128)} custom-call(f32[128,128]{1,0:T(8,128)S(1)} %get-tuple-element.62.gains_ref), custom_call_target="tpu_custom_call" | custom-call | flops 20000000 | bytes 131072 | tf_op jit(solution)/shard_map/pallas_call | solution.py:600
  64.6 1.6 %collective-permute-done.33.refs_2_ = f32[40,128]{1,0:T(8,128)S(1)} collective-permute-done((f32[40,128]{1,0:T(8,128)S(1)}, f32[40,128]{1,0:T(8,128)S(1)}, u32[]{:S(2)}, u32[]{:S(2)}) %collective-permute-start.33) | collective-permute-done | bytes 20512 | tf_op jit(solution)/shard_map/ppermute | solution.py:629
  66.7 0.9 %shard_map.104 = f32[9,8,64]{2,1,0:T(8,128)} custom-call(f32[40,128]{1,0:T(8,128)S(1)} %get-tuple-element.63.refs_0_, f32[40,128]{1,0:T(8,128)S(1)} %collective-permute-done.32.refs_1_, f32[40,128]{1,0:T(8,128)S(1)} %collective-permute-done.33.refs_2_, f32[40,128]{1,0:T(8,128)S(1)} %collective-permute-done.34.refs_3_, ...), custom_call_target="tpu_custom_call" | custom-call | flops 20000000 | bytes 165888 | tf_op jit(solution)/shard_map/pallas_call | solution.py:600
  (59 shorter events, 9.8 us)
Async XLA Ops:
  1.9 12.2 %collective-permute-start.3 = (f32[136,128]{1,0:T(8,128)S(1)}, f32[136,128]{1,0:T(8,128)S(1)}, u32[]{:S(2)}, u32[]{:S(2)}) collective-permute-start(f32[136,128]{1,0:T(8,128)S(1)} %shard_map.86.refs_0_), channel_id=1, source_target_pairs={{0,1},{1,0},{2,3},{3,2},{4,5},{5,4},{6,7},{7,6},{8,9},{9,8},{10,11... | collective-permute-start | bytes 208904 | tf_op jit(solution)/shard_map/ppermute | solution.py:622
  2.5 11.1 %collective-permute-start.2 = (f32[136,128]{1,0:T(8,128)S(1)}, f32[136,128]{1,0:T(8,128)S(1)}, u32[]{:S(2)}, u32[]{:S(2)}) collective-permute-start(f32[136,128]{1,0:T(8,128)S(1)} %shard_map.86.refs_0_), channel_id=1, source_target_pairs={{0,6},{1,7},{2,4},{3,5},{4,2},{5,3},{6,0},{7,1},{8,14},{9,15},{10,... | collective-permute-start | bytes 208904 | tf_op jit(solution)/shard_map/ppermute | solution.py:614
  7.1 6.4 %collective-permute-start.1 = (f32[136,128]{1,0:T(8,128)S(1)}, f32[136,128]{1,0:T(8,128)S(1)}, u32[]{:S(2)}, u32[]{:S(2)}) collective-permute-start(f32[136,128]{1,0:T(8,128)S(1)} %shard_map.86.refs_0_), channel_id=1, source_target_pairs={{0,4},{1,5},{2,6},{3,7},{4,0},{5,1},{6,2},{7,3},{8,12},{9,13},{10,... | collective-permute-start | bytes 208904 | tf_op jit(solution)/shard_map/ppermute | solution.py:614
  7.1 6.4 %collective-permute-start = (f32[136,128]{1,0:T(8,128)S(1)}, f32[136,128]{1,0:T(8,128)S(1)}, u32[]{:S(2)}, u32[]{:S(2)}) collective-permute-start(f32[136,128]{1,0:T(8,128)S(1)} %shard_map.86.refs_0_), channel_id=1, source_target_pairs={{0,2},{1,3},{2,0},{3,1},{4,6},{5,7},{6,4},{7,5},{8,10},{9,11},{10,... | collective-permute-start | bytes 208904 | tf_op jit(solution)/shard_map/ppermute | solution.py:614
  13.6 1.4 %collective-permute-start.4 = (f32[136,128]{1,0:T(8,128)S(1)}, f32[136,128]{1,0:T(8,128)S(1)}, u32[]{:S(2)}, u32[]{:S(2)}) collective-permute-start(f32[136,128]{1,0:T(8,128)S(1)} %get-tuple-element.34.refs_1_), channel_id=1, source_target_pairs={{0,1},{1,0},{2,3},{3,2},{4,5},{5,4},{6,7},{7,6},{8,9},{9,8},{10,11... | collective-permute-start | bytes 208904 | tf_op jit(solution)/shard_map/ppermute | solution.py:622
  13.6 1.4 %collective-permute-start.6 = (f32[136,128]{1,0:T(8,128)S(1)}, f32[136,128]{1,0:T(8,128)S(1)}, u32[]{:S(2)}, u32[]{:S(2)}) collective-permute-start(f32[136,128]{1,0:T(8,128)S(1)} %collective-permute-done.2.refs_3_), channel_id=1, source_target_pairs={{0,1},{1,0},{2,3},{3,2},{4,5},{5,4},{6,7},{7,6},{8,9},{9,8},{10,11... | collective-permute-start | bytes 208904 | tf_op jit(solution)/shard_map/ppermute | solution.py:622
  16.6 9.4 %collective-permute-start.8 = (f32[192,128]{1,0:T(8,128)S(1)}, f32[192,128]{1,0:T(8,128)S(1)}, u32[]{:S(2)}, u32[]{:S(2)}) collective-permute-start(f32[192,128]{1,0:T(8,128)S(1)} %get-tuple-element.38.refs_0_), channel_id=1, source_target_pairs={{0,4},{1,5},{2,6},{3,7},{4,0},{5,1},{6,2},{7,3},{8,12},{9,13},{10,... | collective-permute-start | bytes 294920 | tf_op jit(solution)/shard_map/ppermute | solution.py:614
  17.8 8.2 %collective-permute-start.7 = (f32[192,128]{1,0:T(8,128)S(1)}, f32[192,128]{1,0:T(8,128)S(1)}, u32[]{:S(2)}, u32[]{:S(2)}) collective-permute-start(f32[192,128]{1,0:T(8,128)S(1)} %get-tuple-element.38.refs_0_), channel_id=1, source_target_pairs={{0,2},{1,3},{2,0},{3,1},{4,6},{5,7},{6,4},{7,5},{8,10},{9,11},{10,... | collective-permute-start | bytes 294920 | tf_op jit(solution)/shard_map/ppermute | solution.py:614
  19.8 7.6 %collective-permute-start.9 = (f32[192,128]{1,0:T(8,128)S(1)}, f32[192,128]{1,0:T(8,128)S(1)}, u32[]{:S(2)}, u32[]{:S(2)}) collective-permute-start(f32[192,128]{1,0:T(8,128)S(1)} %get-tuple-element.38.refs_0_), channel_id=1, source_target_pairs={{0,6},{1,7},{2,4},{3,5},{4,2},{5,3},{6,0},{7,1},{8,14},{9,15},{10,... | collective-permute-start | bytes 294920 | tf_op jit(solution)/shard_map/ppermute | solution.py:614
  21.1 6.8 %collective-permute-start.10 = (f32[192,128]{1,0:T(8,128)S(1)}, f32[192,128]{1,0:T(8,128)S(1)}, u32[]{:S(2)}, u32[]{:S(2)}) collective-permute-start(f32[192,128]{1,0:T(8,128)S(1)} %get-tuple-element.38.refs_0_), channel_id=1, source_target_pairs={{0,1},{1,0},{2,3},{3,2},{4,5},{5,4},{6,7},{7,6},{8,9},{9,8},{10,11... | collective-permute-start | bytes 294920 | tf_op jit(solution)/shard_map/ppermute | solution.py:622
  26.0 2.7 %collective-permute-start.11 = (f32[192,128]{1,0:T(8,128)S(1)}, f32[192,128]{1,0:T(8,128)S(1)}, u32[]{:S(2)}, u32[]{:S(2)}) collective-permute-start(f32[192,128]{1,0:T(8,128)S(1)} %get-tuple-element.43.refs_1_), channel_id=1, source_target_pairs={{0,1},{1,0},{2,3},{3,2},{4,5},{5,4},{6,7},{7,6},{8,9},{9,8},{10,11... | collective-permute-start | bytes 294920 | tf_op jit(solution)/shard_map/ppermute | solution.py:622
  27.4 1.5 %collective-permute-start.12 = (f32[192,128]{1,0:T(8,128)S(1)}, f32[192,128]{1,0:T(8,128)S(1)}, u32[]{:S(2)}, u32[]{:S(2)}) collective-permute-start(f32[192,128]{1,0:T(8,128)S(1)} %get-tuple-element.44.refs_2_), channel_id=1, source_target_pairs={{0,1},{1,0},{2,3},{3,2},{4,5},{5,4},{6,7},{7,6},{8,9},{9,8},{10,11... | collective-permute-start | bytes 294920 | tf_op jit(solution)/shard_map/ppermute | solution.py:622
  30.3 8.4 %collective-permute-start.18 = (f32[192,128]{1,0:T(8,128)S(1)}, f32[192,128]{1,0:T(8,128)S(1)}, u32[]{:S(2)}, u32[]{:S(2)}) collective-permute-start(f32[192,128]{1,0:T(8,128)S(1)} %get-tuple-element.48.refs_0_), channel_id=1, source_target_pairs={{0,6},{1,7},{2,4},{3,5},{4,2},{5,3},{6,0},{7,1},{8,14},{9,15},{10,... | collective-permute-start | bytes 294920 | tf_op jit(solution)/shard_map/ppermute | solution.py:614
  32.7 4.4 %collective-permute-start.16 = (f32[144,128]{1,0:T(8,128)S(1)}, f32[144,128]{1,0:T(8,128)S(1)}, u32[]{:S(2)}, u32[]{:S(2)}) collective-permute-start(f32[144,128]{1,0:T(8,128)S(1)} %shard_map.93), channel_id=1, source_target_pairs={{0,8},{8,0},{16,24},{24,16},{1,9},{9,1},{17,25},{25,17},{2,10},{10... | collective-permute-start | bytes 221192 | tf_op jit(solution)/shard_map/ppermute | solution.py:637
  34.2 9.4 %collective-permute-start.19 = (f32[192,128]{1,0:T(8,128)S(1)}, f32[192,128]{1,0:T(8,128)S(1)}, u32[]{:S(2)}, u32[]{:S(2)}) collective-permute-start(f32[192,128]{1,0:T(8,128)S(1)} %get-tuple-element.48.refs_0_), channel_id=1, source_target_pairs={{0,1},{1,0},{2,3},{3,2},{4,5},{5,4},{6,7},{7,6},{8,9},{9,8},{10,11... | collective-permute-start | bytes 294920 | tf_op jit(solution)/shard_map/ppermute | solution.py:622
  34.2 8.9 %collective-permute-start.15 = (f32[192,128]{1,0:T(8,128)S(1)}, f32[192,128]{1,0:T(8,128)S(1)}, u32[]{:S(2)}, u32[]{:S(2)}) collective-permute-start(f32[192,128]{1,0:T(8,128)S(1)} %get-tuple-element.48.refs_0_), channel_id=1, source_target_pairs={{0,4},{1,5},{2,6},{3,7},{4,0},{5,1},{6,2},{7,3},{8,12},{9,13},{10,... | collective-permute-start | bytes 294920 | tf_op jit(solution)/shard_map/ppermute | solution.py:614
  35.7 7.5 %collective-permute-start.14 = (f32[192,128]{1,0:T(8,128)S(1)}, f32[192,128]{1,0:T(8,128)S(1)}, u32[]{:S(2)}, u32[]{:S(2)}) collective-permute-start(f32[192,128]{1,0:T(8,128)S(1)} %get-tuple-element.48.refs_0_), channel_id=1, source_target_pairs={{0,2},{1,3},{2,0},{3,1},{4,6},{5,7},{6,4},{7,5},{8,10},{9,11},{10,... | collective-permute-start | bytes 294920 | tf_op jit(solution)/shard_map/ppermute | solution.py:614
  37.1 4.4 %collective-permute-start.17 = (f32[144,128]{1,0:T(8,128)S(1)}, f32[144,128]{1,0:T(8,128)S(1)}, u32[]{:S(2)}, u32[]{:S(2)}) collective-permute-start(f32[144,128]{1,0:T(8,128)S(1)} %add.6.one_ref), channel_id=1, source_target_pairs={{0,16},{8,24},{16,0},{24,8},{1,17},{9,25},{17,1},{25,9},{2,18},{10... | collective-permute-start | bytes 221192 | tf_op jit(solution)/shard_map/ppermute | solution.py:639
  38.7 5.0 %collective-permute-start.22 = (f32[192,128]{1,0:T(8,128)S(1)}, f32[192,128]{1,0:T(8,128)S(1)}, u32[]{:S(2)}, u32[]{:S(2)}) collective-permute-start(f32[192,128]{1,0:T(8,128)S(1)} %shard_map.96.refs_3_), channel_id=1, source_target_pairs={{0,1},{1,0},{2,3},{3,2},{4,5},{5,4},{6,7},{7,6},{8,9},{9,8},{10,11... | collective-permute-start | bytes 294920 | tf_op jit(solution)/shard_map/ppermute | solution.py:622
  43.1 1.5 %collective-permute-start.21 = (f32[192,128]{1,0:T(8,128)S(1)}, f32[192,128]{1,0:T(8,128)S(1)}, u32[]{:S(2)}, u32[]{:S(2)}) collective-permute-start(f32[192,128]{1,0:T(8,128)S(1)} %get-tuple-element.52.refs_2_), channel_id=1, source_target_pairs={{0,1},{1,0},{2,3},{3,2},{4,5},{5,4},{6,7},{7,6},{8,9},{9,8},{10,11... | collective-permute-start | bytes 294920 | tf_op jit(solution)/shard_map/ppermute | solution.py:622
  46.1 8.3 %collective-permute-start.27 = (f32[192,128]{1,0:T(8,128)S(1)}, f32[192,128]{1,0:T(8,128)S(1)}, u32[]{:S(2)}, u32[]{:S(2)}) collective-permute-start(f32[192,128]{1,0:T(8,128)S(1)} %get-tuple-element.53.refs_0_), channel_id=1, source_target_pairs={{0,6},{1,7},{2,4},{3,5},{4,2},{5,3},{6,0},{7,1},{8,14},{9,15},{10,... | collective-permute-start | bytes 294920 | tf_op jit(solution)/shard_map/ppermute | solution.py:614
  48.4 4.3 %collective-permute-start.25 = (f32[128,128]{1,0:T(8,128)S(1)}, f32[128,128]{1,0:T(8,128)S(1)}, u32[]{:S(2)}, u32[]{:S(2)}) collective-permute-start(f32[128,128]{1,0:T(8,128)S(1)} %shard_map.98), channel_id=1, source_target_pairs={{0,8},{8,0},{16,24},{24,16},{1,9},{9,1},{17,25},{25,17},{2,10},{10... | collective-permute-start | bytes 196616 | tf_op jit(solution)/shard_map/ppermute | solution.py:637
  50.0 8.2 %collective-permute-start.28 = (f32[192,128]{1,0:T(8,128)S(1)}, f32[192,128]{1,0:T(8,128)S(1)}, u32[]{:S(2)}, u32[]{:S(2)}) collective-permute-start(f32[192,128]{1,0:T(8,128)S(1)} %get-tuple-element.53.refs_0_), channel_id=1, source_target_pairs={{0,1},{1,0},{2,3},{3,2},{4,5},{5,4},{6,7},{7,6},{8,9},{9,8},{10,11... | collective-permute-start | bytes 294920 | tf_op jit(solution)/shard_map/ppermute | solution.py:622
  50.0 7.6 %collective-permute-start.24 = (f32[192,128]{1,0:T(8,128)S(1)}, f32[192,128]{1,0:T(8,128)S(1)}, u32[]{:S(2)}, u32[]{:S(2)}) collective-permute-start(f32[192,128]{1,0:T(8,128)S(1)} %get-tuple-element.53.refs_0_), channel_id=1, source_target_pairs={{0,4},{1,5},{2,6},{3,7},{4,0},{5,1},{6,2},{7,3},{8,12},{9,13},{10,... | collective-permute-start | bytes 294920 | tf_op jit(solution)/shard_map/ppermute | solution.py:614
  50.0 7.7 %collective-permute-start.23 = (f32[192,128]{1,0:T(8,128)S(1)}, f32[192,128]{1,0:T(8,128)S(1)}, u32[]{:S(2)}, u32[]{:S(2)}) collective-permute-start(f32[192,128]{1,0:T(8,128)S(1)} %get-tuple-element.53.refs_0_), channel_id=1, source_target_pairs={{0,2},{1,3},{2,0},{3,1},{4,6},{5,7},{6,4},{7,5},{8,10},{9,11},{10,... | collective-permute-start | bytes 294920 | tf_op jit(solution)/shard_map/ppermute | solution.py:614
  52.7 4.3 %collective-permute-start.26 = (f32[128,128]{1,0:T(8,128)S(1)}, f32[128,128]{1,0:T(8,128)S(1)}, u32[]{:S(2)}, u32[]{:S(2)}) collective-permute-start(f32[128,128]{1,0:T(8,128)S(1)} %add.7.one_ref), channel_id=1, source_target_pairs={{0,16},{8,24},{16,0},{24,8},{1,17},{9,25},{17,1},{25,9},{2,18},{10... | collective-permute-start | bytes 196616 | tf_op jit(solution)/shard_map/ppermute | solution.py:639
  54.3 3.9 %collective-permute-start.31 = (f32[192,128]{1,0:T(8,128)S(1)}, f32[192,128]{1,0:T(8,128)S(1)}, u32[]{:S(2)}, u32[]{:S(2)}) collective-permute-start(f32[192,128]{1,0:T(8,128)S(1)} %shard_map.101.refs_3_), channel_id=1, source_target_pairs={{0,1},{1,0},{2,3},{3,2},{4,5},{5,4},{6,7},{7,6},{8,9},{9,8},{10,11... | collective-permute-start | bytes 294920 | tf_op jit(solution)/shard_map/ppermute | solution.py:622
  57.6 1.3 %collective-permute-start.29 = (f32[192,128]{1,0:T(8,128)S(1)}, f32[192,128]{1,0:T(8,128)S(1)}, u32[]{:S(2)}, u32[]{:S(2)}) collective-permute-start(f32[192,128]{1,0:T(8,128)S(1)} %get-tuple-element.58.refs_1_), channel_id=1, source_target_pairs={{0,1},{1,0},{2,3},{3,2},{4,5},{5,4},{6,7},{7,6},{8,9},{9,8},{10,11... | collective-permute-start | bytes 294920 | tf_op jit(solution)/shard_map/ppermute | solution.py:622
  57.7 1.4 %collective-permute-start.30 = (f32[192,128]{1,0:T(8,128)S(1)}, f32[192,128]{1,0:T(8,128)S(1)}, u32[]{:S(2)}, u32[]{:S(2)}) collective-permute-start(f32[192,128]{1,0:T(8,128)S(1)} %get-tuple-element.59.refs_2_), channel_id=1, source_target_pairs={{0,1},{1,0},{2,3},{3,2},{4,5},{5,4},{6,7},{7,6},{8,9},{9,8},{10,11... | collective-permute-start | bytes 294920 | tf_op jit(solution)/shard_map/ppermute | solution.py:622
  59.9 4.7 %collective-permute-start.34 = (f32[40,128]{1,0:T(8,128)S(1)}, f32[40,128]{1,0:T(8,128)S(1)}, u32[]{:S(2)}, u32[]{:S(2)}) collective-permute-start(f32[40,128]{1,0:T(8,128)S(1)} %get-tuple-element.63.refs_0_), channel_id=1, source_target_pairs={{0,24},{8,16},{16,8},{24,0},{1,25},{9,17},{17,9},{25,1},{2,26},{10... | collective-permute-start | bytes 61448 | tf_op jit(solution)/shard_map/ppermute | solution.py:629
  62.4 3.8 %collective-permute-start.33 = (f32[40,128]{1,0:T(8,128)S(1)}, f32[40,128]{1,0:T(8,128)S(1)}, u32[]{:S(2)}, u32[]{:S(2)}) collective-permute-start(f32[40,128]{1,0:T(8,128)S(1)} %get-tuple-element.63.refs_0_), channel_id=1, source_target_pairs={{0,16},{8,24},{16,0},{24,8},{1,17},{9,25},{17,1},{25,9},{2,18},{10... | collective-permute-start | bytes 61448 | tf_op jit(solution)/shard_map/ppermute | solution.py:629
  62.9 3.8 %collective-permute-start.32 = (f32[40,128]{1,0:T(8,128)S(1)}, f32[40,128]{1,0:T(8,128)S(1)}, u32[]{:S(2)}, u32[]{:S(2)}) collective-permute-start(f32[40,128]{1,0:T(8,128)S(1)} %get-tuple-element.63.refs_0_), channel_id=1, source_target_pairs={{0,8},{8,0},{16,24},{24,16},{1,9},{9,1},{17,25},{25,17},{2,10},{10... | collective-permute-start | bytes 61448 | tf_op jit(solution)/shard_map/ppermute | solution.py:629
  (3 other events, 3.9 us)

commit v8 on v7

--- a/solution.py
+++ b/solution.py
@@ -732,7 +732,7 @@
     z, dual, inverse = call(
         first_consensus_kernel, (*sum_band(part), gains, basis), [wide, wide, narrow]
     )
-    pieces = share_base(message, last=(z,), ties=(1, 2), ahead=True)
+    pieces = share_base(message, last=(z,), ties=(2,), ahead=True)
     gains, message = call(
         functools.partial(step_kernel, count),
         (*pieces, select, z, pen, scale, products),
@@ -741,7 +741,7 @@
     )
     (part,) = call(total_kernel, (gains, dual, basis), [narrow])
     z, dual = call(consensus_kernel, (*sum_band(part), gains, dual, basis, inverse), [wide, wide])
-    pieces = share_base(message, last=(z,), ties=(1, 2), ahead=True)
+    pieces = share_base(message, last=(z,), ties=(2,), ahead=True)
     chunks = 8 * owned // LANES
     gains, part = call(
         functools.partial(last_kernel, count, blocks, intervals),

time: 67.8 us -> 67.4 us (level)
  starting transfers between devices: 31.2 us -> 30.1 us
  waiting for transfers between devices: 20.5 us -> 21.2 us
    ppermute x12, waiting for transfers between devices: 7.8 us -> 11.7 us  [share_base(): lax.ppermute(x, 'base', [(d, d ^ 2 * k) for d in range(devices)])]
    ppermute x2, waiting for transfers between devices: 5.57 us -> 2.07 us  [sum_band(): return (x, lax.ppermute(x, 'band', [(d, d ^ step) for d in range(devices)]))]
    ppermute x16, starting transfers between devices: 2.68 us -> 1.63 us  [share_base(): lax.ppermute(y, 'base', [(d, d ^ 1) for d in range(devices)])]
    ppermute x16, waiting for transfers between devices: 4.02 us -> 4.7 us  [share_base(): lax.ppermute(y, 'base', [(d, d ^ 1) for d in range(devices)])]
  transfers between devices with their start and end apart: 35 -> 35, of which waited for: 19 -> 20; matrix products, arithmetic and copies ran while one was open for 0% -> 0% of each run, Pallas kernels for 12% -> 12%
where the time goes in v8:
time: 67.4 us; the launch traced here: 67.2 us
  starting transfers between devices  30.1 us (45%)
  waiting for transfers between devices  21.2 us (31%)
  Pallas kernels  15.2 us (23%)
  between operations  0.77 us (1%)
    ppermute x12, starting transfers between devices, share_base(): lax.ppermute(x, 'base', [(d, d ^ 2 * k) for d in range(devices)])  18.7 us
    pallas_call x13, Pallas kernels, call(): pl.pallas_call(kernel, out_shape=shapes, in_specs=in_specs, out_specs=[vm...  15.2 us
    ppermute x12, waiting for transfers between devices, share_base(): lax.ppermute(x, 'base', [(d, d ^ 2 * k) for d in range(devices)])  11.7 us
    ppermute x16, waiting for transfers between devices, share_base(): lax.ppermute(y, 'base', [(d, d ^ 1) for d in range(devices)])  4.7 us
    ppermute x3, starting transfers between devices, share_band(): lax.ppermute(x, 'band', [(d, d ^ k) for d in range(devices)])  3.52 us
    ppermute x2, starting transfers between devices, sum_band(): return (x, lax.ppermute(x, 'band', [(d, d ^ step) for d in range(devices)]))  3.17 us
    ppermute x2, starting transfers between devices, sum_band(): x = x + lax.ppermute(x, 'band', [(d, d ^ step) for d in range(devices)])  3.11 us
    ppermute x2, waiting for transfers between devices, sum_band(): return (x, lax.ppermute(x, 'band', [(d, d ^ step) for d in range(devices)]))  2.07 us
  transfers between devices with their start and end apart: 35, of which 20 were waited for; matrix products, arithmetic and copies ran while one was open for 0% of the time, Pallas kernels for 12%

profile of v8, /device:TPU:0, one launch (start us, length us, event | category | flops | bytes accessed | tf_op | source)
XLA Modules:
  0.0 67.2 jit_solution(9592253630468927561)
XLA Ops:
  0.6 1.3 %shard_map.86.refs_0_ = f32[136,128]{1,0:T(8,128)S(1)} custom-call(s32[2,2]{1,0:T(2,128)} %pair_hbm.3, f32[8,32,64]{2,1,0:T(8,128)} %start_hbm.1, f32[1,64]{1,0:T(1,128)} %bitcast.6, s32[2,256]{1,0:T(2,128)} %flag_hbm.3), custom_call_target="tpu_custom_call" | custom-call | flops 20000000 | bytes 137488 | tf_op jit(solution)/shard_map/pallas_call | solution.py:600
  2.5 4.7 %collective-permute-start.2 = (f32[136,128]{1,0:T(8,128)S(1)}, f32[136,128]{1,0:T(8,128)S(1)}, u32[]{:S(2)}, u32[]{:S(2)}) collective-permute-start(f32[136,128]{1,0:T(8,128)S(1)} %shard_map.86.refs_0_), channel_id=1, source_target_pairs={{0,6},{1,7},{2,4},{3,5},{4,2},{5,3},{6,0},{7,1},{8,14},{9,15},{10,... | collective-permute-start | bytes 208904 | tf_op jit(solution)/shard_map/ppermute | solution.py:614
  7.8 4.4 %shard_map.87 = (f32[48,8,16,128]{3,2,1,0:T(8,128)S(1)}, f32[256,128]{1,0:T(8,128)S(1)}, f32[256,128]{1,0:T(8,128)S(1)}, f32[256,128]{1,0:T(8,128)S(1)}, f32[8,256]{1,0:T(8,128)S(1)}) custom-call(s32[2,2]{1,0:T(2,128)} %pair_hbm.3, s32[1,64]{1,0:T(1,128)} %bitcast.9, s32[2,256]{1,0:T(2,128)} %flag_hbm.3, bf16[8,128,256]{2,1,0:T(8,128)(2,1)} %bitcast.7, ...), custom_call_target="tpu_custom_call" | custom-call | flops 2000000000 | bytes 4598032 | tf_op jit(solution)/shard_map/pallas_call | solution.py:600
  12.2 1.3 %collective-permute-done.1.refs_1_ = f32[136,128]{1,0:T(8,128)S(1)} collective-permute-done((f32[136,128]{1,0:T(8,128)S(1)}, f32[136,128]{1,0:T(8,128)S(1)}, u32[]{:S(2)}, u32[]{:S(2)}) %collective-permute-start.1) | collective-permute-done | bytes 69664 | tf_op jit(solution)/shard_map/ppermute | solution.py:614
  15.3 1.3 %shard_map.89 = (f32[128,128]{1,0:T(8,128)S(1)}, f32[192,128]{1,0:T(8,128)S(1)}) custom-call(f32[136,128]{1,0:T(8,128)S(1)} %shard_map.86.refs_0_, f32[136,128]{1,0:T(8,128)S(1)} %get-tuple-element.30.refs_1_, f32[136,128]{1,0:T(8,128)S(1)} %get-tuple-element.31.refs_2_, f32[136,128]{1,0:T(8,128)S(1)} %collective-permute-done.2.refs_3_, ...), custom_call_target="tpu_custom_call" | custom-call | flops 20000000 | bytes 3997696 | tf_op jit(solution)/shard_map/pallas_call | solution.py:600
  16.6 1.1 %collective-permute-start.8 = (f32[192,128]{1,0:T(8,128)S(1)}, f32[192,128]{1,0:T(8,128)S(1)}, u32[]{:S(2)}, u32[]{:S(2)}) collective-permute-start(f32[192,128]{1,0:T(8,128)S(1)} %get-tuple-element.34.refs_0_), channel_id=1, source_target_pairs={{0,4},{1,5},{2,6},{3,7},{4,0},{5,1},{6,2},{7,3},{8,12},{9,13},{10,... | collective-permute-start | bytes 294920 | tf_op jit(solution)/shard_map/ppermute | solution.py:614
  17.8 2.0 %collective-permute-start.7 = (f32[192,128]{1,0:T(8,128)S(1)}, f32[192,128]{1,0:T(8,128)S(1)}, u32[]{:S(2)}, u32[]{:S(2)}) collective-permute-start(f32[192,128]{1,0:T(8,128)S(1)} %get-tuple-element.34.refs_0_), channel_id=1, source_target_pairs={{0,2},{1,3},{2,0},{3,1},{4,6},{5,7},{6,4},{7,5},{8,10},{9,11},{10,... | collective-permute-start | bytes 294920 | tf_op jit(solution)/shard_map/ppermute | solution.py:614
  19.8 1.3 %collective-permute-start.9 = (f32[192,128]{1,0:T(8,128)S(1)}, f32[192,128]{1,0:T(8,128)S(1)}, u32[]{:S(2)}, u32[]{:S(2)}) collective-permute-start(f32[192,128]{1,0:T(8,128)S(1)} %get-tuple-element.34.refs_0_), channel_id=1, source_target_pairs={{0,6},{1,7},{2,4},{3,5},{4,2},{5,3},{6,0},{7,1},{8,14},{9,15},{10,... | collective-permute-start | bytes 294920 | tf_op jit(solution)/shard_map/ppermute | solution.py:614
  21.6 4.4 %collective-permute-done.8.refs_1_ = f32[192,128]{1,0:T(8,128)S(1)} collective-permute-done((f32[192,128]{1,0:T(8,128)S(1)}, f32[192,128]{1,0:T(8,128)S(1)}, u32[]{:S(2)}, u32[]{:S(2)}) %collective-permute-start.8) | collective-permute-done | bytes 98336 | tf_op jit(solution)/shard_map/ppermute | solution.py:614
  26.0 1.4 %collective-permute-done.9.refs_3_ = f32[192,128]{1,0:T(8,128)S(1)} collective-permute-done((f32[192,128]{1,0:T(8,128)S(1)}, f32[192,128]{1,0:T(8,128)S(1)}, u32[]{:S(2)}, u32[]{:S(2)}) %collective-permute-start.9) | collective-permute-done | bytes 98336 | tf_op jit(solution)/shard_map/ppermute | solution.py:614
  28.9 1.5 %shard_map.92 = (f32[128,256]{1,0:T(8,128)S(1)}, f32[192,128]{1,0:T(8,128)S(1)}) custom-call(f32[192,128]{1,0:T(8,128)S(1)} %get-tuple-element.34.refs_0_, f32[192,128]{1,0:T(8,128)S(1)} %get-tuple-element.39.refs_1_, f32[192,128]{1,0:T(8,128)S(1)} %get-tuple-element.40.refs_2_, f32[192,128]{1,0:T(8,128)S(1)} %collective-permute-done.9.refs_3_, ...), custom_call_target="tpu_custom_call" | custom-call | flops 20000000 | bytes 4849664 | tf_op jit(solution)/shard_map/pallas_call | solution.py:600
  30.3 2.0 %collective-permute-start.18 = (f32[192,128]{1,0:T(8,128)S(1)}, f32[192,128]{1,0:T(8,128)S(1)}, u32[]{:S(2)}, u32[]{:S(2)}) collective-permute-start(f32[192,128]{1,0:T(8,128)S(1)} %get-tuple-element.44.refs_0_), channel_id=1, source_target_pairs={{0,6},{1,7},{2,4},{3,5},{4,2},{5,3},{6,0},{7,1},{8,14},{9,15},{10,... | collective-permute-start | bytes 294920 | tf_op jit(solution)/shard_map/ppermute | solution.py:614
  32.7 1.6 %collective-permute-start.16 = (f32[144,128]{1,0:T(8,128)S(1)}, f32[144,128]{1,0:T(8,128)S(1)}, u32[]{:S(2)}, u32[]{:S(2)}) collective-permute-start(f32[144,128]{1,0:T(8,128)S(1)} %shard_map.93), channel_id=1, source_target_pairs={{0,8},{8,0},{16,24},{24,16},{1,9},{9,1},{17,25},{25,17},{2,10},{10... | collective-permute-start | bytes 221192 | tf_op jit(solution)/shard_map/ppermute | solution.py:637
  34.2 1.5 %collective-permute-start.15 = (f32[192,128]{1,0:T(8,128)S(1)}, f32[192,128]{1,0:T(8,128)S(1)}, u32[]{:S(2)}, u32[]{:S(2)}) collective-permute-start(f32[192,128]{1,0:T(8,128)S(1)} %get-tuple-element.44.refs_0_), channel_id=1, source_target_pairs={{0,4},{1,5},{2,6},{3,7},{4,0},{5,1},{6,2},{7,3},{8,12},{9,13},{10,... | collective-permute-start | bytes 294920 | tf_op jit(solution)/shard_map/ppermute | solution.py:614
  35.7 1.0 %collective-permute-start.14 = (f32[192,128]{1,0:T(8,128)S(1)}, f32[192,128]{1,0:T(8,128)S(1)}, u32[]{:S(2)}, u32[]{:S(2)}) collective-permute-start(f32[192,128]{1,0:T(8,128)S(1)} %get-tuple-element.44.refs_0_), channel_id=1, source_target_pairs={{0,2},{1,3},{2,0},{3,1},{4,6},{5,7},{6,4},{7,5},{8,10},{9,11},{10,... | collective-permute-start | bytes 294920 | tf_op jit(solution)/shard_map/ppermute | solution.py:614
  37.1 1.6 %collective-permute-start.17 = (f32[144,128]{1,0:T(8,128)S(1)}, f32[144,128]{1,0:T(8,128)S(1)}, u32[]{:S(2)}, u32[]{:S(2)}) collective-permute-start(f32[144,128]{1,0:T(8,128)S(1)} %add.6.one_ref), channel_id=1, source_target_pairs={{0,16},{8,24},{16,0},{24,8},{1,17},{9,25},{17,1},{25,9},{2,18},{10... | collective-permute-start | bytes 221192 | tf_op jit(solution)/shard_map/ppermute | solution.py:639
  38.7 2.2 %collective-permute-done.14.refs_1_ = f32[192,128]{1,0:T(8,128)S(1)} collective-permute-done((f32[192,128]{1,0:T(8,128)S(1)}, f32[192,128]{1,0:T(8,128)S(1)}, u32[]{:S(2)}, u32[]{:S(2)}) %collective-permute-start.14) | collective-permute-done | bytes 98336 | tf_op jit(solution)/shard_map/ppermute | solution.py:614
  41.5 1.0 %shard_map.94 = (f32[128,256]{1,0:T(8,128)S(1)}, f32[128,256]{1,0:T(8,128)S(1)}, f32[128,128]{1,0:T(8,128)S(1)}) custom-call(f32[144,128]{1,0:T(8,128)S(1)} %add.6.one_ref, f32[144,128]{1,0:T(8,128)S(1)} %collective-permute-done.17.two_ref, f32[128,256]{1,0:T(8,128)S(1)} %get-tuple-element.45.gains_ref, f32[256,128]{1,0:T(8,128)S(1)} %get-tuple-element.37.refs_12_.basis_ref), custom_call_target="tpu_custom_call" | custom-call | flops 20000000 | bytes 737280 | tf_op jit(solution)/shard_map/pallas_call | solution.py:600
  43.2 1.3 %collective-permute-done.21.refs_6_ = f32[192,128]{1,0:T(8,128)S(1)} collective-permute-done((f32[192,128]{1,0:T(8,128)S(1)}, f32[192,128]{1,0:T(8,128)S(1)}, u32[]{:S(2)}, u32[]{:S(2)}) %collective-permute-start.21) | collective-permute-done | bytes 98336 | tf_op jit(solution)/shard_map/ppermute | solution.py:622
  44.4 1.5 %shard_map.97 = (f32[128,256]{1,0:T(8,128)S(1)}, f32[192,128]{1,0:T(8,128)S(1)}) custom-call(f32[192,128]{1,0:T(8,128)S(1)} %get-tuple-element.44.refs_0_, f32[192,128]{1,0:T(8,128)S(1)} %collective-permute-done.14.refs_1_, f32[192,128]{1,0:T(8,128)S(1)} %shard_map.95.refs_2_, f32[192,128]{1,0:T(8,128)S(1)} %shard_map.96.refs_3_, ...), custom_call_target="tpu_custom_call" | custom-call | flops 20000000 | bytes 4849664 | tf_op jit(solution)/shard_map/pallas_call | solution.py:600
  45.9 2.1 %collective-permute-start.27 = (f32[192,128]{1,0:T(8,128)S(1)}, f32[192,128]{1,0:T(8,128)S(1)}, u32[]{:S(2)}, u32[]{:S(2)}) collective-permute-start(f32[192,128]{1,0:T(8,128)S(1)} %get-tuple-element.47.refs_0_), channel_id=1, source_target_pairs={{0,6},{1,7},{2,4},{3,5},{4,2},{5,3},{6,0},{7,1},{8,14},{9,15},{10,... | collective-permute-start | bytes 294920 | tf_op jit(solution)/shard_map/ppermute | solution.py:614
  48.2 1.6 %collective-permute-start.25 = (f32[128,128]{1,0:T(8,128)S(1)}, f32[128,128]{1,0:T(8,128)S(1)}, u32[]{:S(2)}, u32[]{:S(2)}) collective-permute-start(f32[128,128]{1,0:T(8,128)S(1)} %shard_map.98), channel_id=1, source_target_pairs={{0,8},{8,0},{16,24},{24,16},{1,9},{9,1},{17,25},{25,17},{2,10},{10... | collective-permute-start | bytes 196616 | tf_op jit(solution)/shard_map/ppermute | solution.py:637
  49.8 2.4 %collective-permute-start.23 = (f32[192,128]{1,0:T(8,128)S(1)}, f32[192,128]{1,0:T(8,128)S(1)}, u32[]{:S(2)}, u32[]{:S(2)}) collective-permute-start(f32[192,128]{1,0:T(8,128)S(1)} %get-tuple-element.47.refs_0_), channel_id=1, source_target_pairs={{0,2},{1,3},{2,0},{3,1},{4,6},{5,7},{6,4},{7,5},{8,10},{9,11},{10,... | collective-permute-start | bytes 294920 | tf_op jit(solution)/shard_map/ppermute | solution.py:614
  52.6 1.6 %collective-permute-start.26 = (f32[128,128]{1,0:T(8,128)S(1)}, f32[128,128]{1,0:T(8,128)S(1)}, u32[]{:S(2)}, u32[]{:S(2)}) collective-permute-start(f32[128,128]{1,0:T(8,128)S(1)} %add.7.one_ref), channel_id=1, source_target_pairs={{0,16},{8,24},{16,0},{24,8},{1,17},{9,25},{17,1},{25,9},{2,18},{10... | collective-permute-start | bytes 196616 | tf_op jit(solution)/shard_map/ppermute | solution.py:639
  54.2 1.3 %collective-permute-done.23.refs_1_ = f32[192,128]{1,0:T(8,128)S(1)} collective-permute-done((f32[192,128]{1,0:T(8,128)S(1)}, f32[192,128]{1,0:T(8,128)S(1)}, u32[]{:S(2)}, u32[]{:S(2)}) %collective-permute-start.23) | collective-permute-done | bytes 98336 | tf_op jit(solution)/shard_map/ppermute | solution.py:614
  55.5 1.4 %collective-permute-done.26.two_ref = f32[128,128]{1,0:T(8,128)S(1)} collective-permute-done((f32[128,128]{1,0:T(8,128)S(1)}, f32[128,128]{1,0:T(8,128)S(1)}, u32[]{:S(2)}, u32[]{:S(2)}) %collective-permute-start.26) | collective-permute-done | bytes 65568 | tf_op jit(solution)/shard_map/ppermute | solution.py:639
  57.9 1.3 %collective-permute-done.30.refs_6_ = f32[192,128]{1,0:T(8,128)S(1)} collective-permute-done((f32[192,128]{1,0:T(8,128)S(1)}, f32[192,128]{1,0:T(8,128)S(1)}, u32[]{:S(2)}, u32[]{:S(2)}) %collective-permute-start.30) | collective-permute-done | bytes 98336 | tf_op jit(solution)/shard_map/ppermute | solution.py:622
  60.0 2.1 %collective-permute-start.34 = (f32[40,128]{1,0:T(8,128)S(1)}, f32[40,128]{1,0:T(8,128)S(1)}, u32[]{:S(2)}, u32[]{:S(2)}) collective-permute-start(f32[40,128]{1,0:T(8,128)S(1)} %get-tuple-element.55.refs_0_), channel_id=1, source_target_pairs={{0,24},{8,16},{16,8},{24,0},{1,25},{9,17},{17,9},{25,1},{2,26},{10... | collective-permute-start | bytes 61448 | tf_op jit(solution)/shard_map/ppermute | solution.py:629
  62.6 0.9 %collective-permute-start.32 = (f32[40,128]{1,0:T(8,128)S(1)}, f32[40,128]{1,0:T(8,128)S(1)}, u32[]{:S(2)}, u32[]{:S(2)}) collective-permute-start(f32[40,128]{1,0:T(8,128)S(1)} %get-tuple-element.55.refs_0_), channel_id=1, source_target_pairs={{0,8},{8,0},{16,24},{24,16},{1,9},{9,1},{17,25},{25,17},{2,10},{10... | collective-permute-start | bytes 61448 | tf_op jit(solution)/shard_map/ppermute | solution.py:629
  63.5 1.0 %shard_map.103 = f32[8,32,64]{2,1,0:T(8,128)} custom-call(f32[128,128]{1,0:T(8,128)S(1)} %get-tuple-element.54.gains_ref), custom_call_target="tpu_custom_call" | custom-call | flops 20000000 | bytes 131072 | tf_op jit(solution)/shard_map/pallas_call | solution.py:600
  64.7 1.1 %collective-permute-done.33.refs_2_ = f32[40,128]{1,0:T(8,128)S(1)} collective-permute-done((f32[40,128]{1,0:T(8,128)S(1)}, f32[40,128]{1,0:T(8,128)S(1)}, u32[]{:S(2)}, u32[]{:S(2)}) %collective-permute-start.33) | collective-permute-done | bytes 20512 | tf_op jit(solution)/shard_map/ppermute | solution.py:629
  66.3 0.9 %shard_map.104 = f32[9,8,64]{2,1,0:T(8,128)} custom-call(f32[40,128]{1,0:T(8,128)S(1)} %get-tuple-element.55.refs_0_, f32[40,128]{1,0:T(8,128)S(1)} %collective-permute-done.32.refs_1_, f32[40,128]{1,0:T(8,128)S(1)} %collective-permute-done.33.refs_2_, f32[40,128]{1,0:T(8,128)S(1)} %collective-permute-done.34.refs_3_, ...), custom_call_target="tpu_custom_call" | custom-call | flops 20000000 | bytes 165888 | tf_op jit(solution)/shard_map/pallas_call | solution.py:600
  (59 shorter events, 10.7 us)
Async XLA Ops:
  1.9 12.2 %collective-permute-start.3 = (f32[136,128]{1,0:T(8,128)S(1)}, f32[136,128]{1,0:T(8,128)S(1)}, u32[]{:S(2)}, u32[]{:S(2)}) collective-permute-start(f32[136,128]{1,0:T(8,128)S(1)} %shard_map.86.refs_0_), channel_id=1, source_target_pairs={{0,1},{1,0},{2,3},{3,2},{4,5},{5,4},{6,7},{7,6},{8,9},{9,8},{10,11... | collective-permute-start | bytes 208904 | tf_op jit(solution)/shard_map/ppermute | solution.py:622
  2.5 11.1 %collective-permute-start.2 = (f32[136,128]{1,0:T(8,128)S(1)}, f32[136,128]{1,0:T(8,128)S(1)}, u32[]{:S(2)}, u32[]{:S(2)}) collective-permute-start(f32[136,128]{1,0:T(8,128)S(1)} %shard_map.86.refs_0_), channel_id=1, source_target_pairs={{0,6},{1,7},{2,4},{3,5},{4,2},{5,3},{6,0},{7,1},{8,14},{9,15},{10,... | collective-permute-start | bytes 208904 | tf_op jit(solution)/shard_map/ppermute | solution.py:614
  7.1 6.4 %collective-permute-start.1 = (f32[136,128]{1,0:T(8,128)S(1)}, f32[136,128]{1,0:T(8,128)S(1)}, u32[]{:S(2)}, u32[]{:S(2)}) collective-permute-start(f32[136,128]{1,0:T(8,128)S(1)} %shard_map.86.refs_0_), channel_id=1, source_target_pairs={{0,4},{1,5},{2,6},{3,7},{4,0},{5,1},{6,2},{7,3},{8,12},{9,13},{10,... | collective-permute-start | bytes 208904 | tf_op jit(solution)/shard_map/ppermute | solution.py:614
  7.1 6.4 %collective-permute-start = (f32[136,128]{1,0:T(8,128)S(1)}, f32[136,128]{1,0:T(8,128)S(1)}, u32[]{:S(2)}, u32[]{:S(2)}) collective-permute-start(f32[136,128]{1,0:T(8,128)S(1)} %shard_map.86.refs_0_), channel_id=1, source_target_pairs={{0,2},{1,3},{2,0},{3,1},{4,6},{5,7},{6,4},{7,5},{8,10},{9,11},{10,... | collective-permute-start | bytes 208904 | tf_op jit(solution)/shard_map/ppermute | solution.py:614
  13.6 1.4 %collective-permute-start.4 = (f32[136,128]{1,0:T(8,128)S(1)}, f32[136,128]{1,0:T(8,128)S(1)}, u32[]{:S(2)}, u32[]{:S(2)}) collective-permute-start(f32[136,128]{1,0:T(8,128)S(1)} %get-tuple-element.30.refs_1_), channel_id=1, source_target_pairs={{0,1},{1,0},{2,3},{3,2},{4,5},{5,4},{6,7},{7,6},{8,9},{9,8},{10,11... | collective-permute-start | bytes 208904 | tf_op jit(solution)/shard_map/ppermute | solution.py:622
  13.6 1.4 %collective-permute-start.6 = (f32[136,128]{1,0:T(8,128)S(1)}, f32[136,128]{1,0:T(8,128)S(1)}, u32[]{:S(2)}, u32[]{:S(2)}) collective-permute-start(f32[136,128]{1,0:T(8,128)S(1)} %collective-permute-done.2.refs_3_), channel_id=1, source_target_pairs={{0,1},{1,0},{2,3},{3,2},{4,5},{5,4},{6,7},{7,6},{8,9},{9,8},{10,11... | collective-permute-start | bytes 208904 | tf_op jit(solution)/shard_map/ppermute | solution.py:622
  16.6 9.4 %collective-permute-start.8 = (f32[192,128]{1,0:T(8,128)S(1)}, f32[192,128]{1,0:T(8,128)S(1)}, u32[]{:S(2)}, u32[]{:S(2)}) collective-permute-start(f32[192,128]{1,0:T(8,128)S(1)} %get-tuple-element.34.refs_0_), channel_id=1, source_target_pairs={{0,4},{1,5},{2,6},{3,7},{4,0},{5,1},{6,2},{7,3},{8,12},{9,13},{10,... | collective-permute-start | bytes 294920 | tf_op jit(solution)/shard_map/ppermute | solution.py:614
  17.8 8.2 %collective-permute-start.7 = (f32[192,128]{1,0:T(8,128)S(1)}, f32[192,128]{1,0:T(8,128)S(1)}, u32[]{:S(2)}, u32[]{:S(2)}) collective-permute-start(f32[192,128]{1,0:T(8,128)S(1)} %get-tuple-element.34.refs_0_), channel_id=1, source_target_pairs={{0,2},{1,3},{2,0},{3,1},{4,6},{5,7},{6,4},{7,5},{8,10},{9,11},{10,... | collective-permute-start | bytes 294920 | tf_op jit(solution)/shard_map/ppermute | solution.py:614
  19.8 7.6 %collective-permute-start.9 = (f32[192,128]{1,0:T(8,128)S(1)}, f32[192,128]{1,0:T(8,128)S(1)}, u32[]{:S(2)}, u32[]{:S(2)}) collective-permute-start(f32[192,128]{1,0:T(8,128)S(1)} %get-tuple-element.34.refs_0_), channel_id=1, source_target_pairs={{0,6},{1,7},{2,4},{3,5},{4,2},{5,3},{6,0},{7,1},{8,14},{9,15},{10,... | collective-permute-start | bytes 294920 | tf_op jit(solution)/shard_map/ppermute | solution.py:614
  21.1 6.8 %collective-permute-start.10 = (f32[192,128]{1,0:T(8,128)S(1)}, f32[192,128]{1,0:T(8,128)S(1)}, u32[]{:S(2)}, u32[]{:S(2)}) collective-permute-start(f32[192,128]{1,0:T(8,128)S(1)} %get-tuple-element.34.refs_0_), channel_id=1, source_target_pairs={{0,1},{1,0},{2,3},{3,2},{4,5},{5,4},{6,7},{7,6},{8,9},{9,8},{10,11... | collective-permute-start | bytes 294920 | tf_op jit(solution)/shard_map/ppermute | solution.py:622
  26.0 2.7 %collective-permute-start.11 = (f32[192,128]{1,0:T(8,128)S(1)}, f32[192,128]{1,0:T(8,128)S(1)}, u32[]{:S(2)}, u32[]{:S(2)}) collective-permute-start(f32[192,128]{1,0:T(8,128)S(1)} %get-tuple-element.39.refs_1_), channel_id=1, source_target_pairs={{0,1},{1,0},{2,3},{3,2},{4,5},{5,4},{6,7},{7,6},{8,9},{9,8},{10,11... | collective-permute-start | bytes 294920 | tf_op jit(solution)/shard_map/ppermute | solution.py:622
  27.4 1.3 %collective-permute-start.13 = (f32[192,128]{1,0:T(8,128)S(1)}, f32[192,128]{1,0:T(8,128)S(1)}, u32[]{:S(2)}, u32[]{:S(2)}) collective-permute-start(f32[192,128]{1,0:T(8,128)S(1)} %collective-permute-done.9.refs_3_), channel_id=1, source_target_pairs={{0,1},{1,0},{2,3},{3,2},{4,5},{5,4},{6,7},{7,6},{8,9},{9,8},{10,11... | collective-permute-start | bytes 294920 | tf_op jit(solution)/shard_map/ppermute | solution.py:622
  27.4 1.5 %collective-permute-start.12 = (f32[192,128]{1,0:T(8,128)S(1)}, f32[192,128]{1,0:T(8,128)S(1)}, u32[]{:S(2)}, u32[]{:S(2)}) collective-permute-start(f32[192,128]{1,0:T(8,128)S(1)} %get-tuple-element.40.refs_2_), channel_id=1, source_target_pairs={{0,1},{1,0},{2,3},{3,2},{4,5},{5,4},{6,7},{7,6},{8,9},{9,8},{10,11... | collective-permute-start | bytes 294920 | tf_op jit(solution)/shard_map/ppermute | solution.py:622
  30.3 8.4 %collective-permute-start.18 = (f32[192,128]{1,0:T(8,128)S(1)}, f32[192,128]{1,0:T(8,128)S(1)}, u32[]{:S(2)}, u32[]{:S(2)}) collective-permute-start(f32[192,128]{1,0:T(8,128)S(1)} %get-tuple-element.44.refs_0_), channel_id=1, source_target_pairs={{0,6},{1,7},{2,4},{3,5},{4,2},{5,3},{6,0},{7,1},{8,14},{9,15},{10,... | collective-permute-start | bytes 294920 | tf_op jit(solution)/shard_map/ppermute | solution.py:614
  32.7 4.4 %collective-permute-start.16 = (f32[144,128]{1,0:T(8,128)S(1)}, f32[144,128]{1,0:T(8,128)S(1)}, u32[]{:S(2)}, u32[]{:S(2)}) collective-permute-start(f32[144,128]{1,0:T(8,128)S(1)} %shard_map.93), channel_id=1, source_target_pairs={{0,8},{8,0},{16,24},{24,16},{1,9},{9,1},{17,25},{25,17},{2,10},{10... | collective-permute-start | bytes 221192 | tf_op jit(solution)/shard_map/ppermute | solution.py:637
  34.2 8.9 %collective-permute-start.19 = (f32[192,128]{1,0:T(8,128)S(1)}, f32[192,128]{1,0:T(8,128)S(1)}, u32[]{:S(2)}, u32[]{:S(2)}) collective-permute-start(f32[192,128]{1,0:T(8,128)S(1)} %get-tuple-element.44.refs_0_), channel_id=1, source_target_pairs={{0,1},{1,0},{2,3},{3,2},{4,5},{5,4},{6,7},{7,6},{8,9},{9,8},{10,11... | collective-permute-start | bytes 294920 | tf_op jit(solution)/shard_map/ppermute | solution.py:622
  34.2 8.9 %collective-permute-start.15 = (f32[192,128]{1,0:T(8,128)S(1)}, f32[192,128]{1,0:T(8,128)S(1)}, u32[]{:S(2)}, u32[]{:S(2)}) collective-permute-start(f32[192,128]{1,0:T(8,128)S(1)} %get-tuple-element.44.refs_0_), channel_id=1, source_target_pairs={{0,4},{1,5},{2,6},{3,7},{4,0},{5,1},{6,2},{7,3},{8,12},{9,13},{10,... | collective-permute-start | bytes 294920 | tf_op jit(solution)/shard_map/ppermute | solution.py:614
  35.7 5.2 %collective-permute-start.14 = (f32[192,128]{1,0:T(8,128)S(1)}, f32[192,128]{1,0:T(8,128)S(1)}, u32[]{:S(2)}, u32[]{:S(2)}) collective-permute-start(f32[192,128]{1,0:T(8,128)S(1)} %get-tuple-element.44.refs_0_), channel_id=1, source_target_pairs={{0,2},{1,3},{2,0},{3,1},{4,6},{5,7},{6,4},{7,5},{8,10},{9,11},{10,... | collective-permute-start | bytes 294920 | tf_op jit(solution)/shard_map/ppermute | solution.py:614
  37.1 4.4 %collective-permute-start.17 = (f32[144,128]{1,0:T(8,128)S(1)}, f32[144,128]{1,0:T(8,128)S(1)}, u32[]{:S(2)}, u32[]{:S(2)}) collective-permute-start(f32[144,128]{1,0:T(8,128)S(1)} %add.6.one_ref), channel_id=1, source_target_pairs={{0,16},{8,24},{16,0},{24,8},{1,17},{9,25},{17,1},{25,9},{2,18},{10... | collective-permute-start | bytes 221192 | tf_op jit(solution)/shard_map/ppermute | solution.py:639
  38.7 4.5 %collective-permute-start.22 = (f32[192,128]{1,0:T(8,128)S(1)}, f32[192,128]{1,0:T(8,128)S(1)}, u32[]{:S(2)}, u32[]{:S(2)}) collective-permute-start(f32[192,128]{1,0:T(8,128)S(1)} %shard_map.96.refs_3_), channel_id=1, source_target_pairs={{0,1},{1,0},{2,3},{3,2},{4,5},{5,4},{6,7},{7,6},{8,9},{9,8},{10,11... | collective-permute-start | bytes 294920 | tf_op jit(solution)/shard_map/ppermute | solution.py:622
  40.8 2.3 %collective-permute-start.20 = (f32[192,128]{1,0:T(8,128)S(1)}, f32[192,128]{1,0:T(8,128)S(1)}, u32[]{:S(2)}, u32[]{:S(2)}) collective-permute-start(f32[192,128]{1,0:T(8,128)S(1)} %collective-permute-done.14.refs_1_), channel_id=1, source_target_pairs={{0,1},{1,0},{2,3},{3,2},{4,5},{5,4},{6,7},{7,6},{8,9},{9,8},{10,11... | collective-permute-start | bytes 294920 | tf_op jit(solution)/shard_map/ppermute | solution.py:622
  45.9 8.3 %collective-permute-start.27 = (f32[192,128]{1,0:T(8,128)S(1)}, f32[192,128]{1,0:T(8,128)S(1)}, u32[]{:S(2)}, u32[]{:S(2)}) collective-permute-start(f32[192,128]{1,0:T(8,128)S(1)} %get-tuple-element.47.refs_0_), channel_id=1, source_target_pairs={{0,6},{1,7},{2,4},{3,5},{4,2},{5,3},{6,0},{7,1},{8,14},{9,15},{10,... | collective-permute-start | bytes 294920 | tf_op jit(solution)/shard_map/ppermute | solution.py:614
  48.2 4.3 %collective-permute-start.25 = (f32[128,128]{1,0:T(8,128)S(1)}, f32[128,128]{1,0:T(8,128)S(1)}, u32[]{:S(2)}, u32[]{:S(2)}) collective-permute-start(f32[128,128]{1,0:T(8,128)S(1)} %shard_map.98), channel_id=1, source_target_pairs={{0,8},{8,0},{16,24},{24,16},{1,9},{9,1},{17,25},{25,17},{2,10},{10... | collective-permute-start | bytes 196616 | tf_op jit(solution)/shard_map/ppermute | solution.py:637
  49.8 8.1 %collective-permute-start.28 = (f32[192,128]{1,0:T(8,128)S(1)}, f32[192,128]{1,0:T(8,128)S(1)}, u32[]{:S(2)}, u32[]{:S(2)}) collective-permute-start(f32[192,128]{1,0:T(8,128)S(1)} %get-tuple-element.47.refs_0_), channel_id=1, source_target_pairs={{0,1},{1,0},{2,3},{3,2},{4,5},{5,4},{6,7},{7,6},{8,9},{9,8},{10,11... | collective-permute-start | bytes 294920 | tf_op jit(solution)/shard_map/ppermute | solution.py:622
  49.8 8.1 %collective-permute-start.24 = (f32[192,128]{1,0:T(8,128)S(1)}, f32[192,128]{1,0:T(8,128)S(1)}, u32[]{:S(2)}, u32[]{:S(2)}) collective-permute-start(f32[192,128]{1,0:T(8,128)S(1)} %get-tuple-element.47.refs_0_), channel_id=1, source_target_pairs={{0,4},{1,5},{2,6},{3,7},{4,0},{5,1},{6,2},{7,3},{8,12},{9,13},{10,... | collective-permute-start | bytes 294920 | tf_op jit(solution)/shard_map/ppermute | solution.py:614
  49.8 5.7 %collective-permute-start.23 = (f32[192,128]{1,0:T(8,128)S(1)}, f32[192,128]{1,0:T(8,128)S(1)}, u32[]{:S(2)}, u32[]{:S(2)}) collective-permute-start(f32[192,128]{1,0:T(8,128)S(1)} %get-tuple-element.47.refs_0_), channel_id=1, source_target_pairs={{0,2},{1,3},{2,0},{3,1},{4,6},{5,7},{6,4},{7,5},{8,10},{9,11},{10,... | collective-permute-start | bytes 294920 | tf_op jit(solution)/shard_map/ppermute | solution.py:614
  52.6 4.3 %collective-permute-start.26 = (f32[128,128]{1,0:T(8,128)S(1)}, f32[128,128]{1,0:T(8,128)S(1)}, u32[]{:S(2)}, u32[]{:S(2)}) collective-permute-start(f32[128,128]{1,0:T(8,128)S(1)} %add.7.one_ref), channel_id=1, source_target_pairs={{0,16},{8,24},{16,0},{24,8},{1,17},{9,25},{17,1},{25,9},{2,18},{10... | collective-permute-start | bytes 196616 | tf_op jit(solution)/shard_map/ppermute | solution.py:639
  54.2 3.7 %collective-permute-start.31 = (f32[192,128]{1,0:T(8,128)S(1)}, f32[192,128]{1,0:T(8,128)S(1)}, u32[]{:S(2)}, u32[]{:S(2)}) collective-permute-start(f32[192,128]{1,0:T(8,128)S(1)} %shard_map.101.refs_3_), channel_id=1, source_target_pairs={{0,1},{1,0},{2,3},{3,2},{4,5},{5,4},{6,7},{7,6},{8,9},{9,8},{10,11... | collective-permute-start | bytes 294920 | tf_op jit(solution)/shard_map/ppermute | solution.py:622
  55.5 2.4 %collective-permute-start.29 = (f32[192,128]{1,0:T(8,128)S(1)}, f32[192,128]{1,0:T(8,128)S(1)}, u32[]{:S(2)}, u32[]{:S(2)}) collective-permute-start(f32[192,128]{1,0:T(8,128)S(1)} %collective-permute-done.23.refs_1_), channel_id=1, source_target_pairs={{0,1},{1,0},{2,3},{3,2},{4,5},{5,4},{6,7},{7,6},{8,9},{9,8},{10,11... | collective-permute-start | bytes 294920 | tf_op jit(solution)/shard_map/ppermute | solution.py:622
  60.0 4.7 %collective-permute-start.34 = (f32[40,128]{1,0:T(8,128)S(1)}, f32[40,128]{1,0:T(8,128)S(1)}, u32[]{:S(2)}, u32[]{:S(2)}) collective-permute-start(f32[40,128]{1,0:T(8,128)S(1)} %get-tuple-element.55.refs_0_), channel_id=1, source_target_pairs={{0,24},{8,16},{16,8},{24,0},{1,25},{9,17},{17,9},{25,1},{2,26},{10... | collective-permute-start | bytes 61448 | tf_op jit(solution)/shard_map/ppermute | solution.py:629
  62.1 3.8 %collective-permute-start.33 = (f32[40,128]{1,0:T(8,128)S(1)}, f32[40,128]{1,0:T(8,128)S(1)}, u32[]{:S(2)}, u32[]{:S(2)}) collective-permute-start(f32[40,128]{1,0:T(8,128)S(1)} %get-tuple-element.55.refs_0_), channel_id=1, source_target_pairs={{0,16},{8,24},{16,0},{24,8},{1,17},{9,25},{17,1},{25,9},{2,18},{10... | collective-permute-start | bytes 61448 | tf_op jit(solution)/shard_map/ppermute | solution.py:629
  62.6 3.8 %collective-permute-start.32 = (f32[40,128]{1,0:T(8,128)S(1)}, f32[40,128]{1,0:T(8,128)S(1)}, u32[]{:S(2)}, u32[]{:S(2)}) collective-permute-start(f32[40,128]{1,0:T(8,128)S(1)} %get-tuple-element.55.refs_0_), channel_id=1, source_target_pairs={{0,8},{8,0},{16,24},{24,16},{1,9},{9,1},{17,25},{25,17},{2,10},{10... | collective-permute-start | bytes 61448 | tf_op jit(solution)/shard_map/ppermute | solution.py:629
  (3 other events, 3.9 us)

commit v9 on v8

--- a/solution.py
+++ b/solution.py
@@ -697,7 +697,7 @@
         hbm=True,
         flops=2_000_000_000,
     )
-    greetings = share_base(greeting, last=(chans,), ties=(1, 2))
+    greetings = share_base(greeting, last=(chans,))
     scratch = [
         pltpu.VMEM((12, BLOCK // 2, LANES), F32),
         pltpu.VMEM((2, 12, BLOCK // 2, LANES), F32),

time: 67.4 us -> 67.4 us (level)
    ppermute x12, waiting for transfers between devices: 11.7 us -> 10.3 us  [share_base(): lax.ppermute(x, 'base', [(d, d ^ 2 * k) for d in range(devices)])]
  transfers between devices with their start and end apart: 35 -> 35, of which waited for: 20 -> 19; matrix products, arithmetic and copies ran while one was open for 0% -> 0% of each run, Pallas kernels for 12% -> 12%
where the time goes in v9:
time: 67.4 us; the launch traced here: 67.2 us
  starting transfers between devices  30.2 us (45%)
  waiting for transfers between devices  21 us (31%)
  Pallas kernels  15.2 us (23%)
  between operations  0.82 us (1%)
    ppermute x12, starting transfers between devices, share_base(): lax.ppermute(x, 'base', [(d, d ^ 2 * k) for d in range(devices)])  18.7 us
    pallas_call x13, Pallas kernels, call(): pl.pallas_call(kernel, out_shape=shapes, in_specs=in_specs, out_specs=[vm...  15.2 us
    ppermute x12, waiting for transfers between devices, share_base(): lax.ppermute(x, 'base', [(d, d ^ 2 * k) for d in range(devices)])  10.3 us
    ppermute x16, waiting for transfers between devices, share_base(): lax.ppermute(y, 'base', [(d, d ^ 1) for d in range(devices)])  4.75 us
    ppermute x3, starting transfers between devices, share_band(): lax.ppermute(x, 'band', [(d, d ^ k) for d in range(devices)])  3.52 us
    ppermute x2, starting transfers between devices, sum_band(): return (x, lax.ppermute(x, 'band', [(d, d ^ step) for d in range(devices)]))  3.17 us
    ppermute x2, starting transfers between devices, sum_band(): x = x + lax.ppermute(x, 'band', [(d, d ^ step) for d in range(devices)])  3.11 us
    ppermute x2, waiting for transfers between devices, sum_band(): return (x, lax.ppermute(x, 'band', [(d, d ^ step) for d in range(devices)]))  2.44 us
  transfers between devices with their start and end apart: 35, of which 19 were waited for; matrix products, arithmetic and copies ran while one was open for 0% of the time, Pallas kernels for 12%

profile of v9, /device:TPU:0, one launch (start us, length us, event | category | flops | bytes accessed | tf_op | source)
XLA Modules:
  0.0 67.2 jit_solution(18231174618346620614)
XLA Ops:
  0.6 1.3 %shard_map.86.refs_0_ = f32[136,128]{1,0:T(8,128)S(1)} custom-call(s32[2,2]{1,0:T(2,128)} %pair_hbm.3, f32[8,32,64]{2,1,0:T(8,128)} %start_hbm.1, f32[1,64]{1,0:T(1,128)} %bitcast.6, s32[2,256]{1,0:T(2,128)} %flag_hbm.3), custom_call_target="tpu_custom_call" | custom-call | flops 20000000 | bytes 137488 | tf_op jit(solution)/shard_map/pallas_call | solution.py:600
  2.5 4.7 %collective-permute-start.2 = (f32[136,128]{1,0:T(8,128)S(1)}, f32[136,128]{1,0:T(8,128)S(1)}, u32[]{:S(2)}, u32[]{:S(2)}) collective-permute-start(f32[136,128]{1,0:T(8,128)S(1)} %shard_map.86.refs_0_), channel_id=1, source_target_pairs={{0,6},{1,7},{2,4},{3,5},{4,2},{5,3},{6,0},{7,1},{8,14},{9,15},{10,... | collective-permute-start | bytes 208904 | tf_op jit(solution)/shard_map/ppermute | solution.py:614
  7.8 4.4 %shard_map.87 = (f32[48,8,16,128]{3,2,1,0:T(8,128)S(1)}, f32[256,128]{1,0:T(8,128)S(1)}, f32[256,128]{1,0:T(8,128)S(1)}, f32[256,128]{1,0:T(8,128)S(1)}, f32[8,256]{1,0:T(8,128)S(1)}) custom-call(s32[2,2]{1,0:T(2,128)} %pair_hbm.3, s32[1,64]{1,0:T(1,128)} %bitcast.9, s32[2,256]{1,0:T(2,128)} %flag_hbm.3, bf16[8,128,256]{2,1,0:T(8,128)(2,1)} %bitcast.7, ...), custom_call_target="tpu_custom_call" | custom-call | flops 2000000000 | bytes 4598032 | tf_op jit(solution)/shard_map/pallas_call | solution.py:600
  13.7 1.1 %collective-permute-done.5.refs_6_ = f32[136,128]{1,0:T(8,128)S(1)} collective-permute-done((f32[136,128]{1,0:T(8,128)S(1)}, f32[136,128]{1,0:T(8,128)S(1)}, u32[]{:S(2)}, u32[]{:S(2)}) %collective-permute-start.5) | collective-permute-done | bytes 69664 | tf_op jit(solution)/shard_map/ppermute | solution.py:622
  14.8 1.3 %shard_map.89 = (f32[128,128]{1,0:T(8,128)S(1)}, f32[192,128]{1,0:T(8,128)S(1)}) custom-call(f32[136,128]{1,0:T(8,128)S(1)} %shard_map.86.refs_0_, f32[136,128]{1,0:T(8,128)S(1)} %collective-permute-done.refs_1_, f32[136,128]{1,0:T(8,128)S(1)} %shard_map.88.refs_2_, f32[136,128]{1,0:T(8,128)S(1)} %collective-permute-done.2.refs_3_, ...), custom_call_target="tpu_custom_call" | custom-call | flops 20000000 | bytes 3997696 | tf_op jit(solution)/shard_map/pallas_call | solution.py:600
  16.1 1.6 %collective-permute-start.8 = (f32[192,128]{1,0:T(8,128)S(1)}, f32[192,128]{1,0:T(8,128)S(1)}, u32[]{:S(2)}, u32[]{:S(2)}) collective-permute-start(f32[192,128]{1,0:T(8,128)S(1)} %get-tuple-element.30.refs_0_), channel_id=1, source_target_pairs={{0,4},{1,5},{2,6},{3,7},{4,0},{5,1},{6,2},{7,3},{8,12},{9,13},{10,... | collective-permute-start | bytes 294920 | tf_op jit(solution)/shard_map/ppermute | solution.py:614
  17.7 2.0 %collective-permute-start.7 = (f32[192,128]{1,0:T(8,128)S(1)}, f32[192,128]{1,0:T(8,128)S(1)}, u32[]{:S(2)}, u32[]{:S(2)}) collective-permute-start(f32[192,128]{1,0:T(8,128)S(1)} %get-tuple-element.30.refs_0_), channel_id=1, source_target_pairs={{0,2},{1,3},{2,0},{3,1},{4,6},{5,7},{6,4},{7,5},{8,10},{9,11},{10,... | collective-permute-start | bytes 294920 | tf_op jit(solution)/shard_map/ppermute | solution.py:614
  21.1 4.1 %collective-permute-done.8.refs_1_ = f32[192,128]{1,0:T(8,128)S(1)} collective-permute-done((f32[192,128]{1,0:T(8,128)S(1)}, f32[192,128]{1,0:T(8,128)S(1)}, u32[]{:S(2)}, u32[]{:S(2)}) %collective-permute-start.8) | collective-permute-done | bytes 98336 | tf_op jit(solution)/shard_map/ppermute | solution.py:614
  25.2 2.0 %collective-permute-done.9.refs_3_ = f32[192,128]{1,0:T(8,128)S(1)} collective-permute-done((f32[192,128]{1,0:T(8,128)S(1)}, f32[192,128]{1,0:T(8,128)S(1)}, u32[]{:S(2)}, u32[]{:S(2)}) %collective-permute-start.9) | collective-permute-done | bytes 98336 | tf_op jit(solution)/shard_map/ppermute | solution.py:614
  28.7 1.5 %shard_map.92 = (f32[128,256]{1,0:T(8,128)S(1)}, f32[192,128]{1,0:T(8,128)S(1)}) custom-call(f32[192,128]{1,0:T(8,128)S(1)} %get-tuple-element.30.refs_0_, f32[192,128]{1,0:T(8,128)S(1)} %get-tuple-element.35.refs_1_, f32[192,128]{1,0:T(8,128)S(1)} %get-tuple-element.36.refs_2_, f32[192,128]{1,0:T(8,128)S(1)} %collective-permute-done.9.refs_3_, ...), custom_call_target="tpu_custom_call" | custom-call | flops 20000000 | bytes 4849664 | tf_op jit(solution)/shard_map/pallas_call | solution.py:600
  30.2 2.0 %collective-permute-start.18 = (f32[192,128]{1,0:T(8,128)S(1)}, f32[192,128]{1,0:T(8,128)S(1)}, u32[]{:S(2)}, u32[]{:S(2)}) collective-permute-start(f32[192,128]{1,0:T(8,128)S(1)} %get-tuple-element.40.refs_0_), channel_id=1, source_target_pairs={{0,6},{1,7},{2,4},{3,5},{4,2},{5,3},{6,0},{7,1},{8,14},{9,15},{10,... | collective-permute-start | bytes 294920 | tf_op jit(solution)/shard_map/ppermute | solution.py:614
  32.5 1.6 %collective-permute-start.16 = (f32[144,128]{1,0:T(8,128)S(1)}, f32[144,128]{1,0:T(8,128)S(1)}, u32[]{:S(2)}, u32[]{:S(2)}) collective-permute-start(f32[144,128]{1,0:T(8,128)S(1)} %shard_map.93), channel_id=1, source_target_pairs={{0,8},{8,0},{16,24},{24,16},{1,9},{9,1},{17,25},{25,17},{2,10},{10... | collective-permute-start | bytes 221192 | tf_op jit(solution)/shard_map/ppermute | solution.py:637
  34.1 1.1 %collective-permute-start.15 = (f32[192,128]{1,0:T(8,128)S(1)}, f32[192,128]{1,0:T(8,128)S(1)}, u32[]{:S(2)}, u32[]{:S(2)}) collective-permute-start(f32[192,128]{1,0:T(8,128)S(1)} %get-tuple-element.40.refs_0_), channel_id=1, source_target_pairs={{0,4},{1,5},{2,6},{3,7},{4,0},{5,1},{6,2},{7,3},{8,12},{9,13},{10,... | collective-permute-start | bytes 294920 | tf_op jit(solution)/shard_map/ppermute | solution.py:614
  35.2 1.3 %collective-permute-start.14 = (f32[192,128]{1,0:T(8,128)S(1)}, f32[192,128]{1,0:T(8,128)S(1)}, u32[]{:S(2)}, u32[]{:S(2)}) collective-permute-start(f32[192,128]{1,0:T(8,128)S(1)} %get-tuple-element.40.refs_0_), channel_id=1, source_target_pairs={{0,2},{1,3},{2,0},{3,1},{4,6},{5,7},{6,4},{7,5},{8,10},{9,11},{10,... | collective-permute-start | bytes 294920 | tf_op jit(solution)/shard_map/ppermute | solution.py:614
  36.9 1.6 %collective-permute-start.17 = (f32[144,128]{1,0:T(8,128)S(1)}, f32[144,128]{1,0:T(8,128)S(1)}, u32[]{:S(2)}, u32[]{:S(2)}) collective-permute-start(f32[144,128]{1,0:T(8,128)S(1)} %add.6.one_ref), channel_id=1, source_target_pairs={{0,16},{8,24},{16,0},{24,8},{1,17},{9,25},{17,1},{25,9},{2,18},{10... | collective-permute-start | bytes 221192 | tf_op jit(solution)/shard_map/ppermute | solution.py:639
  38.5 2.0 %collective-permute-done.14.refs_1_ = f32[192,128]{1,0:T(8,128)S(1)} collective-permute-done((f32[192,128]{1,0:T(8,128)S(1)}, f32[192,128]{1,0:T(8,128)S(1)}, u32[]{:S(2)}, u32[]{:S(2)}) %collective-permute-start.14) | collective-permute-done | bytes 98336 | tf_op jit(solution)/shard_map/ppermute | solution.py:614
  40.5 0.8 %collective-permute-done.17.two_ref = f32[144,128]{1,0:T(8,128)S(1)} collective-permute-done((f32[144,128]{1,0:T(8,128)S(1)}, f32[144,128]{1,0:T(8,128)S(1)}, u32[]{:S(2)}, u32[]{:S(2)}) %collective-permute-start.17) | collective-permute-done | bytes 73760 | tf_op jit(solution)/shard_map/ppermute | solution.py:639
  41.4 1.0 %shard_map.94 = (f32[128,256]{1,0:T(8,128)S(1)}, f32[128,256]{1,0:T(8,128)S(1)}, f32[128,128]{1,0:T(8,128)S(1)}) custom-call(f32[144,128]{1,0:T(8,128)S(1)} %add.6.one_ref, f32[144,128]{1,0:T(8,128)S(1)} %collective-permute-done.17.two_ref, f32[128,256]{1,0:T(8,128)S(1)} %get-tuple-element.41.gains_ref, f32[256,128]{1,0:T(8,128)S(1)} %get-tuple-element.33.refs_12_.basis_ref), custom_call_target="tpu_custom_call" | custom-call | flops 20000000 | bytes 737280 | tf_op jit(solution)/shard_map/pallas_call | solution.py:600
  42.6 1.3 %collective-permute-done.21.refs_6_ = f32[192,128]{1,0:T(8,128)S(1)} collective-permute-done((f32[192,128]{1,0:T(8,128)S(1)}, f32[192,128]{1,0:T(8,128)S(1)}, u32[]{:S(2)}, u32[]{:S(2)}) %collective-permute-start.21) | collective-permute-done | bytes 98336 | tf_op jit(solution)/shard_map/ppermute | solution.py:622
  43.9 1.5 %shard_map.97 = (f32[128,256]{1,0:T(8,128)S(1)}, f32[192,128]{1,0:T(8,128)S(1)}) custom-call(f32[192,128]{1,0:T(8,128)S(1)} %get-tuple-element.40.refs_0_, f32[192,128]{1,0:T(8,128)S(1)} %collective-permute-done.14.refs_1_, f32[192,128]{1,0:T(8,128)S(1)} %shard_map.95.refs_2_, f32[192,128]{1,0:T(8,128)S(1)} %shard_map.96.refs_3_, ...), custom_call_target="tpu_custom_call" | custom-call | flops 20000000 | bytes 4849664 | tf_op jit(solution)/shard_map/pallas_call | solution.py:600
  45.4 2.6 %collective-permute-start.27 = (f32[192,128]{1,0:T(8,128)S(1)}, f32[192,128]{1,0:T(8,128)S(1)}, u32[]{:S(2)}, u32[]{:S(2)}) collective-permute-start(f32[192,128]{1,0:T(8,128)S(1)} %get-tuple-element.43.refs_0_), channel_id=1, source_target_pairs={{0,6},{1,7},{2,4},{3,5},{4,2},{5,3},{6,0},{7,1},{8,14},{9,15},{10,... | collective-permute-start | bytes 294920 | tf_op jit(solution)/shard_map/ppermute | solution.py:614
  48.2 1.6 %collective-permute-start.25 = (f32[128,128]{1,0:T(8,128)S(1)}, f32[128,128]{1,0:T(8,128)S(1)}, u32[]{:S(2)}, u32[]{:S(2)}) collective-permute-start(f32[128,128]{1,0:T(8,128)S(1)} %shard_map.98), channel_id=1, source_target_pairs={{0,8},{8,0},{16,24},{24,16},{1,9},{9,1},{17,25},{25,17},{2,10},{10... | collective-permute-start | bytes 196616 | tf_op jit(solution)/shard_map/ppermute | solution.py:637
  49.8 1.9 %collective-permute-start.23 = (f32[192,128]{1,0:T(8,128)S(1)}, f32[192,128]{1,0:T(8,128)S(1)}, u32[]{:S(2)}, u32[]{:S(2)}) collective-permute-start(f32[192,128]{1,0:T(8,128)S(1)} %get-tuple-element.43.refs_0_), channel_id=1, source_target_pairs={{0,2},{1,3},{2,0},{3,1},{4,6},{5,7},{6,4},{7,5},{8,10},{9,11},{10,... | collective-permute-start | bytes 294920 | tf_op jit(solution)/shard_map/ppermute | solution.py:614
  51.7 0.9 %collective-permute-done.25 = f32[128,128]{1,0:T(8,128)S(1)} collective-permute-done((f32[128,128]{1,0:T(8,128)S(1)}, f32[128,128]{1,0:T(8,128)S(1)}, u32[]{:S(2)}, u32[]{:S(2)}) %collective-permute-start.25) | collective-permute-done | bytes 65568 | tf_op jit(solution)/shard_map/ppermute | solution.py:637
  52.6 1.6 %collective-permute-start.26 = (f32[128,128]{1,0:T(8,128)S(1)}, f32[128,128]{1,0:T(8,128)S(1)}, u32[]{:S(2)}, u32[]{:S(2)}) collective-permute-start(f32[128,128]{1,0:T(8,128)S(1)} %add.7.one_ref), channel_id=1, source_target_pairs={{0,16},{8,24},{16,0},{24,8},{1,17},{9,25},{17,1},{25,9},{2,18},{10... | collective-permute-start | bytes 196616 | tf_op jit(solution)/shard_map/ppermute | solution.py:639
  54.2 1.1 %collective-permute-done.23.refs_1_ = f32[192,128]{1,0:T(8,128)S(1)} collective-permute-done((f32[192,128]{1,0:T(8,128)S(1)}, f32[192,128]{1,0:T(8,128)S(1)}, u32[]{:S(2)}, u32[]{:S(2)}) %collective-permute-start.23) | collective-permute-done | bytes 98336 | tf_op jit(solution)/shard_map/ppermute | solution.py:614
  55.3 1.6 %collective-permute-done.26.two_ref = f32[128,128]{1,0:T(8,128)S(1)} collective-permute-done((f32[128,128]{1,0:T(8,128)S(1)}, f32[128,128]{1,0:T(8,128)S(1)}, u32[]{:S(2)}, u32[]{:S(2)}) %collective-permute-start.26) | collective-permute-done | bytes 65568 | tf_op jit(solution)/shard_map/ppermute | solution.py:639
  57.5 1.3 %collective-permute-done.30.refs_6_ = f32[192,128]{1,0:T(8,128)S(1)} collective-permute-done((f32[192,128]{1,0:T(8,128)S(1)}, f32[192,128]{1,0:T(8,128)S(1)}, u32[]{:S(2)}, u32[]{:S(2)}) %collective-permute-start.30) | collective-permute-done | bytes 98336 | tf_op jit(solution)/shard_map/ppermute | solution.py:622
  59.6 2.5 %collective-permute-start.34 = (f32[40,128]{1,0:T(8,128)S(1)}, f32[40,128]{1,0:T(8,128)S(1)}, u32[]{:S(2)}, u32[]{:S(2)}) collective-permute-start(f32[40,128]{1,0:T(8,128)S(1)} %get-tuple-element.51.refs_0_), channel_id=1, source_target_pairs={{0,24},{8,16},{16,8},{24,0},{1,25},{9,17},{17,9},{25,1},{2,26},{10... | collective-permute-start | bytes 61448 | tf_op jit(solution)/shard_map/ppermute | solution.py:629
  63.1 1.0 %shard_map.103 = f32[8,32,64]{2,1,0:T(8,128)} custom-call(f32[128,128]{1,0:T(8,128)S(1)} %get-tuple-element.50.gains_ref), custom_call_target="tpu_custom_call" | custom-call | flops 20000000 | bytes 131072 | tf_op jit(solution)/shard_map/pallas_call | solution.py:600
  64.3 1.5 %collective-permute-done.33.refs_2_ = f32[40,128]{1,0:T(8,128)S(1)} collective-permute-done((f32[40,128]{1,0:T(8,128)S(1)}, f32[40,128]{1,0:T(8,128)S(1)}, u32[]{:S(2)}, u32[]{:S(2)}) %collective-permute-start.33) | collective-permute-done | bytes 20512 | tf_op jit(solution)/shard_map/ppermute | solution.py:629
  66.3 0.9 %shard_map.104 = f32[9,8,64]{2,1,0:T(8,128)} custom-call(f32[40,128]{1,0:T(8,128)S(1)} %get-tuple-element.51.refs_0_, f32[40,128]{1,0:T(8,128)S(1)} %collective-permute-done.32.refs_1_, f32[40,128]{1,0:T(8,128)S(1)} %collective-permute-done.33.refs_2_, f32[40,128]{1,0:T(8,128)S(1)} %collective-permute-done.34.refs_3_, ...), custom_call_target="tpu_custom_call" | custom-call | flops 20000000 | bytes 165888 | tf_op jit(solution)/shard_map/pallas_call | solution.py:600
  (59 shorter events, 9.9 us)
Async XLA Ops:
  1.9 11.6 %collective-permute-start.3 = (f32[136,128]{1,0:T(8,128)S(1)}, f32[136,128]{1,0:T(8,128)S(1)}, u32[]{:S(2)}, u32[]{:S(2)}) collective-permute-start(f32[136,128]{1,0:T(8,128)S(1)} %shard_map.86.refs_0_), channel_id=1, source_target_pairs={{0,1},{1,0},{2,3},{3,2},{4,5},{5,4},{6,7},{7,6},{8,9},{9,8},{10,11... | collective-permute-start | bytes 208904 | tf_op jit(solution)/shard_map/ppermute | solution.py:622
  2.5 9.8 %collective-permute-start.2 = (f32[136,128]{1,0:T(8,128)S(1)}, f32[136,128]{1,0:T(8,128)S(1)}, u32[]{:S(2)}, u32[]{:S(2)}) collective-permute-start(f32[136,128]{1,0:T(8,128)S(1)} %shard_map.86.refs_0_), channel_id=1, source_target_pairs={{0,6},{1,7},{2,4},{3,5},{4,2},{5,3},{6,0},{7,1},{8,14},{9,15},{10,... | collective-permute-start | bytes 208904 | tf_op jit(solution)/shard_map/ppermute | solution.py:614
  7.1 6.4 %collective-permute-start.1 = (f32[136,128]{1,0:T(8,128)S(1)}, f32[136,128]{1,0:T(8,128)S(1)}, u32[]{:S(2)}, u32[]{:S(2)}) collective-permute-start(f32[136,128]{1,0:T(8,128)S(1)} %shard_map.86.refs_0_), channel_id=1, source_target_pairs={{0,4},{1,5},{2,6},{3,7},{4,0},{5,1},{6,2},{7,3},{8,12},{9,13},{10,... | collective-permute-start | bytes 208904 | tf_op jit(solution)/shard_map/ppermute | solution.py:614
  7.1 5.2 %collective-permute-start = (f32[136,128]{1,0:T(8,128)S(1)}, f32[136,128]{1,0:T(8,128)S(1)}, u32[]{:S(2)}, u32[]{:S(2)}) collective-permute-start(f32[136,128]{1,0:T(8,128)S(1)} %shard_map.86.refs_0_), channel_id=1, source_target_pairs={{0,2},{1,3},{2,0},{3,1},{4,6},{5,7},{6,4},{7,5},{8,10},{9,11},{10,... | collective-permute-start | bytes 208904 | tf_op jit(solution)/shard_map/ppermute | solution.py:614
  12.2 1.3 %collective-permute-start.6 = (f32[136,128]{1,0:T(8,128)S(1)}, f32[136,128]{1,0:T(8,128)S(1)}, u32[]{:S(2)}, u32[]{:S(2)}) collective-permute-start(f32[136,128]{1,0:T(8,128)S(1)} %collective-permute-done.2.refs_3_), channel_id=1, source_target_pairs={{0,1},{1,0},{2,3},{3,2},{4,5},{5,4},{6,7},{7,6},{8,9},{9,8},{10,11... | collective-permute-start | bytes 208904 | tf_op jit(solution)/shard_map/ppermute | solution.py:622
  12.3 1.4 %collective-permute-start.4 = (f32[136,128]{1,0:T(8,128)S(1)}, f32[136,128]{1,0:T(8,128)S(1)}, u32[]{:S(2)}, u32[]{:S(2)}) collective-permute-start(f32[136,128]{1,0:T(8,128)S(1)} %collective-permute-done.refs_1_), channel_id=1, source_target_pairs={{0,1},{1,0},{2,3},{3,2},{4,5},{5,4},{6,7},{7,6},{8,9},{9,8},{10,11... | collective-permute-start | bytes 208904 | tf_op jit(solution)/shard_map/ppermute | solution.py:622
  16.1 9.1 %collective-permute-start.8 = (f32[192,128]{1,0:T(8,128)S(1)}, f32[192,128]{1,0:T(8,128)S(1)}, u32[]{:S(2)}, u32[]{:S(2)}) collective-permute-start(f32[192,128]{1,0:T(8,128)S(1)} %get-tuple-element.30.refs_0_), channel_id=1, source_target_pairs={{0,4},{1,5},{2,6},{3,7},{4,0},{5,1},{6,2},{7,3},{8,12},{9,13},{10,... | collective-permute-start | bytes 294920 | tf_op jit(solution)/shard_map/ppermute | solution.py:614
  17.7 7.4 %collective-permute-start.7 = (f32[192,128]{1,0:T(8,128)S(1)}, f32[192,128]{1,0:T(8,128)S(1)}, u32[]{:S(2)}, u32[]{:S(2)}) collective-permute-start(f32[192,128]{1,0:T(8,128)S(1)} %get-tuple-element.30.refs_0_), channel_id=1, source_target_pairs={{0,2},{1,3},{2,0},{3,1},{4,6},{5,7},{6,4},{7,5},{8,10},{9,11},{10,... | collective-permute-start | bytes 294920 | tf_op jit(solution)/shard_map/ppermute | solution.py:614
  19.8 7.5 %collective-permute-start.9 = (f32[192,128]{1,0:T(8,128)S(1)}, f32[192,128]{1,0:T(8,128)S(1)}, u32[]{:S(2)}, u32[]{:S(2)}) collective-permute-start(f32[192,128]{1,0:T(8,128)S(1)} %get-tuple-element.30.refs_0_), channel_id=1, source_target_pairs={{0,6},{1,7},{2,4},{3,5},{4,2},{5,3},{6,0},{7,1},{8,14},{9,15},{10,... | collective-permute-start | bytes 294920 | tf_op jit(solution)/shard_map/ppermute | solution.py:614
  20.6 7.2 %collective-permute-start.10 = (f32[192,128]{1,0:T(8,128)S(1)}, f32[192,128]{1,0:T(8,128)S(1)}, u32[]{:S(2)}, u32[]{:S(2)}) collective-permute-start(f32[192,128]{1,0:T(8,128)S(1)} %get-tuple-element.30.refs_0_), channel_id=1, source_target_pairs={{0,1},{1,0},{2,3},{3,2},{4,5},{5,4},{6,7},{7,6},{8,9},{9,8},{10,11... | collective-permute-start | bytes 294920 | tf_op jit(solution)/shard_map/ppermute | solution.py:622
  25.2 3.3 %collective-permute-start.11 = (f32[192,128]{1,0:T(8,128)S(1)}, f32[192,128]{1,0:T(8,128)S(1)}, u32[]{:S(2)}, u32[]{:S(2)}) collective-permute-start(f32[192,128]{1,0:T(8,128)S(1)} %get-tuple-element.35.refs_1_), channel_id=1, source_target_pairs={{0,1},{1,0},{2,3},{3,2},{4,5},{5,4},{6,7},{7,6},{8,9},{9,8},{10,11... | collective-permute-start | bytes 294920 | tf_op jit(solution)/shard_map/ppermute | solution.py:622
  27.2 1.5 %collective-permute-start.12 = (f32[192,128]{1,0:T(8,128)S(1)}, f32[192,128]{1,0:T(8,128)S(1)}, u32[]{:S(2)}, u32[]{:S(2)}) collective-permute-start(f32[192,128]{1,0:T(8,128)S(1)} %get-tuple-element.36.refs_2_), channel_id=1, source_target_pairs={{0,1},{1,0},{2,3},{3,2},{4,5},{5,4},{6,7},{7,6},{8,9},{9,8},{10,11... | collective-permute-start | bytes 294920 | tf_op jit(solution)/shard_map/ppermute | solution.py:622
  30.2 8.4 %collective-permute-start.18 = (f32[192,128]{1,0:T(8,128)S(1)}, f32[192,128]{1,0:T(8,128)S(1)}, u32[]{:S(2)}, u32[]{:S(2)}) collective-permute-start(f32[192,128]{1,0:T(8,128)S(1)} %get-tuple-element.40.refs_0_), channel_id=1, source_target_pairs={{0,6},{1,7},{2,4},{3,5},{4,2},{5,3},{6,0},{7,1},{8,14},{9,15},{10,... | collective-permute-start | bytes 294920 | tf_op jit(solution)/shard_map/ppermute | solution.py:614
  32.5 4.4 %collective-permute-start.16 = (f32[144,128]{1,0:T(8,128)S(1)}, f32[144,128]{1,0:T(8,128)S(1)}, u32[]{:S(2)}, u32[]{:S(2)}) collective-permute-start(f32[144,128]{1,0:T(8,128)S(1)} %shard_map.93), channel_id=1, source_target_pairs={{0,8},{8,0},{16,24},{24,16},{1,9},{9,1},{17,25},{25,17},{2,10},{10... | collective-permute-start | bytes 221192 | tf_op jit(solution)/shard_map/ppermute | solution.py:637
  34.1 8.6 %collective-permute-start.19 = (f32[192,128]{1,0:T(8,128)S(1)}, f32[192,128]{1,0:T(8,128)S(1)}, u32[]{:S(2)}, u32[]{:S(2)}) collective-permute-start(f32[192,128]{1,0:T(8,128)S(1)} %get-tuple-element.40.refs_0_), channel_id=1, source_target_pairs={{0,1},{1,0},{2,3},{3,2},{4,5},{5,4},{6,7},{7,6},{8,9},{9,8},{10,11... | collective-permute-start | bytes 294920 | tf_op jit(solution)/shard_map/ppermute | solution.py:622
  34.1 8.6 %collective-permute-start.15 = (f32[192,128]{1,0:T(8,128)S(1)}, f32[192,128]{1,0:T(8,128)S(1)}, u32[]{:S(2)}, u32[]{:S(2)}) collective-permute-start(f32[192,128]{1,0:T(8,128)S(1)} %get-tuple-element.40.refs_0_), channel_id=1, source_target_pairs={{0,4},{1,5},{2,6},{3,7},{4,0},{5,1},{6,2},{7,3},{8,12},{9,13},{10,... | collective-permute-start | bytes 294920 | tf_op jit(solution)/shard_map/ppermute | solution.py:614
  35.2 5.4 %collective-permute-start.14 = (f32[192,128]{1,0:T(8,128)S(1)}, f32[192,128]{1,0:T(8,128)S(1)}, u32[]{:S(2)}, u32[]{:S(2)}) collective-permute-start(f32[192,128]{1,0:T(8,128)S(1)} %get-tuple-element.40.refs_0_), channel_id=1, source_target_pairs={{0,2},{1,3},{2,0},{3,1},{4,6},{5,7},{6,4},{7,5},{8,10},{9,11},{10,... | collective-permute-start | bytes 294920 | tf_op jit(solution)/shard_map/ppermute | solution.py:614
  36.9 4.4 %collective-permute-start.17 = (f32[144,128]{1,0:T(8,128)S(1)}, f32[144,128]{1,0:T(8,128)S(1)}, u32[]{:S(2)}, u32[]{:S(2)}) collective-permute-start(f32[144,128]{1,0:T(8,128)S(1)} %add.6.one_ref), channel_id=1, source_target_pairs={{0,16},{8,24},{16,0},{24,8},{1,17},{9,25},{17,1},{25,9},{2,18},{10... | collective-permute-start | bytes 221192 | tf_op jit(solution)/shard_map/ppermute | solution.py:639
  38.5 4.1 %collective-permute-start.22 = (f32[192,128]{1,0:T(8,128)S(1)}, f32[192,128]{1,0:T(8,128)S(1)}, u32[]{:S(2)}, u32[]{:S(2)}) collective-permute-start(f32[192,128]{1,0:T(8,128)S(1)} %shard_map.96.refs_3_), channel_id=1, source_target_pairs={{0,1},{1,0},{2,3},{3,2},{4,5},{5,4},{6,7},{7,6},{8,9},{9,8},{10,11... | collective-permute-start | bytes 294920 | tf_op jit(solution)/shard_map/ppermute | solution.py:622
  40.5 2.1 %collective-permute-start.20 = (f32[192,128]{1,0:T(8,128)S(1)}, f32[192,128]{1,0:T(8,128)S(1)}, u32[]{:S(2)}, u32[]{:S(2)}) collective-permute-start(f32[192,128]{1,0:T(8,128)S(1)} %collective-permute-done.14.refs_1_), channel_id=1, source_target_pairs={{0,1},{1,0},{2,3},{3,2},{4,5},{5,4},{6,7},{7,6},{8,9},{9,8},{10,11... | collective-permute-start | bytes 294920 | tf_op jit(solution)/shard_map/ppermute | solution.py:622
  45.4 8.8 %collective-permute-start.27 = (f32[192,128]{1,0:T(8,128)S(1)}, f32[192,128]{1,0:T(8,128)S(1)}, u32[]{:S(2)}, u32[]{:S(2)}) collective-permute-start(f32[192,128]{1,0:T(8,128)S(1)} %get-tuple-element.43.refs_0_), channel_id=1, source_target_pairs={{0,6},{1,7},{2,4},{3,5},{4,2},{5,3},{6,0},{7,1},{8,14},{9,15},{10,... | collective-permute-start | bytes 294920 | tf_op jit(solution)/shard_map/ppermute | solution.py:614
  48.2 4.3 %collective-permute-start.25 = (f32[128,128]{1,0:T(8,128)S(1)}, f32[128,128]{1,0:T(8,128)S(1)}, u32[]{:S(2)}, u32[]{:S(2)}) collective-permute-start(f32[128,128]{1,0:T(8,128)S(1)} %shard_map.98), channel_id=1, source_target_pairs={{0,8},{8,0},{16,24},{24,16},{1,9},{9,1},{17,25},{25,17},{2,10},{10... | collective-permute-start | bytes 196616 | tf_op jit(solution)/shard_map/ppermute | solution.py:637
  49.8 7.7 %collective-permute-start.28 = (f32[192,128]{1,0:T(8,128)S(1)}, f32[192,128]{1,0:T(8,128)S(1)}, u32[]{:S(2)}, u32[]{:S(2)}) collective-permute-start(f32[192,128]{1,0:T(8,128)S(1)} %get-tuple-element.43.refs_0_), channel_id=1, source_target_pairs={{0,1},{1,0},{2,3},{3,2},{4,5},{5,4},{6,7},{7,6},{8,9},{9,8},{10,11... | collective-permute-start | bytes 294920 | tf_op jit(solution)/shard_map/ppermute | solution.py:622
  49.8 7.6 %collective-permute-start.24 = (f32[192,128]{1,0:T(8,128)S(1)}, f32[192,128]{1,0:T(8,128)S(1)}, u32[]{:S(2)}, u32[]{:S(2)}) collective-permute-start(f32[192,128]{1,0:T(8,128)S(1)} %get-tuple-element.43.refs_0_), channel_id=1, source_target_pairs={{0,4},{1,5},{2,6},{3,7},{4,0},{5,1},{6,2},{7,3},{8,12},{9,13},{10,... | collective-permute-start | bytes 294920 | tf_op jit(solution)/shard_map/ppermute | solution.py:614
  49.8 5.5 %collective-permute-start.23 = (f32[192,128]{1,0:T(8,128)S(1)}, f32[192,128]{1,0:T(8,128)S(1)}, u32[]{:S(2)}, u32[]{:S(2)}) collective-permute-start(f32[192,128]{1,0:T(8,128)S(1)} %get-tuple-element.43.refs_0_), channel_id=1, source_target_pairs={{0,2},{1,3},{2,0},{3,1},{4,6},{5,7},{6,4},{7,5},{8,10},{9,11},{10,... | collective-permute-start | bytes 294920 | tf_op jit(solution)/shard_map/ppermute | solution.py:614
  52.6 4.3 %collective-permute-start.26 = (f32[128,128]{1,0:T(8,128)S(1)}, f32[128,128]{1,0:T(8,128)S(1)}, u32[]{:S(2)}, u32[]{:S(2)}) collective-permute-start(f32[128,128]{1,0:T(8,128)S(1)} %add.7.one_ref), channel_id=1, source_target_pairs={{0,16},{8,24},{16,0},{24,8},{1,17},{9,25},{17,1},{25,9},{2,18},{10... | collective-permute-start | bytes 196616 | tf_op jit(solution)/shard_map/ppermute | solution.py:639
  54.2 3.4 %collective-permute-start.31 = (f32[192,128]{1,0:T(8,128)S(1)}, f32[192,128]{1,0:T(8,128)S(1)}, u32[]{:S(2)}, u32[]{:S(2)}) collective-permute-start(f32[192,128]{1,0:T(8,128)S(1)} %shard_map.101.refs_3_), channel_id=1, source_target_pairs={{0,1},{1,0},{2,3},{3,2},{4,5},{5,4},{6,7},{7,6},{8,9},{9,8},{10,11... | collective-permute-start | bytes 294920 | tf_op jit(solution)/shard_map/ppermute | solution.py:622
  55.3 2.3 %collective-permute-start.29 = (f32[192,128]{1,0:T(8,128)S(1)}, f32[192,128]{1,0:T(8,128)S(1)}, u32[]{:S(2)}, u32[]{:S(2)}) collective-permute-start(f32[192,128]{1,0:T(8,128)S(1)} %collective-permute-done.23.refs_1_), channel_id=1, source_target_pairs={{0,1},{1,0},{2,3},{3,2},{4,5},{5,4},{6,7},{7,6},{8,9},{9,8},{10,11... | collective-permute-start | bytes 294920 | tf_op jit(solution)/shard_map/ppermute | solution.py:622
  57.4 1.4 %collective-permute-start.30 = (f32[192,128]{1,0:T(8,128)S(1)}, f32[192,128]{1,0:T(8,128)S(1)}, u32[]{:S(2)}, u32[]{:S(2)}) collective-permute-start(f32[192,128]{1,0:T(8,128)S(1)} %shard_map.100.refs_2_), channel_id=1, source_target_pairs={{0,1},{1,0},{2,3},{3,2},{4,5},{5,4},{6,7},{7,6},{8,9},{9,8},{10,11... | collective-permute-start | bytes 294920 | tf_op jit(solution)/shard_map/ppermute | solution.py:622
  59.6 4.7 %collective-permute-start.34 = (f32[40,128]{1,0:T(8,128)S(1)}, f32[40,128]{1,0:T(8,128)S(1)}, u32[]{:S(2)}, u32[]{:S(2)}) collective-permute-start(f32[40,128]{1,0:T(8,128)S(1)} %get-tuple-element.51.refs_0_), channel_id=1, source_target_pairs={{0,24},{8,16},{16,8},{24,0},{1,25},{9,17},{17,9},{25,1},{2,26},{10... | collective-permute-start | bytes 61448 | tf_op jit(solution)/shard_map/ppermute | solution.py:629
  62.0 3.8 %collective-permute-start.33 = (f32[40,128]{1,0:T(8,128)S(1)}, f32[40,128]{1,0:T(8,128)S(1)}, u32[]{:S(2)}, u32[]{:S(2)}) collective-permute-start(f32[40,128]{1,0:T(8,128)S(1)} %get-tuple-element.51.refs_0_), channel_id=1, source_target_pairs={{0,16},{8,24},{16,0},{24,8},{1,17},{9,25},{17,1},{25,9},{2,18},{10... | collective-permute-start | bytes 61448 | tf_op jit(solution)/shard_map/ppermute | solution.py:629
  62.5 3.8 %collective-permute-start.32 = (f32[40,128]{1,0:T(8,128)S(1)}, f32[40,128]{1,0:T(8,128)S(1)}, u32[]{:S(2)}, u32[]{:S(2)}) collective-permute-start(f32[40,128]{1,0:T(8,128)S(1)} %get-tuple-element.51.refs_0_), channel_id=1, source_target_pairs={{0,8},{8,0},{16,24},{24,16},{1,9},{9,1},{17,25},{25,17},{2,10},{10... | collective-permute-start | bytes 61448 | tf_op jit(solution)/shard_map/ppermute | solution.py:629
  (3 other events, 3.9 us)

commit v10 on v8

--- a/solution.py
+++ b/solution.py
@@ -721,7 +721,7 @@
             shape(3 * KPAD, LANES, dtype=BF16),
         ],
     )
-    pieces = share_base(message, last=(scale,), ties=(1, 2))
+    pieces = share_base(message, last=(scale,), ties=(1,))
     gains, message = call(
         functools.partial(step_kernel, count),
         (*pieces, select, z, pen, scale, products),

time: 67.4 us -> 68.3 us (1.013)
  waiting for transfers between devices: 21.2 us -> 22.3 us
    ppermute x12, waiting for transfers between devices: 11.7 us -> 13.5 us  [share_base(): lax.ppermute(x, 'base', [(d, d ^ 2 * k) for d in range(devices)])]
    ppermute x2, waiting for transfers between devices: 2.07 us -> 1 us  [sum_band(): return (x, lax.ppermute(x, 'band', [(d, d ^ step) for d in range(devices)]))]
  transfers between devices with their start and end apart: 35 -> 35, of which waited for: 20 -> 17; matrix products, arithmetic and copies ran while one was open for 0% -> 0% of each run, Pallas kernels for 12% -> 12%
where the time goes in v10:
time: 68.3 us; the launch traced here: 68.1 us
  starting transfers between devices  29.8 us (44%)
  waiting for transfers between devices  22.3 us (33%)
  Pallas kernels  15.2 us (22%)
  between operations  0.8 us (1%)
    ppermute x12, starting transfers between devices, share_base(): lax.ppermute(x, 'base', [(d, d ^ 2 * k) for d in range(devices)])  18.1 us
    pallas_call x13, Pallas kernels, call(): pl.pallas_call(kernel, out_shape=shapes, in_specs=in_specs, out_specs=[vm...  15.2 us
    ppermute x12, waiting for transfers between devices, share_base(): lax.ppermute(x, 'base', [(d, d ^ 2 * k) for d in range(devices)])  13.5 us
    ppermute x16, waiting for transfers between devices, share_base(): lax.ppermute(y, 'base', [(d, d ^ 1) for d in range(devices)])  4.34 us
    ppermute x3, starting transfers between devices, share_band(): lax.ppermute(x, 'band', [(d, d ^ k) for d in range(devices)])  3.52 us
    ppermute x2, starting transfers between devices, sum_band(): return (x, lax.ppermute(x, 'band', [(d, d ^ step) for d in range(devices)]))  3.17 us
    ppermute x2, starting transfers between devices, sum_band(): x = x + lax.ppermute(x, 'band', [(d, d ^ step) for d in range(devices)])  2.74 us
    ppermute x3, waiting for transfers between devices, share_band(): lax.ppermute(x, 'band', [(d, d ^ k) for d in range(devices)])  2.4 us
  transfers between devices with their start and end apart: 35, of which 17 were waited for; matrix products, arithmetic and copies ran while one was open for 0% of the time, Pallas kernels for 12%

profile of v10, /device:TPU:0, one launch (start us, length us, event | category | flops | bytes accessed | tf_op | source)
XLA Modules:
  0.0 68.1 jit_solution(416574338007614754)
XLA Ops:
  0.6 1.3 %shard_map.86.refs_0_ = f32[136,128]{1,0:T(8,128)S(1)} custom-call(s32[2,2]{1,0:T(2,128)} %pair_hbm.3, f32[8,32,64]{2,1,0:T(8,128)} %start_hbm.1, f32[1,64]{1,0:T(1,128)} %bitcast.6, s32[2,256]{1,0:T(2,128)} %flag_hbm.3), custom_call_target="tpu_custom_call" | custom-call | flops 20000000 | bytes 137488 | tf_op jit(solution)/shard_map/pallas_call | solution.py:600
  2.5 4.7 %collective-permute-start.2 = (f32[136,128]{1,0:T(8,128)S(1)}, f32[136,128]{1,0:T(8,128)S(1)}, u32[]{:S(2)}, u32[]{:S(2)}) collective-permute-start(f32[136,128]{1,0:T(8,128)S(1)} %shard_map.86.refs_0_), channel_id=1, source_target_pairs={{0,6},{1,7},{2,4},{3,5},{4,2},{5,3},{6,0},{7,1},{8,14},{9,15},{10,... | collective-permute-start | bytes 208904 | tf_op jit(solution)/shard_map/ppermute | solution.py:614
  7.8 4.4 %shard_map.87 = (f32[48,8,16,128]{3,2,1,0:T(8,128)S(1)}, f32[256,128]{1,0:T(8,128)S(1)}, f32[256,128]{1,0:T(8,128)S(1)}, f32[256,128]{1,0:T(8,128)S(1)}, f32[8,256]{1,0:T(8,128)S(1)}) custom-call(s32[2,2]{1,0:T(2,128)} %pair_hbm.3, s32[1,64]{1,0:T(1,128)} %bitcast.9, s32[2,256]{1,0:T(2,128)} %flag_hbm.3, bf16[8,128,256]{2,1,0:T(8,128)(2,1)} %bitcast.7, ...), custom_call_target="tpu_custom_call" | custom-call | flops 2000000000 | bytes 4598032 | tf_op jit(solution)/shard_map/pallas_call | solution.py:600
  12.2 1.3 %collective-permute-done.1.refs_1_ = f32[136,128]{1,0:T(8,128)S(1)} collective-permute-done((f32[136,128]{1,0:T(8,128)S(1)}, f32[136,128]{1,0:T(8,128)S(1)}, u32[]{:S(2)}, u32[]{:S(2)}) %collective-permute-start.1) | collective-permute-done | bytes 69664 | tf_op jit(solution)/shard_map/ppermute | solution.py:614
  14.1 0.8 %collective-permute-done.6.refs_7_ = f32[136,128]{1,0:T(8,128)S(1)} collective-permute-done((f32[136,128]{1,0:T(8,128)S(1)}, f32[136,128]{1,0:T(8,128)S(1)}, u32[]{:S(2)}, u32[]{:S(2)}) %collective-permute-start.6) | collective-permute-done | bytes 69664 | tf_op jit(solution)/shard_map/ppermute | solution.py:622
  15.3 1.3 %shard_map.89 = (f32[128,128]{1,0:T(8,128)S(1)}, f32[192,128]{1,0:T(8,128)S(1)}) custom-call(f32[136,128]{1,0:T(8,128)S(1)} %shard_map.86.refs_0_, f32[136,128]{1,0:T(8,128)S(1)} %get-tuple-element.28.refs_1_, f32[136,128]{1,0:T(8,128)S(1)} %get-tuple-element.29.refs_2_, f32[136,128]{1,0:T(8,128)S(1)} %collective-permute-done.2.refs_3_, ...), custom_call_target="tpu_custom_call" | custom-call | flops 20000000 | bytes 3997696 | tf_op jit(solution)/shard_map/pallas_call | solution.py:600
  16.6 2.6 %collective-permute-start.9 = (f32[192,128]{1,0:T(8,128)S(1)}, f32[192,128]{1,0:T(8,128)S(1)}, u32[]{:S(2)}, u32[]{:S(2)}) collective-permute-start(f32[192,128]{1,0:T(8,128)S(1)} %get-tuple-element.32.refs_0_), channel_id=1, source_target_pairs={{0,6},{1,7},{2,4},{3,5},{4,2},{5,3},{6,0},{7,1},{8,14},{9,15},{10,... | collective-permute-start | bytes 294920 | tf_op jit(solution)/shard_map/ppermute | solution.py:614
  19.3 1.8 %collective-permute-start.7 = (f32[192,128]{1,0:T(8,128)S(1)}, f32[192,128]{1,0:T(8,128)S(1)}, u32[]{:S(2)}, u32[]{:S(2)}) collective-permute-start(f32[192,128]{1,0:T(8,128)S(1)} %get-tuple-element.32.refs_0_), channel_id=1, source_target_pairs={{0,2},{1,3},{2,0},{3,1},{4,6},{5,7},{6,4},{7,5},{8,10},{9,11},{10,... | collective-permute-start | bytes 294920 | tf_op jit(solution)/shard_map/ppermute | solution.py:614
  21.6 2.6 %collective-permute-done.9.refs_3_ = f32[192,128]{1,0:T(8,128)S(1)} collective-permute-done((f32[192,128]{1,0:T(8,128)S(1)}, f32[192,128]{1,0:T(8,128)S(1)}, u32[]{:S(2)}, u32[]{:S(2)}) %collective-permute-start.9) | collective-permute-done | bytes 98336 | tf_op jit(solution)/shard_map/ppermute | solution.py:614
  24.2 4.2 %collective-permute-done.8.refs_2_ = f32[192,128]{1,0:T(8,128)S(1)} collective-permute-done((f32[192,128]{1,0:T(8,128)S(1)}, f32[192,128]{1,0:T(8,128)S(1)}, u32[]{:S(2)}, u32[]{:S(2)}) %collective-permute-start.8) | collective-permute-done | bytes 98336 | tf_op jit(solution)/shard_map/ppermute | solution.py:614
  29.0 0.8 %collective-permute-done.12.refs_6_ = f32[192,128]{1,0:T(8,128)S(1)} collective-permute-done((f32[192,128]{1,0:T(8,128)S(1)}, f32[192,128]{1,0:T(8,128)S(1)}, u32[]{:S(2)}, u32[]{:S(2)}) %collective-permute-start.12) | collective-permute-done | bytes 98336 | tf_op jit(solution)/shard_map/ppermute | solution.py:622
  29.9 1.4 %shard_map.92 = (f32[128,256]{1,0:T(8,128)S(1)}, f32[192,128]{1,0:T(8,128)S(1)}) custom-call(f32[192,128]{1,0:T(8,128)S(1)} %get-tuple-element.32.refs_0_, f32[192,128]{1,0:T(8,128)S(1)} %shard_map.91.refs_1_, f32[192,128]{1,0:T(8,128)S(1)} %collective-permute-done.8.refs_2_, f32[192,128]{1,0:T(8,128)S(1)} %collective-permute-done.9.refs_3_, ...), custom_call_target="tpu_custom_call" | custom-call | flops 20000000 | bytes 4849664 | tf_op jit(solution)/shard_map/pallas_call | solution.py:600
  31.4 1.7 %collective-permute-start.18 = (f32[192,128]{1,0:T(8,128)S(1)}, f32[192,128]{1,0:T(8,128)S(1)}, u32[]{:S(2)}, u32[]{:S(2)}) collective-permute-start(f32[192,128]{1,0:T(8,128)S(1)} %get-tuple-element.40.refs_0_), channel_id=1, source_target_pairs={{0,6},{1,7},{2,4},{3,5},{4,2},{5,3},{6,0},{7,1},{8,14},{9,15},{10,... | collective-permute-start | bytes 294920 | tf_op jit(solution)/shard_map/ppermute | solution.py:614
  33.4 1.6 %collective-permute-start.16 = (f32[144,128]{1,0:T(8,128)S(1)}, f32[144,128]{1,0:T(8,128)S(1)}, u32[]{:S(2)}, u32[]{:S(2)}) collective-permute-start(f32[144,128]{1,0:T(8,128)S(1)} %shard_map.93), channel_id=1, source_target_pairs={{0,8},{8,0},{16,24},{24,16},{1,9},{9,1},{17,25},{25,17},{2,10},{10... | collective-permute-start | bytes 221192 | tf_op jit(solution)/shard_map/ppermute | solution.py:637
  35.0 2.8 %collective-permute-start.14 = (f32[192,128]{1,0:T(8,128)S(1)}, f32[192,128]{1,0:T(8,128)S(1)}, u32[]{:S(2)}, u32[]{:S(2)}) collective-permute-start(f32[192,128]{1,0:T(8,128)S(1)} %get-tuple-element.40.refs_0_), channel_id=1, source_target_pairs={{0,2},{1,3},{2,0},{3,1},{4,6},{5,7},{6,4},{7,5},{8,10},{9,11},{10,... | collective-permute-start | bytes 294920 | tf_op jit(solution)/shard_map/ppermute | solution.py:614
  37.8 1.6 %collective-permute-start.17 = (f32[144,128]{1,0:T(8,128)S(1)}, f32[144,128]{1,0:T(8,128)S(1)}, u32[]{:S(2)}, u32[]{:S(2)}) collective-permute-start(f32[144,128]{1,0:T(8,128)S(1)} %add.6.one_ref), channel_id=1, source_target_pairs={{0,16},{8,24},{16,0},{24,8},{1,17},{9,25},{17,1},{25,9},{2,18},{10... | collective-permute-start | bytes 221192 | tf_op jit(solution)/shard_map/ppermute | solution.py:639
  39.4 3.6 %collective-permute-done.14.refs_1_ = f32[192,128]{1,0:T(8,128)S(1)} collective-permute-done((f32[192,128]{1,0:T(8,128)S(1)}, f32[192,128]{1,0:T(8,128)S(1)}, u32[]{:S(2)}, u32[]{:S(2)}) %collective-permute-start.14) | collective-permute-done | bytes 98336 | tf_op jit(solution)/shard_map/ppermute | solution.py:614
  43.0 1.0 %shard_map.94 = (f32[128,256]{1,0:T(8,128)S(1)}, f32[128,256]{1,0:T(8,128)S(1)}, f32[128,128]{1,0:T(8,128)S(1)}) custom-call(f32[144,128]{1,0:T(8,128)S(1)} %add.6.one_ref, f32[144,128]{1,0:T(8,128)S(1)} %collective-permute-done.17.two_ref, f32[128,256]{1,0:T(8,128)S(1)} %get-tuple-element.41.gains_ref, f32[256,128]{1,0:T(8,128)S(1)} %get-tuple-element.35.refs_12_.basis_ref), custom_call_target="tpu_custom_call" | custom-call | flops 20000000 | bytes 737280 | tf_op jit(solution)/shard_map/pallas_call | solution.py:600
  44.6 0.9 %collective-permute-done.21.refs_6_ = f32[192,128]{1,0:T(8,128)S(1)} collective-permute-done((f32[192,128]{1,0:T(8,128)S(1)}, f32[192,128]{1,0:T(8,128)S(1)}, u32[]{:S(2)}, u32[]{:S(2)}) %collective-permute-start.21) | collective-permute-done | bytes 98336 | tf_op jit(solution)/shard_map/ppermute | solution.py:622
  45.5 1.4 %shard_map.97 = (f32[128,256]{1,0:T(8,128)S(1)}, f32[192,128]{1,0:T(8,128)S(1)}) custom-call(f32[192,128]{1,0:T(8,128)S(1)} %get-tuple-element.40.refs_0_, f32[192,128]{1,0:T(8,128)S(1)} %collective-permute-done.14.refs_1_, f32[192,128]{1,0:T(8,128)S(1)} %shard_map.95.refs_2_, f32[192,128]{1,0:T(8,128)S(1)} %shard_map.96.refs_3_, ...), custom_call_target="tpu_custom_call" | custom-call | flops 20000000 | bytes 4849664 | tf_op jit(solution)/shard_map/pallas_call | solution.py:600
  47.0 1.7 %collective-permute-start.27 = (f32[192,128]{1,0:T(8,128)S(1)}, f32[192,128]{1,0:T(8,128)S(1)}, u32[]{:S(2)}, u32[]{:S(2)}) collective-permute-start(f32[192,128]{1,0:T(8,128)S(1)} %get-tuple-element.43.refs_0_), channel_id=1, source_target_pairs={{0,6},{1,7},{2,4},{3,5},{4,2},{5,3},{6,0},{7,1},{8,14},{9,15},{10,... | collective-permute-start | bytes 294920 | tf_op jit(solution)/shard_map/ppermute | solution.py:614
  49.0 1.2 %collective-permute-start.25 = (f32[128,128]{1,0:T(8,128)S(1)}, f32[128,128]{1,0:T(8,128)S(1)}, u32[]{:S(2)}, u32[]{:S(2)}) collective-permute-start(f32[128,128]{1,0:T(8,128)S(1)} %shard_map.98), channel_id=1, source_target_pairs={{0,8},{8,0},{16,24},{24,16},{1,9},{9,1},{17,25},{25,17},{2,10},{10... | collective-permute-start | bytes 196616 | tf_op jit(solution)/shard_map/ppermute | solution.py:637
  50.2 2.2 %collective-permute-start.23 = (f32[192,128]{1,0:T(8,128)S(1)}, f32[192,128]{1,0:T(8,128)S(1)}, u32[]{:S(2)}, u32[]{:S(2)}) collective-permute-start(f32[192,128]{1,0:T(8,128)S(1)} %get-tuple-element.43.refs_0_), channel_id=1, source_target_pairs={{0,2},{1,3},{2,0},{3,1},{4,6},{5,7},{6,4},{7,5},{8,10},{9,11},{10,... | collective-permute-start | bytes 294920 | tf_op jit(solution)/shard_map/ppermute | solution.py:614
  52.4 0.9 %collective-permute-done.25 = f32[128,128]{1,0:T(8,128)S(1)} collective-permute-done((f32[128,128]{1,0:T(8,128)S(1)}, f32[128,128]{1,0:T(8,128)S(1)}, u32[]{:S(2)}, u32[]{:S(2)}) %collective-permute-start.25) | collective-permute-done | bytes 65568 | tf_op jit(solution)/shard_map/ppermute | solution.py:637
  53.3 1.6 %collective-permute-start.26 = (f32[128,128]{1,0:T(8,128)S(1)}, f32[128,128]{1,0:T(8,128)S(1)}, u32[]{:S(2)}, u32[]{:S(2)}) collective-permute-start(f32[128,128]{1,0:T(8,128)S(1)} %add.7.one_ref), channel_id=1, source_target_pairs={{0,16},{8,24},{16,0},{24,8},{1,17},{9,25},{17,1},{25,9},{2,18},{10... | collective-permute-start | bytes 196616 | tf_op jit(solution)/shard_map/ppermute | solution.py:639
  54.9 1.7 %collective-permute-done.23.refs_1_ = f32[192,128]{1,0:T(8,128)S(1)} collective-permute-done((f32[192,128]{1,0:T(8,128)S(1)}, f32[192,128]{1,0:T(8,128)S(1)}, u32[]{:S(2)}, u32[]{:S(2)}) %collective-permute-start.23) | collective-permute-done | bytes 98336 | tf_op jit(solution)/shard_map/ppermute | solution.py:614
  56.6 1.0 %collective-permute-done.26.two_ref = f32[128,128]{1,0:T(8,128)S(1)} collective-permute-done((f32[128,128]{1,0:T(8,128)S(1)}, f32[128,128]{1,0:T(8,128)S(1)}, u32[]{:S(2)}, u32[]{:S(2)}) %collective-permute-start.26) | collective-permute-done | bytes 65568 | tf_op jit(solution)/shard_map/ppermute | solution.py:639
  58.3 1.3 %collective-permute-done.30.refs_6_ = f32[192,128]{1,0:T(8,128)S(1)} collective-permute-done((f32[192,128]{1,0:T(8,128)S(1)}, f32[192,128]{1,0:T(8,128)S(1)}, u32[]{:S(2)}, u32[]{:S(2)}) %collective-permute-start.30) | collective-permute-done | bytes 98336 | tf_op jit(solution)/shard_map/ppermute | solution.py:622
  60.3 2.6 %collective-permute-start.34 = (f32[40,128]{1,0:T(8,128)S(1)}, f32[40,128]{1,0:T(8,128)S(1)}, u32[]{:S(2)}, u32[]{:S(2)}) collective-permute-start(f32[40,128]{1,0:T(8,128)S(1)} %get-tuple-element.51.refs_0_), channel_id=1, source_target_pairs={{0,24},{8,16},{16,8},{24,0},{1,25},{9,17},{17,9},{25,1},{2,26},{10... | collective-permute-start | bytes 61448 | tf_op jit(solution)/shard_map/ppermute | solution.py:629
  63.8 1.0 %shard_map.103 = f32[8,32,64]{2,1,0:T(8,128)} custom-call(f32[128,128]{1,0:T(8,128)S(1)} %get-tuple-element.50.gains_ref), custom_call_target="tpu_custom_call" | custom-call | flops 20000000 | bytes 131072 | tf_op jit(solution)/shard_map/pallas_call | solution.py:600
  65.0 1.7 %collective-permute-done.33.refs_2_ = f32[40,128]{1,0:T(8,128)S(1)} collective-permute-done((f32[40,128]{1,0:T(8,128)S(1)}, f32[40,128]{1,0:T(8,128)S(1)}, u32[]{:S(2)}, u32[]{:S(2)}) %collective-permute-start.33) | collective-permute-done | bytes 20512 | tf_op jit(solution)/shard_map/ppermute | solution.py:629
  67.2 0.9 %shard_map.104 = f32[9,8,64]{2,1,0:T(8,128)} custom-call(f32[40,128]{1,0:T(8,128)S(1)} %get-tuple-element.51.refs_0_, f32[40,128]{1,0:T(8,128)S(1)} %collective-permute-done.32.refs_1_, f32[40,128]{1,0:T(8,128)S(1)} %collective-permute-done.33.refs_2_, f32[40,128]{1,0:T(8,128)S(1)} %collective-permute-done.34.refs_3_, ...), custom_call_target="tpu_custom_call" | custom-call | flops 20000000 | bytes 165888 | tf_op jit(solution)/shard_map/pallas_call | solution.py:600
  (59 shorter events, 7.7 us)
Async XLA Ops:
  1.9 12.2 %collective-permute-start.3 = (f32[136,128]{1,0:T(8,128)S(1)}, f32[136,128]{1,0:T(8,128)S(1)}, u32[]{:S(2)}, u32[]{:S(2)}) collective-permute-start(f32[136,128]{1,0:T(8,128)S(1)} %shard_map.86.refs_0_), channel_id=1, source_target_pairs={{0,1},{1,0},{2,3},{3,2},{4,5},{5,4},{6,7},{7,6},{8,9},{9,8},{10,11... | collective-permute-start | bytes 208904 | tf_op jit(solution)/shard_map/ppermute | solution.py:622
  2.5 11.1 %collective-permute-start.2 = (f32[136,128]{1,0:T(8,128)S(1)}, f32[136,128]{1,0:T(8,128)S(1)}, u32[]{:S(2)}, u32[]{:S(2)}) collective-permute-start(f32[136,128]{1,0:T(8,128)S(1)} %shard_map.86.refs_0_), channel_id=1, source_target_pairs={{0,6},{1,7},{2,4},{3,5},{4,2},{5,3},{6,0},{7,1},{8,14},{9,15},{10,... | collective-permute-start | bytes 208904 | tf_op jit(solution)/shard_map/ppermute | solution.py:614
  7.1 6.4 %collective-permute-start.1 = (f32[136,128]{1,0:T(8,128)S(1)}, f32[136,128]{1,0:T(8,128)S(1)}, u32[]{:S(2)}, u32[]{:S(2)}) collective-permute-start(f32[136,128]{1,0:T(8,128)S(1)} %shard_map.86.refs_0_), channel_id=1, source_target_pairs={{0,4},{1,5},{2,6},{3,7},{4,0},{5,1},{6,2},{7,3},{8,12},{9,13},{10,... | collective-permute-start | bytes 208904 | tf_op jit(solution)/shard_map/ppermute | solution.py:614
  7.1 6.4 %collective-permute-start = (f32[136,128]{1,0:T(8,128)S(1)}, f32[136,128]{1,0:T(8,128)S(1)}, u32[]{:S(2)}, u32[]{:S(2)}) collective-permute-start(f32[136,128]{1,0:T(8,128)S(1)} %shard_map.86.refs_0_), channel_id=1, source_target_pairs={{0,2},{1,3},{2,0},{3,1},{4,6},{5,7},{6,4},{7,5},{8,10},{9,11},{10,... | collective-permute-start | bytes 208904 | tf_op jit(solution)/shard_map/ppermute | solution.py:614
  13.6 1.4 %collective-permute-start.4 = (f32[136,128]{1,0:T(8,128)S(1)}, f32[136,128]{1,0:T(8,128)S(1)}, u32[]{:S(2)}, u32[]{:S(2)}) collective-permute-start(f32[136,128]{1,0:T(8,128)S(1)} %get-tuple-element.28.refs_1_), channel_id=1, source_target_pairs={{0,1},{1,0},{2,3},{3,2},{4,5},{5,4},{6,7},{7,6},{8,9},{9,8},{10,11... | collective-permute-start | bytes 208904 | tf_op jit(solution)/shard_map/ppermute | solution.py:622
  13.6 1.4 %collective-permute-start.6 = (f32[136,128]{1,0:T(8,128)S(1)}, f32[136,128]{1,0:T(8,128)S(1)}, u32[]{:S(2)}, u32[]{:S(2)}) collective-permute-start(f32[136,128]{1,0:T(8,128)S(1)} %collective-permute-done.2.refs_3_), channel_id=1, source_target_pairs={{0,1},{1,0},{2,3},{3,2},{4,5},{5,4},{6,7},{7,6},{8,9},{9,8},{10,11... | collective-permute-start | bytes 208904 | tf_op jit(solution)/shard_map/ppermute | solution.py:622
  16.6 7.6 %collective-permute-start.9 = (f32[192,128]{1,0:T(8,128)S(1)}, f32[192,128]{1,0:T(8,128)S(1)}, u32[]{:S(2)}, u32[]{:S(2)}) collective-permute-start(f32[192,128]{1,0:T(8,128)S(1)} %get-tuple-element.32.refs_0_), channel_id=1, source_target_pairs={{0,6},{1,7},{2,4},{3,5},{4,2},{5,3},{6,0},{7,1},{8,14},{9,15},{10,... | collective-permute-start | bytes 294920 | tf_op jit(solution)/shard_map/ppermute | solution.py:614
  19.2 9.2 %collective-permute-start.8 = (f32[192,128]{1,0:T(8,128)S(1)}, f32[192,128]{1,0:T(8,128)S(1)}, u32[]{:S(2)}, u32[]{:S(2)}) collective-permute-start(f32[192,128]{1,0:T(8,128)S(1)} %get-tuple-element.32.refs_0_), channel_id=1, source_target_pairs={{0,4},{1,5},{2,6},{3,7},{4,0},{5,1},{6,2},{7,3},{8,12},{9,13},{10,... | collective-permute-start | bytes 294920 | tf_op jit(solution)/shard_map/ppermute | solution.py:614
  19.3 9.2 %collective-permute-start.7 = (f32[192,128]{1,0:T(8,128)S(1)}, f32[192,128]{1,0:T(8,128)S(1)}, u32[]{:S(2)}, u32[]{:S(2)}) collective-permute-start(f32[192,128]{1,0:T(8,128)S(1)} %get-tuple-element.32.refs_0_), channel_id=1, source_target_pairs={{0,2},{1,3},{2,0},{3,1},{4,6},{5,7},{6,4},{7,5},{8,10},{9,11},{10,... | collective-permute-start | bytes 294920 | tf_op jit(solution)/shard_map/ppermute | solution.py:614
  21.1 7.9 %collective-permute-start.10 = (f32[192,128]{1,0:T(8,128)S(1)}, f32[192,128]{1,0:T(8,128)S(1)}, u32[]{:S(2)}, u32[]{:S(2)}) collective-permute-start(f32[192,128]{1,0:T(8,128)S(1)} %get-tuple-element.32.refs_0_), channel_id=1, source_target_pairs={{0,1},{1,0},{2,3},{3,2},{4,5},{5,4},{6,7},{7,6},{8,9},{9,8},{10,11... | collective-permute-start | bytes 294920 | tf_op jit(solution)/shard_map/ppermute | solution.py:622
  24.2 4.7 %collective-permute-start.13 = (f32[192,128]{1,0:T(8,128)S(1)}, f32[192,128]{1,0:T(8,128)S(1)}, u32[]{:S(2)}, u32[]{:S(2)}) collective-permute-start(f32[192,128]{1,0:T(8,128)S(1)} %collective-permute-done.9.refs_3_), channel_id=1, source_target_pairs={{0,1},{1,0},{2,3},{3,2},{4,5},{5,4},{6,7},{7,6},{8,9},{9,8},{10,11... | collective-permute-start | bytes 294920 | tf_op jit(solution)/shard_map/ppermute | solution.py:622
  28.5 1.5 %collective-permute-start.11 = (f32[192,128]{1,0:T(8,128)S(1)}, f32[192,128]{1,0:T(8,128)S(1)}, u32[]{:S(2)}, u32[]{:S(2)}) collective-permute-start(f32[192,128]{1,0:T(8,128)S(1)} %shard_map.91.refs_1_), channel_id=1, source_target_pairs={{0,1},{1,0},{2,3},{3,2},{4,5},{5,4},{6,7},{7,6},{8,9},{9,8},{10,11... | collective-permute-start | bytes 294920 | tf_op jit(solution)/shard_map/ppermute | solution.py:622
  31.4 8.1 %collective-permute-start.18 = (f32[192,128]{1,0:T(8,128)S(1)}, f32[192,128]{1,0:T(8,128)S(1)}, u32[]{:S(2)}, u32[]{:S(2)}) collective-permute-start(f32[192,128]{1,0:T(8,128)S(1)} %get-tuple-element.40.refs_0_), channel_id=1, source_target_pairs={{0,6},{1,7},{2,4},{3,5},{4,2},{5,3},{6,0},{7,1},{8,14},{9,15},{10,... | collective-permute-start | bytes 294920 | tf_op jit(solution)/shard_map/ppermute | solution.py:614
  33.4 4.4 %collective-permute-start.16 = (f32[144,128]{1,0:T(8,128)S(1)}, f32[144,128]{1,0:T(8,128)S(1)}, u32[]{:S(2)}, u32[]{:S(2)}) collective-permute-start(f32[144,128]{1,0:T(8,128)S(1)} %shard_map.93), channel_id=1, source_target_pairs={{0,8},{8,0},{16,24},{24,16},{1,9},{9,1},{17,25},{25,17},{2,10},{10... | collective-permute-start | bytes 221192 | tf_op jit(solution)/shard_map/ppermute | solution.py:637
  35.0 9.6 %collective-permute-start.19 = (f32[192,128]{1,0:T(8,128)S(1)}, f32[192,128]{1,0:T(8,128)S(1)}, u32[]{:S(2)}, u32[]{:S(2)}) collective-permute-start(f32[192,128]{1,0:T(8,128)S(1)} %get-tuple-element.40.refs_0_), channel_id=1, source_target_pairs={{0,1},{1,0},{2,3},{3,2},{4,5},{5,4},{6,7},{7,6},{8,9},{9,8},{10,11... | collective-permute-start | bytes 294920 | tf_op jit(solution)/shard_map/ppermute | solution.py:622
  35.0 9.0 %collective-permute-start.15 = (f32[192,128]{1,0:T(8,128)S(1)}, f32[192,128]{1,0:T(8,128)S(1)}, u32[]{:S(2)}, u32[]{:S(2)}) collective-permute-start(f32[192,128]{1,0:T(8,128)S(1)} %get-tuple-element.40.refs_0_), channel_id=1, source_target_pairs={{0,4},{1,5},{2,6},{3,7},{4,0},{5,1},{6,2},{7,3},{8,12},{9,13},{10,... | collective-permute-start | bytes 294920 | tf_op jit(solution)/shard_map/ppermute | solution.py:614
  35.0 8.0 %collective-permute-start.14 = (f32[192,128]{1,0:T(8,128)S(1)}, f32[192,128]{1,0:T(8,128)S(1)}, u32[]{:S(2)}, u32[]{:S(2)}) collective-permute-start(f32[192,128]{1,0:T(8,128)S(1)} %get-tuple-element.40.refs_0_), channel_id=1, source_target_pairs={{0,2},{1,3},{2,0},{3,1},{4,6},{5,7},{6,4},{7,5},{8,10},{9,11},{10,... | collective-permute-start | bytes 294920 | tf_op jit(solution)/shard_map/ppermute | solution.py:614
  37.8 5.2 %collective-permute-start.17 = (f32[144,128]{1,0:T(8,128)S(1)}, f32[144,128]{1,0:T(8,128)S(1)}, u32[]{:S(2)}, u32[]{:S(2)}) collective-permute-start(f32[144,128]{1,0:T(8,128)S(1)} %add.6.one_ref), channel_id=1, source_target_pairs={{0,16},{8,24},{16,0},{24,8},{1,17},{9,25},{17,1},{25,9},{2,18},{10... | collective-permute-start | bytes 221192 | tf_op jit(solution)/shard_map/ppermute | solution.py:639
  39.4 5.2 %collective-permute-start.22 = (f32[192,128]{1,0:T(8,128)S(1)}, f32[192,128]{1,0:T(8,128)S(1)}, u32[]{:S(2)}, u32[]{:S(2)}) collective-permute-start(f32[192,128]{1,0:T(8,128)S(1)} %shard_map.96.refs_3_), channel_id=1, source_target_pairs={{0,1},{1,0},{2,3},{3,2},{4,5},{5,4},{6,7},{7,6},{8,9},{9,8},{10,11... | collective-permute-start | bytes 294920 | tf_op jit(solution)/shard_map/ppermute | solution.py:622
  43.0 1.6 %collective-permute-start.20 = (f32[192,128]{1,0:T(8,128)S(1)}, f32[192,128]{1,0:T(8,128)S(1)}, u32[]{:S(2)}, u32[]{:S(2)}) collective-permute-start(f32[192,128]{1,0:T(8,128)S(1)} %collective-permute-done.14.refs_1_), channel_id=1, source_target_pairs={{0,1},{1,0},{2,3},{3,2},{4,5},{5,4},{6,7},{7,6},{8,9},{9,8},{10,11... | collective-permute-start | bytes 294920 | tf_op jit(solution)/shard_map/ppermute | solution.py:622
  44.0 1.5 %collective-permute-start.21 = (f32[192,128]{1,0:T(8,128)S(1)}, f32[192,128]{1,0:T(8,128)S(1)}, u32[]{:S(2)}, u32[]{:S(2)}) collective-permute-start(f32[192,128]{1,0:T(8,128)S(1)} %shard_map.95.refs_2_), channel_id=1, source_target_pairs={{0,1},{1,0},{2,3},{3,2},{4,5},{5,4},{6,7},{7,6},{8,9},{9,8},{10,11... | collective-permute-start | bytes 294920 | tf_op jit(solution)/shard_map/ppermute | solution.py:622
  47.0 7.9 %collective-permute-start.27 = (f32[192,128]{1,0:T(8,128)S(1)}, f32[192,128]{1,0:T(8,128)S(1)}, u32[]{:S(2)}, u32[]{:S(2)}) collective-permute-start(f32[192,128]{1,0:T(8,128)S(1)} %get-tuple-element.43.refs_0_), channel_id=1, source_target_pairs={{0,6},{1,7},{2,4},{3,5},{4,2},{5,3},{6,0},{7,1},{8,14},{9,15},{10,... | collective-permute-start | bytes 294920 | tf_op jit(solution)/shard_map/ppermute | solution.py:614
  49.0 4.3 %collective-permute-start.25 = (f32[128,128]{1,0:T(8,128)S(1)}, f32[128,128]{1,0:T(8,128)S(1)}, u32[]{:S(2)}, u32[]{:S(2)}) collective-permute-start(f32[128,128]{1,0:T(8,128)S(1)} %shard_map.98), channel_id=1, source_target_pairs={{0,8},{8,0},{16,24},{24,16},{1,9},{9,1},{17,25},{25,17},{2,10},{10... | collective-permute-start | bytes 196616 | tf_op jit(solution)/shard_map/ppermute | solution.py:637
  50.2 8.1 %collective-permute-start.28 = (f32[192,128]{1,0:T(8,128)S(1)}, f32[192,128]{1,0:T(8,128)S(1)}, u32[]{:S(2)}, u32[]{:S(2)}) collective-permute-start(f32[192,128]{1,0:T(8,128)S(1)} %get-tuple-element.43.refs_0_), channel_id=1, source_target_pairs={{0,1},{1,0},{2,3},{3,2},{4,5},{5,4},{6,7},{7,6},{8,9},{9,8},{10,11... | collective-permute-start | bytes 294920 | tf_op jit(solution)/shard_map/ppermute | solution.py:622
  50.2 8.0 %collective-permute-start.24 = (f32[192,128]{1,0:T(8,128)S(1)}, f32[192,128]{1,0:T(8,128)S(1)}, u32[]{:S(2)}, u32[]{:S(2)}) collective-permute-start(f32[192,128]{1,0:T(8,128)S(1)} %get-tuple-element.43.refs_0_), channel_id=1, source_target_pairs={{0,4},{1,5},{2,6},{3,7},{4,0},{5,1},{6,2},{7,3},{8,12},{9,13},{10,... | collective-permute-start | bytes 294920 | tf_op jit(solution)/shard_map/ppermute | solution.py:614
  50.2 6.5 %collective-permute-start.23 = (f32[192,128]{1,0:T(8,128)S(1)}, f32[192,128]{1,0:T(8,128)S(1)}, u32[]{:S(2)}, u32[]{:S(2)}) collective-permute-start(f32[192,128]{1,0:T(8,128)S(1)} %get-tuple-element.43.refs_0_), channel_id=1, source_target_pairs={{0,2},{1,3},{2,0},{3,1},{4,6},{5,7},{6,4},{7,5},{8,10},{9,11},{10,... | collective-permute-start | bytes 294920 | tf_op jit(solution)/shard_map/ppermute | solution.py:614
  53.3 4.3 %collective-permute-start.26 = (f32[128,128]{1,0:T(8,128)S(1)}, f32[128,128]{1,0:T(8,128)S(1)}, u32[]{:S(2)}, u32[]{:S(2)}) collective-permute-start(f32[128,128]{1,0:T(8,128)S(1)} %add.7.one_ref), channel_id=1, source_target_pairs={{0,16},{8,24},{16,0},{24,8},{1,17},{9,25},{17,1},{25,9},{2,18},{10... | collective-permute-start | bytes 196616 | tf_op jit(solution)/shard_map/ppermute | solution.py:639
  54.9 3.4 %collective-permute-start.31 = (f32[192,128]{1,0:T(8,128)S(1)}, f32[192,128]{1,0:T(8,128)S(1)}, u32[]{:S(2)}, u32[]{:S(2)}) collective-permute-start(f32[192,128]{1,0:T(8,128)S(1)} %shard_map.101.refs_3_), channel_id=1, source_target_pairs={{0,1},{1,0},{2,3},{3,2},{4,5},{5,4},{6,7},{7,6},{8,9},{9,8},{10,11... | collective-permute-start | bytes 294920 | tf_op jit(solution)/shard_map/ppermute | solution.py:622
  56.6 1.6 %collective-permute-start.29 = (f32[192,128]{1,0:T(8,128)S(1)}, f32[192,128]{1,0:T(8,128)S(1)}, u32[]{:S(2)}, u32[]{:S(2)}) collective-permute-start(f32[192,128]{1,0:T(8,128)S(1)} %collective-permute-done.23.refs_1_), channel_id=1, source_target_pairs={{0,1},{1,0},{2,3},{3,2},{4,5},{5,4},{6,7},{7,6},{8,9},{9,8},{10,11... | collective-permute-start | bytes 294920 | tf_op jit(solution)/shard_map/ppermute | solution.py:622
  60.3 4.7 %collective-permute-start.34 = (f32[40,128]{1,0:T(8,128)S(1)}, f32[40,128]{1,0:T(8,128)S(1)}, u32[]{:S(2)}, u32[]{:S(2)}) collective-permute-start(f32[40,128]{1,0:T(8,128)S(1)} %get-tuple-element.51.refs_0_), channel_id=1, source_target_pairs={{0,24},{8,16},{16,8},{24,0},{1,25},{9,17},{17,9},{25,1},{2,26},{10... | collective-permute-start | bytes 61448 | tf_op jit(solution)/shard_map/ppermute | solution.py:629
  62.9 3.8 %collective-permute-start.33 = (f32[40,128]{1,0:T(8,128)S(1)}, f32[40,128]{1,0:T(8,128)S(1)}, u32[]{:S(2)}, u32[]{:S(2)}) collective-permute-start(f32[40,128]{1,0:T(8,128)S(1)} %get-tuple-element.51.refs_0_), channel_id=1, source_target_pairs={{0,16},{8,24},{16,0},{24,8},{1,17},{9,25},{17,1},{25,9},{2,18},{10... | collective-permute-start | bytes 61448 | tf_op jit(solution)/shard_map/ppermute | solution.py:629
  63.4 3.8 %collective-permute-start.32 = (f32[40,128]{1,0:T(8,128)S(1)}, f32[40,128]{1,0:T(8,128)S(1)}, u32[]{:S(2)}, u32[]{:S(2)}) collective-permute-start(f32[40,128]{1,0:T(8,128)S(1)} %get-tuple-element.51.refs_0_), channel_id=1, source_target_pairs={{0,8},{8,0},{16,24},{24,16},{1,9},{9,1},{17,25},{25,17},{2,10},{10... | collective-permute-start | bytes 61448 | tf_op jit(solution)/shard_map/ppermute | solution.py:629
  (3 other events, 3.9 us)
